TPU v7x, 32 devices: a whole 2x2x4 slice. The times are simulated.
32 devices in a mesh: groups: 2 (over y), prow: 4 (over z), pcol: 4 (over x, core).
Axes of the slice: x: 2, y: 2, z: 4, core: 2. Of those that a mesh axis runs over, the one named last changes fastest.
Arguments:
- right_side: float32 [8, 512, 512], P('groups', 'prow', 'pcol'), parts along dimension 0, may hold values from -6 to 6
- earlier: float32 [8, 512, 512], P('groups', 'prow', 'pcol'), parts along dimension 0, may hold values from -6 to 6
- inverse_diag: float32 [8, 512, 512], P('groups', 'prow', 'pcol'), parts along dimension 0, may hold values from -0.25 to 0.25
- dense_tiles: float32 [8, 7, 512, 512], P('groups', None, 'prow', 'pcol'), parts along dimension 0, may hold values from -0.09375 to 0.09375
- left_factor: float32 [8, 7, 512, 64], P('groups', None, 'prow'), parts along dimension 0, may hold values from -0.25 to 0.25
- right_factor: float32 [8, 7, 512, 64], P('groups', None, 'prow'), parts along dimension 0, may hold values from -0.25 to 0.25
- tile_ranks: int32 [8, 7], P('groups'), parts along dimension 0, may hold values from 1 to 64, as said below
- dense_flags: int32 [8, 7], P('groups'), parts along dimension 0, may hold values 0 or 1
Outputs:
- solved: float32 [8, 512, 512], P('groups', 'prow', 'pcol'), parts along dimension 0
There are 2 independent parts, one for each index of `groups`. A program takes and returns all parts, laid end to end along the dimension named above; each array names one. Nothing has to cross between parts.
Inputs may be any that keep to these rules, and one draw needn't show every extreme that they name: `tile_ranks`: ranks of the low-rank tiles; the padded rank 64 is reached by some tile.
All inputs are finite; a program needn't handle non-finite values.
Results may differ from a plain program's by a relative error of at most 0.0001.
Values sent between devices are 32-bit elements; how exact they have to be, the bound alone decides.
No kernel may reach another device: no remote copies, remote signals or barrier semaphores. Data moves between devices by JAX's collectives and lax.ppermute only.
A program may use at most 64 MiB of HBM per device.

v0:
```python
import jax
import jax.numpy as jnp
from jax import lax
from jax.sharding import PartitionSpec as P

HIGHEST = lax.Precision.HIGHEST


def local(
    right_side,
    earlier,
    inverse_diag,
    dense_tiles,
    left_factor,
    right_factor,
    tile_ranks,
    dense_flags,
):
    count_steps, rows_dev, rhs_dev = right_side.shape
    prev_cols = earlier.shape[0]
    rank_pad = left_factor.shape[3]
    tile_flags = dense_flags.astype(jnp.float32)
    columns = lax.broadcasted_iota(jnp.int32, tile_ranks.shape + (rank_pad,), 2)
    low_mask = (columns < tile_ranks[:, :, None]).astype(jnp.float32) * (1.0 - tile_flags)[
        :, :, None
    ]
    left_eff = left_factor * low_mask[:, :, None, :]
    tile_rows = (
        lax.all_gather(dense_tiles, "pcol", axis=3, tiled=True) * tile_flags[:, :, None, None]
    )
    inverse_rows = lax.all_gather(inverse_diag, "pcol", axis=2, tiled=True)
    early_tiles = tile_rows[:, :prev_cols]
    early_sum = jnp.einsum(
        "kjrc,jcs->krs",
        early_tiles,
        lax.all_gather(earlier, "prow", axis=1, tiled=True),
        precision=HIGHEST,
    )
    partial_value = jnp.einsum(
        "kjcq,jcs->kjqs", right_factor[:, :prev_cols], earlier, precision=HIGHEST
    )
    early_coeffs = lax.psum(partial_value, "prow")
    early_sum = early_sum + jnp.einsum(
        "kjrq,kjqs->krs", left_eff[:, :prev_cols], early_coeffs, precision=HIGHEST
    )
    pending = right_side - early_sum
    outputs = []
    for block_index in range(count_steps):
        residual_whole = lax.all_gather(pending[block_index], "prow", axis=0, tiled=True)
        solved_own = jnp.dot(inverse_rows[block_index], residual_whole, precision=HIGHEST)
        if block_index + 1 < count_steps:
            solved_whole = lax.all_gather(solved_own, "prow", axis=0, tiled=True)
        outputs.append(solved_own)
        if block_index + 1 < count_steps:
            column = prev_cols + block_index
            dense_part = jnp.einsum(
                "krc,cs->krs", tile_rows[block_index + 1 :, column], solved_whole, precision=HIGHEST
            )
            projected = jnp.einsum(
                "kcq,cs->kqs",
                right_factor[block_index + 1 :, column],
                solved_own,
                precision=HIGHEST,
            )
            projected = lax.psum(projected, "prow")
            low_part = jnp.einsum(
                "krq,kqs->krs", left_eff[block_index + 1 :, column], projected, precision=HIGHEST
            )
            pending = pending.at[block_index + 1 :].add(-(dense_part + low_part))
    return jnp.stack(outputs)


def solution(mesh):
    placed = (
        P("groups", "prow", "pcol"),
        P("groups", "prow", "pcol"),
        P("groups", "prow", "pcol"),
        P("groups", None, "prow", "pcol"),
        P("groups", None, "prow", None),
        P("groups", None, "prow", None),
        P("groups", None),
        P("groups", None),
    )
    return jax.shard_map(
        local, mesh=mesh, in_specs=placed, out_specs=P("groups", "prow", "pcol"), check_vma=False
    )
```

profile of v0, /device:TPU:0, one launch (start us, length us, event | category | flops | bytes accessed | tf_op | source)
XLA Modules:
  0.0 332.2 jit_solution(13144287237386075472)
XLA Ops:
  8.1 2.5 convolution_bitcast_fusion
  12.6 0.9 slice.142
  15.1 1.5 broadcast_multiply_fusion.1
  16.5 48.4 %all-gather.8.cloned.1.call-done = f32[4,7,128,512]{3,2,1,0:T(8,128)} async-done(((f32[4,7,128,128]{3,2,1,0:T(8,128)}), f32[4,7,128,512]{3,2,1,0:T(8,128)}) %all-gather.8.cloned.1.call-update) | async-done | bytes 7340048 | tf_op jit(solution)/shard_map/all_gather | solution.py:29
  64.9 7.4 %broadcast_multiply_fusion = f32[4,7,128,512]{3,2,1,0:T(8,128)} fusion(f32[4,7,128,512]{3,2,1,0:T(8,128)} %all-gather.8.cloned.1.call-done, f32[4,7]{1,0:T(4,128)S(1)} %convert_element_type.4), kind=kLoop, calls=%fused_computation | loop fusion | flops 1835008 | bytes 14680176 | tf_op jit(solution)/shard_map/mul | solution.py:29
  72.4 22.1 %all-gather.10.cloned.1.call-done = f32[4,512,128]{2,1,0:T(8,128)} async-done(((f32[4,128,128]{2,1,0:T(8,128)}), f32[4,512,128]{2,1,0:T(8,128)}) %all-gather.10.cloned.1.call-update) | async-done | bytes 1048592 | tf_op jit(solution)/shard_map/all_gather | solution.py:36
  94.5 5.9 %convolution_bitcast_fusion.1 = f32[4,128,128]{2,1,0:T(8,128)S(1)} fusion(f32[4,7,128,512]{3,2,1,0:T(8,128)} %broadcast_multiply_fusion, f32[4,512,128]{2,1,0:T(8,128)} %all-gather.10.cloned.1.call-done), kind=kOutput, calls=%fused_computation.2 | convolution fusion | flops 1610612736 | bytes 8650752 | tf_op jit(solution)/shard_map/kjrc,jcs->krs/dot_general | solution.py:33
  100.4 34.3 %all-reduce.4.cloned.1.call-done = f32[4,4,64,128]{3,2,1,0:T(8,128)} async-done(((f32[4,4,64,128]{3,2,1,0:T(8,128)}), f32[4,4,64,128]{3,2,1,0:T(8,128)}) %all-reduce.4.cloned.1.call-update) | async-done | bytes 524304 | tf_op jit(solution)/shard_map/psum | solution.py:42
  134.7 2.1 fusion.1
  136.8 14.4 %all-gather = f32[1,512,128]{2,1,0:T(8,128)S(1)} all-gather(f32[1,128,128]{2,1,0:T(8,128)S(1)} %slice.156), channel_id=2, replica_groups=mesh['groups'=2,'prow'=4,'pcol'=4] {'prow'}, dimensions={1}, use_global_device_ids=true | all-gather | bytes 327680 | tf_op jit(solution)/shard_map/all_gather | solution.py:49
  151.2 1.7 all-gather.12.cloned.1.call-done
  152.9 1.5 fusion.15
  154.5 13.9 %all_gather.34 = f32[512,128]{0,1:T(8,128)S(1)} all-gather(f32[128,128]{0,1:T(8,128)S(1)} %bitcast.120), channel_id=1, replica_groups=mesh['groups'=2,'prow'=4,'pcol'=4] {'prow'}, dimensions={0}, use_global_device_ids=true | all-gather | bytes 327680 | tf_op jit(solution)/shard_map/all_gather | solution.py:52
  168.4 0.9 fusion.27
  169.4 1.9 fusion.10
  171.3 33.0 %all-reduce.6.cloned.1.call-done = f32[3,64,128]{2,1,0:T(8,128)} async-done(((f32[3,64,128]{2,1,0:T(8,128)}), f32[3,64,128]{2,1,0:T(8,128)}) %all-reduce.6.cloned.1.call-update) | async-done | bytes 98320 | tf_op jit(solution)/shard_map/psum | solution.py:65
  204.3 1.4 fusion.3
  205.7 14.4 %all-gather.1 = f32[1,512,128]{2,1,0:T(8,128)S(1)} all-gather(f32[1,128,128]{2,1,0:T(8,128)S(1)} %slice.161), channel_id=3, replica_groups=mesh['groups'=2,'prow'=4,'pcol'=4] {'prow'}, dimensions={1}, use_global_device_ids=true | all-gather | bytes 327680 | tf_op jit(solution)/shard_map/all_gather | solution.py:49
  220.1 1.5 fusion.14
  221.6 0.9 fusion.28
  222.6 13.9 %all_gather.36 = f32[512,128]{0,1:T(8,128)S(1)} all-gather(f32[128,128]{0,1:T(8,128)S(1)} %bitcast.116), channel_id=1, replica_groups=mesh['groups'=2,'prow'=4,'pcol'=4] {'prow'}, dimensions={0}, use_global_device_ids=true | all-gather | bytes 327680 | tf_op jit(solution)/shard_map/all_gather | solution.py:52
  236.5 19.3 %all-reduce.8.cloned.1.call-done = f32[2,64,128]{2,1,0:T(8,128)} async-done(((f32[2,64,128]{2,1,0:T(8,128)}), f32[2,64,128]{2,1,0:T(8,128)}) %all-reduce.8.cloned.1.call-update) | async-done | bytes 65552 | tf_op jit(solution)/shard_map/psum | solution.py:65
  255.8 1.2 fusion.23
  257.1 1.6 fusion.5
  258.7 14.4 %all-gather.2 = f32[1,512,128]{2,1,0:T(8,128)S(1)} all-gather(f32[1,128,128]{2,1,0:T(8,128)S(1)} %slice.166), channel_id=4, replica_groups=mesh['groups'=2,'prow'=4,'pcol'=4] {'prow'}, dimensions={1}, use_global_device_ids=true | all-gather | bytes 327680 | tf_op jit(solution)/shard_map/all_gather | solution.py:49
  273.1 1.5 fusion.13
  274.7 1.0 convolution_bitcast_fusion.3
  275.6 14.0 %all_gather.38 = f32[512,128]{0,1:T(8,128)S(1)} all-gather(f32[128,128]{0,1:T(8,128)S(1)} %bitcast.118), channel_id=1, replica_groups=mesh['groups'=2,'prow'=4,'pcol'=4] {'prow'}, dimensions={0}, use_global_device_ids=true | all-gather | bytes 327680 | tf_op jit(solution)/shard_map/all_gather | solution.py:52
  289.6 1.3 fusion.12
  290.9 17.9 %psum.31 = f32[64,128]{0,1:T(8,128)S(1)} all-reduce(f32[64,128]{0,1:T(8,128)S(1)} %convolution_bitcast_fusion.3), channel_id=1, replica_groups=mesh['groups'=2,'prow'=4,'pcol'=4] {'prow'}, use_global_device_ids=true, to_apply=%region_3.0 | all-reduce | flops 8192 | bytes 65536 | tf_op jit(solution)/shard_map/psum | solution.py:65
  309.2 13.8 %all-gather.3 = f32[1,512,128]{2,1,0:T(8,128)S(1)} all-gather(f32[1,128,128]{2,1,0:T(8,128)S(1)} %fusion.8), channel_id=5, replica_groups=mesh['groups'=2,'prow'=4,'pcol'=4] {'prow'}, dimensions={1}, use_global_device_ids=true | all-gather | bytes 327680 | tf_op jit(solution)/shard_map/all_gather | solution.py:49
  323.0 1.5 convolution_bitcast_fusion.4
  (24 shorter events, 6.3 us)
Async XLA Ops:
  6.5 58.4 %all-gather.8.cloned.1.call-start = ((), (), s32[]{:S(2)}) async-start(), calls=%async_computation | async-start | bytes 9175040 | tf_op jit(solution)/shard_map/all_gather | solution.py:29
  7.3 87.2 %all-gather.10.cloned.1.call-start = ((), (), s32[]{:S(2)}) async-start(), calls=%async_computation.1 | async-start | bytes 1310720 | tf_op jit(solution)/shard_map/all_gather | solution.py:36
  8.0 126.6 %all-reduce.4.cloned.1.call-start = ((), (), s32[]{:S(2)}) async-start(), calls=%async_computation.2 | async-start | bytes 1048576 | tf_op jit(solution)/shard_map/psum | solution.py:42
  10.6 142.4 %all-gather.12.cloned.1.call-start = ((), (), s32[]{:S(2)}) async-start(), calls=%async_computation.3 | async-start | bytes 1310720 | tf_op jit(solution)/shard_map/all_gather | solution.py:31
  11.1 193.1 %all-reduce.6.cloned.1.call-start = ((), (), s32[]{:S(2)}) async-start(), calls=%async_computation.4 | async-start | bytes 196608 | tf_op jit(solution)/shard_map/psum | solution.py:65
  72.4 62.3 %copy-start = (f32[4,128,128]{2,1,0:T(8,128)S(1)}, f32[4,128,128]{2,1,0:T(8,128)}, u32[]{:S(2)}) copy-start(f32[4,128,128]{2,1,0:T(8,128)} %param.14) | copy-start | bytes 786436
  169.3 86.5 %all-reduce.8.cloned.1.call-start = ((), (), s32[]{:S(2)}) async-start(), calls=%async_computation.5 | async-start | bytes 131072 | tf_op jit(solution)/shard_map/psum | solution.py:65
Sparse Core Ops, SparseCore 0:
  8.9 55.9 all-gather.7
  66.5 27.9 all-gather.9
  96.8 37.7 all-reduce.3
  136.1 16.8 all-gather.11
  169.5 34.7 all-reduce.5
  222.7 33.0 all-reduce.7
where the time goes:
time: 333 us; the launch traced here: 332 us
  waiting for transfers between devices  161 us (48%)
  blocking collectives  117 us (35%)
  matrix products  27.2 us (8%)
  between operations  13.6 us (4%)
  other arithmetic  11 us (3%)
    all_gather x4, blocking collectives, local(): lax.all_gather(pending[block_index], 'prow', axis=0, tiled=True)  57.1 us
    psum x2, waiting for transfers between devices, local(): projected = lax.psum(projected, 'prow')  52.3 us
    all_gather x1, waiting for transfers between devices, local(): lax.all_gather(dense_tiles, 'pcol', axis=3, tiled=True)  48.4 us
    all_gather x3, blocking collectives, local(): solved_whole = lax.all_gather(solved_own, 'prow', axis=0, tiled=True)  41.8 us
    psum x1, waiting for transfers between devices, local(): early_coeffs = lax.psum(partial_value, 'prow')  34.3 us
    all_gather x1, waiting for transfers between devices, local(): lax.all_gather(earlier, 'prow', axis=1, tiled=True)  22.1 us
    psum x1, blocking collectives, local(): projected = lax.psum(projected, 'prow')  17.9 us
    mul x1, other arithmetic, local(): lax.all_gather(dense_tiles, 'pcol', axis=3, tiled=True)  7.42 us
  transfers between devices with their start and end apart: 6, of which 6 were waited for; matrix products, arithmetic and copies ran while one was open for 8% of the time, Pallas kernels for 0%

commit v1 on v0

v1 whole, which is shorter than its diff:
```python
import functools

import jax
import jax.numpy as jnp
from jax import lax
from jax.experimental import pallas as pl
from jax.experimental.pallas import tpu as pltpu
from jax.sharding import PartitionSpec as P

HIGHEST = lax.Precision.HIGHEST
VMEM_LIMIT = 24 * 1024 * 1024


def any_mesh(
    right_side,
    earlier,
    inverse_diag,
    dense_tiles,
    left_factor,
    right_factor,
    tile_ranks,
    dense_flags,
):
    count_steps = right_side.shape[0]
    prev_cols = earlier.shape[0]
    rank_pad = left_factor.shape[3]
    tile_flags = dense_flags.astype(jnp.float32)
    columns = lax.broadcasted_iota(jnp.int32, tile_ranks.shape + (rank_pad,), 2)
    low_mask = (columns < tile_ranks[:, :, None]).astype(jnp.float32) * (1.0 - tile_flags)[
        :, :, None
    ]
    left_eff = left_factor * low_mask[:, :, None, :]
    tile_rows = (
        lax.all_gather(dense_tiles, "pcol", axis=3, tiled=True) * tile_flags[:, :, None, None]
    )
    inverse_rows = lax.all_gather(inverse_diag, "pcol", axis=2, tiled=True)
    early_sum = jnp.einsum(
        "kjrc,jcs->krs",
        tile_rows[:, :prev_cols],
        lax.all_gather(earlier, "prow", axis=1, tiled=True),
        precision=HIGHEST,
    )
    partial_value = jnp.einsum(
        "kjcq,jcs->kjqs", right_factor[:, :prev_cols], earlier, precision=HIGHEST
    )
    early_coeffs = lax.psum(partial_value, "prow")
    early_sum = early_sum + jnp.einsum(
        "kjrq,kjqs->krs", left_eff[:, :prev_cols], early_coeffs, precision=HIGHEST
    )
    pending = right_side - early_sum
    outputs = []
    for block_index in range(count_steps):
        residual_whole = lax.all_gather(pending[block_index], "prow", axis=0, tiled=True)
        solved_own = jnp.dot(inverse_rows[block_index], residual_whole, precision=HIGHEST)
        outputs.append(solved_own)
        if block_index + 1 < count_steps:
            solved_whole = lax.all_gather(solved_own, "prow", axis=0, tiled=True)
            column = prev_cols + block_index
            later = slice(block_index + 1, None)
            dense_part = jnp.einsum(
                "krc,cs->krs", tile_rows[later, column], solved_whole, precision=HIGHEST
            )
            projected = lax.psum(
                jnp.einsum(
                    "kcq,cs->kqs", right_factor[later, column], solved_own, precision=HIGHEST
                ),
                "prow",
            )
            low_part = jnp.einsum(
                "krq,kqs->krs", left_eff[later, column], projected, precision=HIGHEST
            )
            pending = pending.at[later].add(-(dense_part + low_part))
    return jnp.stack(outputs)


def halves(value):
    high = value.astype(jnp.bfloat16)
    low = (value - high.astype(jnp.float32)).astype(jnp.bfloat16)
    return high, low


def dot_split(left, right, dims=(((1,), (0,)), ((), ()))):
    axis_left = 1 - dims[0][0][0]
    axis_right = 1 - dims[0][1][0]
    rows, cols = left.shape[axis_left], right.shape[axis_right]
    left2 = jnp.concatenate(halves(left), axis=axis_left)
    right2 = jnp.concatenate(halves(right), axis=axis_right)
    out = lax.dot_general(left2, right2, dims, preferred_element_type=jnp.float32)
    return (out[:rows, :cols] + (out[:rows, cols:] + out[rows:, :cols])) + out[rows:, cols:]


def merge_kernel(step, count, ranks_ref, flags_ref, dense_ref, left_ref, right_ref, inv_ref, out_ref):
    rank_pad, rows = left_ref.shape[2:]
    row_at = lax.broadcasted_iota(jnp.int32, (rank_pad, rows), 0)
    for col in range(count):
        flag = flags_ref[step, col].astype(jnp.float32)
        mask = jnp.where(row_at < ranks_ref[step, col], 1.0 - flag, 0.0)
        low = dot_split(left_ref[0, col] * mask, right_ref[col], (((0,), (0,)), ((), ())))
        out_ref[col] = dense_ref[0, col] * flag + low
    out_ref[count] = inv_ref[0]


def product_kernel(n, sign, blocks, tiles, *refs):
    strips = refs[:n]
    sources = refs[n : n + n * blocks]
    rest = refs[n + n * blocks :]
    base_ref, (out_ref, source_scr) = (rest[0], rest[1:]) if sign else (None, rest)
    nb = out_ref.shape[-2]
    per_block = tiles // blocks
    turn = lax.axis_index("prow") ^ lax.axis_index("pcol")
    for slot in range(n):
        place = pl.multiple_of((turn ^ slot) * nb, nb)
        for block in range(blocks):
            ref = sources[block * n + slot]
            for tile in range(per_block):
                value = ref[tile] if len(ref.shape) == 3 else ref[...]
                source_scr[block * per_block + tile, pl.ds(place, nb), :] = value
    total = None
    for tile in range(tiles):
        strip = jnp.concatenate([strips[d][tile] for d in range(n)], axis=1)
        part = dot_split(strip, source_scr[tile])
        total = part if total is None else total + part
    if sign:
        base = base_ref[0] if len(base_ref.shape) == 3 else base_ref[...]
        total = base - total
    out_ref[...] = total


def spec_of(shape, index=None):
    if index is None:
        return pl.BlockSpec(shape, lambda i: (0,) * len(shape))
    return pl.BlockSpec(shape, lambda i: index)


def square_mesh(
    n,
    right_side,
    earlier,
    inverse_diag,
    dense_tiles,
    left_factor,
    right_factor,
    tile_ranks,
    dense_flags,
):
    steps, nb, rhs = right_side.shape
    prev = earlier.shape[0]
    cols = dense_tiles.shape[1]
    rank_pad = left_factor.shape[3]
    left_t = jnp.swapaxes(left_factor, 2, 3)
    right_t = jnp.swapaxes(right_factor, 2, 3)
    params = pltpu.CompilerParams(vmem_limit_bytes=VMEM_LIMIT)
    f32 = jnp.float32

    def shift(value, axis, step):
        return lax.ppermute(value, axis, [(i, i ^ step) for i in range(n)])

    def over_rows(value):
        return [value] + [shift(value, "prow", d) for d in range(1, n)]

    flip = [(a * n + b, b * n + a) for a in range(n) for b in range(n)]

    known = over_rows(earlier)
    strips = []
    for step in range(steps):
        count = prev + step
        right_own = lax.ppermute(right_t[step, :count], ("prow", "pcol"), flip)
        own = pl.pallas_call(
            functools.partial(merge_kernel, step, count),
            grid=(1,),
            out_shape=jax.ShapeDtypeStruct((count + 1, nb, nb), f32),
            in_specs=[
                pl.BlockSpec(memory_space=pltpu.SMEM),
                pl.BlockSpec(memory_space=pltpu.SMEM),
                spec_of((1, cols, nb, nb), (step, 0, 0, 0)),
                spec_of((1, cols, rank_pad, nb), (step, 0, 0, 0)),
                spec_of((count, rank_pad, nb)),
                spec_of((1, nb, nb), (step, 0, 0)),
            ],
            out_specs=spec_of((count + 1, nb, nb)),
            compiler_params=params,
            name=f"merge{step}",
        )(tile_ranks, dense_flags, dense_tiles, left_t, right_own, inverse_diag)
        slots = [own]
        reach = n // 2
        while reach >= 1:
            slots = slots + [shift(v, "pcol", reach) for v in slots]
            reach //= 2
        order = [0]
        reach = n // 2
        while reach >= 1:
            order = order + [o ^ reach for o in order]
            reach //= 2
        strips.append([slots[order.index(d)] for d in range(n)])

    def product(step, first, tiles, blocks, base, name):
        args = list(strips[step])
        specs = [spec_of((tiles, nb, nb), (first // tiles, 0, 0))] * n
        for block in blocks:
            for value in block:
                args.append(value)
                specs.append(spec_of(value.shape))
        if base is not None:
            value, index = base
            args.append(value)
            specs.append(
                spec_of((nb, rhs)) if index is None else spec_of((1, nb, rhs), (index, 0, 0))
            )
        return pl.pallas_call(
            functools.partial(
                product_kernel, n, 0 if base is None else 1, len(blocks), tiles
            ),
            grid=(1,),
            out_shape=jax.ShapeDtypeStruct((nb, rhs), f32),
            in_specs=specs,
            out_specs=spec_of((nb, rhs)),
            scratch_shapes=[pltpu.VMEM((tiles, n * nb, rhs), f32)],
            compiler_params=params,
            name=name,
        )(*args)

    pending = [
        product(step, 0, prev, [known], (right_side, step), f"early{step}")
        for step in range(steps)
    ]
    solved = []
    for step in range(steps):
        whole = over_rows(pending[step])
        solved.append(product(step, prev + step, 1, [whole], None, f"solve{step}"))
        if step + 1 < steps:
            block = over_rows(solved[step])
            for later in range(step + 1, steps):
                pending[later] = product(
                    later, prev + step, 1, [block], (pending[later], None), f"update{later}{step}"
                )
    return jnp.stack(solved)


def solution(mesh):
    placed = (
        P("groups", "prow", "pcol"),
        P("groups", "prow", "pcol"),
        P("groups", "prow", "pcol"),
        P("groups", None, "prow", "pcol"),
        P("groups", None, "prow", None),
        P("groups", None, "prow", None),
        P("groups", None),
        P("groups", None),
    )
    n = mesh.shape["prow"]
    square = n == mesh.shape["pcol"] and n & (n - 1) == 0 and n <= 8

    def local(*args):
        nb, cols = args[3].shape[2:]
        if square and nb % 128 == 0 and cols % 128 == 0 and args[0].shape[2] % 128 == 0:
            return square_mesh(n, *args)
        return any_mesh(*args)

    return jax.shard_map(
        local, mesh=mesh, in_specs=placed, out_specs=P("groups", "prow", "pcol"), check_vma=False
    )
```

time: 333 us -> 152 us (0.46)
  blocking collectives: 117 us -> 0 us
  waiting for transfers between devices: 161 us -> 52.6 us
  starting transfers between devices: 0.2 us -> 81.3 us
  matrix products: 27.2 us -> 0 us
  between operations: 13.6 us -> 0.28 us
  other arithmetic: 11 us -> 0.73 us
  Pallas kernels: 0 us -> 8.72 us
  local copies, waits for them, and re-layouts: 2.6 us -> 7.7 us
    all_gather x7 -> x0, blocking collectives: 98.9 us -> none  [the longest x4 57.1 us: local(): lax.all_gather(pending[block_index], 'prow', axis=0, tiled=True)]
    psum x3 -> x0, waiting for transfers between devices: 86.6 us -> none  [the longest x2 52.3 us: local(): projected = lax.psum(projected, 'prow')]
    ppermute x0 -> x40, starting transfers between devices: none -> 81.3 us  [the longest x36 78.6 us: shift(): return lax.ppermute(value, axis, [(i, i ^ step) for i in range(n)])]
    all_gather x3 -> x0, waiting for transfers between devices: 72.2 us -> none  [the longest x1 48.4 us: local(): lax.all_gather(dense_tiles, 'pcol', axis=3, tiled=True)]
    ppermute x0 -> x40, waiting for transfers between devices: none -> 52.6 us  [the longest x36 52.6 us: shift(): return lax.ppermute(value, axis, [(i, i ^ step) for i in range(n)])]
    dot_general x14 -> x0, matrix products: 25.4 us -> none  [the longest x4 6.17 us: local(): jnp.dot(inverse_rows[block_index], residual_whole, precision=HIGHEST)]
    psum x1 -> x0, blocking collectives: 17.9 us -> none  [local(): projected = lax.psum(projected, 'prow')]
    mul x3 -> x0, other arithmetic: 9.66 us -> none  [the longest x1 7.42 us: local(): lax.all_gather(dense_tiles, 'pcol', axis=3, tiled=True)]
  transfers between devices with their start and end apart: 6 -> 40, of which waited for: 6 -> 18; matrix products, arithmetic and copies ran while one was open for 8% -> 2% of each run, Pallas kernels for 0% -> 5%
where the time goes in v1:
time: 152 us; the launch traced here: 151 us
  starting transfers between devices  81.3 us (53%)
  waiting for transfers between devices  52.6 us (35%)
  Pallas kernels  8.72 us (6%)
  local copies, waits for them, and re-layouts  7.7 us (5%)
    ppermute x36, starting transfers between devices, shift(): return lax.ppermute(value, axis, [(i, i ^ step) for i in range(n)])  78.6 us
    ppermute x36, waiting for transfers between devices, shift(): return lax.ppermute(value, axis, [(i, i ^ step) for i in range(n)])  52.6 us
    pallas_call x14, Pallas kernels, product(): pl.pallas_call(functools.partial(product_kernel, n, 0 if base is None els...  4.78 us
    pallas_call x4, Pallas kernels, square_mesh(): pl.pallas_call(functools.partial(merge_kernel, step, count), grid=(1,), o...  3.94 us
    squeeze x4, local copies, waits for them, and re-layouts, square_mesh(): right_own = lax.ppermute(right_t[step, :count], ('prow', 'pcol'), flip)  3.87 us
    unnamed x16, local copies, waits for them, and re-layouts  3.83 us
  transfers between devices with their start and end apart: 40, of which 18 were waited for; matrix products, arithmetic and copies ran while one was open for 2% of the time, Pallas kernels for 5%

profile of v1, /device:TPU:0, one launch (start us, length us, event | category | flops | bytes accessed | tf_op | source)
XLA Modules:
  0.0 151.3 jit_solution(9696854749399267476)
XLA Ops:
  6.6 18.9 %collective-permute-start.6 = (f32[4,128,128]{2,1,0:T(8,128)}, f32[4,128,128]{2,1,0:T(8,128)S(1)}, u32[]{:S(2)}, u32[]{:S(2)}) collective-permute-start(f32[4,128,128]{2,1,0:T(8,128)} %refs_4_.7), channel_id=1, source_target_pairs={{0,12},{4,8},{8,4},{12,0},{1,13},{5,9},{9,5},{13,1},{2,14},{6,10},... | collective-permute-start | bytes 786440 | tf_op jit(solution)/shard_map/ppermute | solution.py:156
  25.6 1.5 copy-done
  30.4 9.0 %collective-permute-start.5 = (f32[4,128,128]{2,1,0:T(8,128)S(1)}, f32[4,128,128]{2,1,0:T(8,128)S(1)}, u32[]{:S(2)}, u32[]{:S(2)}) collective-permute-start(f32[4,128,128]{2,1,0:T(8,128)S(1)} %copy-done.4), channel_id=1, source_target_pairs={{0,8},{4,12},{8,0},{12,4},{1,9},{5,13},{9,1},{13,5},{2,10},{6,14},... | collective-permute-start | bytes 786440 | tf_op jit(solution)/shard_map/ppermute | solution.py:156
  39.5 2.7 %collective-permute-start.1 = (f32[5,128,128]{2,1,0:T(8,128)S(1)}, f32[5,128,128]{2,1,0:T(8,128)S(1)}, u32[]{:S(2)}, u32[]{:S(2)}) collective-permute-start(f32[5,128,128]{2,1,0:T(8,128)S(1)} %merge0.1.refs_0_), channel_id=1, source_target_pairs={{0,1},{1,0},{2,3},{3,2},{4,5},{5,4},{6,7},{7,6},{8,9},{9,8},{10,11... | collective-permute-start | bytes 983048 | tf_op jit(solution)/shard_map/ppermute | solution.py:156
  43.2 11.2 %collective-permute-start.12 = (f32[6,128,128]{2,1,0:T(8,128)S(1)}, f32[6,128,128]{2,1,0:T(8,128)S(1)}, u32[]{:S(2)}, u32[]{:S(2)}) collective-permute-start(f32[6,128,128]{2,1,0:T(8,128)S(1)} %merge1.1.refs_0_), channel_id=1, source_target_pairs={{0,2},{1,3},{2,0},{3,1},{4,6},{5,7},{6,4},{7,5},{8,10},{9,11},{10,... | collective-permute-start | bytes 1179656 | tf_op jit(solution)/shard_map/ppermute | solution.py:156
  55.4 7.3 %collective-permute-done.5.refs_6_ = f32[4,128,128]{2,1,0:T(8,128)S(1)} collective-permute-done((f32[4,128,128]{2,1,0:T(8,128)S(1)}, f32[4,128,128]{2,1,0:T(8,128)S(1)}, u32[]{:S(2)}, u32[]{:S(2)}) %collective-permute-start.5) | collective-permute-done | bytes 262176 | tf_op jit(solution)/shard_map/ppermute | solution.py:156
  63.8 2.1 %collective-permute-start.32 = (f32[8,128,128]{2,1,0:T(8,128)S(1)}, f32[8,128,128]{2,1,0:T(8,128)S(1)}, u32[]{:S(2)}, u32[]{:S(2)}) collective-permute-start(f32[8,128,128]{2,1,0:T(8,128)S(1)} %merge3.1.refs_0_), channel_id=1, source_target_pairs={{0,2},{1,3},{2,0},{3,1},{4,6},{5,7},{6,4},{7,5},{8,10},{9,11},{10,... | collective-permute-start | bytes 1572872 | tf_op jit(solution)/shard_map/ppermute | solution.py:156
  67.8 8.3 %collective-permute-done.22.refs_2_ = f32[7,128,128]{2,1,0:T(8,128)S(1)} collective-permute-done((f32[7,128,128]{2,1,0:T(8,128)S(1)}, f32[7,128,128]{2,1,0:T(8,128)S(1)}, u32[]{:S(2)}, u32[]{:S(2)}) %collective-permute-start.22) | collective-permute-done | bytes 458784 | tf_op jit(solution)/shard_map/ppermute | solution.py:156
  76.1 2.7 %collective-permute-start.8 = (f32[128,128]{1,0:T(8,128)S(1)}, f32[128,128]{1,0:T(8,128)S(1)}, u32[]{:S(2)}, u32[]{:S(2)}) collective-permute-start(f32[128,128]{1,0:T(8,128)S(1)} %early0.1.refs_4_), channel_id=1, source_target_pairs={{0,8},{4,12},{8,0},{12,4},{1,9},{5,13},{9,1},{13,5},{2,10},{6,14},... | collective-permute-start | bytes 196616 | tf_op jit(solution)/shard_map/ppermute | solution.py:156
  81.4 1.7 %collective-permute-done.7.refs_5_ = f32[128,128]{1,0:T(8,128)S(1)} collective-permute-done((f32[128,128]{1,0:T(8,128)S(1)}, f32[128,128]{1,0:T(8,128)S(1)}, u32[]{:S(2)}, u32[]{:S(2)}) %collective-permute-start.7) | collective-permute-done | bytes 65568 | tf_op jit(solution)/shard_map/ppermute | solution.py:156
  83.4 3.5 %collective-permute-start.16 = (f32[128,128]{1,0:T(8,128)S(1)}, f32[128,128]{1,0:T(8,128)S(1)}, u32[]{:S(2)}, u32[]{:S(2)}) collective-permute-start(f32[128,128]{1,0:T(8,128)S(1)} %solve0.1.refs_4_), channel_id=1, source_target_pairs={{0,12},{4,8},{8,4},{12,0},{1,13},{5,9},{9,5},{13,1},{2,14},{6,10},... | collective-permute-start | bytes 196616 | tf_op jit(solution)/shard_map/ppermute | solution.py:156
  86.9 2.8 %collective-permute-start.15 = (f32[128,128]{1,0:T(8,128)S(1)}, f32[128,128]{1,0:T(8,128)S(1)}, u32[]{:S(2)}, u32[]{:S(2)}) collective-permute-start(f32[128,128]{1,0:T(8,128)S(1)} %solve0.1.refs_4_), channel_id=1, source_target_pairs={{0,8},{4,12},{8,0},{12,4},{1,9},{5,13},{9,1},{13,5},{2,10},{6,14},... | collective-permute-start | bytes 196616 | tf_op jit(solution)/shard_map/ppermute | solution.py:156
  89.9 3.0 %collective-permute-done.15.refs_6_ = f32[128,128]{1,0:T(8,128)S(1)} collective-permute-done((f32[128,128]{1,0:T(8,128)S(1)}, f32[128,128]{1,0:T(8,128)S(1)}, u32[]{:S(2)}, u32[]{:S(2)}) %collective-permute-start.15) | collective-permute-done | bytes 65568 | tf_op jit(solution)/shard_map/ppermute | solution.py:156
  92.9 1.8 %collective-permute-start.14 = (f32[128,128]{1,0:T(8,128)S(1)}, f32[128,128]{1,0:T(8,128)S(1)}, u32[]{:S(2)}, u32[]{:S(2)}) collective-permute-start(f32[128,128]{1,0:T(8,128)S(1)} %solve0.1.refs_4_), channel_id=1, source_target_pairs={{0,4},{4,0},{8,12},{12,8},{1,5},{5,1},{9,13},{13,9},{2,6},{6,2},{1... | collective-permute-start | bytes 196616 | tf_op jit(solution)/shard_map/ppermute | solution.py:156
  95.2 2.2 %collective-permute-done.14.refs_5_ = f32[128,128]{1,0:T(8,128)S(1)} collective-permute-done((f32[128,128]{1,0:T(8,128)S(1)}, f32[128,128]{1,0:T(8,128)S(1)}, u32[]{:S(2)}, u32[]{:S(2)}) %collective-permute-start.14) | collective-permute-done | bytes 65568 | tf_op jit(solution)/shard_map/ppermute | solution.py:156
  97.7 2.2 %collective-permute-start.19 = (f32[128,128]{1,0:T(8,128)S(1)}, f32[128,128]{1,0:T(8,128)S(1)}, u32[]{:S(2)}, u32[]{:S(2)}) collective-permute-start(f32[128,128]{1,0:T(8,128)S(1)} %update10.1.refs_4_), channel_id=1, source_target_pairs={{0,12},{4,8},{8,4},{12,0},{1,13},{5,9},{9,5},{13,1},{2,14},{6,10},... | collective-permute-start | bytes 196616 | tf_op jit(solution)/shard_map/ppermute | solution.py:156
  99.9 4.0 %collective-permute-done.19.refs_7_ = f32[128,128]{1,0:T(8,128)S(1)} collective-permute-done((f32[128,128]{1,0:T(8,128)S(1)}, f32[128,128]{1,0:T(8,128)S(1)}, u32[]{:S(2)}, u32[]{:S(2)}) %collective-permute-start.19) | collective-permute-done | bytes 65568 | tf_op jit(solution)/shard_map/ppermute | solution.py:156
  105.2 4.7 %collective-permute-done.18.refs_6_ = f32[128,128]{1,0:T(8,128)S(1)} collective-permute-done((f32[128,128]{1,0:T(8,128)S(1)}, f32[128,128]{1,0:T(8,128)S(1)}, u32[]{:S(2)}, u32[]{:S(2)}) %collective-permute-start.18) | collective-permute-done | bytes 65568 | tf_op jit(solution)/shard_map/ppermute | solution.py:156
  109.9 4.2 %collective-permute-done.17.refs_5_ = f32[128,128]{1,0:T(8,128)S(1)} collective-permute-done((f32[128,128]{1,0:T(8,128)S(1)}, f32[128,128]{1,0:T(8,128)S(1)}, u32[]{:S(2)}, u32[]{:S(2)}) %collective-permute-start.17) | collective-permute-done | bytes 65568 | tf_op jit(solution)/shard_map/ppermute | solution.py:156
  114.4 2.2 %collective-permute-start.26 = (f32[128,128]{1,0:T(8,128)S(1)}, f32[128,128]{1,0:T(8,128)S(1)}, u32[]{:S(2)}, u32[]{:S(2)}) collective-permute-start(f32[128,128]{1,0:T(8,128)S(1)} %solve1.1.refs_4_), channel_id=1, source_target_pairs={{0,12},{4,8},{8,4},{12,0},{1,13},{5,9},{9,5},{13,1},{2,14},{6,10},... | collective-permute-start | bytes 196616 | tf_op jit(solution)/shard_map/ppermute | solution.py:156
  116.6 2.2 %collective-permute-start.24 = (f32[128,128]{1,0:T(8,128)S(1)}, f32[128,128]{1,0:T(8,128)S(1)}, u32[]{:S(2)}, u32[]{:S(2)}) collective-permute-start(f32[128,128]{1,0:T(8,128)S(1)} %solve1.1.refs_4_), channel_id=1, source_target_pairs={{0,4},{4,0},{8,12},{12,8},{1,5},{5,1},{9,13},{13,9},{2,6},{6,2},{1... | collective-permute-start | bytes 196616 | tf_op jit(solution)/shard_map/ppermute | solution.py:156
  120.6 3.5 %collective-permute-done.25.refs_6_ = f32[128,128]{1,0:T(8,128)S(1)} collective-permute-done((f32[128,128]{1,0:T(8,128)S(1)}, f32[128,128]{1,0:T(8,128)S(1)}, u32[]{:S(2)}, u32[]{:S(2)}) %collective-permute-start.25) | collective-permute-done | bytes 65568 | tf_op jit(solution)/shard_map/ppermute | solution.py:156
  124.4 2.2 %collective-permute-start.29 = (f32[128,128]{1,0:T(8,128)S(1)}, f32[128,128]{1,0:T(8,128)S(1)}, u32[]{:S(2)}, u32[]{:S(2)}) collective-permute-start(f32[128,128]{1,0:T(8,128)S(1)} %update21.1.refs_4_), channel_id=1, source_target_pairs={{0,12},{4,8},{8,4},{12,0},{1,13},{5,9},{9,5},{13,1},{2,14},{6,10},... | collective-permute-start | bytes 196616 | tf_op jit(solution)/shard_map/ppermute | solution.py:156
  126.6 2.2 %collective-permute-start.27 = (f32[128,128]{1,0:T(8,128)S(1)}, f32[128,128]{1,0:T(8,128)S(1)}, u32[]{:S(2)}, u32[]{:S(2)}) collective-permute-start(f32[128,128]{1,0:T(8,128)S(1)} %update21.1.refs_4_), channel_id=1, source_target_pairs={{0,4},{4,0},{8,12},{12,8},{1,5},{5,1},{9,13},{13,9},{2,6},{6,2},{1... | collective-permute-start | bytes 196616 | tf_op jit(solution)/shard_map/ppermute | solution.py:156
  128.9 2.4 %collective-permute-done.29.refs_7_ = f32[128,128]{1,0:T(8,128)S(1)} collective-permute-done((f32[128,128]{1,0:T(8,128)S(1)}, f32[128,128]{1,0:T(8,128)S(1)}, u32[]{:S(2)}, u32[]{:S(2)}) %collective-permute-start.29) | collective-permute-done | bytes 65568 | tf_op jit(solution)/shard_map/ppermute | solution.py:156
  131.3 2.2 %collective-permute-done.28.refs_6_ = f32[128,128]{1,0:T(8,128)S(1)} collective-permute-done((f32[128,128]{1,0:T(8,128)S(1)}, f32[128,128]{1,0:T(8,128)S(1)}, u32[]{:S(2)}, u32[]{:S(2)}) %collective-permute-start.28) | collective-permute-done | bytes 65568 | tf_op jit(solution)/shard_map/ppermute | solution.py:156
  133.8 2.1 %collective-permute-start.36 = (f32[128,128]{1,0:T(8,128)S(1)}, f32[128,128]{1,0:T(8,128)S(1)}, u32[]{:S(2)}, u32[]{:S(2)}) collective-permute-start(f32[128,128]{1,0:T(8,128)S(1)} %solve2.1.refs_4_), channel_id=1, source_target_pairs={{0,12},{4,8},{8,4},{12,0},{1,13},{5,9},{9,5},{13,1},{2,14},{6,10},... | collective-permute-start | bytes 196616 | tf_op jit(solution)/shard_map/ppermute | solution.py:156
  135.9 2.3 %collective-permute-start.34 = (f32[128,128]{1,0:T(8,128)S(1)}, f32[128,128]{1,0:T(8,128)S(1)}, u32[]{:S(2)}, u32[]{:S(2)}) collective-permute-start(f32[128,128]{1,0:T(8,128)S(1)} %solve2.1.refs_4_), channel_id=1, source_target_pairs={{0,4},{4,0},{8,12},{12,8},{1,5},{5,1},{9,13},{13,9},{2,6},{6,2},{1... | collective-permute-start | bytes 196616 | tf_op jit(solution)/shard_map/ppermute | solution.py:156
  140.5 2.0 %collective-permute-done.35.refs_6_ = f32[128,128]{1,0:T(8,128)S(1)} collective-permute-done((f32[128,128]{1,0:T(8,128)S(1)}, f32[128,128]{1,0:T(8,128)S(1)}, u32[]{:S(2)}, u32[]{:S(2)}) %collective-permute-start.35) | collective-permute-done | bytes 65568 | tf_op jit(solution)/shard_map/ppermute | solution.py:156
  142.8 2.1 %collective-permute-start.39 = (f32[128,128]{1,0:T(8,128)S(1)}, f32[128,128]{1,0:T(8,128)S(1)}, u32[]{:S(2)}, u32[]{:S(2)}) collective-permute-start(f32[128,128]{1,0:T(8,128)S(1)} %update32.1.refs_4_), channel_id=1, source_target_pairs={{0,12},{4,8},{8,4},{12,0},{1,13},{5,9},{9,5},{13,1},{2,14},{6,10},... | collective-permute-start | bytes 196616 | tf_op jit(solution)/shard_map/ppermute | solution.py:156
  144.9 2.3 %collective-permute-start.37 = (f32[128,128]{1,0:T(8,128)S(1)}, f32[128,128]{1,0:T(8,128)S(1)}, u32[]{:S(2)}, u32[]{:S(2)}) collective-permute-start(f32[128,128]{1,0:T(8,128)S(1)} %update32.1.refs_4_), channel_id=1, source_target_pairs={{0,4},{4,0},{8,12},{12,8},{1,5},{5,1},{9,13},{13,9},{2,6},{6,2},{1... | collective-permute-start | bytes 196616 | tf_op jit(solution)/shard_map/ppermute | solution.py:156
  147.2 1.7 %collective-permute-done.39.refs_7_ = f32[128,128]{1,0:T(8,128)S(1)} collective-permute-done((f32[128,128]{1,0:T(8,128)S(1)}, f32[128,128]{1,0:T(8,128)S(1)}, u32[]{:S(2)}, u32[]{:S(2)}) %collective-permute-start.39) | collective-permute-done | bytes 65568 | tf_op jit(solution)/shard_map/ppermute | solution.py:156
  (87 shorter events, 27.4 us)
Async XLA Ops:
  1.0 24.6 %collective-permute-start = (f32[4,64,128]{2,1,0:T(8,128)S(1)}, f32[4,64,128]{2,1,0:T(8,128)S(1)}, u32[]{:S(2)}, u32[]{:S(2)}) collective-permute-start(f32[4,64,128]{2,1,0:T(8,128)S(1)} %slice_bitcast_fusion.3), channel_id=1, source_target_pairs={{0,0},{1,4},{2,8},{3,12},{4,1},{5,5},{6,9},{7,13},{8,2},{9,6},{10,... | collective-permute-start | bytes 393224 | tf_op jit(solution)/shard_map/ppermute | solution.py:167
  2.6 27.8 %collective-permute-start.10 = (f32[5,64,128]{2,1,0:T(8,128)S(1)}, f32[5,64,128]{2,1,0:T(8,128)S(1)}, u32[]{:S(2)}, u32[]{:S(2)}) collective-permute-start(f32[5,64,128]{2,1,0:T(8,128)S(1)} %slice_bitcast_fusion.2), channel_id=1, source_target_pairs={{0,0},{1,4},{2,8},{3,12},{4,1},{5,5},{6,9},{7,13},{8,2},{9,6},{10,... | collective-permute-start | bytes 491528 | tf_op jit(solution)/shard_map/ppermute | solution.py:167
  4.2 35.2 %collective-permute-start.20 = (f32[6,64,128]{2,1,0:T(8,128)S(1)}, f32[6,64,128]{2,1,0:T(8,128)S(1)}, u32[]{:S(2)}, u32[]{:S(2)}) collective-permute-start(f32[6,64,128]{2,1,0:T(8,128)S(1)} %slice_bitcast_fusion.1), channel_id=1, source_target_pairs={{0,0},{1,4},{2,8},{3,12},{4,1},{5,5},{6,9},{7,13},{8,2},{9,6},{10,... | collective-permute-start | bytes 589832 | tf_op jit(solution)/shard_map/ppermute | solution.py:167
  5.9 33.5 %collective-permute-start.30 = (f32[7,64,128]{2,1,0:T(8,128)S(1)}, f32[7,64,128]{2,1,0:T(8,128)S(1)}, u32[]{:S(2)}, u32[]{:S(2)}) collective-permute-start(f32[7,64,128]{2,1,0:T(8,128)S(1)} %slice_bitcast_fusion), channel_id=1, source_target_pairs={{0,0},{1,4},{2,8},{3,12},{4,1},{5,5},{6,9},{7,13},{8,2},{9,6},{10,... | collective-permute-start | bytes 688136 | tf_op jit(solution)/shard_map/ppermute | solution.py:167
  6.6 36.5 %collective-permute-start.6 = (f32[4,128,128]{2,1,0:T(8,128)}, f32[4,128,128]{2,1,0:T(8,128)S(1)}, u32[]{:S(2)}, u32[]{:S(2)}) collective-permute-start(f32[4,128,128]{2,1,0:T(8,128)} %refs_4_.7), channel_id=1, source_target_pairs={{0,12},{4,8},{8,4},{12,0},{1,13},{5,9},{9,5},{13,1},{2,14},{6,10},... | collective-permute-start | bytes 786440 | tf_op jit(solution)/shard_map/ppermute | solution.py:156
  30.3 32.4 %collective-permute-start.2 = (f32[5,128,128]{2,1,0:T(8,128)S(1)}, f32[5,128,128]{2,1,0:T(8,128)S(1)}, u32[]{:S(2)}, u32[]{:S(2)}) collective-permute-start(f32[5,128,128]{2,1,0:T(8,128)S(1)} %merge0.1.refs_0_), channel_id=1, source_target_pairs={{0,2},{1,3},{2,0},{3,1},{4,6},{5,7},{6,4},{7,5},{8,10},{9,11},{10,... | collective-permute-start | bytes 983048 | tf_op jit(solution)/shard_map/ppermute | solution.py:156
  30.4 32.3 %collective-permute-start.5 = (f32[4,128,128]{2,1,0:T(8,128)S(1)}, f32[4,128,128]{2,1,0:T(8,128)S(1)}, u32[]{:S(2)}, u32[]{:S(2)}) collective-permute-start(f32[4,128,128]{2,1,0:T(8,128)S(1)} %copy-done.4), channel_id=1, source_target_pairs={{0,8},{4,12},{8,0},{12,4},{1,9},{5,13},{9,1},{13,5},{2,10},{6,14},... | collective-permute-start | bytes 786440 | tf_op jit(solution)/shard_map/ppermute | solution.py:156
  39.5 24.3 %collective-permute-start.4 = (f32[4,128,128]{2,1,0:T(8,128)S(1)}, f32[4,128,128]{2,1,0:T(8,128)S(1)}, u32[]{:S(2)}, u32[]{:S(2)}) collective-permute-start(f32[4,128,128]{2,1,0:T(8,128)S(1)} %copy-done.4), channel_id=1, source_target_pairs={{0,4},{4,0},{8,12},{12,8},{1,5},{5,1},{9,13},{13,9},{2,6},{6,2},{1... | collective-permute-start | bytes 786440 | tf_op jit(solution)/shard_map/ppermute | solution.py:156
  39.5 26.4 %collective-permute-start.1 = (f32[5,128,128]{2,1,0:T(8,128)S(1)}, f32[5,128,128]{2,1,0:T(8,128)S(1)}, u32[]{:S(2)}, u32[]{:S(2)}) collective-permute-start(f32[5,128,128]{2,1,0:T(8,128)S(1)} %merge0.1.refs_0_), channel_id=1, source_target_pairs={{0,1},{1,0},{2,3},{3,2},{4,5},{5,4},{6,7},{7,6},{8,9},{9,8},{10,11... | collective-permute-start | bytes 983048 | tf_op jit(solution)/shard_map/ppermute | solution.py:156
  43.2 23.0 %collective-permute-start.12 = (f32[6,128,128]{2,1,0:T(8,128)S(1)}, f32[6,128,128]{2,1,0:T(8,128)S(1)}, u32[]{:S(2)}, u32[]{:S(2)}) collective-permute-start(f32[6,128,128]{2,1,0:T(8,128)S(1)} %merge1.1.refs_0_), channel_id=1, source_target_pairs={{0,2},{1,3},{2,0},{3,1},{4,6},{5,7},{6,4},{7,5},{8,10},{9,11},{10,... | collective-permute-start | bytes 1179656 | tf_op jit(solution)/shard_map/ppermute | solution.py:156
  62.7 13.4 %collective-permute-start.22 = (f32[7,128,128]{2,1,0:T(8,128)S(1)}, f32[7,128,128]{2,1,0:T(8,128)S(1)}, u32[]{:S(2)}, u32[]{:S(2)}) collective-permute-start(f32[7,128,128]{2,1,0:T(8,128)S(1)} %merge2.1.refs_0_), channel_id=1, source_target_pairs={{0,2},{1,3},{2,0},{3,1},{4,6},{5,7},{6,4},{7,5},{8,10},{9,11},{10,... | collective-permute-start | bytes 1376264 | tf_op jit(solution)/shard_map/ppermute | solution.py:156
  63.8 23.1 %collective-permute-start.32 = (f32[8,128,128]{2,1,0:T(8,128)S(1)}, f32[8,128,128]{2,1,0:T(8,128)S(1)}, u32[]{:S(2)}, u32[]{:S(2)}) collective-permute-start(f32[8,128,128]{2,1,0:T(8,128)S(1)} %merge3.1.refs_0_), channel_id=1, source_target_pairs={{0,2},{1,3},{2,0},{3,1},{4,6},{5,7},{6,4},{7,5},{8,10},{9,11},{10,... | collective-permute-start | bytes 1572872 | tf_op jit(solution)/shard_map/ppermute | solution.py:156
  65.9 17.5 %collective-permute-start.11 = (f32[6,128,128]{2,1,0:T(8,128)S(1)}, f32[6,128,128]{2,1,0:T(8,128)S(1)}, u32[]{:S(2)}, u32[]{:S(2)}) collective-permute-start(f32[6,128,128]{2,1,0:T(8,128)S(1)} %merge1.1.refs_0_), channel_id=1, source_target_pairs={{0,1},{1,0},{2,3},{3,2},{4,5},{5,4},{6,7},{7,6},{8,9},{9,8},{10,11... | collective-permute-start | bytes 1179656 | tf_op jit(solution)/shard_map/ppermute | solution.py:156
  66.1 26.8 %collective-permute-start.13 = (f32[6,128,128]{2,1,0:T(8,128)S(1)}, f32[6,128,128]{2,1,0:T(8,128)S(1)}, u32[]{:S(2)}, u32[]{:S(2)}) collective-permute-start(f32[6,128,128]{2,1,0:T(8,128)S(1)} %collective-permute-done.12.refs_2_), channel_id=1, source_target_pairs={{0,1},{1,0},{2,3},{3,2},{4,5},{5,4},{6,7},{7,6},{8,9},{9,8},{10,11... | collective-permute-start | bytes 1179656 | tf_op jit(solution)/shard_map/ppermute | solution.py:156
  67.0 11.9 %collective-permute-start.9 = (f32[128,128]{1,0:T(8,128)S(1)}, f32[128,128]{1,0:T(8,128)S(1)}, u32[]{:S(2)}, u32[]{:S(2)}) collective-permute-start(f32[128,128]{1,0:T(8,128)S(1)} %early0.1.refs_4_), channel_id=1, source_target_pairs={{0,12},{4,8},{8,4},{12,0},{1,13},{5,9},{9,5},{13,1},{2,14},{6,10},... | collective-permute-start | bytes 196616 | tf_op jit(solution)/shard_map/ppermute | solution.py:156
  81.4 35.2 %collective-permute-start.21 = (f32[7,128,128]{2,1,0:T(8,128)S(1)}, f32[7,128,128]{2,1,0:T(8,128)S(1)}, u32[]{:S(2)}, u32[]{:S(2)}) collective-permute-start(f32[7,128,128]{2,1,0:T(8,128)S(1)} %merge2.1.refs_0_), channel_id=1, source_target_pairs={{0,1},{1,0},{2,3},{3,2},{4,5},{5,4},{6,7},{7,6},{8,9},{9,8},{10,11... | collective-permute-start | bytes 1376264 | tf_op jit(solution)/shard_map/ppermute | solution.py:156
  83.1 33.5 %collective-permute-start.23 = (f32[7,128,128]{2,1,0:T(8,128)S(1)}, f32[7,128,128]{2,1,0:T(8,128)S(1)}, u32[]{:S(2)}, u32[]{:S(2)}) collective-permute-start(f32[7,128,128]{2,1,0:T(8,128)S(1)} %collective-permute-done.22.refs_2_), channel_id=1, source_target_pairs={{0,1},{1,0},{2,3},{3,2},{4,5},{5,4},{6,7},{7,6},{8,9},{9,8},{10,11... | collective-permute-start | bytes 1376264 | tf_op jit(solution)/shard_map/ppermute | solution.py:156
  83.4 6.5 %collective-permute-start.16 = (f32[128,128]{1,0:T(8,128)S(1)}, f32[128,128]{1,0:T(8,128)S(1)}, u32[]{:S(2)}, u32[]{:S(2)}) collective-permute-start(f32[128,128]{1,0:T(8,128)S(1)} %solve0.1.refs_4_), channel_id=1, source_target_pairs={{0,12},{4,8},{8,4},{12,0},{1,13},{5,9},{9,5},{13,1},{2,14},{6,10},... | collective-permute-start | bytes 196616 | tf_op jit(solution)/shard_map/ppermute | solution.py:156
  86.9 6.0 %collective-permute-start.15 = (f32[128,128]{1,0:T(8,128)S(1)}, f32[128,128]{1,0:T(8,128)S(1)}, u32[]{:S(2)}, u32[]{:S(2)}) collective-permute-start(f32[128,128]{1,0:T(8,128)S(1)} %solve0.1.refs_4_), channel_id=1, source_target_pairs={{0,8},{4,12},{8,0},{12,4},{1,9},{5,13},{9,1},{13,5},{2,10},{6,14},... | collective-permute-start | bytes 196616 | tf_op jit(solution)/shard_map/ppermute | solution.py:156
  89.9 48.4 %collective-permute-start.31 = (f32[8,128,128]{2,1,0:T(8,128)S(1)}, f32[8,128,128]{2,1,0:T(8,128)S(1)}, u32[]{:S(2)}, u32[]{:S(2)}) collective-permute-start(f32[8,128,128]{2,1,0:T(8,128)S(1)} %merge3.1.refs_0_), channel_id=1, source_target_pairs={{0,1},{1,0},{2,3},{3,2},{4,5},{5,4},{6,7},{7,6},{8,9},{9,8},{10,11... | collective-permute-start | bytes 1572872 | tf_op jit(solution)/shard_map/ppermute | solution.py:156
  92.9 45.4 %collective-permute-start.33 = (f32[8,128,128]{2,1,0:T(8,128)S(1)}, f32[8,128,128]{2,1,0:T(8,128)S(1)}, u32[]{:S(2)}, u32[]{:S(2)}) collective-permute-start(f32[8,128,128]{2,1,0:T(8,128)S(1)} %collective-permute-done.32.refs_2_), channel_id=1, source_target_pairs={{0,1},{1,0},{2,3},{3,2},{4,5},{5,4},{6,7},{7,6},{8,9},{9,8},{10,11... | collective-permute-start | bytes 1572872 | tf_op jit(solution)/shard_map/ppermute | solution.py:156
  97.7 6.2 %collective-permute-start.19 = (f32[128,128]{1,0:T(8,128)S(1)}, f32[128,128]{1,0:T(8,128)S(1)}, u32[]{:S(2)}, u32[]{:S(2)}) collective-permute-start(f32[128,128]{1,0:T(8,128)S(1)} %update10.1.refs_4_), channel_id=1, source_target_pairs={{0,12},{4,8},{8,4},{12,0},{1,13},{5,9},{9,5},{13,1},{2,14},{6,10},... | collective-permute-start | bytes 196616 | tf_op jit(solution)/shard_map/ppermute | solution.py:156
  114.4 6.2 %collective-permute-start.26 = (f32[128,128]{1,0:T(8,128)S(1)}, f32[128,128]{1,0:T(8,128)S(1)}, u32[]{:S(2)}, u32[]{:S(2)}) collective-permute-start(f32[128,128]{1,0:T(8,128)S(1)} %solve1.1.refs_4_), channel_id=1, source_target_pairs={{0,12},{4,8},{8,4},{12,0},{1,13},{5,9},{9,5},{13,1},{2,14},{6,10},... | collective-permute-start | bytes 196616 | tf_op jit(solution)/shard_map/ppermute | solution.py:156
  116.6 7.5 %collective-permute-start.25 = (f32[128,128]{1,0:T(8,128)S(1)}, f32[128,128]{1,0:T(8,128)S(1)}, u32[]{:S(2)}, u32[]{:S(2)}) collective-permute-start(f32[128,128]{1,0:T(8,128)S(1)} %solve1.1.refs_4_), channel_id=1, source_target_pairs={{0,8},{4,12},{8,0},{12,4},{1,9},{5,13},{9,1},{13,5},{2,10},{6,14},... | collective-permute-start | bytes 196616 | tf_op jit(solution)/shard_map/ppermute | solution.py:156
  116.6 7.5 %collective-permute-start.24 = (f32[128,128]{1,0:T(8,128)S(1)}, f32[128,128]{1,0:T(8,128)S(1)}, u32[]{:S(2)}, u32[]{:S(2)}) collective-permute-start(f32[128,128]{1,0:T(8,128)S(1)} %solve1.1.refs_4_), channel_id=1, source_target_pairs={{0,4},{4,0},{8,12},{12,8},{1,5},{5,1},{9,13},{13,9},{2,6},{6,2},{1... | collective-permute-start | bytes 196616 | tf_op jit(solution)/shard_map/ppermute | solution.py:156
  124.4 6.9 %collective-permute-start.29 = (f32[128,128]{1,0:T(8,128)S(1)}, f32[128,128]{1,0:T(8,128)S(1)}, u32[]{:S(2)}, u32[]{:S(2)}) collective-permute-start(f32[128,128]{1,0:T(8,128)S(1)} %update21.1.refs_4_), channel_id=1, source_target_pairs={{0,12},{4,8},{8,4},{12,0},{1,13},{5,9},{9,5},{13,1},{2,14},{6,10},... | collective-permute-start | bytes 196616 | tf_op jit(solution)/shard_map/ppermute | solution.py:156
  126.6 6.9 %collective-permute-start.28 = (f32[128,128]{1,0:T(8,128)S(1)}, f32[128,128]{1,0:T(8,128)S(1)}, u32[]{:S(2)}, u32[]{:S(2)}) collective-permute-start(f32[128,128]{1,0:T(8,128)S(1)} %update21.1.refs_4_), channel_id=1, source_target_pairs={{0,8},{4,12},{8,0},{12,4},{1,9},{5,13},{9,1},{13,5},{2,10},{6,14},... | collective-permute-start | bytes 196616 | tf_op jit(solution)/shard_map/ppermute | solution.py:156
  126.6 6.9 %collective-permute-start.27 = (f32[128,128]{1,0:T(8,128)S(1)}, f32[128,128]{1,0:T(8,128)S(1)}, u32[]{:S(2)}, u32[]{:S(2)}) collective-permute-start(f32[128,128]{1,0:T(8,128)S(1)} %update21.1.refs_4_), channel_id=1, source_target_pairs={{0,4},{4,0},{8,12},{12,8},{1,5},{5,1},{9,13},{13,9},{2,6},{6,2},{1... | collective-permute-start | bytes 196616 | tf_op jit(solution)/shard_map/ppermute | solution.py:156
  133.8 6.7 %collective-permute-start.36 = (f32[128,128]{1,0:T(8,128)S(1)}, f32[128,128]{1,0:T(8,128)S(1)}, u32[]{:S(2)}, u32[]{:S(2)}) collective-permute-start(f32[128,128]{1,0:T(8,128)S(1)} %solve2.1.refs_4_), channel_id=1, source_target_pairs={{0,12},{4,8},{8,4},{12,0},{1,13},{5,9},{9,5},{13,1},{2,14},{6,10},... | collective-permute-start | bytes 196616 | tf_op jit(solution)/shard_map/ppermute | solution.py:156
  135.9 6.6 %collective-permute-start.35 = (f32[128,128]{1,0:T(8,128)S(1)}, f32[128,128]{1,0:T(8,128)S(1)}, u32[]{:S(2)}, u32[]{:S(2)}) collective-permute-start(f32[128,128]{1,0:T(8,128)S(1)} %solve2.1.refs_4_), channel_id=1, source_target_pairs={{0,8},{4,12},{8,0},{12,4},{1,9},{5,13},{9,1},{13,5},{2,10},{6,14},... | collective-permute-start | bytes 196616 | tf_op jit(solution)/shard_map/ppermute | solution.py:156
  135.9 6.6 %collective-permute-start.34 = (f32[128,128]{1,0:T(8,128)S(1)}, f32[128,128]{1,0:T(8,128)S(1)}, u32[]{:S(2)}, u32[]{:S(2)}) collective-permute-start(f32[128,128]{1,0:T(8,128)S(1)} %solve2.1.refs_4_), channel_id=1, source_target_pairs={{0,4},{4,0},{8,12},{12,8},{1,5},{5,1},{9,13},{13,9},{2,6},{6,2},{1... | collective-permute-start | bytes 196616 | tf_op jit(solution)/shard_map/ppermute | solution.py:156
  142.8 6.1 %collective-permute-start.39 = (f32[128,128]{1,0:T(8,128)S(1)}, f32[128,128]{1,0:T(8,128)S(1)}, u32[]{:S(2)}, u32[]{:S(2)}) collective-permute-start(f32[128,128]{1,0:T(8,128)S(1)} %update32.1.refs_4_), channel_id=1, source_target_pairs={{0,12},{4,8},{8,4},{12,0},{1,13},{5,9},{9,5},{13,1},{2,14},{6,10},... | collective-permute-start | bytes 196616 | tf_op jit(solution)/shard_map/ppermute | solution.py:156
  (16 other events, 124.3 us)

commit v2 on v1

--- a/solution.py
+++ b/solution.py
@@ -89,6 +89,10 @@
     return (out[:rows, :cols] + (out[:rows, cols:] + out[rows:, :cols])) + out[rows:, cols:]
 
 
+def pack_kernel(count, right_ref, *refs):
+    refs[-1][...] = right_ref[0, :count]
+
+
 def merge_kernel(step, count, ranks_ref, flags_ref, dense_ref, left_ref, right_ref, inv_ref, out_ref):
     rank_pad, rows = left_ref.shape[2:]
     row_at = lax.broadcasted_iota(jnp.int32, (rank_pad, rows), 0)
@@ -100,11 +104,11 @@
     out_ref[count] = inv_ref[0]
 
 
-def product_kernel(n, sign, blocks, tiles, *refs):
+def product_kernel(n, based, blocks, tiles, before, *refs):
     strips = refs[:n]
     sources = refs[n : n + n * blocks]
     rest = refs[n + n * blocks :]
-    base_ref, (out_ref, source_scr) = (rest[0], rest[1:]) if sign else (None, rest)
+    out_ref, source_scr = rest[-2:]
     nb = out_ref.shape[-2]
     per_block = tiles // blocks
     turn = lax.axis_index("prow") ^ lax.axis_index("pcol")
@@ -120,10 +124,16 @@
         strip = jnp.concatenate([strips[d][tile] for d in range(n)], axis=1)
         part = dot_split(strip, source_scr[tile])
         total = part if total is None else total + part
-    if sign:
+    if based:
+        base_ref = rest[0]
         base = base_ref[0] if len(base_ref.shape) == 3 else base_ref[...]
         total = base - total
-    out_ref[...] = total
+    if before < 0:
+        out_ref[...] = total
+    else:
+        for index in range(before):
+            out_ref[index] = rest[index][...]
+        out_ref[before] = total
 
 
 def spec_of(shape, index=None):
@@ -158,14 +168,31 @@
     def over_rows(value):
         return [value] + [shift(value, "prow", d) for d in range(1, n)]
 
-    flip = [(a * n + b, b * n + a) for a in range(n) for b in range(n)]
-
+    flip = []
+    for owner in range(n):
+        for row in range(n):
+            source = row ^ owner
+            source = (source >> 1) | ((source & 1) * (n // 2)) if n > 1 else 0
+            flip.append((owner * n + source, row * n + owner))
+
+    any_spec = pl.BlockSpec(memory_space=pl.ANY)
     known = over_rows(earlier)
     strips = []
+    own = []
     for step in range(steps):
         count = prev + step
-        right_own = lax.ppermute(right_t[step, :count], ("prow", "pcol"), flip)
-        own = pl.pallas_call(
+        after = [] if step < 2 else [own[0]]
+        packed = pl.pallas_call(
+            functools.partial(pack_kernel, count),
+            grid=(1,),
+            out_shape=jax.ShapeDtypeStruct((count, rank_pad, nb), f32),
+            in_specs=[spec_of((1, cols, rank_pad, nb), (step, 0, 0, 0))] + [any_spec] * len(after),
+            out_specs=spec_of((count, rank_pad, nb)),
+            compiler_params=params,
+            name=f"pack{step}",
+        )(right_t, *after)
+        right_own = lax.ppermute(packed, ("prow", "pcol"), flip)
+        own.append(pl.pallas_call(
             functools.partial(merge_kernel, step, count),
             grid=(1,),
             out_shape=jax.ShapeDtypeStruct((count + 1, nb, nb), f32),
@@ -180,8 +207,8 @@
             out_specs=spec_of((count + 1, nb, nb)),
             compiler_params=params,
             name=f"merge{step}",
-        )(tile_ranks, dense_flags, dense_tiles, left_t, right_own, inverse_diag)
-        slots = [own]
+        )(tile_ranks, dense_flags, dense_tiles, left_t, right_own, inverse_diag))
+        slots = [own[step]]
         reach = n // 2
         while reach >= 1:
             slots = slots + [shift(v, "pcol", reach) for v in slots]
@@ -193,7 +220,7 @@
             reach //= 2
         strips.append([slots[order.index(d)] for d in range(n)])
 
-    def product(step, first, tiles, blocks, base, name):
+    def product(step, first, tiles, blocks, name, base=None, after=(), stacked=None):
         args = list(strips[step])
         specs = [spec_of((tiles, nb, nb), (first // tiles, 0, 0))] * n
         for block in blocks:
@@ -206,34 +233,49 @@
             specs.append(
                 spec_of((nb, rhs)) if index is None else spec_of((1, nb, rhs), (index, 0, 0))
             )
+        shape, before = (nb, rhs), -1
+        if stacked is not None:
+            before = len(stacked)
+            shape = (before + 1, nb, rhs)
+            args += stacked
+            specs += [spec_of((nb, rhs))] * before
+        args += after
+        specs += [any_spec] * len(after)
         return pl.pallas_call(
-            functools.partial(
-                product_kernel, n, 0 if base is None else 1, len(blocks), tiles
-            ),
+            functools.partial(product_kernel, n, base is not None, len(blocks), tiles, before),
             grid=(1,),
-            out_shape=jax.ShapeDtypeStruct((nb, rhs), f32),
+            out_shape=jax.ShapeDtypeStruct(shape, f32),
             in_specs=specs,
-            out_specs=spec_of((nb, rhs)),
+            out_specs=spec_of(shape),
             scratch_shapes=[pltpu.VMEM((tiles, n * nb, rhs), f32)],
             compiler_params=params,
             name=name,
         )(*args)
 
-    pending = [
-        product(step, 0, prev, [known], (right_side, step), f"early{step}")
-        for step in range(steps)
-    ]
+    def early(step):
+        return product(step, 0, prev, [known], f"early{step}", (right_side, step))
+
+    pending = [early(step) for step in range(steps)]
+    waits = {("solve", 0): 1, ("update", 1): 2, ("solve", 1): 3}
+    fronts = list(pending)
     solved = []
     for step in range(steps):
         whole = over_rows(pending[step])
-        solved.append(product(step, prev + step, 1, [whole], None, f"solve{step}"))
-        if step + 1 < steps:
-            block = over_rows(solved[step])
-            for later in range(step + 1, steps):
-                pending[later] = product(
-                    later, prev + step, 1, [block], (pending[later], None), f"update{later}{step}"
-                )
-    return jnp.stack(solved)
+        ahead = waits.get(("solve", step), 0)
+        after = [fronts[ahead]] if step < ahead < steps else []
+        stacked = solved if step + 1 == steps else None
+        block = product(step, prev + step, 1, [whole], f"solve{step}", after=after, stacked=stacked)
+        if stacked is not None:
+            return block
+        solved.append(block)
+        spread = over_rows(block)
+        for later in range(step + 1, steps):
+            ahead = waits.get(("update", later), 0) if later == step + 1 else 0
+            after = [fronts[ahead]] if later < ahead < steps else []
+            pending[later] = product(
+                later, prev + step, 1, [spread], f"update{later}{step}", (pending[later], None), after
+            )
+    return None
 
 
 def solution(mesh):

time: 152 us -> 148 us (0.974)
  starting transfers between devices: 81.3 us -> 88.1 us
  waiting for transfers between devices: 52.6 us -> 47 us
  local copies, waits for them, and re-layouts: 7.7 us -> 2.52 us
    ppermute x36, starting transfers between devices: 78.6 us -> 85 us  [shift(): return lax.ppermute(value, axis, [(i, i ^ step) for i in range(n)])]
    ppermute x36, waiting for transfers between devices: 52.6 us -> 47 us  [shift(): return lax.ppermute(value, axis, [(i, i ^ step) for i in range(n)])]
    squeeze x4 -> x0, local copies, waits for them, and re-layouts: 3.87 us -> none  [square_mesh(): right_own = lax.ppermute(right_t[step, :count], ('prow', 'pcol'), flip)]
    unnamed x16 -> x20, local copies, waits for them, and re-layouts: 3.83 us -> 2.52 us
    pallas_call x14 -> x18, Pallas kernels: 4.78 us -> 5.6 us  [the longest x14 5.55 us: product(): pl.pallas_call(functools.partial(product_kernel, n, base is not None, len...]
  transfers between devices with their start and end apart: 40 -> 40, of which waited for: 18 -> 15; matrix products, arithmetic and copies ran while one was open for 2% -> 0% of each run, Pallas kernels for 5% -> 5%
where the time goes in v2:
time: 148 us
  starting transfers between devices  88.1 us (60%)
  waiting for transfers between devices  47 us (32%)
  Pallas kernels  9.54 us (6%)
  local copies, waits for them, and re-layouts  2.52 us (2%)
    ppermute x36, starting transfers between devices, shift(): return lax.ppermute(value, axis, [(i, i ^ step) for i in range(n)])  85 us
    ppermute x36, waiting for transfers between devices, shift(): return lax.ppermute(value, axis, [(i, i ^ step) for i in range(n)])  47 us
    pallas_call x14, Pallas kernels, product(): pl.pallas_call(functools.partial(product_kernel, n, base is not None, len...  5.55 us
    pallas_call x4, Pallas kernels, square_mesh(): pl.pallas_call(functools.partial(merge_kernel, step, count), grid=(1,), o...  3.94 us
    ppermute x4, starting transfers between devices, square_mesh(): right_own = lax.ppermute(packed, ('prow', 'pcol'), flip)  3.08 us
  transfers between devices with their start and end apart: 40, of which 15 were waited for; matrix products, arithmetic and copies ran while one was open for 0% of the time, Pallas kernels for 5%

profile of v2, /device:TPU:0, one launch (start us, length us, event | category | flops | bytes accessed | tf_op | source)
XLA Modules:
  0.0 147.5 jit_solution(12697728221810043973)
XLA Ops:
  0.0 1.3 copy-done.1
  2.1 4.3 %collective-permute-start.16 = (f32[4,128,128]{2,1,0:T(8,128)}, f32[4,128,128]{2,1,0:T(8,128)S(1)}, u32[]{:S(2)}, u32[]{:S(2)}) collective-permute-start(f32[4,128,128]{2,1,0:T(8,128)} %refs_4_.7), channel_id=1, source_target_pairs={{0,4},{4,0},{8,12},{12,8},{1,5},{5,1},{9,13},{13,9},{2,6},{6,2},{1... | collective-permute-start | bytes 786440 | tf_op jit(solution)/shard_map/ppermute | solution.py:166
  10.4 8.0 %collective-permute-start.14 = (f32[5,128,128]{2,1,0:T(8,128)S(1)}, f32[5,128,128]{2,1,0:T(8,128)S(1)}, u32[]{:S(2)}, u32[]{:S(2)}) collective-permute-start(f32[5,128,128]{2,1,0:T(8,128)S(1)} %merge0.1.refs_0_), channel_id=1, source_target_pairs={{0,2},{1,3},{2,0},{3,1},{4,6},{5,7},{6,4},{7,5},{8,10},{9,11},{10,... | collective-permute-start | bytes 983048 | tf_op jit(solution)/shard_map/ppermute | solution.py:166
  18.3 4.2 %collective-permute-start.13 = (f32[5,128,128]{2,1,0:T(8,128)S(1)}, f32[5,128,128]{2,1,0:T(8,128)S(1)}, u32[]{:S(2)}, u32[]{:S(2)}) collective-permute-start(f32[5,128,128]{2,1,0:T(8,128)S(1)} %merge0.1.refs_0_), channel_id=1, source_target_pairs={{0,1},{1,0},{2,3},{3,2},{4,5},{5,4},{6,7},{7,6},{8,9},{9,8},{10,11... | collective-permute-start | bytes 983048 | tf_op jit(solution)/shard_map/ppermute | solution.py:166
  23.3 7.1 %collective-permute-start.18 = (f32[4,128,128]{2,1,0:T(8,128)S(1)}, f32[4,128,128]{2,1,0:T(8,128)S(1)}, u32[]{:S(2)}, u32[]{:S(2)}) collective-permute-start(f32[4,128,128]{2,1,0:T(8,128)S(1)} %copy-done.6), channel_id=1, source_target_pairs={{0,12},{4,8},{8,4},{12,0},{1,13},{5,9},{9,5},{13,1},{2,14},{6,10},... | collective-permute-start | bytes 786440 | tf_op jit(solution)/shard_map/ppermute | solution.py:166
  31.4 19.5 %collective-permute-start.7 = (f32[7,128,128]{2,1,0:T(8,128)S(1)}, f32[7,128,128]{2,1,0:T(8,128)S(1)}, u32[]{:S(2)}, u32[]{:S(2)}) collective-permute-start(f32[7,128,128]{2,1,0:T(8,128)S(1)} %merge2.1.refs_0_), channel_id=1, source_target_pairs={{0,2},{1,3},{2,0},{3,1},{4,6},{5,7},{6,4},{7,5},{8,10},{9,11},{10,... | collective-permute-start | bytes 1376264 | tf_op jit(solution)/shard_map/ppermute | solution.py:166
  53.0 2.1 %collective-permute-start.11 = (f32[6,128,128]{2,1,0:T(8,128)S(1)}, f32[6,128,128]{2,1,0:T(8,128)S(1)}, u32[]{:S(2)}, u32[]{:S(2)}) collective-permute-start(f32[6,128,128]{2,1,0:T(8,128)S(1)} %merge1.1.refs_0_), channel_id=1, source_target_pairs={{0,2},{1,3},{2,0},{3,1},{4,6},{5,7},{6,4},{7,5},{8,10},{9,11},{10,... | collective-permute-start | bytes 1179656 | tf_op jit(solution)/shard_map/ppermute | solution.py:166
  55.6 1.7 %collective-permute-done.15.refs_3_ = f32[5,128,128]{2,1,0:T(8,128)S(1)} collective-permute-done((f32[5,128,128]{2,1,0:T(8,128)S(1)}, f32[5,128,128]{2,1,0:T(8,128)S(1)}, u32[]{:S(2)}, u32[]{:S(2)}) %collective-permute-start.15) | collective-permute-done | bytes 327712 | tf_op jit(solution)/shard_map/ppermute | solution.py:166
  57.9 13.6 %collective-permute-done.11.refs_2_ = f32[6,128,128]{2,1,0:T(8,128)S(1)} collective-permute-done((f32[6,128,128]{2,1,0:T(8,128)S(1)}, f32[6,128,128]{2,1,0:T(8,128)S(1)}, u32[]{:S(2)}, u32[]{:S(2)}) %collective-permute-start.11) | collective-permute-done | bytes 393248 | tf_op jit(solution)/shard_map/ppermute | solution.py:166
  72.0 1.6 %collective-permute-start.20 = (f32[128,128]{1,0:T(8,128)S(1)}, f32[128,128]{1,0:T(8,128)S(1)}, u32[]{:S(2)}, u32[]{:S(2)}) collective-permute-start(f32[128,128]{1,0:T(8,128)S(1)} %early0.1.refs_4_), channel_id=1, source_target_pairs={{0,8},{4,12},{8,0},{12,4},{1,9},{5,13},{9,1},{13,5},{2,10},{6,14},... | collective-permute-start | bytes 196616 | tf_op jit(solution)/shard_map/ppermute | solution.py:166
  73.8 3.4 %collective-permute-done.20.refs_6_ = f32[128,128]{1,0:T(8,128)S(1)} collective-permute-done((f32[128,128]{1,0:T(8,128)S(1)}, f32[128,128]{1,0:T(8,128)S(1)}, u32[]{:S(2)}, u32[]{:S(2)}) %collective-permute-start.20) | collective-permute-done | bytes 65568 | tf_op jit(solution)/shard_map/ppermute | solution.py:166
  77.7 9.2 %collective-permute-start.21 = (f32[128,128]{1,0:T(8,128)S(1)}, f32[128,128]{1,0:T(8,128)S(1)}, u32[]{:S(2)}, u32[]{:S(2)}) collective-permute-start(f32[128,128]{1,0:T(8,128)S(1)} %early0.1.refs_4_), channel_id=1, source_target_pairs={{0,12},{4,8},{8,4},{12,0},{1,13},{5,9},{9,5},{13,1},{2,14},{6,10},... | collective-permute-start | bytes 196616 | tf_op jit(solution)/shard_map/ppermute | solution.py:166
  87.4 1.8 %collective-permute-done.21.refs_7_ = f32[128,128]{1,0:T(8,128)S(1)} collective-permute-done((f32[128,128]{1,0:T(8,128)S(1)}, f32[128,128]{1,0:T(8,128)S(1)}, u32[]{:S(2)}, u32[]{:S(2)}) %collective-permute-start.21) | collective-permute-done | bytes 65568 | tf_op jit(solution)/shard_map/ppermute | solution.py:166
  89.4 2.5 %collective-permute-start.22 = (f32[128,128]{1,0:T(8,128)S(1)}, f32[128,128]{1,0:T(8,128)S(1)}, u32[]{:S(2)}, u32[]{:S(2)}) collective-permute-start(f32[128,128]{1,0:T(8,128)S(1)} %solve0.1.refs_4_.refs_8_), channel_id=1, source_target_pairs={{0,4},{4,0},{8,12},{12,8},{1,5},{5,1},{9,13},{13,9},{2,6},{6,2},{1... | collective-permute-start | bytes 196616 | tf_op jit(solution)/shard_map/ppermute | solution.py:166
  91.9 1.9 %collective-permute-start.23 = (f32[128,128]{1,0:T(8,128)S(1)}, f32[128,128]{1,0:T(8,128)S(1)}, u32[]{:S(2)}, u32[]{:S(2)}) collective-permute-start(f32[128,128]{1,0:T(8,128)S(1)} %solve0.1.refs_4_.refs_8_), channel_id=1, source_target_pairs={{0,8},{4,12},{8,0},{12,4},{1,9},{5,13},{9,1},{13,5},{2,10},{6,14},... | collective-permute-start | bytes 196616 | tf_op jit(solution)/shard_map/ppermute | solution.py:166
  95.0 3.5 %collective-permute-done.23.refs_6_ = f32[128,128]{1,0:T(8,128)S(1)} collective-permute-done((f32[128,128]{1,0:T(8,128)S(1)}, f32[128,128]{1,0:T(8,128)S(1)}, u32[]{:S(2)}, u32[]{:S(2)}) %collective-permute-start.23) | collective-permute-done | bytes 65568 | tf_op jit(solution)/shard_map/ppermute | solution.py:166
  98.5 1.4 collective-permute-done.24.refs_7_
  100.3 1.9 %collective-permute-start.26 = (f32[128,128]{1,0:T(8,128)S(1)}, f32[128,128]{1,0:T(8,128)S(1)}, u32[]{:S(2)}, u32[]{:S(2)}) collective-permute-start(f32[128,128]{1,0:T(8,128)S(1)} %update10.1.refs_4_), channel_id=1, source_target_pairs={{0,8},{4,12},{8,0},{12,4},{1,9},{5,13},{9,1},{13,5},{2,10},{6,14},... | collective-permute-start | bytes 196616 | tf_op jit(solution)/shard_map/ppermute | solution.py:166
  102.2 2.5 %collective-permute-start.27 = (f32[128,128]{1,0:T(8,128)S(1)}, f32[128,128]{1,0:T(8,128)S(1)}, u32[]{:S(2)}, u32[]{:S(2)}) collective-permute-start(f32[128,128]{1,0:T(8,128)S(1)} %update10.1.refs_4_), channel_id=1, source_target_pairs={{0,12},{4,8},{8,4},{12,0},{1,13},{5,9},{9,5},{13,1},{2,14},{6,10},... | collective-permute-start | bytes 196616 | tf_op jit(solution)/shard_map/ppermute | solution.py:166
  105.9 2.4 %collective-permute-done.27.refs_7_ = f32[128,128]{1,0:T(8,128)S(1)} collective-permute-done((f32[128,128]{1,0:T(8,128)S(1)}, f32[128,128]{1,0:T(8,128)S(1)}, u32[]{:S(2)}, u32[]{:S(2)}) %collective-permute-start.27) | collective-permute-done | bytes 65568 | tf_op jit(solution)/shard_map/ppermute | solution.py:166
  108.7 3.6 %collective-permute-start.29 = (f32[128,128]{1,0:T(8,128)S(1)}, f32[128,128]{1,0:T(8,128)S(1)}, u32[]{:S(2)}, u32[]{:S(2)}) collective-permute-start(f32[128,128]{1,0:T(8,128)S(1)} %solve1.1.refs_4_.refs_9_), channel_id=1, source_target_pairs={{0,8},{4,12},{8,0},{12,4},{1,9},{5,13},{9,1},{13,5},{2,10},{6,14},... | collective-permute-start | bytes 196616 | tf_op jit(solution)/shard_map/ppermute | solution.py:166
  113.4 1.2 collective-permute-done.29.refs_6_
  114.6 4.2 %collective-permute-done.30.refs_7_ = f32[128,128]{1,0:T(8,128)S(1)} collective-permute-done((f32[128,128]{1,0:T(8,128)S(1)}, f32[128,128]{1,0:T(8,128)S(1)}, u32[]{:S(2)}, u32[]{:S(2)}) %collective-permute-start.30) | collective-permute-done | bytes 65568 | tf_op jit(solution)/shard_map/ppermute | solution.py:166
  120.3 3.2 %collective-permute-start.33 = (f32[128,128]{1,0:T(8,128)S(1)}, f32[128,128]{1,0:T(8,128)S(1)}, u32[]{:S(2)}, u32[]{:S(2)}) collective-permute-start(f32[128,128]{1,0:T(8,128)S(1)} %update21.1.refs_4_), channel_id=1, source_target_pairs={{0,12},{4,8},{8,4},{12,0},{1,13},{5,9},{9,5},{13,1},{2,14},{6,10},... | collective-permute-start | bytes 196616 | tf_op jit(solution)/shard_map/ppermute | solution.py:166
  123.5 1.6 %collective-permute-done.31.refs_5_ = f32[128,128]{1,0:T(8,128)S(1)} collective-permute-done((f32[128,128]{1,0:T(8,128)S(1)}, f32[128,128]{1,0:T(8,128)S(1)}, u32[]{:S(2)}, u32[]{:S(2)}) %collective-permute-start.31) | collective-permute-done | bytes 65568 | tf_op jit(solution)/shard_map/ppermute | solution.py:166
  125.1 2.7 %collective-permute-done.32.refs_6_ = f32[128,128]{1,0:T(8,128)S(1)} collective-permute-done((f32[128,128]{1,0:T(8,128)S(1)}, f32[128,128]{1,0:T(8,128)S(1)}, u32[]{:S(2)}, u32[]{:S(2)}) %collective-permute-start.32) | collective-permute-done | bytes 65568 | tf_op jit(solution)/shard_map/ppermute | solution.py:166
  128.0 2.0 %collective-permute-start.34 = (f32[128,128]{1,0:T(8,128)S(1)}, f32[128,128]{1,0:T(8,128)S(1)}, u32[]{:S(2)}, u32[]{:S(2)}) collective-permute-start(f32[128,128]{1,0:T(8,128)S(1)} %solve2.1.refs_4_.refs_10_), channel_id=1, source_target_pairs={{0,4},{4,0},{8,12},{12,8},{1,5},{5,1},{9,13},{13,9},{2,6},{6,2},{1... | collective-permute-start | bytes 196616 | tf_op jit(solution)/shard_map/ppermute | solution.py:166
  130.7 1.9 %collective-permute-start.36 = (f32[128,128]{1,0:T(8,128)S(1)}, f32[128,128]{1,0:T(8,128)S(1)}, u32[]{:S(2)}, u32[]{:S(2)}) collective-permute-start(f32[128,128]{1,0:T(8,128)S(1)} %solve2.1.refs_4_.refs_10_), channel_id=1, source_target_pairs={{0,12},{4,8},{8,4},{12,0},{1,13},{5,9},{9,5},{13,1},{2,14},{6,10},... | collective-permute-start | bytes 196616 | tf_op jit(solution)/shard_map/ppermute | solution.py:166
  133.1 4.7 %collective-permute-done.35.refs_6_ = f32[128,128]{1,0:T(8,128)S(1)} collective-permute-done((f32[128,128]{1,0:T(8,128)S(1)}, f32[128,128]{1,0:T(8,128)S(1)}, u32[]{:S(2)}, u32[]{:S(2)}) %collective-permute-start.35) | collective-permute-done | bytes 65568 | tf_op jit(solution)/shard_map/ppermute | solution.py:166
  138.1 1.7 %collective-permute-start.37 = (f32[128,128]{1,0:T(8,128)S(1)}, f32[128,128]{1,0:T(8,128)S(1)}, u32[]{:S(2)}, u32[]{:S(2)}) collective-permute-start(f32[128,128]{1,0:T(8,128)S(1)} %update32.1.refs_4_), channel_id=1, source_target_pairs={{0,4},{4,0},{8,12},{12,8},{1,5},{5,1},{9,13},{13,9},{2,6},{6,2},{1... | collective-permute-start | bytes 196616 | tf_op jit(solution)/shard_map/ppermute | solution.py:166
  140.4 2.1 %collective-permute-start.39 = (f32[128,128]{1,0:T(8,128)S(1)}, f32[128,128]{1,0:T(8,128)S(1)}, u32[]{:S(2)}, u32[]{:S(2)}) collective-permute-start(f32[128,128]{1,0:T(8,128)S(1)} %update32.1.refs_4_), channel_id=1, source_target_pairs={{0,12},{4,8},{8,4},{12,0},{1,13},{5,9},{9,5},{13,1},{2,14},{6,10},... | collective-permute-start | bytes 196616 | tf_op jit(solution)/shard_map/ppermute | solution.py:166
  142.5 2.9 %collective-permute-done.38.refs_6_ = f32[128,128]{1,0:T(8,128)S(1)} collective-permute-done((f32[128,128]{1,0:T(8,128)S(1)}, f32[128,128]{1,0:T(8,128)S(1)}, u32[]{:S(2)}, u32[]{:S(2)}) %collective-permute-start.38) | collective-permute-done | bytes 65568 | tf_op jit(solution)/shard_map/ppermute | solution.py:166
  (90 shorter events, 21.4 us)
Async XLA Ops:
  1.3 6.0 %collective-permute-start = (f32[4,64,128]{2,1,0:T(8,128)S(1)}, f32[4,64,128]{2,1,0:T(8,128)S(1)}, u32[]{:S(2)}, u32[]{:S(2)}) collective-permute-start(f32[4,64,128]{2,1,0:T(8,128)S(1)} %pack0.1), channel_id=1, source_target_pairs={{0,0},{2,4},{1,8},{3,12},{6,1},{4,5},{7,9},{5,13},{9,2},{11,6},{8,... | collective-permute-start | bytes 393224 | tf_op jit(solution)/shard_map/ppermute | solution.py:194
  2.1 20.5 %collective-permute-start.16 = (f32[4,128,128]{2,1,0:T(8,128)}, f32[4,128,128]{2,1,0:T(8,128)S(1)}, u32[]{:S(2)}, u32[]{:S(2)}) collective-permute-start(f32[4,128,128]{2,1,0:T(8,128)} %refs_4_.7), channel_id=1, source_target_pairs={{0,4},{4,0},{8,12},{12,8},{1,5},{5,1},{9,13},{13,9},{2,6},{6,2},{1... | collective-permute-start | bytes 786440 | tf_op jit(solution)/shard_map/ppermute | solution.py:166
  6.5 16.1 %collective-permute-start.9 = (f32[5,64,128]{2,1,0:T(8,128)S(1)}, f32[5,64,128]{2,1,0:T(8,128)S(1)}, u32[]{:S(2)}, u32[]{:S(2)}) collective-permute-start(f32[5,64,128]{2,1,0:T(8,128)S(1)} %pack1.1), channel_id=1, source_target_pairs={{0,0},{2,4},{1,8},{3,12},{6,1},{4,5},{7,9},{5,13},{9,2},{11,6},{8,... | collective-permute-start | bytes 491528 | tf_op jit(solution)/shard_map/ppermute | solution.py:194
  9.5 13.8 %collective-permute-start.5 = (f32[6,64,128]{2,1,0:T(8,128)S(1)}, f32[6,64,128]{2,1,0:T(8,128)S(1)}, u32[]{:S(2)}, u32[]{:S(2)}) collective-permute-start(f32[6,64,128]{2,1,0:T(8,128)S(1)} %pack2.1), channel_id=1, source_target_pairs={{0,0},{2,4},{1,8},{3,12},{6,1},{4,5},{7,9},{5,13},{9,2},{11,6},{8,... | collective-permute-start | bytes 589832 | tf_op jit(solution)/shard_map/ppermute | solution.py:194
  10.4 44.7 %collective-permute-start.14 = (f32[5,128,128]{2,1,0:T(8,128)S(1)}, f32[5,128,128]{2,1,0:T(8,128)S(1)}, u32[]{:S(2)}, u32[]{:S(2)}) collective-permute-start(f32[5,128,128]{2,1,0:T(8,128)S(1)} %merge0.1.refs_0_), channel_id=1, source_target_pairs={{0,2},{1,3},{2,0},{3,1},{4,6},{5,7},{6,4},{7,5},{8,10},{9,11},{10,... | collective-permute-start | bytes 983048 | tf_op jit(solution)/shard_map/ppermute | solution.py:166
  18.3 36.8 %collective-permute-start.13 = (f32[5,128,128]{2,1,0:T(8,128)S(1)}, f32[5,128,128]{2,1,0:T(8,128)S(1)}, u32[]{:S(2)}, u32[]{:S(2)}) collective-permute-start(f32[5,128,128]{2,1,0:T(8,128)S(1)} %merge0.1.refs_0_), channel_id=1, source_target_pairs={{0,1},{1,0},{2,3},{3,2},{4,5},{5,4},{6,7},{7,6},{8,9},{9,8},{10,11... | collective-permute-start | bytes 983048 | tf_op jit(solution)/shard_map/ppermute | solution.py:166
  22.6 29.4 %collective-permute-start.17 = (f32[4,128,128]{2,1,0:T(8,128)S(1)}, f32[4,128,128]{2,1,0:T(8,128)S(1)}, u32[]{:S(2)}, u32[]{:S(2)}) collective-permute-start(f32[4,128,128]{2,1,0:T(8,128)S(1)} %copy-done.6), channel_id=1, source_target_pairs={{0,8},{4,12},{8,0},{12,4},{1,9},{5,13},{9,1},{13,5},{2,10},{6,14},... | collective-permute-start | bytes 786440 | tf_op jit(solution)/shard_map/ppermute | solution.py:166
  22.6 8.8 %collective-permute-start.1 = (f32[7,64,128]{2,1,0:T(8,128)S(1)}, f32[7,64,128]{2,1,0:T(8,128)S(1)}, u32[]{:S(2)}, u32[]{:S(2)}) collective-permute-start(f32[7,64,128]{2,1,0:T(8,128)S(1)} %pack3.1), channel_id=1, source_target_pairs={{0,0},{2,4},{1,8},{3,12},{6,1},{4,5},{7,9},{5,13},{9,2},{11,6},{8,... | collective-permute-start | bytes 688136 | tf_op jit(solution)/shard_map/ppermute | solution.py:194
  23.3 29.7 %collective-permute-start.18 = (f32[4,128,128]{2,1,0:T(8,128)S(1)}, f32[4,128,128]{2,1,0:T(8,128)S(1)}, u32[]{:S(2)}, u32[]{:S(2)}) collective-permute-start(f32[4,128,128]{2,1,0:T(8,128)S(1)} %copy-done.6), channel_id=1, source_target_pairs={{0,12},{4,8},{8,4},{12,0},{1,13},{5,9},{9,5},{13,1},{2,14},{6,10},... | collective-permute-start | bytes 786440 | tf_op jit(solution)/shard_map/ppermute | solution.py:166
  31.4 40.6 %collective-permute-start.7 = (f32[7,128,128]{2,1,0:T(8,128)S(1)}, f32[7,128,128]{2,1,0:T(8,128)S(1)}, u32[]{:S(2)}, u32[]{:S(2)}) collective-permute-start(f32[7,128,128]{2,1,0:T(8,128)S(1)} %merge2.1.refs_0_), channel_id=1, source_target_pairs={{0,2},{1,3},{2,0},{3,1},{4,6},{5,7},{6,4},{7,5},{8,10},{9,11},{10,... | collective-permute-start | bytes 1376264 | tf_op jit(solution)/shard_map/ppermute | solution.py:166
  51.9 25.2 %collective-permute-start.3 = (f32[8,128,128]{2,1,0:T(8,128)S(1)}, f32[8,128,128]{2,1,0:T(8,128)S(1)}, u32[]{:S(2)}, u32[]{:S(2)}) collective-permute-start(f32[8,128,128]{2,1,0:T(8,128)S(1)} %merge3.1.refs_0_), channel_id=1, source_target_pairs={{0,2},{1,3},{2,0},{3,1},{4,6},{5,7},{6,4},{7,5},{8,10},{9,11},{10,... | collective-permute-start | bytes 1572872 | tf_op jit(solution)/shard_map/ppermute | solution.py:166
  53.0 18.5 %collective-permute-start.11 = (f32[6,128,128]{2,1,0:T(8,128)S(1)}, f32[6,128,128]{2,1,0:T(8,128)S(1)}, u32[]{:S(2)}, u32[]{:S(2)}) collective-permute-start(f32[6,128,128]{2,1,0:T(8,128)S(1)} %merge1.1.refs_0_), channel_id=1, source_target_pairs={{0,2},{1,3},{2,0},{3,1},{4,6},{5,7},{6,4},{7,5},{8,10},{9,11},{10,... | collective-permute-start | bytes 1179656 | tf_op jit(solution)/shard_map/ppermute | solution.py:166
  55.1 16.4 %collective-permute-start.10 = (f32[6,128,128]{2,1,0:T(8,128)S(1)}, f32[6,128,128]{2,1,0:T(8,128)S(1)}, u32[]{:S(2)}, u32[]{:S(2)}) collective-permute-start(f32[6,128,128]{2,1,0:T(8,128)S(1)} %merge1.1.refs_0_), channel_id=1, source_target_pairs={{0,1},{1,0},{2,3},{3,2},{4,5},{5,4},{6,7},{7,6},{8,9},{9,8},{10,11... | collective-permute-start | bytes 1179656 | tf_op jit(solution)/shard_map/ppermute | solution.py:166
  57.8 15.8 %collective-permute-start.19 = (f32[128,128]{1,0:T(8,128)S(1)}, f32[128,128]{1,0:T(8,128)S(1)}, u32[]{:S(2)}, u32[]{:S(2)}) collective-permute-start(f32[128,128]{1,0:T(8,128)S(1)} %early0.1.refs_4_), channel_id=1, source_target_pairs={{0,4},{4,0},{8,12},{12,8},{1,5},{5,1},{9,13},{13,9},{2,6},{6,2},{1... | collective-permute-start | bytes 196616 | tf_op jit(solution)/shard_map/ppermute | solution.py:166
  71.5 6.2 %collective-permute-start.12 = (f32[6,128,128]{2,1,0:T(8,128)S(1)}, f32[6,128,128]{2,1,0:T(8,128)S(1)}, u32[]{:S(2)}, u32[]{:S(2)}) collective-permute-start(f32[6,128,128]{2,1,0:T(8,128)S(1)} %collective-permute-done.11.refs_2_), channel_id=1, source_target_pairs={{0,1},{1,0},{2,3},{3,2},{4,5},{5,4},{6,7},{7,6},{8,9},{9,8},{10,11... | collective-permute-start | bytes 1179656 | tf_op jit(solution)/shard_map/ppermute | solution.py:166
  71.5 20.4 %collective-permute-start.6 = (f32[7,128,128]{2,1,0:T(8,128)S(1)}, f32[7,128,128]{2,1,0:T(8,128)S(1)}, u32[]{:S(2)}, u32[]{:S(2)}) collective-permute-start(f32[7,128,128]{2,1,0:T(8,128)S(1)} %merge2.1.refs_0_), channel_id=1, source_target_pairs={{0,1},{1,0},{2,3},{3,2},{4,5},{5,4},{6,7},{7,6},{8,9},{9,8},{10,11... | collective-permute-start | bytes 1376264 | tf_op jit(solution)/shard_map/ppermute | solution.py:166
  73.6 20.3 %collective-permute-start.8 = (f32[7,128,128]{2,1,0:T(8,128)S(1)}, f32[7,128,128]{2,1,0:T(8,128)S(1)}, u32[]{:S(2)}, u32[]{:S(2)}) collective-permute-start(f32[7,128,128]{2,1,0:T(8,128)S(1)} %collective-permute-done.7.refs_2_), channel_id=1, source_target_pairs={{0,1},{1,0},{2,3},{3,2},{4,5},{5,4},{6,7},{7,6},{8,9},{9,8},{10,11... | collective-permute-start | bytes 1376264 | tf_op jit(solution)/shard_map/ppermute | solution.py:166
  77.2 27.5 %collective-permute-start.2 = (f32[8,128,128]{2,1,0:T(8,128)S(1)}, f32[8,128,128]{2,1,0:T(8,128)S(1)}, u32[]{:S(2)}, u32[]{:S(2)}) collective-permute-start(f32[8,128,128]{2,1,0:T(8,128)S(1)} %merge3.1.refs_0_), channel_id=1, source_target_pairs={{0,1},{1,0},{2,3},{3,2},{4,5},{5,4},{6,7},{7,6},{8,9},{9,8},{10,11... | collective-permute-start | bytes 1572872 | tf_op jit(solution)/shard_map/ppermute | solution.py:166
  77.2 27.5 %collective-permute-start.4 = (f32[8,128,128]{2,1,0:T(8,128)S(1)}, f32[8,128,128]{2,1,0:T(8,128)S(1)}, u32[]{:S(2)}, u32[]{:S(2)}) collective-permute-start(f32[8,128,128]{2,1,0:T(8,128)S(1)} %collective-permute-done.3.refs_2_), channel_id=1, source_target_pairs={{0,1},{1,0},{2,3},{3,2},{4,5},{5,4},{6,7},{7,6},{8,9},{9,8},{10,11... | collective-permute-start | bytes 1572872 | tf_op jit(solution)/shard_map/ppermute | solution.py:166
  77.7 11.5 %collective-permute-start.21 = (f32[128,128]{1,0:T(8,128)S(1)}, f32[128,128]{1,0:T(8,128)S(1)}, u32[]{:S(2)}, u32[]{:S(2)}) collective-permute-start(f32[128,128]{1,0:T(8,128)S(1)} %early0.1.refs_4_), channel_id=1, source_target_pairs={{0,12},{4,8},{8,4},{12,0},{1,13},{5,9},{9,5},{13,1},{2,14},{6,10},... | collective-permute-start | bytes 196616 | tf_op jit(solution)/shard_map/ppermute | solution.py:166
  91.9 6.6 %collective-permute-start.23 = (f32[128,128]{1,0:T(8,128)S(1)}, f32[128,128]{1,0:T(8,128)S(1)}, u32[]{:S(2)}, u32[]{:S(2)}) collective-permute-start(f32[128,128]{1,0:T(8,128)S(1)} %solve0.1.refs_4_.refs_8_), channel_id=1, source_target_pairs={{0,8},{4,12},{8,0},{12,4},{1,9},{5,13},{9,1},{13,5},{2,10},{6,14},... | collective-permute-start | bytes 196616 | tf_op jit(solution)/shard_map/ppermute | solution.py:166
  93.9 6.1 %collective-permute-start.24 = (f32[128,128]{1,0:T(8,128)S(1)}, f32[128,128]{1,0:T(8,128)S(1)}, u32[]{:S(2)}, u32[]{:S(2)}) collective-permute-start(f32[128,128]{1,0:T(8,128)S(1)} %solve0.1.refs_4_.refs_8_), channel_id=1, source_target_pairs={{0,12},{4,8},{8,4},{12,0},{1,13},{5,9},{9,5},{13,1},{2,14},{6,10},... | collective-permute-start | bytes 196616 | tf_op jit(solution)/shard_map/ppermute | solution.py:166
  100.2 5.7 %collective-permute-start.25 = (f32[128,128]{1,0:T(8,128)S(1)}, f32[128,128]{1,0:T(8,128)S(1)}, u32[]{:S(2)}, u32[]{:S(2)}) collective-permute-start(f32[128,128]{1,0:T(8,128)S(1)} %update10.1.refs_4_), channel_id=1, source_target_pairs={{0,4},{4,0},{8,12},{12,8},{1,5},{5,1},{9,13},{13,9},{2,6},{6,2},{1... | collective-permute-start | bytes 196616 | tf_op jit(solution)/shard_map/ppermute | solution.py:166
  102.2 6.2 %collective-permute-start.27 = (f32[128,128]{1,0:T(8,128)S(1)}, f32[128,128]{1,0:T(8,128)S(1)}, u32[]{:S(2)}, u32[]{:S(2)}) collective-permute-start(f32[128,128]{1,0:T(8,128)S(1)} %update10.1.refs_4_), channel_id=1, source_target_pairs={{0,12},{4,8},{8,4},{12,0},{1,13},{5,9},{9,5},{13,1},{2,14},{6,10},... | collective-permute-start | bytes 196616 | tf_op jit(solution)/shard_map/ppermute | solution.py:166
  108.7 5.9 %collective-permute-start.29 = (f32[128,128]{1,0:T(8,128)S(1)}, f32[128,128]{1,0:T(8,128)S(1)}, u32[]{:S(2)}, u32[]{:S(2)}) collective-permute-start(f32[128,128]{1,0:T(8,128)S(1)} %solve1.1.refs_4_.refs_9_), channel_id=1, source_target_pairs={{0,8},{4,12},{8,0},{12,4},{1,9},{5,13},{9,1},{13,5},{2,10},{6,14},... | collective-permute-start | bytes 196616 | tf_op jit(solution)/shard_map/ppermute | solution.py:166
  112.4 6.4 %collective-permute-start.30 = (f32[128,128]{1,0:T(8,128)S(1)}, f32[128,128]{1,0:T(8,128)S(1)}, u32[]{:S(2)}, u32[]{:S(2)}) collective-permute-start(f32[128,128]{1,0:T(8,128)S(1)} %solve1.1.refs_4_.refs_9_), channel_id=1, source_target_pairs={{0,12},{4,8},{8,4},{12,0},{1,13},{5,9},{9,5},{13,1},{2,14},{6,10},... | collective-permute-start | bytes 196616 | tf_op jit(solution)/shard_map/ppermute | solution.py:166
  119.1 6.0 %collective-permute-start.31 = (f32[128,128]{1,0:T(8,128)S(1)}, f32[128,128]{1,0:T(8,128)S(1)}, u32[]{:S(2)}, u32[]{:S(2)}) collective-permute-start(f32[128,128]{1,0:T(8,128)S(1)} %update21.1.refs_4_), channel_id=1, source_target_pairs={{0,4},{4,0},{8,12},{12,8},{1,5},{5,1},{9,13},{13,9},{2,6},{6,2},{1... | collective-permute-start | bytes 196616 | tf_op jit(solution)/shard_map/ppermute | solution.py:166
  119.1 8.6 %collective-permute-start.32 = (f32[128,128]{1,0:T(8,128)S(1)}, f32[128,128]{1,0:T(8,128)S(1)}, u32[]{:S(2)}, u32[]{:S(2)}) collective-permute-start(f32[128,128]{1,0:T(8,128)S(1)} %update21.1.refs_4_), channel_id=1, source_target_pairs={{0,8},{4,12},{8,0},{12,4},{1,9},{5,13},{9,1},{13,5},{2,10},{6,14},... | collective-permute-start | bytes 196616 | tf_op jit(solution)/shard_map/ppermute | solution.py:166
  120.3 7.4 %collective-permute-start.33 = (f32[128,128]{1,0:T(8,128)S(1)}, f32[128,128]{1,0:T(8,128)S(1)}, u32[]{:S(2)}, u32[]{:S(2)}) collective-permute-start(f32[128,128]{1,0:T(8,128)S(1)} %update21.1.refs_4_), channel_id=1, source_target_pairs={{0,12},{4,8},{8,4},{12,0},{1,13},{5,9},{9,5},{13,1},{2,14},{6,10},... | collective-permute-start | bytes 196616 | tf_op jit(solution)/shard_map/ppermute | solution.py:166
  130.1 7.7 %collective-permute-start.35 = (f32[128,128]{1,0:T(8,128)S(1)}, f32[128,128]{1,0:T(8,128)S(1)}, u32[]{:S(2)}, u32[]{:S(2)}) collective-permute-start(f32[128,128]{1,0:T(8,128)S(1)} %solve2.1.refs_4_.refs_10_), channel_id=1, source_target_pairs={{0,8},{4,12},{8,0},{12,4},{1,9},{5,13},{9,1},{13,5},{2,10},{6,14},... | collective-permute-start | bytes 196616 | tf_op jit(solution)/shard_map/ppermute | solution.py:166
  130.7 7.1 %collective-permute-start.36 = (f32[128,128]{1,0:T(8,128)S(1)}, f32[128,128]{1,0:T(8,128)S(1)}, u32[]{:S(2)}, u32[]{:S(2)}) collective-permute-start(f32[128,128]{1,0:T(8,128)S(1)} %solve2.1.refs_4_.refs_10_), channel_id=1, source_target_pairs={{0,12},{4,8},{8,4},{12,0},{1,13},{5,9},{9,5},{13,1},{2,14},{6,10},... | collective-permute-start | bytes 196616 | tf_op jit(solution)/shard_map/ppermute | solution.py:166
  140.4 6.2 %collective-permute-start.39 = (f32[128,128]{1,0:T(8,128)S(1)}, f32[128,128]{1,0:T(8,128)S(1)}, u32[]{:S(2)}, u32[]{:S(2)}) collective-permute-start(f32[128,128]{1,0:T(8,128)S(1)} %update32.1.refs_4_), channel_id=1, source_target_pairs={{0,12},{4,8},{8,4},{12,0},{1,13},{5,9},{9,5},{13,1},{2,14},{6,10},... | collective-permute-start | bytes 196616 | tf_op jit(solution)/shard_map/ppermute | solution.py:166
  (18 other events, 109.6 us)

commit v3 on v2

--- a/solution.py
+++ b/solution.py
@@ -89,40 +89,52 @@
     return (out[:rows, :cols] + (out[:rows, cols:] + out[rows:, :cols])) + out[rows:, cols:]
 
 
-def pack_kernel(count, right_ref, *refs):
-    refs[-1][...] = right_ref[0, :count]
-
-
-def merge_kernel(step, count, ranks_ref, flags_ref, dense_ref, left_ref, right_ref, inv_ref, out_ref):
+def pack_kernel(pieces, right_ref, *refs):
+    out_ref = refs[-1]
+    place = 0
+    for index, count in enumerate(pieces):
+        out_ref[place : place + count] = right_ref[index, :count]
+        place += count
+
+
+def merge_kernel(order, ranks_ref, flags_ref, dense_ref, left_ref, right_ref, inv_ref, *refs):
+    out_ref = refs[-1]
     rank_pad, rows = left_ref.shape[2:]
     row_at = lax.broadcasted_iota(jnp.int32, (rank_pad, rows), 0)
-    for col in range(count):
+    for place, (first, step, col, packed) in enumerate(order):
+        if col is None:
+            out_ref[place] = inv_ref[step - first]
+            continue
         flag = flags_ref[step, col].astype(jnp.float32)
         mask = jnp.where(row_at < ranks_ref[step, col], 1.0 - flag, 0.0)
-        low = dot_split(left_ref[0, col] * mask, right_ref[col], (((0,), (0,)), ((), ())))
-        out_ref[col] = dense_ref[0, col] * flag + low
-    out_ref[count] = inv_ref[0]
-
-
-def product_kernel(n, based, blocks, tiles, before, *refs):
-    strips = refs[:n]
-    sources = refs[n : n + n * blocks]
-    rest = refs[n + n * blocks :]
+        left = left_ref[step - first, col] * mask
+        low = dot_split(left, right_ref[packed], (((0,), (0,)), ((), ())))
+        out_ref[place] = dense_ref[step - first, col] * flag + low
+
+
+def product_kernel(n, slots, wholes, based, tiles, before, *refs):
+    count = n if slots else 1
+    strips = refs[:count]
+    sources = refs[count : count + (1 if wholes else n)]
+    rest = refs[count + len(sources) :]
     out_ref, source_scr = rest[-2:]
     nb = out_ref.shape[-2]
-    per_block = tiles // blocks
-    turn = lax.axis_index("prow") ^ lax.axis_index("pcol")
+    turn = 0
+    if slots:
+        turn = turn ^ lax.axis_index("pcol")
+    if not wholes:
+        turn = turn ^ lax.axis_index("prow")
     for slot in range(n):
-        place = pl.multiple_of((turn ^ slot) * nb, nb)
-        for block in range(blocks):
-            ref = sources[block * n + slot]
-            for tile in range(per_block):
-                value = ref[tile] if len(ref.shape) == 3 else ref[...]
-                source_scr[block * per_block + tile, pl.ds(place, nb), :] = value
+        place = (turn ^ slot) * nb
+        if slots or not wholes:
+            place = pl.multiple_of(place, nb)
+        for tile in range(tiles):
+            value = sources[0][slot, tile] if wholes else sources[slot][...]
+            source_scr[tile, pl.ds(place, nb), :] = value
     total = None
     for tile in range(tiles):
-        strip = jnp.concatenate([strips[d][tile] for d in range(n)], axis=1)
-        part = dot_split(strip, source_scr[tile])
+        parts = [strips[d][tile] if slots else strips[0][d, tile] for d in range(n)]
+        part = dot_split(jnp.concatenate(parts, axis=1), source_scr[tile])
         total = part if total is None else total + part
     if based:
         base_ref = rest[0]
@@ -176,57 +188,62 @@
             flip.append((owner * n + source, row * n + owner))
 
     any_spec = pl.BlockSpec(memory_space=pl.ANY)
-    known = over_rows(earlier)
-    strips = []
-    own = []
-    for step in range(steps):
-        count = prev + step
-        after = [] if step < 2 else [own[0]]
-        packed = pl.pallas_call(
-            functools.partial(pack_kernel, count),
+
+    def packed(first, pieces, after=()):
+        shape = (sum(pieces), rank_pad, nb)
+        own = pl.pallas_call(
+            functools.partial(pack_kernel, pieces),
             grid=(1,),
-            out_shape=jax.ShapeDtypeStruct((count, rank_pad, nb), f32),
-            in_specs=[spec_of((1, cols, rank_pad, nb), (step, 0, 0, 0))] + [any_spec] * len(after),
-            out_specs=spec_of((count, rank_pad, nb)),
+            out_shape=jax.ShapeDtypeStruct(shape, f32),
+            in_specs=[spec_of((len(pieces), cols, rank_pad, nb), (first // len(pieces), 0, 0, 0))]
+            + [any_spec] * len(after),
+            out_specs=spec_of(shape),
             compiler_params=params,
-            name=f"pack{step}",
+            name=f"pack{first}",
         )(right_t, *after)
-        right_own = lax.ppermute(packed, ("prow", "pcol"), flip)
-        own.append(pl.pallas_call(
-            functools.partial(merge_kernel, step, count),
+        return lax.ppermute(own, ("prow", "pcol"), flip)
+
+    def merged(order, block_rows, right_own, after=()):
+        first = order[0][0]
+        shape = (len(order), nb, nb)
+        index = first // block_rows
+        return pl.pallas_call(
+            functools.partial(merge_kernel, order),
             grid=(1,),
-            out_shape=jax.ShapeDtypeStruct((count + 1, nb, nb), f32),
+            out_shape=jax.ShapeDtypeStruct(shape, f32),
             in_specs=[
                 pl.BlockSpec(memory_space=pltpu.SMEM),
                 pl.BlockSpec(memory_space=pltpu.SMEM),
-                spec_of((1, cols, nb, nb), (step, 0, 0, 0)),
-                spec_of((1, cols, rank_pad, nb), (step, 0, 0, 0)),
-                spec_of((count, rank_pad, nb)),
-                spec_of((1, nb, nb), (step, 0, 0)),
-            ],
-            out_specs=spec_of((count + 1, nb, nb)),
+                spec_of((block_rows, cols, nb, nb), (index, 0, 0, 0)),
+                spec_of((block_rows, cols, rank_pad, nb), (index, 0, 0, 0)),
+                spec_of(right_own.shape),
+                spec_of((block_rows, nb, nb), (index, 0, 0)),
+            ]
+            + [any_spec] * len(after),
+            out_specs=spec_of(shape),
             compiler_params=params,
-            name=f"merge{step}",
-        )(tile_ranks, dense_flags, dense_tiles, left_t, right_own, inverse_diag))
-        slots = [own[step]]
+            name=f"merge{first}",
+        )(tile_ranks, dense_flags, dense_tiles, left_t, right_own, inverse_diag, *after)
+
+    def by_distance(own):
+        held = {0: own}
         reach = n // 2
         while reach >= 1:
-            slots = slots + [shift(v, "pcol", reach) for v in slots]
+            held |= {d ^ reach: shift(v, "pcol", reach) for d, v in held.items()}
             reach //= 2
-        order = [0]
-        reach = n // 2
-        while reach >= 1:
-            order = order + [o ^ reach for o in order]
-            reach //= 2
-        strips.append([slots[order.index(d)] for d in range(n)])
-
-    def product(step, first, tiles, blocks, name, base=None, after=(), stacked=None):
-        args = list(strips[step])
-        specs = [spec_of((tiles, nb, nb), (first // tiles, 0, 0))] * n
-        for block in blocks:
-            for value in block:
-                args.append(value)
-                specs.append(spec_of(value.shape))
+        return [held[d] for d in range(n)]
+
+    def product(strip, first, tiles, source, name, base=None, stacked=None):
+        slots, wholes = isinstance(strip, list), not isinstance(source, list)
+        if slots:
+            args = list(strip)
+            specs = [spec_of((tiles, nb, nb), (first // tiles, 0, 0))] * n
+        else:
+            args = [strip]
+            specs = [spec_of((n, tiles, nb, nb), (0, first // tiles, 0, 0))]
+        values = [source] if wholes else source
+        args += values
+        specs += [spec_of(value.shape) for value in values]
         if base is not None:
             value, index = base
             args.append(value)
@@ -239,10 +256,8 @@
             shape = (before + 1, nb, rhs)
             args += stacked
             specs += [spec_of((nb, rhs))] * before
-        args += after
-        specs += [any_spec] * len(after)
         return pl.pallas_call(
-            functools.partial(product_kernel, n, base is not None, len(blocks), tiles, before),
+            functools.partial(product_kernel, n, slots, wholes, base is not None, tiles, before),
             grid=(1,),
             out_shape=jax.ShapeDtypeStruct(shape, f32),
             in_specs=specs,
@@ -252,29 +267,50 @@
             name=name,
         )(*args)
 
-    def early(step):
-        return product(step, 0, prev, [known], f"early{step}", (right_side, step))
-
-    pending = [early(step) for step in range(steps)]
-    waits = {("solve", 0): 1, ("update", 1): 2, ("solve", 1): 3}
-    fronts = list(pending)
-    solved = []
+    known = lax.all_gather(earlier, "prow", axis=0)
+
+    ahead = 2 if steps % 2 == 0 else 1
+    groups = [tuple(range(ahead))] + [(step,) for step in range(ahead, steps)]
+    strips, where, orders = [], {}, []
+    for number, rows in enumerate(groups):
+        starts = {step: sum(prev + other for other in rows if other < step) for step in rows}
+        order = [(step, col) for step in rows for col in range(prev)]
+        order += [(step, prev + col) for step in rows for col in range(step)]
+        order += [(step, None) for step in rows]
+        for place, key in enumerate(order):
+            where[key] = (number, place)
+        orders.append(
+            tuple((rows[0], s, c, None if c is None else starts[s] + c) for s, c in order)
+        )
+
+    right_ahead = packed(0, tuple(prev + step for step in groups[0]))
+    own = merged(orders[0], ahead, right_ahead)
+    strips.append(by_distance(own))
+    later = [packed(step, (prev + step,), [own]) for step in range(ahead, steps)]
+
+    def merge_next(whole):
+        number = len(strips)
+        if number < len(groups):
+            own = merged(orders[number], 1, later[number - 1], whole[1:])
+            strips.append(lax.all_gather(own, "pcol", axis=0))
+
+    def times(key, tiles, source, name, **rest):
+        number, place = where[key]
+        return product(strips[number], place, tiles, source, name, **rest)
+
+    solved, spread = [], []
     for step in range(steps):
-        whole = over_rows(pending[step])
-        ahead = waits.get(("solve", step), 0)
-        after = [fronts[ahead]] if step < ahead < steps else []
-        stacked = solved if step + 1 == steps else None
-        block = product(step, prev + step, 1, [whole], f"solve{step}", after=after, stacked=stacked)
-        if stacked is not None:
-            return block
-        solved.append(block)
-        spread = over_rows(block)
-        for later in range(step + 1, steps):
-            ahead = waits.get(("update", later), 0) if later == step + 1 else 0
-            after = [fronts[ahead]] if later < ahead < steps else []
-            pending[later] = product(
-                later, prev + step, 1, [spread], f"update{later}{step}", (pending[later], None), after
-            )
+        pending = times((step, 0), prev, known, f"early{step}", base=(right_side, step))
+        for index in range(step):
+            name = f"update{step}{index}"
+            pending = times((step, prev + index), 1, spread[index], name, base=(pending, None))
+        whole = over_rows(pending)
+        merge_next(whole)
+        if step + 1 == steps:
+            return times((step, None), 1, whole, f"solve{step}", stacked=solved)
+        solved.append(times((step, None), 1, whole, f"solve{step}"))
+        spread.append(over_rows(solved[step]))
+        merge_next(spread[step])
     return None
 
 

time: 148 us -> 138 us (0.932)
  starting transfers between devices: 88.1 us -> 51.7 us
  local copies, waits for them, and re-layouts: 2.52 us -> 19.8 us
  between operations: 0.37 us -> 13.5 us
  waiting for transfers between devices: 47 us -> 42.9 us
    ppermute x36 -> x24, starting transfers between devices: 85 us -> 47 us  [shift(): return lax.ppermute(value, axis, [(i, i ^ step) for i in range(n)])]
    unnamed x20 -> x72, local copies, waits for them, and re-layouts: 2.52 us -> 19.8 us
    ppermute x36 -> x24, waiting for transfers between devices: 47 us -> 42.8 us  [shift(): return lax.ppermute(value, axis, [(i, i ^ step) for i in range(n)])]
    ppermute x4 -> x3, starting transfers between devices: 3.08 us -> 4.6 us  [packed(): return lax.ppermute(own, ('prow', 'pcol'), flip)]
    pallas_call x22 -> x20, Pallas kernels: 9.54 us -> 9.52 us  [the longest x14 5.29 us: product(): pl.pallas_call(functools.partial(product_kernel, n, slots, wholes, base i...]
  transfers between devices with their start and end apart: 40 -> 30, of which waited for: 15 -> 12; matrix products, arithmetic and copies ran while one was open for 0% -> 0% of each run, Pallas kernels for 5% -> 5%
where the time goes in v3:
time: 138 us; the launch traced here: 137 us
  starting transfers between devices  51.7 us (37%)
  waiting for transfers between devices  42.9 us (31%)
  local copies, waits for them, and re-layouts  19.8 us (14%)
  between operations  13.5 us (10%)
  Pallas kernels  9.52 us (7%)
    ppermute x24, starting transfers between devices, shift(): return lax.ppermute(value, axis, [(i, i ^ step) for i in range(n)])  47 us
    ppermute x24, waiting for transfers between devices, shift(): return lax.ppermute(value, axis, [(i, i ^ step) for i in range(n)])  42.8 us
    unnamed x72, local copies, waits for them, and re-layouts  19.8 us
    pallas_call x14, Pallas kernels, product(): pl.pallas_call(functools.partial(product_kernel, n, slots, wholes, base i...  5.29 us
    ppermute x3, starting transfers between devices, packed(): return lax.ppermute(own, ('prow', 'pcol'), flip)  4.6 us
    pallas_call x3, Pallas kernels, merged(): pl.pallas_call(functools.partial(merge_kernel, order), grid=(1,), out_sha...  3.5 us
  transfers between devices with their start and end apart: 30, of which 12 were waited for; matrix products, arithmetic and copies ran while one was open for 0% of the time, Pallas kernels for 5%

profile of v3, /device:TPU:0, one launch (start us, length us, event | category | flops | bytes accessed | tf_op | source)
XLA Modules:
  0.0 137.3 jit_solution(5094156126427869635)
XLA Ops:
  8.9 1.5 %copy-done.8 = f32[4,7,128,128]{3,2,1,0:T(8,128)S(1)} copy-done((f32[4,7,128,128]{3,2,1,0:T(8,128)S(1)}, f32[4,7,128,128]{3,2,1,0:T(8,128)}, u32[]{:S(2)}) %copy-start.8) | copy-done | bytes 1835032
  13.8 15.0 %collective-permute-start.3 = (f32[11,128,128]{2,1,0:T(8,128)S(1)}, f32[11,128,128]{2,1,0:T(8,128)S(1)}, u32[]{:S(2)}, u32[]{:S(2)}) collective-permute-start(f32[11,128,128]{2,1,0:T(8,128)S(1)} %merge0.1.refs_0_), channel_id=1, source_target_pairs={{0,2},{1,3},{2,0},{3,1},{4,6},{5,7},{6,4},{7,5},{8,10},{9,11},{10,... | collective-permute-start | bytes 2162696 | tf_op jit(solution)/shard_map/ppermute | solution.py:178
  28.8 15.4 %collective-permute-done.3.refs_2_ = f32[11,128,128]{2,1,0:T(8,128)S(1)} collective-permute-done((f32[11,128,128]{2,1,0:T(8,128)S(1)}, f32[11,128,128]{2,1,0:T(8,128)S(1)}, u32[]{:S(2)}, u32[]{:S(2)}) %collective-permute-start.3) | collective-permute-done | bytes 720928 | tf_op jit(solution)/shard_map/ppermute | solution.py:178
  44.9 3.0 %collective-permute-start.11 = (f32[6,64,128]{2,1,0:T(8,128)}, f32[6,64,128]{2,1,0:T(8,128)}, u32[]{:S(2)}, u32[]{:S(2)}) collective-permute-start(f32[6,64,128]{2,1,0:T(8,128)} %pack2.1), channel_id=1, source_target_pairs={{0,0},{2,4},{1,8},{3,12},{6,1},{4,5},{7,9},{5,13},{9,2},{11,6},{8,... | collective-permute-start | bytes 589832 | tf_op jit(solution)/shard_map/ppermute | solution.py:204
  47.9 1.2 copy-done.4
  49.7 2.9 %collective-permute-start.7 = (f32[128,128]{1,0:T(8,128)S(1)}, f32[128,128]{1,0:T(8,128)S(1)}, u32[]{:S(2)}, u32[]{:S(2)}) collective-permute-start(f32[128,128]{1,0:T(8,128)S(1)} %early0.1.refs_4_), channel_id=1, source_target_pairs={{0,12},{4,8},{8,4},{12,0},{1,13},{5,9},{9,5},{13,1},{2,14},{6,10},... | collective-permute-start | bytes 196616 | tf_op jit(solution)/shard_map/ppermute | solution.py:178
  52.6 1.5 %collective-permute-start.5 = (f32[128,128]{1,0:T(8,128)S(1)}, f32[128,128]{1,0:T(8,128)S(1)}, u32[]{:S(2)}, u32[]{:S(2)}) collective-permute-start(f32[128,128]{1,0:T(8,128)S(1)} %early0.1.refs_4_), channel_id=1, source_target_pairs={{0,4},{4,0},{8,12},{12,8},{1,5},{5,1},{9,13},{13,9},{2,6},{6,2},{1... | collective-permute-start | bytes 196616 | tf_op jit(solution)/shard_map/ppermute | solution.py:178
  54.1 1.7 %collective-permute-done.7.refs_7_.refs_2_ = f32[128,128]{1,0:T(8,128)S(1)} collective-permute-done((f32[128,128]{1,0:T(8,128)S(1)}, f32[128,128]{1,0:T(8,128)S(1)}, u32[]{:S(2)}, u32[]{:S(2)}) %collective-permute-start.7) | collective-permute-done | bytes 65568 | tf_op jit(solution)/shard_map/ppermute | solution.py:178
  55.8 3.9 %collective-permute-done.6.refs_6_.refs_1_ = f32[128,128]{1,0:T(8,128)S(1)} collective-permute-done((f32[128,128]{1,0:T(8,128)S(1)}, f32[128,128]{1,0:T(8,128)S(1)}, u32[]{:S(2)}, u32[]{:S(2)}) %collective-permute-start.6) | collective-permute-done | bytes 65568 | tf_op jit(solution)/shard_map/ppermute | solution.py:178
  59.7 1.4 merge2.1
  65.5 4.6 %collective-permute-start.10 = (f32[128,128]{1,0:T(8,128)S(1)}, f32[128,128]{1,0:T(8,128)S(1)}, u32[]{:S(2)}, u32[]{:S(2)}) collective-permute-start(f32[128,128]{1,0:T(8,128)S(1)} %solve0.1.refs_4_.refs_1_.refs_5_), channel_id=1, source_target_pairs={{0,12},{4,8},{8,4},{12,0},{1,13},{5,9},{9,5},{13,1},{2,14},{6,10},... | collective-permute-start | bytes 196616 | tf_op jit(solution)/shard_map/ppermute | solution.py:178
  70.8 2.4 %collective-permute-done.10.refs_2_.refs_7_.refs_4_ = f32[128,128]{1,0:T(8,128)S(1)} collective-permute-done((f32[128,128]{1,0:T(8,128)S(1)}, f32[128,128]{1,0:T(8,128)S(1)}, u32[]{:S(2)}, u32[]{:S(2)}) %collective-permute-start.10) | collective-permute-done | bytes 65568 | tf_op jit(solution)/shard_map/ppermute | solution.py:178
  73.3 5.2 %collective-permute-done.9.refs_1_.refs_6_.refs_3_ = f32[128,128]{1,0:T(8,128)S(1)} collective-permute-done((f32[128,128]{1,0:T(8,128)S(1)}, f32[128,128]{1,0:T(8,128)S(1)}, u32[]{:S(2)}, u32[]{:S(2)}) %collective-permute-start.9) | collective-permute-done | bytes 65568 | tf_op jit(solution)/shard_map/ppermute | solution.py:178
  83.9 2.9 %collective-permute-start.14 = (f32[128,128]{1,0:T(8,128)S(1)}, f32[128,128]{1,0:T(8,128)S(1)}, u32[]{:S(2)}, u32[]{:S(2)}) collective-permute-start(f32[128,128]{1,0:T(8,128)S(1)} %update10.1.refs_4_), channel_id=1, source_target_pairs={{0,12},{4,8},{8,4},{12,0},{1,13},{5,9},{9,5},{13,1},{2,14},{6,10},... | collective-permute-start | bytes 196616 | tf_op jit(solution)/shard_map/ppermute | solution.py:178
  86.9 1.5 %collective-permute-start.12 = (f32[128,128]{1,0:T(8,128)S(1)}, f32[128,128]{1,0:T(8,128)S(1)}, u32[]{:S(2)}, u32[]{:S(2)}) collective-permute-start(f32[128,128]{1,0:T(8,128)S(1)} %update10.1.refs_4_), channel_id=1, source_target_pairs={{0,4},{4,0},{8,12},{12,8},{1,5},{5,1},{9,13},{13,9},{2,6},{6,2},{1... | collective-permute-start | bytes 196616 | tf_op jit(solution)/shard_map/ppermute | solution.py:178
  88.4 1.7 %collective-permute-done.14.refs_7_ = f32[128,128]{1,0:T(8,128)S(1)} collective-permute-done((f32[128,128]{1,0:T(8,128)S(1)}, f32[128,128]{1,0:T(8,128)S(1)}, u32[]{:S(2)}, u32[]{:S(2)}) %collective-permute-start.14) | collective-permute-done | bytes 65568 | tf_op jit(solution)/shard_map/ppermute | solution.py:178
  90.1 3.5 %collective-permute-done.13.refs_6_ = f32[128,128]{1,0:T(8,128)S(1)} collective-permute-done((f32[128,128]{1,0:T(8,128)S(1)}, f32[128,128]{1,0:T(8,128)S(1)}, u32[]{:S(2)}, u32[]{:S(2)}) %collective-permute-start.13) | collective-permute-done | bytes 65568 | tf_op jit(solution)/shard_map/ppermute | solution.py:178
  93.9 2.8 %collective-permute-start.17 = (f32[128,128]{1,0:T(8,128)S(1)}, f32[128,128]{1,0:T(8,128)S(1)}, u32[]{:S(2)}, u32[]{:S(2)}) collective-permute-start(f32[128,128]{1,0:T(8,128)S(1)} %solve1.1.refs_1_.refs_6_), channel_id=1, source_target_pairs={{0,12},{4,8},{8,4},{12,0},{1,13},{5,9},{9,5},{13,1},{2,14},{6,10},... | collective-permute-start | bytes 196616 | tf_op jit(solution)/shard_map/ppermute | solution.py:178
  96.7 1.6 %collective-permute-start.15 = (f32[128,128]{1,0:T(8,128)S(1)}, f32[128,128]{1,0:T(8,128)S(1)}, u32[]{:S(2)}, u32[]{:S(2)}) collective-permute-start(f32[128,128]{1,0:T(8,128)S(1)} %solve1.1.refs_1_.refs_6_), channel_id=1, source_target_pairs={{0,4},{4,0},{8,12},{12,8},{1,5},{5,1},{9,13},{13,9},{2,6},{6,2},{1... | collective-permute-start | bytes 196616 | tf_op jit(solution)/shard_map/ppermute | solution.py:178
  98.3 1.5 %copy-done.2 = f32[28,128,128]{2,1,0:T(8,128)S(1)} copy-done((f32[28,128,128]{2,1,0:T(8,128)S(1)}, f32[28,128,128]{2,1,0:T(8,128)}, u32[]{:S(2)}) %copy-start.2) | copy-done | bytes 1835032
  99.8 1.2 copy-done.6
  103.1 2.9 %collective-permute-start.20 = (f32[128,128]{1,0:T(8,128)S(1)}, f32[128,128]{1,0:T(8,128)S(1)}, u32[]{:S(2)}, u32[]{:S(2)}) collective-permute-start(f32[128,128]{1,0:T(8,128)S(1)} %update21.1.refs_1_), channel_id=1, source_target_pairs={{0,12},{4,8},{8,4},{12,0},{1,13},{5,9},{9,5},{13,1},{2,14},{6,10},... | collective-permute-start | bytes 196616 | tf_op jit(solution)/shard_map/ppermute | solution.py:178
  106.0 1.6 %collective-permute-start.18 = (f32[128,128]{1,0:T(8,128)S(1)}, f32[128,128]{1,0:T(8,128)S(1)}, u32[]{:S(2)}, u32[]{:S(2)}) collective-permute-start(f32[128,128]{1,0:T(8,128)S(1)} %update21.1.refs_1_), channel_id=1, source_target_pairs={{0,4},{4,0},{8,12},{12,8},{1,5},{5,1},{9,13},{13,9},{2,6},{6,2},{1... | collective-permute-start | bytes 196616 | tf_op jit(solution)/shard_map/ppermute | solution.py:178
  107.6 2.1 %collective-permute-done.20.refs_4_ = f32[128,128]{1,0:T(8,128)S(1)} collective-permute-done((f32[128,128]{1,0:T(8,128)S(1)}, f32[128,128]{1,0:T(8,128)S(1)}, u32[]{:S(2)}, u32[]{:S(2)}) %collective-permute-start.20) | collective-permute-done | bytes 65568 | tf_op jit(solution)/shard_map/ppermute | solution.py:178
  109.7 2.2 %collective-permute-done.19.refs_3_ = f32[128,128]{1,0:T(8,128)S(1)} collective-permute-done((f32[128,128]{1,0:T(8,128)S(1)}, f32[128,128]{1,0:T(8,128)S(1)}, u32[]{:S(2)}, u32[]{:S(2)}) %collective-permute-start.19) | collective-permute-done | bytes 65568 | tf_op jit(solution)/shard_map/ppermute | solution.py:178
  112.2 2.4 %collective-permute-start.23 = (f32[128,128]{1,0:T(8,128)S(1)}, f32[128,128]{1,0:T(8,128)S(1)}, u32[]{:S(2)}, u32[]{:S(2)}) collective-permute-start(f32[128,128]{1,0:T(8,128)S(1)} %solve2.1.refs_1_.refs_7_), channel_id=1, source_target_pairs={{0,12},{4,8},{8,4},{12,0},{1,13},{5,9},{9,5},{13,1},{2,14},{6,10},... | collective-permute-start | bytes 196616 | tf_op jit(solution)/shard_map/ppermute | solution.py:178
  114.6 2.0 %collective-permute-start.21 = (f32[128,128]{1,0:T(8,128)S(1)}, f32[128,128]{1,0:T(8,128)S(1)}, u32[]{:S(2)}, u32[]{:S(2)}) collective-permute-start(f32[128,128]{1,0:T(8,128)S(1)} %solve2.1.refs_1_.refs_7_), channel_id=1, source_target_pairs={{0,4},{4,0},{8,12},{12,8},{1,5},{5,1},{9,13},{13,9},{2,6},{6,2},{1... | collective-permute-start | bytes 196616 | tf_op jit(solution)/shard_map/ppermute | solution.py:178
  116.6 1.6 %copy-done = f32[32,128,128]{2,1,0:T(8,128)S(1)} copy-done((f32[32,128,128]{2,1,0:T(8,128)S(1)}, f32[32,128,128]{2,1,0:T(8,128)}, u32[]{:S(2)}) %copy-start) | copy-done | bytes 2097176
  121.1 2.4 %collective-permute-start.26 = (f32[128,128]{1,0:T(8,128)S(1)}, f32[128,128]{1,0:T(8,128)S(1)}, u32[]{:S(2)}, u32[]{:S(2)}) collective-permute-start(f32[128,128]{1,0:T(8,128)S(1)} %update32.1.refs_1_), channel_id=1, source_target_pairs={{0,12},{4,8},{8,4},{12,0},{1,13},{5,9},{9,5},{13,1},{2,14},{6,10},... | collective-permute-start | bytes 196616 | tf_op jit(solution)/shard_map/ppermute | solution.py:178
  123.6 2.0 %collective-permute-start.24 = (f32[128,128]{1,0:T(8,128)S(1)}, f32[128,128]{1,0:T(8,128)S(1)}, u32[]{:S(2)}, u32[]{:S(2)}) collective-permute-start(f32[128,128]{1,0:T(8,128)S(1)} %update32.1.refs_1_), channel_id=1, source_target_pairs={{0,4},{4,0},{8,12},{12,8},{1,5},{5,1},{9,13},{13,9},{2,6},{6,2},{1... | collective-permute-start | bytes 196616 | tf_op jit(solution)/shard_map/ppermute | solution.py:178
  125.6 2.3 %collective-permute-done.26.refs_4_ = f32[128,128]{1,0:T(8,128)S(1)} collective-permute-done((f32[128,128]{1,0:T(8,128)S(1)}, f32[128,128]{1,0:T(8,128)S(1)}, u32[]{:S(2)}, u32[]{:S(2)}) %collective-permute-start.26) | collective-permute-done | bytes 65568 | tf_op jit(solution)/shard_map/ppermute | solution.py:178
  127.8 2.0 %collective-permute-done.25.refs_3_ = f32[128,128]{1,0:T(8,128)S(1)} collective-permute-done((f32[128,128]{1,0:T(8,128)S(1)}, f32[128,128]{1,0:T(8,128)S(1)}, u32[]{:S(2)}, u32[]{:S(2)}) %collective-permute-start.25) | collective-permute-done | bytes 65568 | tf_op jit(solution)/shard_map/ppermute | solution.py:178
  (123 shorter events, 23.9 us)
Async XLA Ops:
  6.5 41.3 %all-gather.7.cloned.1.call-start = ((), (), s32[]{:S(2)}) async-start(), calls=%async_computation | async-start | bytes 1310720 | tf_op jit(solution)/shard_map/all_gather | solution.py:270
  7.7 0.9 collective-permute-start
  8.6 89.7 %all-gather.11.cloned.1.call-start = ((), (), s32[]{:S(2)}) async-start(), calls=%async_computation.2 | async-start | bytes 2293760 | tf_op jit(solution)/shard_map/all_gather | solution.py:295
  12.7 31.5 %copy-start.12 = (f32[4,7,128,64]{2,3,1,0:T(8,128)S(1)}, f32[4,7,128,64]{2,3,1,0:T(8,128)}, u32[]{:S(2)}) copy-start(f32[4,7,128,64]{2,3,1,0:T(8,128)} %param.13) | copy-start | bytes 2752516
  13.8 34.1 %copy-start.17 = (f32[4,128,128]{2,1,0:T(8,128)S(1)}, f32[4,128,128]{2,1,0:T(8,128)}, u32[]{:S(2)}) copy-start(f32[4,128,128]{2,1,0:T(8,128)} %refs_2_.3) | copy-start | bytes 786436
  13.8 30.4 %collective-permute-start.3 = (f32[11,128,128]{2,1,0:T(8,128)S(1)}, f32[11,128,128]{2,1,0:T(8,128)S(1)}, u32[]{:S(2)}, u32[]{:S(2)}) collective-permute-start(f32[11,128,128]{2,1,0:T(8,128)S(1)} %merge0.1.refs_0_), channel_id=1, source_target_pairs={{0,2},{1,3},{2,0},{3,1},{4,6},{5,7},{6,4},{7,5},{8,10},{9,11},{10,... | collective-permute-start | bytes 2162696 | tf_op jit(solution)/shard_map/ppermute | solution.py:178
  28.8 19.0 %collective-permute-start.2 = (f32[11,128,128]{2,1,0:T(8,128)S(1)}, f32[11,128,128]{2,1,0:T(8,128)S(1)}, u32[]{:S(2)}, u32[]{:S(2)}) collective-permute-start(f32[11,128,128]{2,1,0:T(8,128)S(1)} %merge0.1.refs_0_), channel_id=1, source_target_pairs={{0,1},{1,0},{2,3},{3,2},{4,5},{5,4},{6,7},{7,6},{8,9},{9,8},{10,11... | collective-permute-start | bytes 2162696 | tf_op jit(solution)/shard_map/ppermute | solution.py:178
  44.2 3.7 %collective-permute-start.4 = (f32[11,128,128]{2,1,0:T(8,128)S(1)}, f32[11,128,128]{2,1,0:T(8,128)S(1)}, u32[]{:S(2)}, u32[]{:S(2)}) collective-permute-start(f32[11,128,128]{2,1,0:T(8,128)S(1)} %collective-permute-done.3.refs_2_), channel_id=1, source_target_pairs={{0,1},{1,0},{2,3},{3,2},{4,5},{5,4},{6,7},{7,6},{8,9},{9,8},{10,11... | collective-permute-start | bytes 2162696 | tf_op jit(solution)/shard_map/ppermute | solution.py:178
  44.9 9.2 %collective-permute-start.11 = (f32[6,64,128]{2,1,0:T(8,128)}, f32[6,64,128]{2,1,0:T(8,128)}, u32[]{:S(2)}, u32[]{:S(2)}) collective-permute-start(f32[6,64,128]{2,1,0:T(8,128)} %pack2.1), channel_id=1, source_target_pairs={{0,0},{2,4},{1,8},{3,12},{6,1},{4,5},{7,9},{5,13},{9,2},{11,6},{8,... | collective-permute-start | bytes 589832 | tf_op jit(solution)/shard_map/ppermute | solution.py:204
  49.7 6.1 %collective-permute-start.7 = (f32[128,128]{1,0:T(8,128)S(1)}, f32[128,128]{1,0:T(8,128)S(1)}, u32[]{:S(2)}, u32[]{:S(2)}) collective-permute-start(f32[128,128]{1,0:T(8,128)S(1)} %early0.1.refs_4_), channel_id=1, source_target_pairs={{0,12},{4,8},{8,4},{12,0},{1,13},{5,9},{9,5},{13,1},{2,14},{6,10},... | collective-permute-start | bytes 196616 | tf_op jit(solution)/shard_map/ppermute | solution.py:178
  52.6 7.1 %collective-permute-start.6 = (f32[128,128]{1,0:T(8,128)S(1)}, f32[128,128]{1,0:T(8,128)S(1)}, u32[]{:S(2)}, u32[]{:S(2)}) collective-permute-start(f32[128,128]{1,0:T(8,128)S(1)} %early0.1.refs_4_), channel_id=1, source_target_pairs={{0,8},{4,12},{8,0},{12,4},{1,9},{5,13},{9,1},{13,5},{2,10},{6,14},... | collective-permute-start | bytes 196616 | tf_op jit(solution)/shard_map/ppermute | solution.py:178
  52.6 7.1 %collective-permute-start.5 = (f32[128,128]{1,0:T(8,128)S(1)}, f32[128,128]{1,0:T(8,128)S(1)}, u32[]{:S(2)}, u32[]{:S(2)}) collective-permute-start(f32[128,128]{1,0:T(8,128)S(1)} %early0.1.refs_4_), channel_id=1, source_target_pairs={{0,4},{4,0},{8,12},{12,8},{1,5},{5,1},{9,13},{13,9},{2,6},{6,2},{1... | collective-permute-start | bytes 196616 | tf_op jit(solution)/shard_map/ppermute | solution.py:178
  63.1 53.5 %all-gather.9.cloned.1.call-start = ((), (), s32[]{:S(2)}) async-start(), calls=%async_computation.1 | async-start | bytes 2621440 | tf_op jit(solution)/shard_map/all_gather | solution.py:295
  64.4 6.4 %collective-permute-start.1 = (f32[7,64,128]{2,1,0:T(8,128)S(1)}, f32[7,64,128]{2,1,0:T(8,128)S(1)}, u32[]{:S(2)}, u32[]{:S(2)}) collective-permute-start(f32[7,64,128]{2,1,0:T(8,128)S(1)} %pack3.1), channel_id=1, source_target_pairs={{0,0},{2,4},{1,8},{3,12},{6,1},{4,5},{7,9},{5,13},{9,2},{11,6},{8,... | collective-permute-start | bytes 688136 | tf_op jit(solution)/shard_map/ppermute | solution.py:204
  65.5 7.7 %collective-permute-start.10 = (f32[128,128]{1,0:T(8,128)S(1)}, f32[128,128]{1,0:T(8,128)S(1)}, u32[]{:S(2)}, u32[]{:S(2)}) collective-permute-start(f32[128,128]{1,0:T(8,128)S(1)} %solve0.1.refs_4_.refs_1_.refs_5_), channel_id=1, source_target_pairs={{0,12},{4,8},{8,4},{12,0},{1,13},{5,9},{9,5},{13,1},{2,14},{6,10},... | collective-permute-start | bytes 196616 | tf_op jit(solution)/shard_map/ppermute | solution.py:178
  70.2 8.3 %collective-permute-start.9 = (f32[128,128]{1,0:T(8,128)S(1)}, f32[128,128]{1,0:T(8,128)S(1)}, u32[]{:S(2)}, u32[]{:S(2)}) collective-permute-start(f32[128,128]{1,0:T(8,128)S(1)} %solve0.1.refs_4_.refs_1_.refs_5_), channel_id=1, source_target_pairs={{0,8},{4,12},{8,0},{12,4},{1,9},{5,13},{9,1},{13,5},{2,10},{6,14},... | collective-permute-start | bytes 196616 | tf_op jit(solution)/shard_map/ppermute | solution.py:178
  70.2 8.3 %collective-permute-start.8 = (f32[128,128]{1,0:T(8,128)S(1)}, f32[128,128]{1,0:T(8,128)S(1)}, u32[]{:S(2)}, u32[]{:S(2)}) collective-permute-start(f32[128,128]{1,0:T(8,128)S(1)} %solve0.1.refs_4_.refs_1_.refs_5_), channel_id=1, source_target_pairs={{0,4},{4,0},{8,12},{12,8},{1,5},{5,1},{9,13},{13,9},{2,6},{6,2},{1... | collective-permute-start | bytes 196616 | tf_op jit(solution)/shard_map/ppermute | solution.py:178
  83.9 6.1 %collective-permute-start.14 = (f32[128,128]{1,0:T(8,128)S(1)}, f32[128,128]{1,0:T(8,128)S(1)}, u32[]{:S(2)}, u32[]{:S(2)}) collective-permute-start(f32[128,128]{1,0:T(8,128)S(1)} %update10.1.refs_4_), channel_id=1, source_target_pairs={{0,12},{4,8},{8,4},{12,0},{1,13},{5,9},{9,5},{13,1},{2,14},{6,10},... | collective-permute-start | bytes 196616 | tf_op jit(solution)/shard_map/ppermute | solution.py:178
  86.9 6.7 %collective-permute-start.13 = (f32[128,128]{1,0:T(8,128)S(1)}, f32[128,128]{1,0:T(8,128)S(1)}, u32[]{:S(2)}, u32[]{:S(2)}) collective-permute-start(f32[128,128]{1,0:T(8,128)S(1)} %update10.1.refs_4_), channel_id=1, source_target_pairs={{0,8},{4,12},{8,0},{12,4},{1,9},{5,13},{9,1},{13,5},{2,10},{6,14},... | collective-permute-start | bytes 196616 | tf_op jit(solution)/shard_map/ppermute | solution.py:178
  86.9 6.7 %collective-permute-start.12 = (f32[128,128]{1,0:T(8,128)S(1)}, f32[128,128]{1,0:T(8,128)S(1)}, u32[]{:S(2)}, u32[]{:S(2)}) collective-permute-start(f32[128,128]{1,0:T(8,128)S(1)} %update10.1.refs_4_), channel_id=1, source_target_pairs={{0,4},{4,0},{8,12},{12,8},{1,5},{5,1},{9,13},{13,9},{2,6},{6,2},{1... | collective-permute-start | bytes 196616 | tf_op jit(solution)/shard_map/ppermute | solution.py:178
  93.9 9.0 %collective-permute-start.17 = (f32[128,128]{1,0:T(8,128)S(1)}, f32[128,128]{1,0:T(8,128)S(1)}, u32[]{:S(2)}, u32[]{:S(2)}) collective-permute-start(f32[128,128]{1,0:T(8,128)S(1)} %solve1.1.refs_1_.refs_6_), channel_id=1, source_target_pairs={{0,12},{4,8},{8,4},{12,0},{1,13},{5,9},{9,5},{13,1},{2,14},{6,10},... | collective-permute-start | bytes 196616 | tf_op jit(solution)/shard_map/ppermute | solution.py:178
  96.7 6.2 %collective-permute-start.16 = (f32[128,128]{1,0:T(8,128)S(1)}, f32[128,128]{1,0:T(8,128)S(1)}, u32[]{:S(2)}, u32[]{:S(2)}) collective-permute-start(f32[128,128]{1,0:T(8,128)S(1)} %solve1.1.refs_1_.refs_6_), channel_id=1, source_target_pairs={{0,8},{4,12},{8,0},{12,4},{1,9},{5,13},{9,1},{13,5},{2,10},{6,14},... | collective-permute-start | bytes 196616 | tf_op jit(solution)/shard_map/ppermute | solution.py:178
  96.7 6.2 %collective-permute-start.15 = (f32[128,128]{1,0:T(8,128)S(1)}, f32[128,128]{1,0:T(8,128)S(1)}, u32[]{:S(2)}, u32[]{:S(2)}) collective-permute-start(f32[128,128]{1,0:T(8,128)S(1)} %solve1.1.refs_1_.refs_6_), channel_id=1, source_target_pairs={{0,4},{4,0},{8,12},{12,8},{1,5},{5,1},{9,13},{13,9},{2,6},{6,2},{1... | collective-permute-start | bytes 196616 | tf_op jit(solution)/shard_map/ppermute | solution.py:178
  103.1 6.5 %collective-permute-start.20 = (f32[128,128]{1,0:T(8,128)S(1)}, f32[128,128]{1,0:T(8,128)S(1)}, u32[]{:S(2)}, u32[]{:S(2)}) collective-permute-start(f32[128,128]{1,0:T(8,128)S(1)} %update21.1.refs_1_), channel_id=1, source_target_pairs={{0,12},{4,8},{8,4},{12,0},{1,13},{5,9},{9,5},{13,1},{2,14},{6,10},... | collective-permute-start | bytes 196616 | tf_op jit(solution)/shard_map/ppermute | solution.py:178
  106.0 5.9 %collective-permute-start.19 = (f32[128,128]{1,0:T(8,128)S(1)}, f32[128,128]{1,0:T(8,128)S(1)}, u32[]{:S(2)}, u32[]{:S(2)}) collective-permute-start(f32[128,128]{1,0:T(8,128)S(1)} %update21.1.refs_1_), channel_id=1, source_target_pairs={{0,8},{4,12},{8,0},{12,4},{1,9},{5,13},{9,1},{13,5},{2,10},{6,14},... | collective-permute-start | bytes 196616 | tf_op jit(solution)/shard_map/ppermute | solution.py:178
  106.0 5.9 %collective-permute-start.18 = (f32[128,128]{1,0:T(8,128)S(1)}, f32[128,128]{1,0:T(8,128)S(1)}, u32[]{:S(2)}, u32[]{:S(2)}) collective-permute-start(f32[128,128]{1,0:T(8,128)S(1)} %update21.1.refs_1_), channel_id=1, source_target_pairs={{0,4},{4,0},{8,12},{12,8},{1,5},{5,1},{9,13},{13,9},{2,6},{6,2},{1... | collective-permute-start | bytes 196616 | tf_op jit(solution)/shard_map/ppermute | solution.py:178
  112.2 8.2 %collective-permute-start.23 = (f32[128,128]{1,0:T(8,128)S(1)}, f32[128,128]{1,0:T(8,128)S(1)}, u32[]{:S(2)}, u32[]{:S(2)}) collective-permute-start(f32[128,128]{1,0:T(8,128)S(1)} %solve2.1.refs_1_.refs_7_), channel_id=1, source_target_pairs={{0,12},{4,8},{8,4},{12,0},{1,13},{5,9},{9,5},{13,1},{2,14},{6,10},... | collective-permute-start | bytes 196616 | tf_op jit(solution)/shard_map/ppermute | solution.py:178
  114.6 6.3 %collective-permute-start.22 = (f32[128,128]{1,0:T(8,128)S(1)}, f32[128,128]{1,0:T(8,128)S(1)}, u32[]{:S(2)}, u32[]{:S(2)}) collective-permute-start(f32[128,128]{1,0:T(8,128)S(1)} %solve2.1.refs_1_.refs_7_), channel_id=1, source_target_pairs={{0,8},{4,12},{8,0},{12,4},{1,9},{5,13},{9,1},{13,5},{2,10},{6,14},... | collective-permute-start | bytes 196616 | tf_op jit(solution)/shard_map/ppermute | solution.py:178
  114.6 6.3 %collective-permute-start.21 = (f32[128,128]{1,0:T(8,128)S(1)}, f32[128,128]{1,0:T(8,128)S(1)}, u32[]{:S(2)}, u32[]{:S(2)}) collective-permute-start(f32[128,128]{1,0:T(8,128)S(1)} %solve2.1.refs_1_.refs_7_), channel_id=1, source_target_pairs={{0,4},{4,0},{8,12},{12,8},{1,5},{5,1},{9,13},{13,9},{2,6},{6,2},{1... | collective-permute-start | bytes 196616 | tf_op jit(solution)/shard_map/ppermute | solution.py:178
  121.1 6.7 %collective-permute-start.26 = (f32[128,128]{1,0:T(8,128)S(1)}, f32[128,128]{1,0:T(8,128)S(1)}, u32[]{:S(2)}, u32[]{:S(2)}) collective-permute-start(f32[128,128]{1,0:T(8,128)S(1)} %update32.1.refs_1_), channel_id=1, source_target_pairs={{0,12},{4,8},{8,4},{12,0},{1,13},{5,9},{9,5},{13,1},{2,14},{6,10},... | collective-permute-start | bytes 196616 | tf_op jit(solution)/shard_map/ppermute | solution.py:178
  123.5 6.3 %collective-permute-start.25 = (f32[128,128]{1,0:T(8,128)S(1)}, f32[128,128]{1,0:T(8,128)S(1)}, u32[]{:S(2)}, u32[]{:S(2)}) collective-permute-start(f32[128,128]{1,0:T(8,128)S(1)} %update32.1.refs_1_), channel_id=1, source_target_pairs={{0,8},{4,12},{8,0},{12,4},{1,9},{5,13},{9,1},{13,5},{2,10},{6,14},... | collective-permute-start | bytes 196616 | tf_op jit(solution)/shard_map/ppermute | solution.py:178
  123.6 6.3 %collective-permute-start.24 = (f32[128,128]{1,0:T(8,128)S(1)}, f32[128,128]{1,0:T(8,128)S(1)}, u32[]{:S(2)}, u32[]{:S(2)}) collective-permute-start(f32[128,128]{1,0:T(8,128)S(1)} %update32.1.refs_1_), channel_id=1, source_target_pairs={{0,4},{4,0},{8,12},{12,8},{1,5},{5,1},{9,13},{13,9},{2,6},{6,2},{1... | collective-permute-start | bytes 196616 | tf_op jit(solution)/shard_map/ppermute | solution.py:178
  (34 other events, 125.7 us)
Sparse Core Ops, SparseCore 0:
  8.9 32.1 all-gather.6
  63.3 23.4 all-gather.10
  88.3 21.7 all-gather.8

commit v4 on v3

--- a/solution.py
+++ b/solution.py
@@ -73,20 +73,26 @@
     return jnp.stack(outputs)
 
 
-def halves(value):
+def halves(value, axis):
     high = value.astype(jnp.bfloat16)
     low = (value - high.astype(jnp.float32)).astype(jnp.bfloat16)
-    return high, low
-
-
-def dot_split(left, right, dims=(((1,), (0,)), ((), ()))):
-    axis_left = 1 - dims[0][0][0]
-    axis_right = 1 - dims[0][1][0]
-    rows, cols = left.shape[axis_left], right.shape[axis_right]
-    left2 = jnp.concatenate(halves(left), axis=axis_left)
-    right2 = jnp.concatenate(halves(right), axis=axis_right)
+    return jnp.concatenate([high, low], axis=axis)
+
+
+def dot_halves(left2, right2, dims=(((1,), (0,)), ((), ()))):
+    rows = left2.shape[1 - dims[0][0][0]] // 2
+    cols = right2.shape[1 - dims[0][1][0]] // 2
     out = lax.dot_general(left2, right2, dims, preferred_element_type=jnp.float32)
     return (out[:rows, :cols] + (out[:rows, cols:] + out[rows:, :cols])) + out[rows:, cols:]
+
+
+def place_slots(scratch, refs, turn, nb):
+    for slot, ref in enumerate(refs):
+        place = pl.multiple_of((turn ^ slot) * nb, nb)
+        if len(ref.shape) == 3:
+            scratch[:, pl.ds(place, nb), :] = ref[...]
+        else:
+            scratch[pl.ds(place, nb), :] = ref[...]
 
 
 def pack_kernel(pieces, right_ref, *refs):
@@ -108,44 +114,68 @@
         flag = flags_ref[step, col].astype(jnp.float32)
         mask = jnp.where(row_at < ranks_ref[step, col], 1.0 - flag, 0.0)
         left = left_ref[step - first, col] * mask
-        low = dot_split(left, right_ref[packed], (((0,), (0,)), ((), ())))
+        over_rows = (((0,), (0,)), ((), ()))
+        low = dot_halves(halves(left, 1), halves(right_ref[packed], 1), over_rows)
         out_ref[place] = dense_ref[step - first, col] * flag + low
 
 
-def product_kernel(n, slots, wholes, based, tiles, before, *refs):
-    count = n if slots else 1
-    strips = refs[:count]
-    sources = refs[count : count + (1 if wholes else n)]
-    rest = refs[count + len(sources) :]
-    out_ref, source_scr = rest[-2:]
-    nb = out_ref.shape[-2]
-    turn = 0
-    if slots:
-        turn = turn ^ lax.axis_index("pcol")
-    if not wholes:
-        turn = turn ^ lax.axis_index("prow")
-    for slot in range(n):
-        place = (turn ^ slot) * nb
-        if slots or not wholes:
-            place = pl.multiple_of(place, nb)
-        for tile in range(tiles):
-            value = sources[0][slot, tile] if wholes else sources[slot][...]
-            source_scr[tile, pl.ds(place, nb), :] = value
-    total = None
-    for tile in range(tiles):
+def early_kernel(n, slots, tiles, picks, solved_at, *refs):
+    refs = list(refs)
+    strips = [refs.pop(0) for _ in range(n if slots else 1)]
+    sources = [refs.pop(0) for _ in range(n)]
+    solved = [refs.pop(0) for _ in solved_at]
+    base_ref = refs.pop(0)
+    out_ref, *picked, source_scr = refs
+    nb = out_ref.shape[0]
+    turn = lax.axis_index("pcol") if slots else 0
+
+    def strip(tile):
         parts = [strips[d][tile] if slots else strips[0][d, tile] for d in range(n)]
-        part = dot_split(jnp.concatenate(parts, axis=1), source_scr[tile])
-        total = part if total is None else total + part
-    if based:
-        base_ref = rest[0]
-        base = base_ref[0] if len(base_ref.shape) == 3 else base_ref[...]
-        total = base - total
-    if before < 0:
-        out_ref[...] = total
-    else:
-        for index in range(before):
-            out_ref[index] = rest[index][...]
-        out_ref[before] = total
+        return halves(jnp.concatenate(parts, axis=1), 0)
+
+    place_slots(source_scr, sources, lax.axis_index("prow") ^ turn, nb)
+    total = base_ref[0]
+    for index in range(source_scr.shape[0]):
+        total = total - dot_halves(strip(tiles + index), halves(source_scr[index], 1))
+    for tile, ref in zip(solved_at, solved):
+        total = total - dot_halves(strip(tile), halves(ref[...], 1))
+    out_ref[...] = total
+    if picks:
+        for index, tile in enumerate(picks):
+            for d in range(n):
+                value = strips[d][tile] if slots else strips[0][d, tile]
+                place = pl.multiple_of((turn ^ d) * nb, nb) if slots else d * nb
+                picked[0][index, :, pl.ds(place, nb)] = halves(value, 0)
+
+
+def inverse_kernel(n, whole_ref, *out_refs):
+    nb = whole_ref.shape[-1]
+    for step, out_ref in enumerate(out_refs):
+        for row in range(n):
+            for col in range(n):
+                both = halves(whole_ref[row * n + col, step], 0)
+                at = pl.ds(col * nb, nb)
+                out_ref[pl.ds(row * nb, nb), at] = both[:nb]
+                out_ref[pl.ds((n + row) * nb, nb), at] = both[nb:]
+
+
+def step_kernel(n, *refs):
+    inverse_ref, strip_ref, base_ref, pending_ref, solved_ref, scratch = refs[n:]
+    nb = base_ref.shape[0]
+    place_slots(scratch, refs[:n], lax.axis_index("prow"), nb)
+    solved = dot_halves(inverse_ref[...], halves(scratch[...], 1))
+    solved_ref[...] = solved
+    pending_ref[...] = base_ref[...] - dot_halves(strip_ref[0], halves(solved, 1))
+
+
+def last_kernel(n, *refs):
+    strip_ref, *solved, out_ref, scratch = refs[n:]
+    nb = out_ref.shape[1]
+    own = lax.axis_index("prow")
+    place_slots(scratch, refs[:n], own, nb)
+    for step, ref in enumerate(solved):
+        out_ref[step] = ref[pl.ds(pl.multiple_of(own * nb, nb), nb), :]
+    out_ref[len(solved)] = dot_halves(strip_ref[0], halves(scratch[...], 1))
 
 
 def spec_of(shape, index=None):
@@ -233,41 +263,27 @@
             reach //= 2
         return [held[d] for d in range(n)]
 
-    def product(strip, first, tiles, source, name, base=None, stacked=None):
-        slots, wholes = isinstance(strip, list), not isinstance(source, list)
-        if slots:
-            args = list(strip)
-            specs = [spec_of((tiles, nb, nb), (first // tiles, 0, 0))] * n
-        else:
-            args = [strip]
-            specs = [spec_of((n, tiles, nb, nb), (0, first // tiles, 0, 0))]
-        values = [source] if wholes else source
-        args += values
-        specs += [spec_of(value.shape) for value in values]
-        if base is not None:
-            value, index = base
-            args.append(value)
-            specs.append(
-                spec_of((nb, rhs)) if index is None else spec_of((1, nb, rhs), (index, 0, 0))
-            )
-        shape, before = (nb, rhs), -1
-        if stacked is not None:
-            before = len(stacked)
-            shape = (before + 1, nb, rhs)
-            args += stacked
-            specs += [spec_of((nb, rhs))] * before
+    def call(kernel, name, shapes, args, specs=None, scratch=()):
+        specs = specs or [spec_of(value.shape) for value in args]
+        many = isinstance(shapes, list)
+        out_specs = [spec_of(x.shape) for x in shapes] if many else spec_of(shapes.shape)
         return pl.pallas_call(
-            functools.partial(product_kernel, n, slots, wholes, base is not None, tiles, before),
+            kernel,
             grid=(1,),
-            out_shape=jax.ShapeDtypeStruct(shape, f32),
+            out_shape=shapes,
             in_specs=specs,
-            out_specs=spec_of(shape),
-            scratch_shapes=[pltpu.VMEM((tiles, n * nb, rhs), f32)],
+            out_specs=out_specs,
+            scratch_shapes=list(scratch),
             compiler_params=params,
             name=name,
         )(*args)
 
-    known = lax.all_gather(earlier, "prow", axis=0)
+    known = over_rows(earlier)
+    bf16 = jnp.bfloat16
+    rows_all = n * nb
+    block_shape = jax.ShapeDtypeStruct((nb, rhs), f32)
+    whole_shape = jax.ShapeDtypeStruct((rows_all, rhs), f32)
+    inverse_blocks = lax.all_gather(inverse_diag[: steps - 1], ("prow", "pcol"), axis=0)
 
     ahead = 2 if steps % 2 == 0 else 1
     groups = [tuple(range(ahead))] + [(step,) for step in range(ahead, steps)]
@@ -276,7 +292,7 @@
         starts = {step: sum(prev + other for other in rows if other < step) for step in rows}
         order = [(step, col) for step in rows for col in range(prev)]
         order += [(step, prev + col) for step in rows for col in range(step)]
-        order += [(step, None) for step in rows]
+        order += [(step, None) for step in rows if step + 1 == steps]
         for place, key in enumerate(order):
             where[key] = (number, place)
         orders.append(
@@ -287,31 +303,60 @@
     own = merged(orders[0], ahead, right_ahead)
     strips.append(by_distance(own))
     later = [packed(step, (prev + step,), [own]) for step in range(ahead, steps)]
-
-    def merge_next(whole):
-        number = len(strips)
-        if number < len(groups):
+    def merge_later(whole):
+        for number in range(1, len(groups)):
             own = merged(orders[number], 1, later[number - 1], whole[1:])
             strips.append(lax.all_gather(own, "pcol", axis=0))
 
-    def times(key, tiles, source, name, **rest):
-        number, place = where[key]
-        return product(strips[number], place, tiles, source, name, **rest)
-
-    solved, spread = [], []
-    for step in range(steps):
-        pending = times((step, 0), prev, known, f"early{step}", base=(right_side, step))
-        for index in range(step):
-            name = f"update{step}{index}"
-            pending = times((step, prev + index), 1, spread[index], name, base=(pending, None))
+    def early(step, solved):
+        number, tiles = where[(step, 0)]
+        strip = strips[number]
+        slots = isinstance(strip, list)
+        keys = [(step, prev + step - 1)] if step else []
+        keys += [(step, None)] if step + 1 == steps else []
+        picks = [where[key][1] for key in keys]
+        solved_at = [where[(step, prev + index)][1] for index in range(len(solved))]
+        args = (strip if slots else [strip]) + known + solved + [right_side]
+        specs = [spec_of(value.shape) for value in args[:-1]] + [spec_of((1, nb, rhs), (step, 0, 0))]
+        shapes = [block_shape]
+        if picks:
+            shapes.append(jax.ShapeDtypeStruct((len(picks), 2 * nb, rows_all), bf16))
+        return call(
+            functools.partial(early_kernel, n, slots, tiles, picks, solved_at),
+            f"early{step}",
+            shapes,
+            args,
+            specs,
+            [pltpu.VMEM((prev, rows_all, rhs), f32)],
+        )
+
+    inverse = call(
+        functools.partial(inverse_kernel, n),
+        "inverses",
+        [jax.ShapeDtypeStruct((2 * rows_all, rows_all), bf16)] * (steps - 1),
+        [inverse_blocks],
+    )
+    room = [pltpu.VMEM((rows_all, rhs), f32)]
+    strip_spec = spec_of((1, 2 * nb, rows_all), (0, 0, 0))
+    pending, solved = early(0, [])[0], []
+    for step in range(steps - 1):
         whole = over_rows(pending)
-        merge_next(whole)
-        if step + 1 == steps:
-            return times((step, None), 1, whole, f"solve{step}", stacked=solved)
-        solved.append(times((step, None), 1, whole, f"solve{step}"))
-        spread.append(over_rows(solved[step]))
-        merge_next(spread[step])
-    return None
+        if step == 0:
+            merge_later(whole)
+        base, chain = early(step + 1, solved)
+        args = whole + [inverse[step], chain, base]
+        specs = [spec_of(value.shape) for value in args]
+        specs[n + 1] = strip_spec
+        pending, block = call(
+            functools.partial(step_kernel, n), f"step{step}", [block_shape, whole_shape], args, specs, room
+        )
+        solved.append(block)
+    whole = over_rows(pending)
+    args = whole + [chain] + solved
+    specs = [spec_of(value.shape) for value in args]
+    specs[n] = spec_of((1, 2 * nb, rows_all), (1, 0, 0))
+    shape = jax.ShapeDtypeStruct((steps, nb, rhs), f32)
+    return call(functools.partial(last_kernel, n), "last", shape, args, specs, room)
 
 
 def solution(mesh):
@@ -326,7 +371,7 @@
         P("groups", None),
     )
     n = mesh.shape["prow"]
-    square = n == mesh.shape["pcol"] and n & (n - 1) == 0 and n <= 8
+    square = n > 1 and n == mesh.shape["pcol"] and n & (n - 1) == 0 and n <= 8
 
     def local(*args):
         nb, cols = args[3].shape[2:]

time: 138 us -> 159 us (1.15)
  waiting for transfers between devices: 42.9 us -> 60.7 us
  local copies, waits for them, and re-layouts: 19.8 us -> 23.1 us
    ppermute x24 -> x18, waiting for transfers between devices: 42.8 us -> 53.8 us  [shift(): return lax.ppermute(value, axis, [(i, i ^ step) for i in range(n)])]
    all_gather x3, waiting for transfers between devices: 0.01 us -> 6.77 us  [the longest x2 6.75 us: merge_later(): strips.append(lax.all_gather(own, 'pcol', axis=0))]
    ppermute x3, starting transfers between devices: 4.6 us -> 2.28 us  [packed(): return lax.ppermute(own, ('prow', 'pcol'), flip)]
    ppermute x24 -> x18, starting transfers between devices: 47 us -> 48.9 us  [shift(): return lax.ppermute(value, axis, [(i, i ^ step) for i in range(n)])]
    unnamed x72 -> x92, local copies, waits for them, and re-layouts: 19.8 us -> 21.5 us
    slice x0 -> x1, local copies, waits for them, and re-layouts: none -> 1.62 us  [square_mesh(): inverse_diag[:steps - 1]]
    pallas_call x14 -> x9, Pallas kernels: 5.29 us -> 6.05 us  [call(): pl.pallas_call(kernel, grid=(1,), out_shape=shapes, in_specs=specs, out_s...]
  transfers between devices with their start and end apart: 30 -> 24, of which waited for: 12 -> 10; matrix products, arithmetic and copies ran while one was open for 0% -> 0% of each run, Pallas kernels for 5% -> 5%
where the time goes in v4:
time: 159 us; the launch traced here: 158 us
  waiting for transfers between devices  60.7 us (38%)
  starting transfers between devices  51.2 us (32%)
  local copies, waits for them, and re-layouts  23.1 us (15%)
  between operations  13.6 us (9%)
  Pallas kernels  9.26 us (6%)
    ppermute x18, waiting for transfers between devices, shift(): return lax.ppermute(value, axis, [(i, i ^ step) for i in range(n)])  53.8 us
    ppermute x18, starting transfers between devices, shift(): return lax.ppermute(value, axis, [(i, i ^ step) for i in range(n)])  48.9 us
    unnamed x92, local copies, waits for them, and re-layouts  21.5 us
    all_gather x2, waiting for transfers between devices, merge_later(): strips.append(lax.all_gather(own, 'pcol', axis=0))  6.75 us
    pallas_call x9, Pallas kernels, call(): pl.pallas_call(kernel, grid=(1,), out_shape=shapes, in_specs=specs, out_s...  6.05 us
  transfers between devices with their start and end apart: 24, of which 10 were waited for; matrix products, arithmetic and copies ran while one was open for 0% of the time, Pallas kernels for 5%

profile of v4, /device:TPU:0, one launch (start us, length us, event | category | flops | bytes accessed | tf_op | source)
XLA Modules:
  0.0 157.9 jit_solution(15667054118362226994)
XLA Ops:
  6.5 1.6 %slice.3 = f32[3,128,128]{2,1,0:T(8,128)} slice(f32[4,128,128]{2,1,0:T(8,128)} %inv_ref.5), slice={[0:3], [0:128], [0:128]} | slice | bytes 393216 | tf_op jit(solution)/shard_map/slice | solution.py:286
  8.2 1.2 copy-done.2
  10.3 1.5 copy-done
  11.8 1.2 copy-done.4
  15.3 1.1 merge0.1.refs_0_
  16.4 15.5 %collective-permute-start.2 = (f32[9,128,128]{2,1,0:T(8,128)S(1)}, f32[9,128,128]{2,1,0:T(8,128)S(1)}, u32[]{:S(2)}, u32[]{:S(2)}) collective-permute-start(f32[9,128,128]{2,1,0:T(8,128)S(1)} %merge0.1.refs_0_), channel_id=1, source_target_pairs={{0,2},{1,3},{2,0},{3,1},{4,6},{5,7},{6,4},{7,5},{8,10},{9,11},{10,... | collective-permute-start | bytes 1769480 | tf_op jit(solution)/shard_map/ppermute | solution.py:208
  31.8 18.6 %collective-permute-done.2.refs_2_ = f32[9,128,128]{2,1,0:T(8,128)S(1)} collective-permute-done((f32[9,128,128]{2,1,0:T(8,128)S(1)}, f32[9,128,128]{2,1,0:T(8,128)S(1)}, u32[]{:S(2)}, u32[]{:S(2)}) %collective-permute-start.2) | collective-permute-done | bytes 589856 | tf_op jit(solution)/shard_map/ppermute | solution.py:208
  50.5 5.8 %collective-permute-start.6 = (f32[4,128,128]{2,1,0:T(8,128)S(1)}, f32[4,128,128]{2,1,0:T(8,128)S(1)}, u32[]{:S(2)}, u32[]{:S(2)}) collective-permute-start(f32[4,128,128]{2,1,0:T(8,128)S(1)} %copy-done.7), channel_id=1, source_target_pairs={{0,12},{4,8},{8,4},{12,0},{1,13},{5,9},{9,5},{13,1},{2,14},{6,10},... | collective-permute-start | bytes 786440 | tf_op jit(solution)/shard_map/ppermute | solution.py:208
  57.0 11.4 %collective-permute-done.6.refs_7_.refs_4_ = f32[4,128,128]{2,1,0:T(8,128)S(1)} collective-permute-done((f32[4,128,128]{2,1,0:T(8,128)S(1)}, f32[4,128,128]{2,1,0:T(8,128)S(1)}, u32[]{:S(2)}, u32[]{:S(2)}) %collective-permute-start.6) | collective-permute-done | bytes 262176 | tf_op jit(solution)/shard_map/ppermute | solution.py:208
  69.1 12.3 %collective-permute-done.5.refs_6_.refs_3_ = f32[4,128,128]{2,1,0:T(8,128)S(1)} collective-permute-done((f32[4,128,128]{2,1,0:T(8,128)S(1)}, f32[4,128,128]{2,1,0:T(8,128)S(1)}, u32[]{:S(2)}, u32[]{:S(2)}) %collective-permute-start.5) | collective-permute-done | bytes 262176 | tf_op jit(solution)/shard_map/ppermute | solution.py:208
  82.0 1.1 collective-permute-start.9
  83.2 3.3 %collective-permute-start.7 = (f32[128,128]{1,0:T(8,128)S(1)}, f32[128,128]{1,0:T(8,128)S(1)}, u32[]{:S(2)}, u32[]{:S(2)}) collective-permute-start(f32[128,128]{1,0:T(8,128)S(1)} %early0.1.refs_0_), channel_id=1, source_target_pairs={{0,4},{4,0},{8,12},{12,8},{1,5},{5,1},{9,13},{13,9},{2,6},{6,2},{1... | collective-permute-start | bytes 196616 | tf_op jit(solution)/shard_map/ppermute | solution.py:208
  86.5 2.1 %collective-permute-done.9.refs_3_.refs_2_ = f32[128,128]{1,0:T(8,128)S(1)} collective-permute-done((f32[128,128]{1,0:T(8,128)S(1)}, f32[128,128]{1,0:T(8,128)S(1)}, u32[]{:S(2)}, u32[]{:S(2)}) %collective-permute-start.9) | collective-permute-done | bytes 65568 | tf_op jit(solution)/shard_map/ppermute | solution.py:208
  88.6 1.7 %collective-permute-done.8.refs_2_.refs_1_ = f32[128,128]{1,0:T(8,128)S(1)} collective-permute-done((f32[128,128]{1,0:T(8,128)S(1)}, f32[128,128]{1,0:T(8,128)S(1)}, u32[]{:S(2)}, u32[]{:S(2)}) %collective-permute-start.8) | collective-permute-done | bytes 65568 | tf_op jit(solution)/shard_map/ppermute | solution.py:208
  90.4 1.0 merge2.1
  96.7 1.0 merge3.1
  99.6 1.1 copy-done.23
  100.7 1.1 copy-done.25
  101.8 1.1 copy-done.27
  103.5 1.9 %copy-done.21 = f32[48,128,128]{2,1,0:T(8,128)S(1)} copy-done((f32[48,128,128]{2,1,0:T(8,128)S(1)}, f32[48,128,128]{2,1,0:T(8,128)}, u32[]{:S(2)}) %copy-start.21) | copy-done | bytes 3145752
  105.9 1.0 copy-done.32
  107.6 12.9 %collective-permute-start.12 = (f32[128,128]{1,0:T(8,128)S(1)}, f32[128,128]{1,0:T(8,128)S(1)}, u32[]{:S(2)}, u32[]{:S(2)}) collective-permute-start(f32[128,128]{1,0:T(8,128)S(1)} %get-tuple-element.23.refs_0_), channel_id=1, source_target_pairs={{0,12},{4,8},{8,4},{12,0},{1,13},{5,9},{9,5},{13,1},{2,14},{6,10},... | collective-permute-start | bytes 196616 | tf_op jit(solution)/shard_map/ppermute | solution.py:208
  121.2 1.5 copy-done.30
  123.3 2.5 %collective-permute-done.11.refs_2_ = f32[128,128]{1,0:T(8,128)S(1)} collective-permute-done((f32[128,128]{1,0:T(8,128)S(1)}, f32[128,128]{1,0:T(8,128)S(1)}, u32[]{:S(2)}, u32[]{:S(2)}) %collective-permute-start.11) | collective-permute-done | bytes 65568 | tf_op jit(solution)/shard_map/ppermute | solution.py:208
  126.7 2.1 %collective-permute-start.16 = (f32[128,128]{1,0:T(8,128)S(1)}, f32[128,128]{1,0:T(8,128)S(1)}, u32[]{:S(2)}, u32[]{:S(2)}) collective-permute-start(f32[128,128]{1,0:T(8,128)S(1)} %get-tuple-element.28.refs_0_), channel_id=1, source_target_pairs={{0,12},{4,8},{8,4},{12,0},{1,13},{5,9},{9,5},{13,1},{2,14},{6,10},... | collective-permute-start | bytes 196616 | tf_op jit(solution)/shard_map/ppermute | solution.py:208
  128.8 2.4 %collective-permute-start.14 = (f32[128,128]{1,0:T(8,128)S(1)}, f32[128,128]{1,0:T(8,128)S(1)}, u32[]{:S(2)}, u32[]{:S(2)}) collective-permute-start(f32[128,128]{1,0:T(8,128)S(1)} %get-tuple-element.28.refs_0_), channel_id=1, source_target_pairs={{0,4},{4,0},{8,12},{12,8},{1,5},{5,1},{9,13},{13,9},{2,6},{6,2},{1... | collective-permute-start | bytes 196616 | tf_op jit(solution)/shard_map/ppermute | solution.py:208
  131.1 6.7 %all-gather.11.cloned.1.call-done = f32[32,128,128]{2,1,0:T(8,128)} async-done(((f32[8,128,128]{2,1,0:T(8,128)}), f32[32,128,128]{2,1,0:T(8,128)}) %all-gather.11.cloned.1.call-update) | async-done | bytes 2097168 | tf_op jit(solution)/shard_map/all_gather | solution.py:309
  137.9 1.6 %copy-done.29 = f32[32,128,128]{2,1,0:T(8,128)S(1)} copy-done((f32[32,128,128]{2,1,0:T(8,128)S(1)}, f32[32,128,128]{2,1,0:T(8,128)}, u32[]{:S(2)}) %copy-start.29) | copy-done | bytes 2097176
  140.9 3.4 %collective-permute-start.20 = (f32[128,128]{1,0:T(8,128)S(1)}, f32[128,128]{1,0:T(8,128)S(1)}, u32[]{:S(2)}, u32[]{:S(2)}) collective-permute-start(f32[128,128]{1,0:T(8,128)S(1)} %get-tuple-element.33.refs_0_), channel_id=1, source_target_pairs={{0,12},{4,8},{8,4},{12,0},{1,13},{5,9},{9,5},{13,1},{2,14},{6,10},... | collective-permute-start | bytes 196616 | tf_op jit(solution)/shard_map/ppermute | solution.py:208
  144.3 1.1 collective-permute-start.18
  145.4 2.0 %collective-permute-done.20.refs_3_ = f32[128,128]{1,0:T(8,128)S(1)} collective-permute-done((f32[128,128]{1,0:T(8,128)S(1)}, f32[128,128]{1,0:T(8,128)S(1)}, u32[]{:S(2)}, u32[]{:S(2)}) %collective-permute-start.20) | collective-permute-done | bytes 65568 | tf_op jit(solution)/shard_map/ppermute | solution.py:208
  147.4 3.0 %collective-permute-done.19.refs_2_ = f32[128,128]{1,0:T(8,128)S(1)} collective-permute-done((f32[128,128]{1,0:T(8,128)S(1)}, f32[128,128]{1,0:T(8,128)S(1)}, u32[]{:S(2)}, u32[]{:S(2)}) %collective-permute-start.19) | collective-permute-done | bytes 65568 | tf_op jit(solution)/shard_map/ppermute | solution.py:208
  (127 shorter events, 18.5 us)
Async XLA Ops:
  6.5 96.9 %all-gather.7.cloned.1.call-start = ((), (), s32[]{:S(2)}) async-start(), calls=%async_computation | async-start | bytes 3342336 | tf_op jit(solution)/shard_map/all_gather | solution.py:286
  8.2 113.0 %all-gather.9.cloned.1.call-start = ((), (), s32[]{:S(2)}) async-start(), calls=%async_computation.1 | async-start | bytes 1966080 | tf_op jit(solution)/shard_map/all_gather | solution.py:309
  9.4 41.0 %copy-start.7 = (f32[4,128,128]{2,1,0:T(8,128)S(1)}, f32[4,128,128]{2,1,0:T(8,128)}, u32[]{:S(2)}) copy-start(f32[4,128,128]{2,1,0:T(8,128)} %refs_1_.3) | copy-start | bytes 786436
  9.4 47.5 %copy-start.3 = (f32[4,7,128,64]{2,3,1,0:T(8,128)S(1)}, f32[4,7,128,64]{2,3,1,0:T(8,128)}, u32[]{:S(2)}) copy-start(f32[4,7,128,64]{2,3,1,0:T(8,128)} %param.13) | copy-start | bytes 2752516
  9.4 0.8 collective-permute-start
  15.3 66.2 %copy-start.9 = (f32[4,128,128]{2,1,0:T(8,128)S(1)}, f32[4,128,128]{2,1,0:T(8,128)}, u32[]{:S(2)}) copy-start(f32[4,128,128]{2,1,0:T(8,128)} %refs_7_.1) | copy-start | bytes 786436
  16.4 34.1 %collective-permute-start.2 = (f32[9,128,128]{2,1,0:T(8,128)S(1)}, f32[9,128,128]{2,1,0:T(8,128)S(1)}, u32[]{:S(2)}, u32[]{:S(2)}) collective-permute-start(f32[9,128,128]{2,1,0:T(8,128)S(1)} %merge0.1.refs_0_), channel_id=1, source_target_pairs={{0,2},{1,3},{2,0},{3,1},{4,6},{5,7},{6,4},{7,5},{8,10},{9,11},{10,... | collective-permute-start | bytes 1769480 | tf_op jit(solution)/shard_map/ppermute | solution.py:208
  31.8 49.6 %collective-permute-start.1 = (f32[9,128,128]{2,1,0:T(8,128)S(1)}, f32[9,128,128]{2,1,0:T(8,128)S(1)}, u32[]{:S(2)}, u32[]{:S(2)}) collective-permute-start(f32[9,128,128]{2,1,0:T(8,128)S(1)} %merge0.1.refs_0_), channel_id=1, source_target_pairs={{0,1},{1,0},{2,3},{3,2},{4,5},{5,4},{6,7},{7,6},{8,9},{9,8},{10,11... | collective-permute-start | bytes 1769480 | tf_op jit(solution)/shard_map/ppermute | solution.py:208
  50.5 31.0 %collective-permute-start.3 = (f32[9,128,128]{2,1,0:T(8,128)S(1)}, f32[9,128,128]{2,1,0:T(8,128)S(1)}, u32[]{:S(2)}, u32[]{:S(2)}) collective-permute-start(f32[9,128,128]{2,1,0:T(8,128)S(1)} %collective-permute-done.2.refs_2_), channel_id=1, source_target_pairs={{0,1},{1,0},{2,3},{3,2},{4,5},{5,4},{6,7},{7,6},{8,9},{9,8},{10,11... | collective-permute-start | bytes 1769480 | tf_op jit(solution)/shard_map/ppermute | solution.py:208
  50.5 18.0 %collective-permute-start.6 = (f32[4,128,128]{2,1,0:T(8,128)S(1)}, f32[4,128,128]{2,1,0:T(8,128)S(1)}, u32[]{:S(2)}, u32[]{:S(2)}) collective-permute-start(f32[4,128,128]{2,1,0:T(8,128)S(1)} %copy-done.7), channel_id=1, source_target_pairs={{0,12},{4,8},{8,4},{12,0},{1,13},{5,9},{9,5},{13,1},{2,14},{6,10},... | collective-permute-start | bytes 786440 | tf_op jit(solution)/shard_map/ppermute | solution.py:208
  56.3 25.1 %collective-permute-start.5 = (f32[4,128,128]{2,1,0:T(8,128)S(1)}, f32[4,128,128]{2,1,0:T(8,128)S(1)}, u32[]{:S(2)}, u32[]{:S(2)}) collective-permute-start(f32[4,128,128]{2,1,0:T(8,128)S(1)} %copy-done.7), channel_id=1, source_target_pairs={{0,8},{4,12},{8,0},{12,4},{1,9},{5,13},{9,1},{13,5},{2,10},{6,14},... | collective-permute-start | bytes 786440 | tf_op jit(solution)/shard_map/ppermute | solution.py:208
  56.3 25.1 %collective-permute-start.4 = (f32[4,128,128]{2,1,0:T(8,128)S(1)}, f32[4,128,128]{2,1,0:T(8,128)S(1)}, u32[]{:S(2)}, u32[]{:S(2)}) collective-permute-start(f32[4,128,128]{2,1,0:T(8,128)S(1)} %copy-done.7), channel_id=1, source_target_pairs={{0,4},{4,0},{8,12},{12,8},{1,5},{5,1},{9,13},{13,9},{2,6},{6,2},{1... | collective-permute-start | bytes 786440 | tf_op jit(solution)/shard_map/ppermute | solution.py:208
  57.0 33.4 %copy-start.1 = (f32[4,7,128,128]{3,2,1,0:T(8,128)S(1)}, f32[4,7,128,128]{3,2,1,0:T(8,128)}, u32[]{:S(2)}) copy-start(f32[4,7,128,128]{3,2,1,0:T(8,128)} %dense_ref.5) | copy-start | bytes 5505028
  57.0 33.4 %copy-start.5 = (f32[4,7,128,64]{2,3,1,0:T(8,128)S(1)}, f32[4,7,128,64]{2,3,1,0:T(8,128)}, u32[]{:S(2)}) copy-start(f32[4,7,128,64]{2,3,1,0:T(8,128)} %param.12) | copy-start | bytes 2752516
  57.0 33.4 %copy-start.19 = (f32[4,128,128]{2,1,0:T(8,128)S(1)}, f32[4,128,128]{2,1,0:T(8,128)}, u32[]{:S(2)}) copy-start(f32[4,128,128]{2,1,0:T(8,128)} %inv_ref.5) | copy-start | bytes 786436
  57.0 33.4 %copy-start.43 = (s32[4,7]{1,0:T(4,128)S(1)}, s32[4,7]{1,0:T(4,128)}, u32[]{:S(2)}) copy-start(s32[4,7]{1,0:T(4,128)} %ranks_ref.5) | copy-start | bytes 340
  57.0 33.4 %copy-start.45 = (s32[4,7]{1,0:T(4,128)S(1)}, s32[4,7]{1,0:T(4,128)}, u32[]{:S(2)}) copy-start(s32[4,7]{1,0:T(4,128)} %flags_ref.5) | copy-start | bytes 340
  68.4 18.1 %collective-permute-start.13 = (f32[6,64,128]{2,1,0:T(8,128)S(1)}, f32[6,64,128]{2,1,0:T(8,128)S(1)}, u32[]{:S(2)}, u32[]{:S(2)}) collective-permute-start(f32[6,64,128]{2,1,0:T(8,128)S(1)} %pack2.1), channel_id=1, source_target_pairs={{0,0},{2,4},{1,8},{3,12},{6,1},{4,5},{7,9},{5,13},{9,2},{11,6},{8,... | collective-permute-start | bytes 589832 | tf_op jit(solution)/shard_map/ppermute | solution.py:234
  82.0 6.6 %collective-permute-start.9 = (f32[128,128]{1,0:T(8,128)S(1)}, f32[128,128]{1,0:T(8,128)S(1)}, u32[]{:S(2)}, u32[]{:S(2)}) collective-permute-start(f32[128,128]{1,0:T(8,128)S(1)} %early0.1.refs_0_), channel_id=1, source_target_pairs={{0,12},{4,8},{8,4},{12,0},{1,13},{5,9},{9,5},{13,1},{2,14},{6,10},... | collective-permute-start | bytes 196616 | tf_op jit(solution)/shard_map/ppermute | solution.py:208
  83.2 7.2 %collective-permute-start.8 = (f32[128,128]{1,0:T(8,128)S(1)}, f32[128,128]{1,0:T(8,128)S(1)}, u32[]{:S(2)}, u32[]{:S(2)}) collective-permute-start(f32[128,128]{1,0:T(8,128)S(1)} %early0.1.refs_0_), channel_id=1, source_target_pairs={{0,8},{4,12},{8,0},{12,4},{1,9},{5,13},{9,1},{13,5},{2,10},{6,14},... | collective-permute-start | bytes 196616 | tf_op jit(solution)/shard_map/ppermute | solution.py:208
  83.2 7.2 %collective-permute-start.7 = (f32[128,128]{1,0:T(8,128)S(1)}, f32[128,128]{1,0:T(8,128)S(1)}, u32[]{:S(2)}, u32[]{:S(2)}) collective-permute-start(f32[128,128]{1,0:T(8,128)S(1)} %early0.1.refs_0_), channel_id=1, source_target_pairs={{0,4},{4,0},{8,12},{12,8},{1,5},{5,1},{9,13},{13,9},{2,6},{6,2},{1... | collective-permute-start | bytes 196616 | tf_op jit(solution)/shard_map/ppermute | solution.py:208
  92.9 45.0 %all-gather.11.cloned.1.call-start = ((), (), s32[]{:S(2)}) async-start(), calls=%async_computation.2 | async-start | bytes 2621440 | tf_op jit(solution)/shard_map/all_gather | solution.py:309
  93.0 0.8 collective-permute-start.17
  107.6 15.7 %collective-permute-start.12 = (f32[128,128]{1,0:T(8,128)S(1)}, f32[128,128]{1,0:T(8,128)S(1)}, u32[]{:S(2)}, u32[]{:S(2)}) collective-permute-start(f32[128,128]{1,0:T(8,128)S(1)} %get-tuple-element.23.refs_0_), channel_id=1, source_target_pairs={{0,12},{4,8},{8,4},{12,0},{1,13},{5,9},{9,5},{13,1},{2,14},{6,10},... | collective-permute-start | bytes 196616 | tf_op jit(solution)/shard_map/ppermute | solution.py:208
  120.5 5.3 %collective-permute-start.11 = (f32[128,128]{1,0:T(8,128)S(1)}, f32[128,128]{1,0:T(8,128)S(1)}, u32[]{:S(2)}, u32[]{:S(2)}) collective-permute-start(f32[128,128]{1,0:T(8,128)S(1)} %get-tuple-element.23.refs_0_), channel_id=1, source_target_pairs={{0,8},{4,12},{8,0},{12,4},{1,9},{5,13},{9,1},{13,5},{2,10},{6,14},... | collective-permute-start | bytes 196616 | tf_op jit(solution)/shard_map/ppermute | solution.py:208
  120.8 5.1 %collective-permute-start.10 = (f32[128,128]{1,0:T(8,128)S(1)}, f32[128,128]{1,0:T(8,128)S(1)}, u32[]{:S(2)}, u32[]{:S(2)}) collective-permute-start(f32[128,128]{1,0:T(8,128)S(1)} %get-tuple-element.23.refs_0_), channel_id=1, source_target_pairs={{0,4},{4,0},{8,12},{12,8},{1,5},{5,1},{9,13},{13,9},{2,6},{6,2},{1... | collective-permute-start | bytes 196616 | tf_op jit(solution)/shard_map/ppermute | solution.py:208
  126.7 13.5 %collective-permute-start.16 = (f32[128,128]{1,0:T(8,128)S(1)}, f32[128,128]{1,0:T(8,128)S(1)}, u32[]{:S(2)}, u32[]{:S(2)}) collective-permute-start(f32[128,128]{1,0:T(8,128)S(1)} %get-tuple-element.28.refs_0_), channel_id=1, source_target_pairs={{0,12},{4,8},{8,4},{12,0},{1,13},{5,9},{9,5},{13,1},{2,14},{6,10},... | collective-permute-start | bytes 196616 | tf_op jit(solution)/shard_map/ppermute | solution.py:208
  128.8 11.4 %collective-permute-start.15 = (f32[128,128]{1,0:T(8,128)S(1)}, f32[128,128]{1,0:T(8,128)S(1)}, u32[]{:S(2)}, u32[]{:S(2)}) collective-permute-start(f32[128,128]{1,0:T(8,128)S(1)} %get-tuple-element.28.refs_0_), channel_id=1, source_target_pairs={{0,8},{4,12},{8,0},{12,4},{1,9},{5,13},{9,1},{13,5},{2,10},{6,14},... | collective-permute-start | bytes 196616 | tf_op jit(solution)/shard_map/ppermute | solution.py:208
  128.8 11.5 %collective-permute-start.14 = (f32[128,128]{1,0:T(8,128)S(1)}, f32[128,128]{1,0:T(8,128)S(1)}, u32[]{:S(2)}, u32[]{:S(2)}) collective-permute-start(f32[128,128]{1,0:T(8,128)S(1)} %get-tuple-element.28.refs_0_), channel_id=1, source_target_pairs={{0,4},{4,0},{8,12},{12,8},{1,5},{5,1},{9,13},{13,9},{2,6},{6,2},{1... | collective-permute-start | bytes 196616 | tf_op jit(solution)/shard_map/ppermute | solution.py:208
  140.9 6.5 %collective-permute-start.20 = (f32[128,128]{1,0:T(8,128)S(1)}, f32[128,128]{1,0:T(8,128)S(1)}, u32[]{:S(2)}, u32[]{:S(2)}) collective-permute-start(f32[128,128]{1,0:T(8,128)S(1)} %get-tuple-element.33.refs_0_), channel_id=1, source_target_pairs={{0,12},{4,8},{8,4},{12,0},{1,13},{5,9},{9,5},{13,1},{2,14},{6,10},... | collective-permute-start | bytes 196616 | tf_op jit(solution)/shard_map/ppermute | solution.py:208
  144.3 6.1 %collective-permute-start.19 = (f32[128,128]{1,0:T(8,128)S(1)}, f32[128,128]{1,0:T(8,128)S(1)}, u32[]{:S(2)}, u32[]{:S(2)}) collective-permute-start(f32[128,128]{1,0:T(8,128)S(1)} %get-tuple-element.33.refs_0_), channel_id=1, source_target_pairs={{0,8},{4,12},{8,0},{12,4},{1,9},{5,13},{9,1},{13,5},{2,10},{6,14},... | collective-permute-start | bytes 196616 | tf_op jit(solution)/shard_map/ppermute | solution.py:208
  144.3 6.1 %collective-permute-start.18 = (f32[128,128]{1,0:T(8,128)S(1)}, f32[128,128]{1,0:T(8,128)S(1)}, u32[]{:S(2)}, u32[]{:S(2)}) collective-permute-start(f32[128,128]{1,0:T(8,128)S(1)} %get-tuple-element.33.refs_0_), channel_id=1, source_target_pairs={{0,4},{4,0},{8,12},{12,8},{1,5},{5,1},{9,13},{13,9},{2,6},{6,2},{1... | collective-permute-start | bytes 196616 | tf_op jit(solution)/shard_map/ppermute | solution.py:208
  (38 other events, 148.2 us)
Sparse Core Ops, SparseCore 0:
  9.6 57.6 all-gather.6
  93.0 20.6 all-gather.8
  115.2 22.5 all-gather.10

commit v5 on v0

v5 whole, which is shorter than its diff:
```python
import functools

import jax
import jax.numpy as jnp
from jax import lax
from jax.experimental import pallas as pl
from jax.experimental.pallas import tpu as pltpu
from jax.sharding import PartitionSpec as P

HIGHEST = lax.Precision.HIGHEST
VMEM_LIMIT = 24 * 1024 * 1024


def any_mesh(
    right_side,
    earlier,
    inverse_diag,
    dense_tiles,
    left_factor,
    right_factor,
    tile_ranks,
    dense_flags,
):
    count_steps = right_side.shape[0]
    prev_cols = earlier.shape[0]
    rank_pad = left_factor.shape[3]
    tile_flags = dense_flags.astype(jnp.float32)
    columns = lax.broadcasted_iota(jnp.int32, tile_ranks.shape + (rank_pad,), 2)
    low_mask = (columns < tile_ranks[:, :, None]).astype(jnp.float32) * (1.0 - tile_flags)[
        :, :, None
    ]
    left_eff = left_factor * low_mask[:, :, None, :]
    tile_rows = (
        lax.all_gather(dense_tiles, "pcol", axis=3, tiled=True) * tile_flags[:, :, None, None]
    )
    inverse_rows = lax.all_gather(inverse_diag, "pcol", axis=2, tiled=True)
    early_sum = jnp.einsum(
        "kjrc,jcs->krs",
        tile_rows[:, :prev_cols],
        lax.all_gather(earlier, "prow", axis=1, tiled=True),
        precision=HIGHEST,
    )
    partial_value = jnp.einsum(
        "kjcq,jcs->kjqs", right_factor[:, :prev_cols], earlier, precision=HIGHEST
    )
    early_coeffs = lax.psum(partial_value, "prow")
    early_sum = early_sum + jnp.einsum(
        "kjrq,kjqs->krs", left_eff[:, :prev_cols], early_coeffs, precision=HIGHEST
    )
    pending = right_side - early_sum
    outputs = []
    for block_index in range(count_steps):
        residual_whole = lax.all_gather(pending[block_index], "prow", axis=0, tiled=True)
        solved_own = jnp.dot(inverse_rows[block_index], residual_whole, precision=HIGHEST)
        outputs.append(solved_own)
        if block_index + 1 < count_steps:
            solved_whole = lax.all_gather(solved_own, "prow", axis=0, tiled=True)
            column = prev_cols + block_index
            later = slice(block_index + 1, None)
            dense_part = jnp.einsum(
                "krc,cs->krs", tile_rows[later, column], solved_whole, precision=HIGHEST
            )
            projected = lax.psum(
                jnp.einsum(
                    "kcq,cs->kqs", right_factor[later, column], solved_own, precision=HIGHEST
                ),
                "prow",
            )
            low_part = jnp.einsum(
                "krq,kqs->krs", left_eff[later, column], projected, precision=HIGHEST
            )
            pending = pending.at[later].add(-(dense_part + low_part))
    return jnp.stack(outputs)


def halves(value, axis):
    high = value.astype(jnp.bfloat16)
    low = (value - high.astype(jnp.float32)).astype(jnp.bfloat16)
    return jnp.concatenate([high, low], axis=axis)


def dot_halves(left2, right2, dims=(((1,), (0,)), ((), ()))):
    rows = left2.shape[1 - dims[0][0][0]] // 2
    cols = right2.shape[1 - dims[0][1][0]] // 2
    out = lax.dot_general(left2, right2, dims, preferred_element_type=jnp.float32)
    return (out[:rows, :cols] + (out[:rows, cols:] + out[rows:, :cols])) + out[rows:, cols:]


def pack_kernel(pieces, right_ref, *refs):
    out_ref = refs[-1]
    place = 0
    for index, count in enumerate(pieces):
        out_ref[place : place + count] = right_ref[index, :count]
        place += count


def merge_kernel(order, ranks_ref, flags_ref, dense_ref, left_ref, right_ref, inv_ref, *refs):
    out_ref = refs[-1]
    rank_pad, rows = left_ref.shape[2:]
    row_at = lax.broadcasted_iota(jnp.int32, (rank_pad, rows), 0)
    for place, (first, step, col, packed) in enumerate(order):
        if col is None:
            out_ref[place] = inv_ref[step - first]
            continue
        flag = flags_ref[step, col].astype(jnp.float32)
        mask = jnp.where(row_at < ranks_ref[step, col], 1.0 - flag, 0.0)
        left = left_ref[step - first, col] * mask
        over_rows = (((0,), (0,)), ((), ()))
        low = dot_halves(halves(left, 1), halves(right_ref[packed], 1), over_rows)
        out_ref[place] = dense_ref[step - first, col] * flag + low


def first_kernel(prev, flags_ref, known_ref, dense_ref, right_ref, inv_ref, sent_ref, own_ref):
    nb = own_ref.shape[-1]
    rank_pad = right_ref.shape[2]
    for col in range(prev):
        known = known_ref[col]
        sent_ref[col * nb : (col + 1) * nb] = known
        at = prev * nb + col * rank_pad
        sent_ref[at : at + rank_pad] = dot_halves(halves(right_ref[0, col], 0), halves(known, 1))
        own_ref[col] = dense_ref[0, col] * flags_ref[0, col].astype(jnp.float32)
    own_ref[prev] = inv_ref[0]


def early_kernel(n, prev, step, tiles, picks, solved_at, low, *refs):
    refs = list(refs)
    strips = [refs.pop(0) for _ in range(n)]
    sources = [refs.pop(0) for _ in range(n)]
    solved = [[refs.pop(0) for _ in range(n)] for _ in solved_at]
    ranks_ref, flags_ref, left_ref = [refs.pop(0) for _ in range(3)] if low else (None,) * 3
    base_ref, out_ref, picked_ref, scratch = refs
    nb = out_ref.shape[0]
    own_col = lax.axis_index("pcol")
    turn = own_col ^ lax.axis_index("prow")

    def strip(tile):
        return halves(jnp.concatenate([ref[tile] for ref in strips], axis=1), 0)

    def take(total, tile, blocks):
        for slot, block in enumerate(blocks):
            scratch[pl.ds(pl.multiple_of((turn ^ slot) * nb, nb), nb), :] = block
        return total - dot_halves(strip(tile), halves(scratch[...], 1))

    total = base_ref[0]
    for col in range(prev):
        total = take(total, tiles + col, [ref[col * nb : (col + 1) * nb] for ref in sources])
    for tile, blocks in zip(solved_at, solved):
        total = take(total, tile, [ref[...] for ref in blocks])
    if low:
        rank_pad, rows = left_ref.shape[2:]
        row_at = lax.broadcasted_iota(jnp.int32, (rank_pad, rows), 0)
        lefts, coeffs = [], []
        for col in range(prev):
            flag = flags_ref[step, col].astype(jnp.float32)
            mask = jnp.where(row_at < ranks_ref[step, col], 1.0 - flag, 0.0)
            lefts.append(left_ref[0, col] * mask)
            at = prev * nb + col * rank_pad
            coeffs.append(sum(ref[at : at + rank_pad] for ref in sources))
        left2 = halves(jnp.concatenate(lefts, axis=0), 1)
        coeff2 = halves(jnp.concatenate(coeffs, axis=0), 1)
        total = total - dot_halves(left2, coeff2, (((0,), (0,)), ((), ())))
    out_ref[...] = total
    for index, tile in enumerate(picks):
        for slot, ref in enumerate(strips):
            place = pl.multiple_of((own_col ^ slot) * nb, nb)
            picked_ref[index, :, pl.ds(place, nb)] = halves(ref[tile], 0)


def chain_kernel(n, minus, stacked, *refs):
    strip_ref, *rest, out_ref, scratch = refs[n:]
    nb = out_ref.shape[-2]
    own = lax.axis_index("prow")
    for slot, ref in enumerate(refs[:n]):
        scratch[pl.ds(pl.multiple_of((own ^ slot) * nb, nb), nb), :] = ref[...]
    total = dot_halves(strip_ref[0], halves(scratch[...], 1))
    if minus:
        total = rest[0][...] - total
    if stacked:
        for index, ref in enumerate(rest):
            out_ref[index] = ref[...]
        out_ref[len(rest)] = total
    else:
        out_ref[...] = total


def spec_of(shape, index=None):
    if index is None:
        return pl.BlockSpec(shape, lambda i: (0,) * len(shape))
    return pl.BlockSpec(shape, lambda i: index)


def square_mesh(
    n,
    right_side,
    earlier,
    inverse_diag,
    dense_tiles,
    left_factor,
    right_factor,
    tile_ranks,
    dense_flags,
):
    steps, nb, rhs = right_side.shape
    prev = earlier.shape[0]
    cols = dense_tiles.shape[1]
    rank_pad = left_factor.shape[3]
    left_t = jnp.swapaxes(left_factor, 2, 3)
    right_t = jnp.swapaxes(right_factor, 2, 3)
    params = pltpu.CompilerParams(vmem_limit_bytes=VMEM_LIMIT)
    f32 = jnp.float32

    def shift(value, axis, step):
        return lax.ppermute(value, axis, [(i, i ^ step) for i in range(n)])

    def over_rows(value):
        return [value] + [shift(value, "prow", d) for d in range(1, n)]

    flip = []
    for owner in range(n):
        for row in range(n):
            source = row ^ owner
            source = (source >> 1) | ((source & 1) * (n // 2)) if n > 1 else 0
            flip.append((owner * n + source, row * n + owner))

    any_spec = pl.BlockSpec(memory_space=pl.ANY)
    smem = pl.BlockSpec(memory_space=pltpu.SMEM)
    bf16 = jnp.bfloat16

    def pinned(value):
        return pltpu.with_memory_space_constraint(value, pltpu.HBM)

    def shaped(*shape, dtype=f32):
        return jax.ShapeDtypeStruct(shape, dtype)

    def call(kernel, name, shapes, args, specs, scratch=()):
        many = isinstance(shapes, list)
        out_specs = [spec_of(x.shape) for x in shapes] if many else spec_of(shapes.shape)
        return pl.pallas_call(
            kernel,
            grid=(1,),
            out_shape=shapes,
            in_specs=specs,
            out_specs=out_specs,
            scratch_shapes=list(scratch),
            compiler_params=params,
            name=name,
        )(*args)

    def packed(step, after):
        own = call(
            functools.partial(pack_kernel, (prev + step,)),
            f"pack{step}",
            shaped(prev + step, rank_pad, nb),
            [pinned(right_t), *after],
            [spec_of((1, cols, rank_pad, nb), (step, 0, 0, 0))] + [any_spec] * len(after),
        )
        return lax.ppermute(own, ("prow", "pcol"), flip)

    def merged(step, right_own, after):
        order = tuple((step, step, col, col) for col in range(prev + step)) + ((step, step, None, None),)
        return call(
            functools.partial(merge_kernel, order),
            f"merge{step}",
            shaped(len(order), nb, nb),
            [tile_ranks, dense_flags]
            + [pinned(dense_tiles), pinned(left_t), right_own, pinned(inverse_diag), *after],
            [
                smem,
                smem,
                spec_of((1, cols, nb, nb), (step, 0, 0, 0)),
                spec_of((1, cols, rank_pad, nb), (step, 0, 0, 0)),
                spec_of(right_own.shape),
                spec_of((1, nb, nb), (step, 0, 0)),
            ]
            + [any_spec] * len(after),
        )

    def over_cols(own, near):
        held = {0: own}
        reach = n // 2
        while near and reach >= 1:
            held |= {d ^ reach: shift(v, "pcol", reach) for d, v in held.items()}
            reach //= 2
        return [held[d] if d in held else shift(own, "pcol", d) for d in range(n)]

    sent, own = call(
        functools.partial(first_kernel, prev),
        "first",
        [shaped(prev * (nb + rank_pad), rhs), shaped(prev + 1, nb, nb)],
        [dense_flags, pinned(earlier), pinned(dense_tiles), pinned(right_t), pinned(inverse_diag)],
        [
            smem,
            spec_of(earlier.shape),
            spec_of((1, cols, nb, nb), (0, 0, 0, 0)),
            spec_of((1, cols, rank_pad, nb), (0, 0, 0, 0)),
            spec_of((1, nb, nb), (0, 0, 0)),
        ],
    )
    known = over_rows(sent)
    strips = [over_cols(own, True)]
    right_own = [None] + [packed(step, known[1:] if step > 1 else []) for step in range(1, steps)]

    def early(step, spread):
        low = step == 0
        tiles = 0
        picks = ([prev + step - 1] if step else []) + [prev + step]
        solved_at = [prev + index for index in range(len(spread))]
        args = strips[step] + known + [ref for blocks in spread for ref in blocks]
        specs = [spec_of(value.shape) for value in strips[step]]
        specs += [spec_of((prev * (nb + rank_pad) if low else prev * nb, rhs))] * n
        specs += [spec_of((nb, rhs))] * (n * len(spread))
        if low:
            args += [tile_ranks, dense_flags, pinned(left_t)]
            specs += [smem, smem, spec_of((1, cols, rank_pad, nb), (0, 0, 0, 0))]
        return call(
            functools.partial(early_kernel, n, prev, step, tiles, picks, solved_at, low),
            f"early{step}",
            [shaped(nb, rhs), shaped(len(picks), 2 * nb, n * nb, dtype=bf16)],
            args + [pinned(right_side)],
            specs + [spec_of((1, nb, rhs), (step, 0, 0))],
            [pltpu.VMEM((n * nb, rhs), f32)],
        )

    def chain(name, chain_strips, place, slots, rest, minus, stacked=False):
        return call(
            functools.partial(chain_kernel, n, minus, stacked),
            name,
            shaped(len(rest) + 1, nb, rhs) if stacked else shaped(nb, rhs),
            slots + [chain_strips] + rest,
            [spec_of((nb, rhs))] * n
            + [spec_of((1, 2 * nb, n * nb), (place, 0, 0))]
            + [spec_of((nb, rhs))] * len(rest),
            [pltpu.VMEM((n * nb, rhs), f32)],
        )

    pending, picked = early(0, [])
    solved, spread = [], []
    for step in range(steps):
        whole = over_rows(pending)
        if step == 0:
            strips.append(over_cols(merged(1, right_own[1], []), True))
            strips.append(over_cols(merged(2, right_own[2], whole[1:]), False))
        last = step + 1 == steps
        rest = solved if last else []
        block = chain(f"solve{step}", picked, 1 if step else 0, whole, rest, False, last)
        if last:
            return block
        solved.append(block)
        blocks = over_rows(block)
        if step == 0:
            strips.append(over_cols(merged(3, right_own[3], blocks[1:]), False))
        base, picked = early(step + 1, spread)
        pending = chain(f"update{step + 1}", picked, 0, blocks, [base], True)
        spread.append(blocks)
    return None


def solution(mesh):
    placed = (
        P("groups", "prow", "pcol"),
        P("groups", "prow", "pcol"),
        P("groups", "prow", "pcol"),
        P("groups", None, "prow", "pcol"),
        P("groups", None, "prow", None),
        P("groups", None, "prow", None),
        P("groups", None),
        P("groups", None),
    )
    n = mesh.shape["prow"]
    square = n > 1 and n == mesh.shape["pcol"] and n & (n - 1) == 0 and n <= 8

    def local(*args):
        nb, cols = args[3].shape[2:]
        if square and nb % 128 == 0 and cols % 128 == 0 and args[0].shape[2] % 128 == 0:
            return square_mesh(n, *args)
        return any_mesh(*args)

    return jax.shard_map(
        local, mesh=mesh, in_specs=placed, out_specs=P("groups", "prow", "pcol"), check_vma=False
    )
```

time: 333 us -> 136 us (0.41)
  waiting for transfers between devices: 161 us -> 33.4 us
  blocking collectives: 117 us -> 0 us
  starting transfers between devices: 0.2 us -> 83 us
  matrix products: 27.2 us -> 0 us
  Pallas kernels: 0 us -> 18 us
  between operations: 13.6 us -> 0.21 us
  other arithmetic: 11 us -> 0 us
    all_gather x7 -> x0, blocking collectives: 98.9 us -> none  [the longest x4 57.1 us: local(): lax.all_gather(pending[block_index], 'prow', axis=0, tiled=True)]
    psum x3 -> x0, waiting for transfers between devices: 86.6 us -> none  [the longest x2 52.3 us: local(): projected = lax.psum(projected, 'prow')]
    ppermute x0 -> x39, starting transfers between devices: none -> 83 us  [the longest x36 81 us: shift(): return lax.ppermute(value, axis, [(i, i ^ step) for i in range(n)])]
    all_gather x3 -> x0, waiting for transfers between devices: 72.2 us -> none  [the longest x1 48.4 us: local(): lax.all_gather(dense_tiles, 'pcol', axis=3, tiled=True)]
    ppermute x0 -> x39, waiting for transfers between devices: none -> 33.4 us  [the longest x36 33.4 us: shift(): return lax.ppermute(value, axis, [(i, i ^ step) for i in range(n)])]
    dot_general x14 -> x0, matrix products: 25.4 us -> none  [the longest x4 6.17 us: local(): jnp.dot(inverse_rows[block_index], residual_whole, precision=HIGHEST)]
    pallas_call x0 -> x18, Pallas kernels: none -> 18 us  [call(): pl.pallas_call(kernel, grid=(1,), out_shape=shapes, in_specs=specs, out_s...]
    psum x1 -> x0, blocking collectives: 17.9 us -> none  [local(): projected = lax.psum(projected, 'prow')]
  transfers between devices with their start and end apart: 6 -> 39, of which waited for: 6 -> 18; matrix products, arithmetic and copies ran while one was open for 8% -> 0% of each run, Pallas kernels for 0% -> 11%
where the time goes in v5:
time: 136 us; the launch traced here: 135 us
  starting transfers between devices  83 us (61%)
  waiting for transfers between devices  33.4 us (25%)
  Pallas kernels  18 us (13%)
    ppermute x36, starting transfers between devices, shift(): return lax.ppermute(value, axis, [(i, i ^ step) for i in range(n)])  81 us
    ppermute x36, waiting for transfers between devices, shift(): return lax.ppermute(value, axis, [(i, i ^ step) for i in range(n)])  33.4 us
    pallas_call x18, Pallas kernels, call(): pl.pallas_call(kernel, grid=(1,), out_shape=shapes, in_specs=specs, out_s...  18 us
  transfers between devices with their start and end apart: 39, of which 18 were waited for; matrix products, arithmetic and copies ran while one was open for 0% of the time, Pallas kernels for 11%

profile of v5, /device:TPU:0, one launch (start us, length us, event | category | flops | bytes accessed | tf_op | source)
XLA Modules:
  0.0 135.3 jit_solution(4798353865327522705)
XLA Ops:
  2.1 5.1 %collective-permute-start.5 = (f32[768,128]{1,0:T(8,128)S(1)}, f32[768,128]{1,0:T(8,128)S(1)}, u32[]{:S(2)}, u32[]{:S(2)}) collective-permute-start(f32[768,128]{1,0:T(8,128)S(1)} %get-tuple-element.16.refs_4_), channel_id=1, source_target_pairs={{0,12},{4,8},{8,4},{12,0},{1,13},{5,9},{9,5},{13,1},{2,14},{6,10},... | collective-permute-start | bytes 1179656 | tf_op jit(solution)/shard_map/ppermute | solution.py:213
  8.9 2.8 %collective-permute-start.1 = (f32[5,128,128]{2,1,0:T(8,128)S(1)}, f32[5,128,128]{2,1,0:T(8,128)S(1)}, u32[]{:S(2)}, u32[]{:S(2)}) collective-permute-start(f32[5,128,128]{2,1,0:T(8,128)S(1)} %get-tuple-element.15.refs_0_), channel_id=1, source_target_pairs={{0,2},{1,3},{2,0},{3,1},{4,6},{5,7},{6,4},{7,5},{8,10},{9,11},{10,... | collective-permute-start | bytes 983048 | tf_op jit(solution)/shard_map/ppermute | solution.py:213
  14.4 25.4 %collective-permute-start.14 = (f32[6,128,128]{2,1,0:T(8,128)S(1)}, f32[6,128,128]{2,1,0:T(8,128)S(1)}, u32[]{:S(2)}, u32[]{:S(2)}) collective-permute-start(f32[6,128,128]{2,1,0:T(8,128)S(1)} %merge1.1.refs_0_), channel_id=1, source_target_pairs={{0,2},{1,3},{2,0},{3,1},{4,6},{5,7},{6,4},{7,5},{8,10},{9,11},{10,... | collective-permute-start | bytes 1179656 | tf_op jit(solution)/shard_map/ppermute | solution.py:213
  40.2 3.3 %collective-permute-done.4.refs_6_.refs_1_ = f32[768,128]{1,0:T(8,128)S(1)} collective-permute-done((f32[768,128]{1,0:T(8,128)S(1)}, f32[768,128]{1,0:T(8,128)S(1)}, u32[]{:S(2)}, u32[]{:S(2)}) %collective-permute-start.4) | collective-permute-done | bytes 393248 | tf_op jit(solution)/shard_map/ppermute | solution.py:213
  47.1 1.7 %early0.1 = (f32[128,128]{1,0:T(8,128)S(1)}, bf16[1,256,512]{2,1,0:T(8,128)(2,1)S(1)}) custom-call(f32[5,128,128]{2,1,0:T(8,128)S(1)} %get-tuple-element.15.refs_0_, f32[5,128,128]{2,1,0:T(8,128)S(1)} %collective-permute-done.refs_1_, f32[5,128,128]{2,1,0:T(8,128)S(1)} %collective-permute-done.1.refs_2_, f32[5,128,128]{2,1,0:T(8,128)S(1)} %collective-permute-done.2.refs_3_, ...), custom_call_target="tpu_custom_call" | custom-call | tf_op jit(solution)/shard_map/early0/pallas_call | solution.py:238
  48.7 3.7 %collective-permute-start.8 = (f32[128,128]{1,0:T(8,128)S(1)}, f32[128,128]{1,0:T(8,128)S(1)}, u32[]{:S(2)}, u32[]{:S(2)}) collective-permute-start(f32[128,128]{1,0:T(8,128)S(1)} %get-tuple-element.17.refs_0_), channel_id=1, source_target_pairs={{0,12},{4,8},{8,4},{12,0},{1,13},{5,9},{9,5},{13,1},{2,14},{6,10},... | collective-permute-start | bytes 196616 | tf_op jit(solution)/shard_map/ppermute | solution.py:213
  55.3 4.3 %collective-permute-done.7.refs_2_.refs_1_ = f32[128,128]{1,0:T(8,128)S(1)} collective-permute-done((f32[128,128]{1,0:T(8,128)S(1)}, f32[128,128]{1,0:T(8,128)S(1)}, u32[]{:S(2)}, u32[]{:S(2)}) %collective-permute-start.7) | collective-permute-done | bytes 65568 | tf_op jit(solution)/shard_map/ppermute | solution.py:213
  62.9 2.4 %collective-permute-start.11 = (f32[128,128]{1,0:T(8,128)S(1)}, f32[128,128]{1,0:T(8,128)S(1)}, u32[]{:S(2)}, u32[]{:S(2)}) collective-permute-start(f32[128,128]{1,0:T(8,128)S(1)} %solve0.1.refs_0_.refs_8_.refs_5_), channel_id=1, source_target_pairs={{0,12},{4,8},{8,4},{12,0},{1,13},{5,9},{9,5},{13,1},{2,14},{6,10},... | collective-permute-start | bytes 196616 | tf_op jit(solution)/shard_map/ppermute | solution.py:213
  65.4 2.0 %collective-permute-start.9 = (f32[128,128]{1,0:T(8,128)S(1)}, f32[128,128]{1,0:T(8,128)S(1)}, u32[]{:S(2)}, u32[]{:S(2)}) collective-permute-start(f32[128,128]{1,0:T(8,128)S(1)} %solve0.1.refs_0_.refs_8_.refs_5_), channel_id=1, source_target_pairs={{0,4},{4,0},{8,12},{12,8},{1,5},{5,1},{9,13},{13,9},{2,6},{6,2},{1... | collective-permute-start | bytes 196616 | tf_op jit(solution)/shard_map/ppermute | solution.py:213
  72.1 3.0 %collective-permute-start.18 = (f32[128,128]{1,0:T(8,128)S(1)}, f32[128,128]{1,0:T(8,128)S(1)}, u32[]{:S(2)}, u32[]{:S(2)}) collective-permute-start(f32[128,128]{1,0:T(8,128)S(1)} %update1.1.refs_0_), channel_id=1, source_target_pairs={{0,12},{4,8},{8,4},{12,0},{1,13},{5,9},{9,5},{13,1},{2,14},{6,10},... | collective-permute-start | bytes 196616 | tf_op jit(solution)/shard_map/ppermute | solution.py:213
  75.9 2.3 %collective-permute-done.18.refs_3_ = f32[128,128]{1,0:T(8,128)S(1)} collective-permute-done((f32[128,128]{1,0:T(8,128)S(1)}, f32[128,128]{1,0:T(8,128)S(1)}, u32[]{:S(2)}, u32[]{:S(2)}) %collective-permute-start.18) | collective-permute-done | bytes 65568 | tf_op jit(solution)/shard_map/ppermute | solution.py:213
  78.3 4.0 %collective-permute-start.17 = (f32[128,128]{1,0:T(8,128)S(1)}, f32[128,128]{1,0:T(8,128)S(1)}, u32[]{:S(2)}, u32[]{:S(2)}) collective-permute-start(f32[128,128]{1,0:T(8,128)S(1)} %update1.1.refs_0_), channel_id=1, source_target_pairs={{0,8},{4,12},{8,0},{12,4},{1,9},{5,13},{9,1},{13,5},{2,10},{6,14},... | collective-permute-start | bytes 196616 | tf_op jit(solution)/shard_map/ppermute | solution.py:213
  82.3 2.2 %collective-permute-done.17.refs_2_ = f32[128,128]{1,0:T(8,128)S(1)} collective-permute-done((f32[128,128]{1,0:T(8,128)S(1)}, f32[128,128]{1,0:T(8,128)S(1)}, u32[]{:S(2)}, u32[]{:S(2)}) %collective-permute-start.17) | collective-permute-done | bytes 65568 | tf_op jit(solution)/shard_map/ppermute | solution.py:213
  84.5 1.7 %collective-permute-start.16 = (f32[128,128]{1,0:T(8,128)S(1)}, f32[128,128]{1,0:T(8,128)S(1)}, u32[]{:S(2)}, u32[]{:S(2)}) collective-permute-start(f32[128,128]{1,0:T(8,128)S(1)} %update1.1.refs_0_), channel_id=1, source_target_pairs={{0,4},{4,0},{8,12},{12,8},{1,5},{5,1},{9,13},{13,9},{2,6},{6,2},{1... | collective-permute-start | bytes 196616 | tf_op jit(solution)/shard_map/ppermute | solution.py:213
  86.2 2.5 %collective-permute-done.16.refs_1_ = f32[128,128]{1,0:T(8,128)S(1)} collective-permute-done((f32[128,128]{1,0:T(8,128)S(1)}, f32[128,128]{1,0:T(8,128)S(1)}, u32[]{:S(2)}, u32[]{:S(2)}) %collective-permute-start.16) | collective-permute-done | bytes 65568 | tf_op jit(solution)/shard_map/ppermute | solution.py:213
  89.0 3.0 %collective-permute-start.21 = (f32[128,128]{1,0:T(8,128)S(1)}, f32[128,128]{1,0:T(8,128)S(1)}, u32[]{:S(2)}, u32[]{:S(2)}) collective-permute-start(f32[128,128]{1,0:T(8,128)S(1)} %solve1.1.refs_0_.refs_12_.refs_6_), channel_id=1, source_target_pairs={{0,12},{4,8},{8,4},{12,0},{1,13},{5,9},{9,5},{13,1},{2,14},{6,10},... | collective-permute-start | bytes 196616 | tf_op jit(solution)/shard_map/ppermute | solution.py:213
  92.1 1.6 %merge3.1.refs_0_ = f32[8,128,128]{2,1,0:T(8,128)S(1)} custom-call(s32[4,7]{1,0:T(4,128)S(1)} %copy-done.2, s32[4,7]{1,0:T(4,128)S(1)} %copy-done.1, f32[4,7,128,128]{3,2,1,0:T(8,128)} %dense_ref.7, f32[4,7,64,128]{3,2,1,0:T(8,128)} %bitcast.9, f32[7,64,128]{2,1,0:T(8,128)S(1)} %collective-permute-done.32.right_ref, f32[4,128,128]{2,1,0:T(8,128)} %inv_ref.7, ...), custom_call_target="tpu_custom_call" | custom-call | tf_op jit(solution)/shard_map/merge3/pallas_call | solution.py:238
  94.1 1.8 %collective-permute-done.21.refs_3_.refs_15_ = f32[128,128]{1,0:T(8,128)S(1)} collective-permute-done((f32[128,128]{1,0:T(8,128)S(1)}, f32[128,128]{1,0:T(8,128)S(1)}, u32[]{:S(2)}, u32[]{:S(2)}) %collective-permute-start.21) | collective-permute-done | bytes 65568 | tf_op jit(solution)/shard_map/ppermute | solution.py:213
  95.9 3.6 %collective-permute-start.34 = (f32[8,128,128]{2,1,0:T(8,128)S(1)}, f32[8,128,128]{2,1,0:T(8,128)S(1)}, u32[]{:S(2)}, u32[]{:S(2)}) collective-permute-start(f32[8,128,128]{2,1,0:T(8,128)S(1)} %merge3.1.refs_0_), channel_id=1, source_target_pairs={{0,2},{1,3},{2,0},{3,1},{4,6},{5,7},{6,4},{7,5},{8,10},{9,11},{10,... | collective-permute-start | bytes 1572872 | tf_op jit(solution)/shard_map/ppermute | solution.py:213
  99.7 3.4 %collective-permute-start.19 = (f32[128,128]{1,0:T(8,128)S(1)}, f32[128,128]{1,0:T(8,128)S(1)}, u32[]{:S(2)}, u32[]{:S(2)}) collective-permute-start(f32[128,128]{1,0:T(8,128)S(1)} %solve1.1.refs_0_.refs_12_.refs_6_), channel_id=1, source_target_pairs={{0,4},{4,0},{8,12},{12,8},{1,5},{5,1},{9,13},{13,9},{2,6},{6,2},{1... | collective-permute-start | bytes 196616 | tf_op jit(solution)/shard_map/ppermute | solution.py:213
  103.0 1.6 %early2.1 = (f32[128,128]{1,0:T(8,128)S(1)}, bf16[2,256,512]{2,1,0:T(8,128)(2,1)S(1)}) custom-call(f32[7,128,128]{2,1,0:T(8,128)S(1)} %merge2.1.refs_0_, f32[7,128,128]{2,1,0:T(8,128)S(1)} %collective-permute-done.23.refs_1_, f32[7,128,128]{2,1,0:T(8,128)S(1)} %collective-permute-done.24.refs_2_, f32[7,128,128]{2,1,0:T(8,128)S(1)} %collective-permute-done.25.refs_3_, ...), custom_call_target="tpu_custom_call" | custom-call | tf_op jit(solution)/shard_map/early2/pallas_call | solution.py:238
  104.7 1.8 %collective-permute-done.20.refs_2_.refs_14_ = f32[128,128]{1,0:T(8,128)S(1)} collective-permute-done((f32[128,128]{1,0:T(8,128)S(1)}, f32[128,128]{1,0:T(8,128)S(1)}, u32[]{:S(2)}, u32[]{:S(2)}) %collective-permute-start.20) | collective-permute-done | bytes 65568 | tf_op jit(solution)/shard_map/ppermute | solution.py:213
  106.8 1.9 %collective-permute-start.28 = (f32[128,128]{1,0:T(8,128)S(1)}, f32[128,128]{1,0:T(8,128)S(1)}, u32[]{:S(2)}, u32[]{:S(2)}) collective-permute-start(f32[128,128]{1,0:T(8,128)S(1)} %update2.1.refs_0_), channel_id=1, source_target_pairs={{0,12},{4,8},{8,4},{12,0},{1,13},{5,9},{9,5},{13,1},{2,14},{6,10},... | collective-permute-start | bytes 196616 | tf_op jit(solution)/shard_map/ppermute | solution.py:213
  109.1 4.0 %collective-permute-done.28.refs_3_ = f32[128,128]{1,0:T(8,128)S(1)} collective-permute-done((f32[128,128]{1,0:T(8,128)S(1)}, f32[128,128]{1,0:T(8,128)S(1)}, u32[]{:S(2)}, u32[]{:S(2)}) %collective-permute-start.28) | collective-permute-done | bytes 65568 | tf_op jit(solution)/shard_map/ppermute | solution.py:213
  113.1 1.9 %collective-permute-start.26 = (f32[128,128]{1,0:T(8,128)S(1)}, f32[128,128]{1,0:T(8,128)S(1)}, u32[]{:S(2)}, u32[]{:S(2)}) collective-permute-start(f32[128,128]{1,0:T(8,128)S(1)} %update2.1.refs_0_), channel_id=1, source_target_pairs={{0,4},{4,0},{8,12},{12,8},{1,5},{5,1},{9,13},{13,9},{2,6},{6,2},{1... | collective-permute-start | bytes 196616 | tf_op jit(solution)/shard_map/ppermute | solution.py:213
  115.7 1.7 %collective-permute-done.26.refs_1_ = f32[128,128]{1,0:T(8,128)S(1)} collective-permute-done((f32[128,128]{1,0:T(8,128)S(1)}, f32[128,128]{1,0:T(8,128)S(1)}, u32[]{:S(2)}, u32[]{:S(2)}) %collective-permute-start.26) | collective-permute-done | bytes 65568 | tf_op jit(solution)/shard_map/ppermute | solution.py:213
  117.7 1.9 %collective-permute-start.31 = (f32[128,128]{1,0:T(8,128)S(1)}, f32[128,128]{1,0:T(8,128)S(1)}, u32[]{:S(2)}, u32[]{:S(2)}) collective-permute-start(f32[128,128]{1,0:T(8,128)S(1)} %solve2.1.refs_0_.refs_7_), channel_id=1, source_target_pairs={{0,12},{4,8},{8,4},{12,0},{1,13},{5,9},{9,5},{13,1},{2,14},{6,10},... | collective-permute-start | bytes 196616 | tf_op jit(solution)/shard_map/ppermute | solution.py:213
  122.1 1.7 %early3.1 = (f32[128,128]{1,0:T(8,128)S(1)}, bf16[2,256,512]{2,1,0:T(8,128)(2,1)S(1)}) custom-call(f32[8,128,128]{2,1,0:T(8,128)S(1)} %merge3.1.refs_0_, f32[8,128,128]{2,1,0:T(8,128)S(1)} %collective-permute-done.33.refs_1_, f32[8,128,128]{2,1,0:T(8,128)S(1)} %collective-permute-done.34.refs_2_, f32[8,128,128]{2,1,0:T(8,128)S(1)} %collective-permute-done.35.refs_3_, ...), custom_call_target="tpu_custom_call" | custom-call | tf_op jit(solution)/shard_map/early3/pallas_call | solution.py:238
  123.9 2.0 %collective-permute-done.30.refs_2_ = f32[128,128]{1,0:T(8,128)S(1)} collective-permute-done((f32[128,128]{1,0:T(8,128)S(1)}, f32[128,128]{1,0:T(8,128)S(1)}, u32[]{:S(2)}, u32[]{:S(2)}) %collective-permute-start.30) | collective-permute-done | bytes 65568 | tf_op jit(solution)/shard_map/ppermute | solution.py:213
  128.2 2.7 %collective-permute-start.36 = (f32[128,128]{1,0:T(8,128)S(1)}, f32[128,128]{1,0:T(8,128)S(1)}, u32[]{:S(2)}, u32[]{:S(2)}) collective-permute-start(f32[128,128]{1,0:T(8,128)S(1)} %update3.1.refs_0_), channel_id=1, source_target_pairs={{0,4},{4,0},{8,12},{12,8},{1,5},{5,1},{9,13},{13,9},{2,6},{6,2},{1... | collective-permute-start | bytes 196616 | tf_op jit(solution)/shard_map/ppermute | solution.py:213
  130.9 1.8 %collective-permute-done.38.refs_3_ = f32[128,128]{1,0:T(8,128)S(1)} collective-permute-done((f32[128,128]{1,0:T(8,128)S(1)}, f32[128,128]{1,0:T(8,128)S(1)}, u32[]{:S(2)}, u32[]{:S(2)}) %collective-permute-start.38) | collective-permute-done | bytes 65568 | tf_op jit(solution)/shard_map/ppermute | solution.py:213
  132.7 1.6 %collective-permute-done.37.refs_2_ = f32[128,128]{1,0:T(8,128)S(1)} collective-permute-done((f32[128,128]{1,0:T(8,128)S(1)}, f32[128,128]{1,0:T(8,128)S(1)}, u32[]{:S(2)}, u32[]{:S(2)}) %collective-permute-start.37) | collective-permute-done | bytes 65568 | tf_op jit(solution)/shard_map/ppermute | solution.py:213
  (70 shorter events, 30.4 us)
Async XLA Ops:
  2.1 37.6 %collective-permute-start.5 = (f32[768,128]{1,0:T(8,128)S(1)}, f32[768,128]{1,0:T(8,128)S(1)}, u32[]{:S(2)}, u32[]{:S(2)}) collective-permute-start(f32[768,128]{1,0:T(8,128)S(1)} %get-tuple-element.16.refs_4_), channel_id=1, source_target_pairs={{0,12},{4,8},{8,4},{12,0},{1,13},{5,9},{9,5},{13,1},{2,14},{6,10},... | collective-permute-start | bytes 1179656 | tf_op jit(solution)/shard_map/ppermute | solution.py:213
  8.9 30.9 %collective-permute-start.1 = (f32[5,128,128]{2,1,0:T(8,128)S(1)}, f32[5,128,128]{2,1,0:T(8,128)S(1)}, u32[]{:S(2)}, u32[]{:S(2)}) collective-permute-start(f32[5,128,128]{2,1,0:T(8,128)S(1)} %get-tuple-element.15.refs_0_), channel_id=1, source_target_pairs={{0,2},{1,3},{2,0},{3,1},{4,6},{5,7},{6,4},{7,5},{8,10},{9,11},{10,... | collective-permute-start | bytes 983048 | tf_op jit(solution)/shard_map/ppermute | solution.py:213
  11.7 31.8 %collective-permute-start.4 = (f32[768,128]{1,0:T(8,128)S(1)}, f32[768,128]{1,0:T(8,128)S(1)}, u32[]{:S(2)}, u32[]{:S(2)}) collective-permute-start(f32[768,128]{1,0:T(8,128)S(1)} %get-tuple-element.16.refs_4_), channel_id=1, source_target_pairs={{0,8},{4,12},{8,0},{12,4},{1,9},{5,13},{9,1},{13,5},{2,10},{6,14},... | collective-permute-start | bytes 1179656 | tf_op jit(solution)/shard_map/ppermute | solution.py:213
  12.4 31.7 %collective-permute-start.3 = (f32[768,128]{1,0:T(8,128)S(1)}, f32[768,128]{1,0:T(8,128)S(1)}, u32[]{:S(2)}, u32[]{:S(2)}) collective-permute-start(f32[768,128]{1,0:T(8,128)S(1)} %get-tuple-element.16.refs_4_), channel_id=1, source_target_pairs={{0,4},{4,0},{8,12},{12,8},{1,5},{5,1},{9,13},{13,9},{2,6},{6,2},{1... | collective-permute-start | bytes 1179656 | tf_op jit(solution)/shard_map/ppermute | solution.py:213
  14.4 31.4 %collective-permute-start.14 = (f32[6,128,128]{2,1,0:T(8,128)S(1)}, f32[6,128,128]{2,1,0:T(8,128)S(1)}, u32[]{:S(2)}, u32[]{:S(2)}) collective-permute-start(f32[6,128,128]{2,1,0:T(8,128)S(1)} %merge1.1.refs_0_), channel_id=1, source_target_pairs={{0,2},{1,3},{2,0},{3,1},{4,6},{5,7},{6,4},{7,5},{8,10},{9,11},{10,... | collective-permute-start | bytes 1179656 | tf_op jit(solution)/shard_map/ppermute | solution.py:213
  39.7 7.4 %collective-permute-start = (f32[5,128,128]{2,1,0:T(8,128)S(1)}, f32[5,128,128]{2,1,0:T(8,128)S(1)}, u32[]{:S(2)}, u32[]{:S(2)}) collective-permute-start(f32[5,128,128]{2,1,0:T(8,128)S(1)} %get-tuple-element.15.refs_0_), channel_id=1, source_target_pairs={{0,1},{1,0},{2,3},{3,2},{4,5},{5,4},{6,7},{7,6},{8,9},{9,8},{10,11... | collective-permute-start | bytes 983048 | tf_op jit(solution)/shard_map/ppermute | solution.py:213
  39.7 7.4 %collective-permute-start.2 = (f32[5,128,128]{2,1,0:T(8,128)S(1)}, f32[5,128,128]{2,1,0:T(8,128)S(1)}, u32[]{:S(2)}, u32[]{:S(2)}) collective-permute-start(f32[5,128,128]{2,1,0:T(8,128)S(1)} %collective-permute-done.1.refs_2_), channel_id=1, source_target_pairs={{0,1},{1,0},{2,3},{3,2},{4,5},{5,4},{6,7},{7,6},{8,9},{9,8},{10,11... | collective-permute-start | bytes 983048 | tf_op jit(solution)/shard_map/ppermute | solution.py:213
  43.5 21.9 %collective-permute-start.13 = (f32[6,128,128]{2,1,0:T(8,128)S(1)}, f32[6,128,128]{2,1,0:T(8,128)S(1)}, u32[]{:S(2)}, u32[]{:S(2)}) collective-permute-start(f32[6,128,128]{2,1,0:T(8,128)S(1)} %merge1.1.refs_0_), channel_id=1, source_target_pairs={{0,1},{1,0},{2,3},{3,2},{4,5},{5,4},{6,7},{7,6},{8,9},{9,8},{10,11... | collective-permute-start | bytes 1179656 | tf_op jit(solution)/shard_map/ppermute | solution.py:213
  45.1 8.0 %collective-permute-start.22 = (f32[6,64,128]{2,1,0:T(8,128)S(1)}, f32[6,64,128]{2,1,0:T(8,128)S(1)}, u32[]{:S(2)}, u32[]{:S(2)}) collective-permute-start(f32[6,64,128]{2,1,0:T(8,128)S(1)} %pack2.1), channel_id=1, source_target_pairs={{0,0},{2,4},{1,8},{3,12},{6,1},{4,5},{7,9},{5,13},{9,2},{11,6},{8,... | collective-permute-start | bytes 589832 | tf_op jit(solution)/shard_map/ppermute | solution.py:257
  45.8 22.6 %collective-permute-start.15 = (f32[6,128,128]{2,1,0:T(8,128)S(1)}, f32[6,128,128]{2,1,0:T(8,128)S(1)}, u32[]{:S(2)}, u32[]{:S(2)}) collective-permute-start(f32[6,128,128]{2,1,0:T(8,128)S(1)} %collective-permute-done.14.refs_2_), channel_id=1, source_target_pairs={{0,1},{1,0},{2,3},{3,2},{4,5},{5,4},{6,7},{7,6},{8,9},{9,8},{10,11... | collective-permute-start | bytes 1179656 | tf_op jit(solution)/shard_map/ppermute | solution.py:213
  48.7 6.6 %collective-permute-start.8 = (f32[128,128]{1,0:T(8,128)S(1)}, f32[128,128]{1,0:T(8,128)S(1)}, u32[]{:S(2)}, u32[]{:S(2)}) collective-permute-start(f32[128,128]{1,0:T(8,128)S(1)} %get-tuple-element.17.refs_0_), channel_id=1, source_target_pairs={{0,12},{4,8},{8,4},{12,0},{1,13},{5,9},{9,5},{13,1},{2,14},{6,10},... | collective-permute-start | bytes 196616 | tf_op jit(solution)/shard_map/ppermute | solution.py:213
  52.5 7.1 %collective-permute-start.7 = (f32[128,128]{1,0:T(8,128)S(1)}, f32[128,128]{1,0:T(8,128)S(1)}, u32[]{:S(2)}, u32[]{:S(2)}) collective-permute-start(f32[128,128]{1,0:T(8,128)S(1)} %get-tuple-element.17.refs_0_), channel_id=1, source_target_pairs={{0,8},{4,12},{8,0},{12,4},{1,9},{5,13},{9,1},{13,5},{2,10},{6,14},... | collective-permute-start | bytes 196616 | tf_op jit(solution)/shard_map/ppermute | solution.py:213
  53.1 6.5 %collective-permute-start.6 = (f32[128,128]{1,0:T(8,128)S(1)}, f32[128,128]{1,0:T(8,128)S(1)}, u32[]{:S(2)}, u32[]{:S(2)}) collective-permute-start(f32[128,128]{1,0:T(8,128)S(1)} %get-tuple-element.17.refs_0_), channel_id=1, source_target_pairs={{0,4},{4,0},{8,12},{12,8},{1,5},{5,1},{9,13},{13,9},{2,6},{6,2},{1... | collective-permute-start | bytes 196616 | tf_op jit(solution)/shard_map/ppermute | solution.py:213
  61.2 38.4 %collective-permute-start.25 = (f32[7,128,128]{2,1,0:T(8,128)S(1)}, f32[7,128,128]{2,1,0:T(8,128)S(1)}, u32[]{:S(2)}, u32[]{:S(2)}) collective-permute-start(f32[7,128,128]{2,1,0:T(8,128)S(1)} %merge2.1.refs_0_), channel_id=1, source_target_pairs={{0,3},{1,2},{2,1},{3,0},{4,7},{5,6},{6,5},{7,4},{8,11},{9,10},{10,... | collective-permute-start | bytes 1376264 | tf_op jit(solution)/shard_map/ppermute | solution.py:213
  62.9 7.6 %collective-permute-start.11 = (f32[128,128]{1,0:T(8,128)S(1)}, f32[128,128]{1,0:T(8,128)S(1)}, u32[]{:S(2)}, u32[]{:S(2)}) collective-permute-start(f32[128,128]{1,0:T(8,128)S(1)} %solve0.1.refs_0_.refs_8_.refs_5_), channel_id=1, source_target_pairs={{0,12},{4,8},{8,4},{12,0},{1,13},{5,9},{9,5},{13,1},{2,14},{6,10},... | collective-permute-start | bytes 196616 | tf_op jit(solution)/shard_map/ppermute | solution.py:213
  65.3 6.4 %collective-permute-start.10 = (f32[128,128]{1,0:T(8,128)S(1)}, f32[128,128]{1,0:T(8,128)S(1)}, u32[]{:S(2)}, u32[]{:S(2)}) collective-permute-start(f32[128,128]{1,0:T(8,128)S(1)} %solve0.1.refs_0_.refs_8_.refs_5_), channel_id=1, source_target_pairs={{0,8},{4,12},{8,0},{12,4},{1,9},{5,13},{9,1},{13,5},{2,10},{6,14},... | collective-permute-start | bytes 196616 | tf_op jit(solution)/shard_map/ppermute | solution.py:213
  65.4 6.4 %collective-permute-start.9 = (f32[128,128]{1,0:T(8,128)S(1)}, f32[128,128]{1,0:T(8,128)S(1)}, u32[]{:S(2)}, u32[]{:S(2)}) collective-permute-start(f32[128,128]{1,0:T(8,128)S(1)} %solve0.1.refs_0_.refs_8_.refs_5_), channel_id=1, source_target_pairs={{0,4},{4,0},{8,12},{12,8},{1,5},{5,1},{9,13},{13,9},{2,6},{6,2},{1... | collective-permute-start | bytes 196616 | tf_op jit(solution)/shard_map/ppermute | solution.py:213
  68.4 23.7 %collective-permute-start.32 = (f32[7,64,128]{2,1,0:T(8,128)S(1)}, f32[7,64,128]{2,1,0:T(8,128)S(1)}, u32[]{:S(2)}, u32[]{:S(2)}) collective-permute-start(f32[7,64,128]{2,1,0:T(8,128)S(1)} %pack3.1), channel_id=1, source_target_pairs={{0,0},{2,4},{1,8},{3,12},{6,1},{4,5},{7,9},{5,13},{9,2},{11,6},{8,... | collective-permute-start | bytes 688136 | tf_op jit(solution)/shard_map/ppermute | solution.py:257
  75.0 24.5 %collective-permute-start.24 = (f32[7,128,128]{2,1,0:T(8,128)S(1)}, f32[7,128,128]{2,1,0:T(8,128)S(1)}, u32[]{:S(2)}, u32[]{:S(2)}) collective-permute-start(f32[7,128,128]{2,1,0:T(8,128)S(1)} %merge2.1.refs_0_), channel_id=1, source_target_pairs={{0,2},{1,3},{2,0},{3,1},{4,6},{5,7},{6,4},{7,5},{8,10},{9,11},{10,... | collective-permute-start | bytes 1376264 | tf_op jit(solution)/shard_map/ppermute | solution.py:213
  75.9 23.7 %collective-permute-start.23 = (f32[7,128,128]{2,1,0:T(8,128)S(1)}, f32[7,128,128]{2,1,0:T(8,128)S(1)}, u32[]{:S(2)}, u32[]{:S(2)}) collective-permute-start(f32[7,128,128]{2,1,0:T(8,128)S(1)} %merge2.1.refs_0_), channel_id=1, source_target_pairs={{0,1},{1,0},{2,3},{3,2},{4,5},{5,4},{6,7},{7,6},{8,9},{9,8},{10,11... | collective-permute-start | bytes 1376264 | tf_op jit(solution)/shard_map/ppermute | solution.py:213
  89.0 6.9 %collective-permute-start.21 = (f32[128,128]{1,0:T(8,128)S(1)}, f32[128,128]{1,0:T(8,128)S(1)}, u32[]{:S(2)}, u32[]{:S(2)}) collective-permute-start(f32[128,128]{1,0:T(8,128)S(1)} %solve1.1.refs_0_.refs_12_.refs_6_), channel_id=1, source_target_pairs={{0,12},{4,8},{8,4},{12,0},{1,13},{5,9},{9,5},{13,1},{2,14},{6,10},... | collective-permute-start | bytes 196616 | tf_op jit(solution)/shard_map/ppermute | solution.py:213
  93.7 27.4 %collective-permute-start.35 = (f32[8,128,128]{2,1,0:T(8,128)S(1)}, f32[8,128,128]{2,1,0:T(8,128)S(1)}, u32[]{:S(2)}, u32[]{:S(2)}) collective-permute-start(f32[8,128,128]{2,1,0:T(8,128)S(1)} %merge3.1.refs_0_), channel_id=1, source_target_pairs={{0,3},{1,2},{2,1},{3,0},{4,7},{5,6},{6,5},{7,4},{8,11},{9,10},{10,... | collective-permute-start | bytes 1572872 | tf_op jit(solution)/shard_map/ppermute | solution.py:213
  95.9 26.2 %collective-permute-start.34 = (f32[8,128,128]{2,1,0:T(8,128)S(1)}, f32[8,128,128]{2,1,0:T(8,128)S(1)}, u32[]{:S(2)}, u32[]{:S(2)}) collective-permute-start(f32[8,128,128]{2,1,0:T(8,128)S(1)} %merge3.1.refs_0_), channel_id=1, source_target_pairs={{0,2},{1,3},{2,0},{3,1},{4,6},{5,7},{6,4},{7,5},{8,10},{9,11},{10,... | collective-permute-start | bytes 1572872 | tf_op jit(solution)/shard_map/ppermute | solution.py:213
  99.6 22.6 %collective-permute-start.33 = (f32[8,128,128]{2,1,0:T(8,128)S(1)}, f32[8,128,128]{2,1,0:T(8,128)S(1)}, u32[]{:S(2)}, u32[]{:S(2)}) collective-permute-start(f32[8,128,128]{2,1,0:T(8,128)S(1)} %merge3.1.refs_0_), channel_id=1, source_target_pairs={{0,1},{1,0},{2,3},{3,2},{4,5},{5,4},{6,7},{7,6},{8,9},{9,8},{10,11... | collective-permute-start | bytes 1572872 | tf_op jit(solution)/shard_map/ppermute | solution.py:213
  99.6 6.9 %collective-permute-start.20 = (f32[128,128]{1,0:T(8,128)S(1)}, f32[128,128]{1,0:T(8,128)S(1)}, u32[]{:S(2)}, u32[]{:S(2)}) collective-permute-start(f32[128,128]{1,0:T(8,128)S(1)} %solve1.1.refs_0_.refs_12_.refs_6_), channel_id=1, source_target_pairs={{0,8},{4,12},{8,0},{12,4},{1,9},{5,13},{9,1},{13,5},{2,10},{6,14},... | collective-permute-start | bytes 196616 | tf_op jit(solution)/shard_map/ppermute | solution.py:213
  99.7 6.9 %collective-permute-start.19 = (f32[128,128]{1,0:T(8,128)S(1)}, f32[128,128]{1,0:T(8,128)S(1)}, u32[]{:S(2)}, u32[]{:S(2)}) collective-permute-start(f32[128,128]{1,0:T(8,128)S(1)} %solve1.1.refs_0_.refs_12_.refs_6_), channel_id=1, source_target_pairs={{0,4},{4,0},{8,12},{12,8},{1,5},{5,1},{9,13},{13,9},{2,6},{6,2},{1... | collective-permute-start | bytes 196616 | tf_op jit(solution)/shard_map/ppermute | solution.py:213
  106.8 6.3 %collective-permute-start.28 = (f32[128,128]{1,0:T(8,128)S(1)}, f32[128,128]{1,0:T(8,128)S(1)}, u32[]{:S(2)}, u32[]{:S(2)}) collective-permute-start(f32[128,128]{1,0:T(8,128)S(1)} %update2.1.refs_0_), channel_id=1, source_target_pairs={{0,12},{4,8},{8,4},{12,0},{1,13},{5,9},{9,5},{13,1},{2,14},{6,10},... | collective-permute-start | bytes 196616 | tf_op jit(solution)/shard_map/ppermute | solution.py:213
  108.7 6.9 %collective-permute-start.27 = (f32[128,128]{1,0:T(8,128)S(1)}, f32[128,128]{1,0:T(8,128)S(1)}, u32[]{:S(2)}, u32[]{:S(2)}) collective-permute-start(f32[128,128]{1,0:T(8,128)S(1)} %update2.1.refs_0_), channel_id=1, source_target_pairs={{0,8},{4,12},{8,0},{12,4},{1,9},{5,13},{9,1},{13,5},{2,10},{6,14},... | collective-permute-start | bytes 196616 | tf_op jit(solution)/shard_map/ppermute | solution.py:213
  117.7 6.3 %collective-permute-start.31 = (f32[128,128]{1,0:T(8,128)S(1)}, f32[128,128]{1,0:T(8,128)S(1)}, u32[]{:S(2)}, u32[]{:S(2)}) collective-permute-start(f32[128,128]{1,0:T(8,128)S(1)} %solve2.1.refs_0_.refs_7_), channel_id=1, source_target_pairs={{0,12},{4,8},{8,4},{12,0},{1,13},{5,9},{9,5},{13,1},{2,14},{6,10},... | collective-permute-start | bytes 196616 | tf_op jit(solution)/shard_map/ppermute | solution.py:213
  119.6 6.4 %collective-permute-start.30 = (f32[128,128]{1,0:T(8,128)S(1)}, f32[128,128]{1,0:T(8,128)S(1)}, u32[]{:S(2)}, u32[]{:S(2)}) collective-permute-start(f32[128,128]{1,0:T(8,128)S(1)} %solve2.1.refs_0_.refs_7_), channel_id=1, source_target_pairs={{0,8},{4,12},{8,0},{12,4},{1,9},{5,13},{9,1},{13,5},{2,10},{6,14},... | collective-permute-start | bytes 196616 | tf_op jit(solution)/shard_map/ppermute | solution.py:213
  126.4 6.3 %collective-permute-start.38 = (f32[128,128]{1,0:T(8,128)S(1)}, f32[128,128]{1,0:T(8,128)S(1)}, u32[]{:S(2)}, u32[]{:S(2)}) collective-permute-start(f32[128,128]{1,0:T(8,128)S(1)} %update3.1.refs_0_), channel_id=1, source_target_pairs={{0,12},{4,8},{8,4},{12,0},{1,13},{5,9},{9,5},{13,1},{2,14},{6,10},... | collective-permute-start | bytes 196616 | tf_op jit(solution)/shard_map/ppermute | solution.py:213
  127.9 6.4 %collective-permute-start.37 = (f32[128,128]{1,0:T(8,128)S(1)}, f32[128,128]{1,0:T(8,128)S(1)}, u32[]{:S(2)}, u32[]{:S(2)}) collective-permute-start(f32[128,128]{1,0:T(8,128)S(1)} %update3.1.refs_0_), channel_id=1, source_target_pairs={{0,8},{4,12},{8,0},{12,4},{1,9},{5,13},{9,1},{13,5},{2,10},{6,14},... | collective-permute-start | bytes 196616 | tf_op jit(solution)/shard_map/ppermute | solution.py:213
  (10 other events, 61.7 us)

commit v6 on v5

--- a/solution.py
+++ b/solution.py
@@ -122,9 +122,9 @@
     own_ref[prev] = inv_ref[0]
 
 
-def early_kernel(n, prev, step, tiles, picks, solved_at, low, *refs):
+def early_kernel(n, prev, step, at, picks, solved_at, low, *refs):
     refs = list(refs)
-    strips = [refs.pop(0) for _ in range(n)]
+    arrays = [refs.pop(0) for _ in range(1 + max(index for index, _ in at))]
     sources = [refs.pop(0) for _ in range(n)]
     solved = [[refs.pop(0) for _ in range(n)] for _ in solved_at]
     ranks_ref, flags_ref, left_ref = [refs.pop(0) for _ in range(3)] if low else (None,) * 3
@@ -133,17 +133,21 @@
     own_col = lax.axis_index("pcol")
     turn = own_col ^ lax.axis_index("prow")
 
+    def block(slot, tile):
+        index, begin = at[slot]
+        return arrays[index][begin + tile]
+
     def strip(tile):
-        return halves(jnp.concatenate([ref[tile] for ref in strips], axis=1), 0)
+        return halves(jnp.concatenate([block(slot, tile) for slot in range(n)], axis=1), 0)
 
     def take(total, tile, blocks):
-        for slot, block in enumerate(blocks):
-            scratch[pl.ds(pl.multiple_of((turn ^ slot) * nb, nb), nb), :] = block
+        for slot, value in enumerate(blocks):
+            scratch[pl.ds(pl.multiple_of((turn ^ slot) * nb, nb), nb), :] = value
         return total - dot_halves(strip(tile), halves(scratch[...], 1))
 
     total = base_ref[0]
     for col in range(prev):
-        total = take(total, tiles + col, [ref[col * nb : (col + 1) * nb] for ref in sources])
+        total = take(total, col, [ref[col * nb : (col + 1) * nb] for ref in sources])
     for tile, blocks in zip(solved_at, solved):
         total = take(total, tile, [ref[...] for ref in blocks])
     if low:
@@ -154,16 +158,22 @@
             flag = flags_ref[step, col].astype(jnp.float32)
             mask = jnp.where(row_at < ranks_ref[step, col], 1.0 - flag, 0.0)
             lefts.append(left_ref[0, col] * mask)
-            at = prev * nb + col * rank_pad
-            coeffs.append(sum(ref[at : at + rank_pad] for ref in sources))
+            place = prev * nb + col * rank_pad
+            coeffs.append(sum(ref[place : place + rank_pad] for ref in sources))
         left2 = halves(jnp.concatenate(lefts, axis=0), 1)
         coeff2 = halves(jnp.concatenate(coeffs, axis=0), 1)
         total = total - dot_halves(left2, coeff2, (((0,), (0,)), ((), ())))
     out_ref[...] = total
     for index, tile in enumerate(picks):
-        for slot, ref in enumerate(strips):
+        for slot in range(n):
             place = pl.multiple_of((own_col ^ slot) * nb, nb)
-            picked_ref[index, :, pl.ds(place, nb)] = halves(ref[tile], 0)
+            picked_ref[index, :, pl.ds(place, nb)] = halves(block(slot, tile), 0)
+
+
+def pair_kernel(near_ref, far_ref, out_ref):
+    count = near_ref.shape[0]
+    out_ref[:count] = near_ref[...]
+    out_ref[count:] = far_ref[...]
 
 
 def chain_kernel(n, minus, stacked, *refs):
@@ -232,38 +242,43 @@
     def shaped(*shape, dtype=f32):
         return jax.ShapeDtypeStruct(shape, dtype)
 
-    def call(kernel, name, shapes, args, specs, scratch=()):
+    def call(kernel, name, shapes, args, specs, scratch=(), after=()):
         many = isinstance(shapes, list)
         out_specs = [spec_of(x.shape) for x in shapes] if many else spec_of(shapes.shape)
+
+        def body(*refs):
+            kernel(*refs[: len(args)], *refs[len(args) + len(after) :])
+
         return pl.pallas_call(
-            kernel,
+            body,
             grid=(1,),
             out_shape=shapes,
-            in_specs=specs,
+            in_specs=specs + [any_spec] * len(after),
             out_specs=out_specs,
             scratch_shapes=list(scratch),
             compiler_params=params,
             name=name,
-        )(*args)
+        )(*args, *after)
 
     def packed(step, after):
         own = call(
             functools.partial(pack_kernel, (prev + step,)),
             f"pack{step}",
             shaped(prev + step, rank_pad, nb),
-            [pinned(right_t), *after],
-            [spec_of((1, cols, rank_pad, nb), (step, 0, 0, 0))] + [any_spec] * len(after),
+            [pinned(right_t)],
+            [spec_of((1, cols, rank_pad, nb), (step, 0, 0, 0))],
+            after=after,
         )
         return lax.ppermute(own, ("prow", "pcol"), flip)
 
-    def merged(step, right_own, after):
+    def merged(step, right_own, after=()):
         order = tuple((step, step, col, col) for col in range(prev + step)) + ((step, step, None, None),)
         return call(
             functools.partial(merge_kernel, order),
             f"merge{step}",
             shaped(len(order), nb, nb),
             [tile_ranks, dense_flags]
-            + [pinned(dense_tiles), pinned(left_t), right_own, pinned(inverse_diag), *after],
+            + [pinned(dense_tiles), pinned(left_t), right_own, pinned(inverse_diag)],
             [
                 smem,
                 smem,
@@ -271,17 +286,29 @@
                 spec_of((1, cols, rank_pad, nb), (step, 0, 0, 0)),
                 spec_of(right_own.shape),
                 spec_of((1, nb, nb), (step, 0, 0)),
-            ]
-            + [any_spec] * len(after),
+            ],
+            after=after,
         )
 
-    def over_cols(own, near):
+    def over_cols(own):
         held = {0: own}
         reach = n // 2
-        while near and reach >= 1:
+        while reach >= 1:
             held |= {d ^ reach: shift(v, "pcol", reach) for d, v in held.items()}
             reach //= 2
-        return [held[d] if d in held else shift(own, "pcol", d) for d in range(n)]
+        return [held[d] for d in range(n)], [(d, 0) for d in range(n)]
+
+    def over_cols_paired(own, far, after):
+        count = own.shape[0]
+        both = call(
+            pair_kernel,
+            f"pair{count}",
+            shaped(2 * count, nb, nb),
+            [own, far],
+            [spec_of(own.shape)] * 2,
+            after=after,
+        )
+        return [both, shift(both, "pcol", 1)], [(d & 1, (d >> 1) * count) for d in range(n)]
 
     sent, own = call(
         functools.partial(first_kernel, prev),
@@ -297,62 +324,73 @@
         ],
     )
     known = over_rows(sent)
-    strips = [over_cols(own, True)]
-    right_own = [None] + [packed(step, known[1:] if step > 1 else []) for step in range(1, steps)]
-
-    def early(step, spread):
+    strips = {0: over_cols(own)}
+
+    def early(step, spread, after=()):
         low = step == 0
-        tiles = 0
+        arrays, at = strips[step]
         picks = ([prev + step - 1] if step else []) + [prev + step]
         solved_at = [prev + index for index in range(len(spread))]
-        args = strips[step] + known + [ref for blocks in spread for ref in blocks]
-        specs = [spec_of(value.shape) for value in strips[step]]
+        args = arrays + known + [ref for blocks in spread for ref in blocks]
+        specs = [spec_of(value.shape) for value in arrays]
         specs += [spec_of((prev * (nb + rank_pad) if low else prev * nb, rhs))] * n
         specs += [spec_of((nb, rhs))] * (n * len(spread))
         if low:
             args += [tile_ranks, dense_flags, pinned(left_t)]
             specs += [smem, smem, spec_of((1, cols, rank_pad, nb), (0, 0, 0, 0))]
         return call(
-            functools.partial(early_kernel, n, prev, step, tiles, picks, solved_at, low),
+            functools.partial(early_kernel, n, prev, step, at, picks, solved_at, low),
             f"early{step}",
             [shaped(nb, rhs), shaped(len(picks), 2 * nb, n * nb, dtype=bf16)],
             args + [pinned(right_side)],
             specs + [spec_of((1, nb, rhs), (step, 0, 0))],
             [pltpu.VMEM((n * nb, rhs), f32)],
+            after=after,
         )
 
-    def chain(name, chain_strips, place, slots, rest, minus, stacked=False):
+    def chain(name, picked, place, slots, rest, minus, stacked=False, after=()):
         return call(
             functools.partial(chain_kernel, n, minus, stacked),
             name,
             shaped(len(rest) + 1, nb, rhs) if stacked else shaped(nb, rhs),
-            slots + [chain_strips] + rest,
+            slots + [picked] + rest,
             [spec_of((nb, rhs))] * n
             + [spec_of((1, 2 * nb, n * nb), (place, 0, 0))]
             + [spec_of((nb, rhs))] * len(rest),
             [pltpu.VMEM((n * nb, rhs), f32)],
+            after=after,
         )
 
-    pending, picked = early(0, [])
-    solved, spread = [], []
-    for step in range(steps):
-        whole = over_rows(pending)
-        if step == 0:
-            strips.append(over_cols(merged(1, right_own[1], []), True))
-            strips.append(over_cols(merged(2, right_own[2], whole[1:]), False))
-        last = step + 1 == steps
-        rest = solved if last else []
-        block = chain(f"solve{step}", picked, 1 if step else 0, whole, rest, False, last)
-        if last:
-            return block
-        solved.append(block)
-        blocks = over_rows(block)
-        if step == 0:
-            strips.append(over_cols(merged(3, right_own[3], blocks[1:]), False))
-        base, picked = early(step + 1, spread)
-        pending = chain(f"update{step + 1}", picked, 0, blocks, [base], True)
-        spread.append(blocks)
-    return None
+    strips[1] = over_cols(merged(1, packed(1, [])))
+    pending, picked0 = early(0, [])
+    right2 = packed(2, known[1:])
+    whole = over_rows(pending)
+    solved0 = chain("solve0", picked0, 0, whole, [], False, after=[right2])
+
+    own2 = merged(2, right2, [solved0])
+    far2 = shift(own2, "pcol", n // 2)
+    right3 = packed(3, [solved0])
+    blocks0 = over_rows(solved0)
+    base, picked1 = early(1, [])
+    pending = chain("update1", picked1, 0, blocks0, [base], True, after=[far2])
+    strips[2] = over_cols_paired(own2, far2, [pending])
+    whole = over_rows(pending)
+    solved1 = chain("solve1", picked1, 1, whole, [], False, after=[right3] + strips[2][0][1:])
+
+    own3 = merged(3, right3, [solved1])
+    far3 = shift(own3, "pcol", n // 2)
+    blocks1 = over_rows(solved1)
+    base, picked2 = early(2, [blocks0])
+    pending = chain("update2", picked2, 0, blocks1, [base], True)
+    whole = over_rows(pending)
+    solved2 = chain("solve2", picked2, 1, whole, [], False, after=[far3])
+
+    strips[3] = over_cols_paired(own3, far3, [solved2])
+    blocks2 = over_rows(solved2)
+    base, picked3 = early(3, [blocks0, blocks1])
+    pending = chain("update3", picked3, 0, blocks2, [base], True)
+    whole = over_rows(pending)
+    return chain("solve3", picked3, 1, whole, [solved0, solved1, solved2], False, True)
 
 
 def solution(mesh):
@@ -367,11 +405,12 @@
         P("groups", None),
     )
     n = mesh.shape["prow"]
-    square = n > 1 and n == mesh.shape["pcol"] and n & (n - 1) == 0 and n <= 8
+    square = n == 4 and n == mesh.shape["pcol"]
 
     def local(*args):
         nb, cols = args[3].shape[2:]
-        if square and nb % 128 == 0 and cols % 128 == 0 and args[0].shape[2] % 128 == 0:
+        steps = args[0].shape[0]
+        if square and steps == 4 and nb % 128 == 0 and cols % 128 == 0 and args[0].shape[2] % 128 == 0:
             return square_mesh(n, *args)
         return any_mesh(*args)
 

time: 136 us -> 135 us (level)
  waiting for transfers between devices: 33.4 us -> 27.4 us
  starting transfers between devices: 83 us -> 88.1 us
    ppermute x36 -> x34, waiting for transfers between devices: 33.4 us -> 27.4 us  [shift(): return lax.ppermute(value, axis, [(i, i ^ step) for i in range(n)])]
    ppermute x36 -> x34, starting transfers between devices: 81 us -> 86.1 us  [shift(): return lax.ppermute(value, axis, [(i, i ^ step) for i in range(n)])]
    pallas_call x18 -> x20, Pallas kernels: 18 us -> 18.1 us  [call(): pl.pallas_call(body, grid=(1,), out_shape=shapes, in_specs=specs + [any_s...]
  transfers between devices with their start and end apart: 39 -> 37, of which waited for: 18 -> 14; matrix products, arithmetic and copies ran while one was open for 0% -> 0% of each run, Pallas kernels for 11% -> 10%
where the time goes in v6:
time: 135 us; the launch traced here: 134 us
  starting transfers between devices  88.1 us (65%)
  waiting for transfers between devices  27.4 us (20%)
  Pallas kernels  18.1 us (13%)
    ppermute x34, starting transfers between devices, shift(): return lax.ppermute(value, axis, [(i, i ^ step) for i in range(n)])  86.1 us
    ppermute x34, waiting for transfers between devices, shift(): return lax.ppermute(value, axis, [(i, i ^ step) for i in range(n)])  27.4 us
    pallas_call x20, Pallas kernels, call(): pl.pallas_call(body, grid=(1,), out_shape=shapes, in_specs=specs + [any_s...  18.1 us
  transfers between devices with their start and end apart: 37, of which 14 were waited for; matrix products, arithmetic and copies ran while one was open for 0% of the time, Pallas kernels for 10%

profile of v6, /device:TPU:0, one launch (start us, length us, event | category | flops | bytes accessed | tf_op | source)
XLA Modules:
  0.0 134.4 jit_solution(13618444039318972273)
XLA Ops:
  2.1 3.0 %collective-permute-start.1 = (f32[5,128,128]{2,1,0:T(8,128)S(1)}, f32[5,128,128]{2,1,0:T(8,128)S(1)}, u32[]{:S(2)}, u32[]{:S(2)}) collective-permute-start(f32[5,128,128]{2,1,0:T(8,128)S(1)} %get-tuple-element.15.refs_0_), channel_id=1, source_target_pairs={{0,2},{1,3},{2,0},{3,1},{4,6},{5,7},{6,4},{7,5},{8,10},{9,11},{10,... | collective-permute-start | bytes 983048 | tf_op jit(solution)/shard_map/ppermute | solution.py:223
  5.1 3.6 %collective-permute-start.5 = (f32[768,128]{1,0:T(8,128)S(1)}, f32[768,128]{1,0:T(8,128)S(1)}, u32[]{:S(2)}, u32[]{:S(2)}) collective-permute-start(f32[768,128]{1,0:T(8,128)S(1)} %get-tuple-element.16.refs_4_.refs_2_), channel_id=1, source_target_pairs={{0,12},{4,8},{8,4},{12,0},{1,13},{5,9},{9,5},{13,1},{2,14},{6,10},... | collective-permute-start | bytes 1179656 | tf_op jit(solution)/shard_map/ppermute | solution.py:223
  11.1 24.5 %collective-permute-start = (f32[5,128,128]{2,1,0:T(8,128)S(1)}, f32[5,128,128]{2,1,0:T(8,128)S(1)}, u32[]{:S(2)}, u32[]{:S(2)}) collective-permute-start(f32[5,128,128]{2,1,0:T(8,128)S(1)} %get-tuple-element.15.refs_0_), channel_id=1, source_target_pairs={{0,1},{1,0},{2,3},{3,2},{4,5},{5,4},{6,7},{7,6},{8,9},{9,8},{10,11... | collective-permute-start | bytes 983048 | tf_op jit(solution)/shard_map/ppermute | solution.py:223
  37.2 11.9 %collective-permute-start.15 = (f32[6,128,128]{2,1,0:T(8,128)S(1)}, f32[6,128,128]{2,1,0:T(8,128)S(1)}, u32[]{:S(2)}, u32[]{:S(2)}) collective-permute-start(f32[6,128,128]{2,1,0:T(8,128)S(1)} %merge1.1.refs_0_), channel_id=1, source_target_pairs={{0,2},{1,3},{2,0},{3,1},{4,6},{5,7},{6,4},{7,5},{8,10},{9,11},{10,... | collective-permute-start | bytes 1179656 | tf_op jit(solution)/shard_map/ppermute | solution.py:223
  50.7 1.7 %early0.1 = (f32[128,128]{1,0:T(8,128)S(1)}, bf16[1,256,512]{2,1,0:T(8,128)(2,1)S(1)}) custom-call(f32[5,128,128]{2,1,0:T(8,128)S(1)} %get-tuple-element.15.refs_0_, f32[5,128,128]{2,1,0:T(8,128)S(1)} %collective-permute-done.refs_1_, f32[5,128,128]{2,1,0:T(8,128)S(1)} %collective-permute-done.1.refs_2_, f32[5,128,128]{2,1,0:T(8,128)S(1)} %collective-permute-done.2.refs_3_, ...), custom_call_target="tpu_custom_call" | custom-call | tf_op jit(solution)/shard_map/early0/pallas_call | solution.py:252
  52.4 3.5 %collective-permute-start.8 = (f32[128,128]{1,0:T(8,128)S(1)}, f32[128,128]{1,0:T(8,128)S(1)}, u32[]{:S(2)}, u32[]{:S(2)}) collective-permute-start(f32[128,128]{1,0:T(8,128)S(1)} %get-tuple-element.17.refs_0_), channel_id=1, source_target_pairs={{0,12},{4,8},{8,4},{12,0},{1,13},{5,9},{9,5},{13,1},{2,14},{6,10},... | collective-permute-start | bytes 196616 | tf_op jit(solution)/shard_map/ppermute | solution.py:223
  56.9 4.4 %collective-permute-start.14 = (f32[6,128,128]{2,1,0:T(8,128)S(1)}, f32[6,128,128]{2,1,0:T(8,128)S(1)}, u32[]{:S(2)}, u32[]{:S(2)}) collective-permute-start(f32[6,128,128]{2,1,0:T(8,128)S(1)} %merge1.1.refs_0_), channel_id=1, source_target_pairs={{0,1},{1,0},{2,3},{3,2},{4,5},{5,4},{6,7},{7,6},{8,9},{9,8},{10,11... | collective-permute-start | bytes 1179656 | tf_op jit(solution)/shard_map/ppermute | solution.py:223
  64.2 2.7 %collective-permute-start.17 = (f32[7,128,128]{2,1,0:T(8,128)S(1)}, f32[7,128,128]{2,1,0:T(8,128)S(1)}, u32[]{:S(2)}, u32[]{:S(2)}) collective-permute-start(f32[7,128,128]{2,1,0:T(8,128)S(1)} %merge2.1.refs_0_), channel_id=1, source_target_pairs={{0,2},{1,3},{2,0},{3,1},{4,6},{5,7},{6,4},{7,5},{8,10},{9,11},{10,... | collective-permute-start | bytes 1376264 | tf_op jit(solution)/shard_map/ppermute | solution.py:223
  66.9 1.9 %collective-permute-start.12 = (f32[128,128]{1,0:T(8,128)S(1)}, f32[128,128]{1,0:T(8,128)S(1)}, u32[]{:S(2)}, u32[]{:S(2)}) collective-permute-start(f32[128,128]{1,0:T(8,128)S(1)} %solve0.1.refs_6_.refs_0_.refs_1_.refs_5_), channel_id=1, source_target_pairs={{0,12},{4,8},{8,4},{12,0},{1,13},{5,9},{9,5},{13,1},{2,14},{6,10},... | collective-permute-start | bytes 196616 | tf_op jit(solution)/shard_map/ppermute | solution.py:223
  68.8 2.5 %collective-permute-start.10 = (f32[128,128]{1,0:T(8,128)S(1)}, f32[128,128]{1,0:T(8,128)S(1)}, u32[]{:S(2)}, u32[]{:S(2)}) collective-permute-start(f32[128,128]{1,0:T(8,128)S(1)} %solve0.1.refs_6_.refs_0_.refs_1_.refs_5_), channel_id=1, source_target_pairs={{0,4},{4,0},{8,12},{12,8},{1,5},{5,1},{9,13},{13,9},{2,6},{6,2},{1... | collective-permute-start | bytes 196616 | tf_op jit(solution)/shard_map/ppermute | solution.py:223
  73.7 2.3 %collective-permute-done.11.refs_2_.refs_8_ = f32[128,128]{1,0:T(8,128)S(1)} collective-permute-done((f32[128,128]{1,0:T(8,128)S(1)}, f32[128,128]{1,0:T(8,128)S(1)}, u32[]{:S(2)}, u32[]{:S(2)}) %collective-permute-start.11) | collective-permute-done | bytes 65568 | tf_op jit(solution)/shard_map/ppermute | solution.py:223
  76.0 2.2 %collective-permute-done.17.refs_6_.refs_1_ = f32[7,128,128]{2,1,0:T(8,128)S(1)} collective-permute-done((f32[7,128,128]{2,1,0:T(8,128)S(1)}, f32[7,128,128]{2,1,0:T(8,128)S(1)}, u32[]{:S(2)}, u32[]{:S(2)}) %collective-permute-start.17) | collective-permute-done | bytes 458784 | tf_op jit(solution)/shard_map/ppermute | solution.py:223
  80.3 4.4 %collective-permute-start.20 = (f32[128,128]{1,0:T(8,128)S(1)}, f32[128,128]{1,0:T(8,128)S(1)}, u32[]{:S(2)}, u32[]{:S(2)}) collective-permute-start(f32[128,128]{1,0:T(8,128)S(1)} %update1.1.refs_2_.refs_0_), channel_id=1, source_target_pairs={{0,12},{4,8},{8,4},{12,0},{1,13},{5,9},{9,5},{13,1},{2,14},{6,10},... | collective-permute-start | bytes 196616 | tf_op jit(solution)/shard_map/ppermute | solution.py:223
  85.4 2.4 %collective-permute-done.20.refs_3_ = f32[128,128]{1,0:T(8,128)S(1)} collective-permute-done((f32[128,128]{1,0:T(8,128)S(1)}, f32[128,128]{1,0:T(8,128)S(1)}, u32[]{:S(2)}, u32[]{:S(2)}) %collective-permute-start.20) | collective-permute-done | bytes 65568 | tf_op jit(solution)/shard_map/ppermute | solution.py:223
  87.8 4.8 %collective-permute-done.19.refs_2_ = f32[128,128]{1,0:T(8,128)S(1)} collective-permute-done((f32[128,128]{1,0:T(8,128)S(1)}, f32[128,128]{1,0:T(8,128)S(1)}, u32[]{:S(2)}, u32[]{:S(2)}) %collective-permute-start.19) | collective-permute-done | bytes 65568 | tf_op jit(solution)/shard_map/ppermute | solution.py:223
  92.8 1.6 %merge3.1.refs_0_ = f32[8,128,128]{2,1,0:T(8,128)S(1)} custom-call(s32[4,7]{1,0:T(4,128)S(1)} %copy-done.2, s32[4,7]{1,0:T(4,128)S(1)} %copy-done.1, f32[4,7,128,128]{3,2,1,0:T(8,128)} %refs_2_.7, f32[4,7,64,128]{3,2,1,0:T(8,128)} %bitcast.9, f32[7,64,128]{2,1,0:T(8,128)S(1)} %collective-permute-done.21.refs_5_.refs_4_, f32[4,128,128]{2,1,0:T(8,128)} %refs_5_.5, ...), custom_call_target="tpu_custom_call" | custom-call | tf_op jit(solution)/shard_map/merge3/pallas_call | solution.py:252
  94.4 3.2 %collective-permute-start.29 = (f32[8,128,128]{2,1,0:T(8,128)S(1)}, f32[8,128,128]{2,1,0:T(8,128)S(1)}, u32[]{:S(2)}, u32[]{:S(2)}) collective-permute-start(f32[8,128,128]{2,1,0:T(8,128)S(1)} %merge3.1.refs_0_), channel_id=1, source_target_pairs={{0,2},{1,3},{2,0},{3,1},{4,6},{5,7},{6,4},{7,5},{8,10},{9,11},{10,... | collective-permute-start | bytes 1572872 | tf_op jit(solution)/shard_map/ppermute | solution.py:223
  99.1 3.0 %collective-permute-start.23 = (f32[128,128]{1,0:T(8,128)S(1)}, f32[128,128]{1,0:T(8,128)S(1)}, u32[]{:S(2)}, u32[]{:S(2)}) collective-permute-start(f32[128,128]{1,0:T(8,128)S(1)} %solve1.1.refs_0_.refs_6_.refs_10_), channel_id=1, source_target_pairs={{0,4},{4,0},{8,12},{12,8},{1,5},{5,1},{9,13},{13,9},{2,6},{6,2},{1... | collective-permute-start | bytes 196616 | tf_op jit(solution)/shard_map/ppermute | solution.py:223
  102.0 1.6 %early2.1 = (f32[128,128]{1,0:T(8,128)S(1)}, bf16[2,256,512]{2,1,0:T(8,128)(2,1)S(1)}) custom-call(f32[14,128,128]{2,1,0:T(8,128)S(1)} %pair7.1.refs_0_, f32[14,128,128]{2,1,0:T(8,128)S(1)} %collective-permute-done.22.refs_6_.refs_1_, f32[768,128]{1,0:T(8,128)S(1)} %get-tuple-element.16.refs_4_.refs_2_, ...), custom_call_target="tpu_custom_call" | custom-call | tf_op jit(solution)/shard_map/early2/pallas_call | solution.py:252
  104.4 1.6 %collective-permute-done.24.refs_2_.refs_12_ = f32[128,128]{1,0:T(8,128)S(1)} collective-permute-done((f32[128,128]{1,0:T(8,128)S(1)}, f32[128,128]{1,0:T(8,128)S(1)}, u32[]{:S(2)}, u32[]{:S(2)}) %collective-permute-start.24) | collective-permute-done | bytes 65568 | tf_op jit(solution)/shard_map/ppermute | solution.py:223
  106.3 1.7 %collective-permute-start.28 = (f32[128,128]{1,0:T(8,128)S(1)}, f32[128,128]{1,0:T(8,128)S(1)}, u32[]{:S(2)}, u32[]{:S(2)}) collective-permute-start(f32[128,128]{1,0:T(8,128)S(1)} %update2.1.refs_0_), channel_id=1, source_target_pairs={{0,12},{4,8},{8,4},{12,0},{1,13},{5,9},{9,5},{13,1},{2,14},{6,10},... | collective-permute-start | bytes 196616 | tf_op jit(solution)/shard_map/ppermute | solution.py:223
  108.1 2.6 %collective-permute-start.26 = (f32[128,128]{1,0:T(8,128)S(1)}, f32[128,128]{1,0:T(8,128)S(1)}, u32[]{:S(2)}, u32[]{:S(2)}) collective-permute-start(f32[128,128]{1,0:T(8,128)S(1)} %update2.1.refs_0_), channel_id=1, source_target_pairs={{0,4},{4,0},{8,12},{12,8},{1,5},{5,1},{9,13},{13,9},{2,6},{6,2},{1... | collective-permute-start | bytes 196616 | tf_op jit(solution)/shard_map/ppermute | solution.py:223
  110.7 2.4 %collective-permute-done.28.refs_3_ = f32[128,128]{1,0:T(8,128)S(1)} collective-permute-done((f32[128,128]{1,0:T(8,128)S(1)}, f32[128,128]{1,0:T(8,128)S(1)}, u32[]{:S(2)}, u32[]{:S(2)}) %collective-permute-start.28) | collective-permute-done | bytes 65568 | tf_op jit(solution)/shard_map/ppermute | solution.py:223
  113.1 1.8 %collective-permute-done.27.refs_2_ = f32[128,128]{1,0:T(8,128)S(1)} collective-permute-done((f32[128,128]{1,0:T(8,128)S(1)}, f32[128,128]{1,0:T(8,128)S(1)}, u32[]{:S(2)}, u32[]{:S(2)}) %collective-permute-start.27) | collective-permute-done | bytes 65568 | tf_op jit(solution)/shard_map/ppermute | solution.py:223
  115.4 1.6 %collective-permute-start.32 = (f32[128,128]{1,0:T(8,128)S(1)}, f32[128,128]{1,0:T(8,128)S(1)}, u32[]{:S(2)}, u32[]{:S(2)}) collective-permute-start(f32[128,128]{1,0:T(8,128)S(1)} %solve2.1.refs_2_.refs_0_.refs_7_), channel_id=1, source_target_pairs={{0,12},{4,8},{8,4},{12,0},{1,13},{5,9},{9,5},{13,1},{2,14},{6,10},... | collective-permute-start | bytes 196616 | tf_op jit(solution)/shard_map/ppermute | solution.py:223
  117.0 2.8 %collective-permute-start.30 = (f32[128,128]{1,0:T(8,128)S(1)}, f32[128,128]{1,0:T(8,128)S(1)}, u32[]{:S(2)}, u32[]{:S(2)}) collective-permute-start(f32[128,128]{1,0:T(8,128)S(1)} %solve2.1.refs_2_.refs_0_.refs_7_), channel_id=1, source_target_pairs={{0,4},{4,0},{8,12},{12,8},{1,5},{5,1},{9,13},{13,9},{2,6},{6,2},{1... | collective-permute-start | bytes 196616 | tf_op jit(solution)/shard_map/ppermute | solution.py:223
  119.8 1.7 %early3.1 = (f32[128,128]{1,0:T(8,128)S(1)}, bf16[2,256,512]{2,1,0:T(8,128)(2,1)S(1)}) custom-call(f32[16,128,128]{2,1,0:T(8,128)S(1)} %pair8.1.refs_0_, f32[16,128,128]{2,1,0:T(8,128)S(1)} %collective-permute-done.33.refs_1_, f32[768,128]{1,0:T(8,128)S(1)} %get-tuple-element.16.refs_4_.refs_2_, ...), custom_call_target="tpu_custom_call" | custom-call | tf_op jit(solution)/shard_map/early3/pallas_call | solution.py:252
  122.2 2.3 %collective-permute-done.31.refs_2_ = f32[128,128]{1,0:T(8,128)S(1)} collective-permute-done((f32[128,128]{1,0:T(8,128)S(1)}, f32[128,128]{1,0:T(8,128)S(1)}, u32[]{:S(2)}, u32[]{:S(2)}) %collective-permute-start.31) | collective-permute-done | bytes 65568 | tf_op jit(solution)/shard_map/ppermute | solution.py:223
  124.8 1.6 %collective-permute-start.36 = (f32[128,128]{1,0:T(8,128)S(1)}, f32[128,128]{1,0:T(8,128)S(1)}, u32[]{:S(2)}, u32[]{:S(2)}) collective-permute-start(f32[128,128]{1,0:T(8,128)S(1)} %update3.1.refs_0_), channel_id=1, source_target_pairs={{0,12},{4,8},{8,4},{12,0},{1,13},{5,9},{9,5},{13,1},{2,14},{6,10},... | collective-permute-start | bytes 196616 | tf_op jit(solution)/shard_map/ppermute | solution.py:223
  126.4 2.8 %collective-permute-start.34 = (f32[128,128]{1,0:T(8,128)S(1)}, f32[128,128]{1,0:T(8,128)S(1)}, u32[]{:S(2)}, u32[]{:S(2)}) collective-permute-start(f32[128,128]{1,0:T(8,128)S(1)} %update3.1.refs_0_), channel_id=1, source_target_pairs={{0,4},{4,0},{8,12},{12,8},{1,5},{5,1},{9,13},{13,9},{2,6},{6,2},{1... | collective-permute-start | bytes 196616 | tf_op jit(solution)/shard_map/ppermute | solution.py:223
  129.2 2.4 %collective-permute-done.36.refs_3_ = f32[128,128]{1,0:T(8,128)S(1)} collective-permute-done((f32[128,128]{1,0:T(8,128)S(1)}, f32[128,128]{1,0:T(8,128)S(1)}, u32[]{:S(2)}, u32[]{:S(2)}) %collective-permute-start.36) | collective-permute-done | bytes 65568 | tf_op jit(solution)/shard_map/ppermute | solution.py:223
  131.6 1.9 %collective-permute-done.35.refs_2_ = f32[128,128]{1,0:T(8,128)S(1)} collective-permute-done((f32[128,128]{1,0:T(8,128)S(1)}, f32[128,128]{1,0:T(8,128)S(1)}, u32[]{:S(2)}, u32[]{:S(2)}) %collective-permute-start.35) | collective-permute-done | bytes 65568 | tf_op jit(solution)/shard_map/ppermute | solution.py:223
  (68 shorter events, 21.8 us)
Async XLA Ops:
  2.1 33.5 %collective-permute-start.1 = (f32[5,128,128]{2,1,0:T(8,128)S(1)}, f32[5,128,128]{2,1,0:T(8,128)S(1)}, u32[]{:S(2)}, u32[]{:S(2)}) collective-permute-start(f32[5,128,128]{2,1,0:T(8,128)S(1)} %get-tuple-element.15.refs_0_), channel_id=1, source_target_pairs={{0,2},{1,3},{2,0},{3,1},{4,6},{5,7},{6,4},{7,5},{8,10},{9,11},{10,... | collective-permute-start | bytes 983048 | tf_op jit(solution)/shard_map/ppermute | solution.py:223
  5.1 32.1 %collective-permute-start.5 = (f32[768,128]{1,0:T(8,128)S(1)}, f32[768,128]{1,0:T(8,128)S(1)}, u32[]{:S(2)}, u32[]{:S(2)}) collective-permute-start(f32[768,128]{1,0:T(8,128)S(1)} %get-tuple-element.16.refs_4_.refs_2_), channel_id=1, source_target_pairs={{0,12},{4,8},{8,4},{12,0},{1,13},{5,9},{9,5},{13,1},{2,14},{6,10},... | collective-permute-start | bytes 1179656 | tf_op jit(solution)/shard_map/ppermute | solution.py:223
  8.7 40.4 %collective-permute-start.4 = (f32[768,128]{1,0:T(8,128)S(1)}, f32[768,128]{1,0:T(8,128)S(1)}, u32[]{:S(2)}, u32[]{:S(2)}) collective-permute-start(f32[768,128]{1,0:T(8,128)S(1)} %get-tuple-element.16.refs_4_.refs_2_), channel_id=1, source_target_pairs={{0,8},{4,12},{8,0},{12,4},{1,9},{5,13},{9,1},{13,5},{2,10},{6,14},... | collective-permute-start | bytes 1179656 | tf_op jit(solution)/shard_map/ppermute | solution.py:223
  8.7 40.4 %collective-permute-start.3 = (f32[768,128]{1,0:T(8,128)S(1)}, f32[768,128]{1,0:T(8,128)S(1)}, u32[]{:S(2)}, u32[]{:S(2)}) collective-permute-start(f32[768,128]{1,0:T(8,128)S(1)} %get-tuple-element.16.refs_4_.refs_2_), channel_id=1, source_target_pairs={{0,4},{4,0},{8,12},{12,8},{1,5},{5,1},{9,13},{13,9},{2,6},{6,2},{1... | collective-permute-start | bytes 1179656 | tf_op jit(solution)/shard_map/ppermute | solution.py:223
  11.1 39.6 %collective-permute-start = (f32[5,128,128]{2,1,0:T(8,128)S(1)}, f32[5,128,128]{2,1,0:T(8,128)S(1)}, u32[]{:S(2)}, u32[]{:S(2)}) collective-permute-start(f32[5,128,128]{2,1,0:T(8,128)S(1)} %get-tuple-element.15.refs_0_), channel_id=1, source_target_pairs={{0,1},{1,0},{2,3},{3,2},{4,5},{5,4},{6,7},{7,6},{8,9},{9,8},{10,11... | collective-permute-start | bytes 983048 | tf_op jit(solution)/shard_map/ppermute | solution.py:223
  35.6 15.1 %collective-permute-start.2 = (f32[5,128,128]{2,1,0:T(8,128)S(1)}, f32[5,128,128]{2,1,0:T(8,128)S(1)}, u32[]{:S(2)}, u32[]{:S(2)}) collective-permute-start(f32[5,128,128]{2,1,0:T(8,128)S(1)} %collective-permute-done.1.refs_2_), channel_id=1, source_target_pairs={{0,1},{1,0},{2,3},{3,2},{4,5},{5,4},{6,7},{7,6},{8,9},{9,8},{10,11... | collective-permute-start | bytes 983048 | tf_op jit(solution)/shard_map/ppermute | solution.py:223
  37.2 29.7 %collective-permute-start.15 = (f32[6,128,128]{2,1,0:T(8,128)S(1)}, f32[6,128,128]{2,1,0:T(8,128)S(1)}, u32[]{:S(2)}, u32[]{:S(2)}) collective-permute-start(f32[6,128,128]{2,1,0:T(8,128)S(1)} %merge1.1.refs_0_), channel_id=1, source_target_pairs={{0,2},{1,3},{2,0},{3,1},{4,6},{5,7},{6,4},{7,5},{8,10},{9,11},{10,... | collective-permute-start | bytes 1179656 | tf_op jit(solution)/shard_map/ppermute | solution.py:223
  50.0 6.8 %collective-permute-start.9 = (f32[6,64,128]{2,1,0:T(8,128)S(1)}, f32[6,64,128]{2,1,0:T(8,128)S(1)}, u32[]{:S(2)}, u32[]{:S(2)}) collective-permute-start(f32[6,64,128]{2,1,0:T(8,128)S(1)} %pack2.1), channel_id=1, source_target_pairs={{0,0},{2,4},{1,8},{3,12},{6,1},{4,5},{7,9},{5,13},{9,2},{11,6},{8,... | collective-permute-start | bytes 589832 | tf_op jit(solution)/shard_map/ppermute | solution.py:272
  52.4 8.9 %collective-permute-start.8 = (f32[128,128]{1,0:T(8,128)S(1)}, f32[128,128]{1,0:T(8,128)S(1)}, u32[]{:S(2)}, u32[]{:S(2)}) collective-permute-start(f32[128,128]{1,0:T(8,128)S(1)} %get-tuple-element.17.refs_0_), channel_id=1, source_target_pairs={{0,12},{4,8},{8,4},{12,0},{1,13},{5,9},{9,5},{13,1},{2,14},{6,10},... | collective-permute-start | bytes 196616 | tf_op jit(solution)/shard_map/ppermute | solution.py:223
  55.9 6.4 %collective-permute-start.7 = (f32[128,128]{1,0:T(8,128)S(1)}, f32[128,128]{1,0:T(8,128)S(1)}, u32[]{:S(2)}, u32[]{:S(2)}) collective-permute-start(f32[128,128]{1,0:T(8,128)S(1)} %get-tuple-element.17.refs_0_), channel_id=1, source_target_pairs={{0,8},{4,12},{8,0},{12,4},{1,9},{5,13},{9,1},{13,5},{2,10},{6,14},... | collective-permute-start | bytes 196616 | tf_op jit(solution)/shard_map/ppermute | solution.py:223
  56.9 11.9 %collective-permute-start.14 = (f32[6,128,128]{2,1,0:T(8,128)S(1)}, f32[6,128,128]{2,1,0:T(8,128)S(1)}, u32[]{:S(2)}, u32[]{:S(2)}) collective-permute-start(f32[6,128,128]{2,1,0:T(8,128)S(1)} %merge1.1.refs_0_), channel_id=1, source_target_pairs={{0,1},{1,0},{2,3},{3,2},{4,5},{5,4},{6,7},{7,6},{8,9},{9,8},{10,11... | collective-permute-start | bytes 1179656 | tf_op jit(solution)/shard_map/ppermute | solution.py:223
  64.2 14.0 %collective-permute-start.17 = (f32[7,128,128]{2,1,0:T(8,128)S(1)}, f32[7,128,128]{2,1,0:T(8,128)S(1)}, u32[]{:S(2)}, u32[]{:S(2)}) collective-permute-start(f32[7,128,128]{2,1,0:T(8,128)S(1)} %merge2.1.refs_0_), channel_id=1, source_target_pairs={{0,2},{1,3},{2,0},{3,1},{4,6},{5,7},{6,4},{7,5},{8,10},{9,11},{10,... | collective-permute-start | bytes 1376264 | tf_op jit(solution)/shard_map/ppermute | solution.py:223
  66.9 6.8 %collective-permute-start.12 = (f32[128,128]{1,0:T(8,128)S(1)}, f32[128,128]{1,0:T(8,128)S(1)}, u32[]{:S(2)}, u32[]{:S(2)}) collective-permute-start(f32[128,128]{1,0:T(8,128)S(1)} %solve0.1.refs_6_.refs_0_.refs_1_.refs_5_), channel_id=1, source_target_pairs={{0,12},{4,8},{8,4},{12,0},{1,13},{5,9},{9,5},{13,1},{2,14},{6,10},... | collective-permute-start | bytes 196616 | tf_op jit(solution)/shard_map/ppermute | solution.py:223
  68.8 7.2 %collective-permute-start.11 = (f32[128,128]{1,0:T(8,128)S(1)}, f32[128,128]{1,0:T(8,128)S(1)}, u32[]{:S(2)}, u32[]{:S(2)}) collective-permute-start(f32[128,128]{1,0:T(8,128)S(1)} %solve0.1.refs_6_.refs_0_.refs_1_.refs_5_), channel_id=1, source_target_pairs={{0,8},{4,12},{8,0},{12,4},{1,9},{5,13},{9,1},{13,5},{2,10},{6,14},... | collective-permute-start | bytes 196616 | tf_op jit(solution)/shard_map/ppermute | solution.py:223
  68.8 7.2 %collective-permute-start.10 = (f32[128,128]{1,0:T(8,128)S(1)}, f32[128,128]{1,0:T(8,128)S(1)}, u32[]{:S(2)}, u32[]{:S(2)}) collective-permute-start(f32[128,128]{1,0:T(8,128)S(1)} %solve0.1.refs_6_.refs_0_.refs_1_.refs_5_), channel_id=1, source_target_pairs={{0,4},{4,0},{8,12},{12,8},{1,5},{5,1},{9,13},{13,9},{2,6},{6,2},{1... | collective-permute-start | bytes 196616 | tf_op jit(solution)/shard_map/ppermute | solution.py:223
  78.5 14.0 %collective-permute-start.22 = (f32[14,128,128]{2,1,0:T(8,128)S(1)}, f32[14,128,128]{2,1,0:T(8,128)S(1)}, u32[]{:S(2)}, u32[]{:S(2)}) collective-permute-start(f32[14,128,128]{2,1,0:T(8,128)S(1)} %pair7.1.refs_0_), channel_id=1, source_target_pairs={{0,1},{1,0},{2,3},{3,2},{4,5},{5,4},{6,7},{7,6},{8,9},{9,8},{10,11... | collective-permute-start | bytes 2752520 | tf_op jit(solution)/shard_map/ppermute | solution.py:223
  80.3 7.4 %collective-permute-start.20 = (f32[128,128]{1,0:T(8,128)S(1)}, f32[128,128]{1,0:T(8,128)S(1)}, u32[]{:S(2)}, u32[]{:S(2)}) collective-permute-start(f32[128,128]{1,0:T(8,128)S(1)} %update1.1.refs_2_.refs_0_), channel_id=1, source_target_pairs={{0,12},{4,8},{8,4},{12,0},{1,13},{5,9},{9,5},{13,1},{2,14},{6,10},... | collective-permute-start | bytes 196616 | tf_op jit(solution)/shard_map/ppermute | solution.py:223
  84.7 7.8 %collective-permute-start.19 = (f32[128,128]{1,0:T(8,128)S(1)}, f32[128,128]{1,0:T(8,128)S(1)}, u32[]{:S(2)}, u32[]{:S(2)}) collective-permute-start(f32[128,128]{1,0:T(8,128)S(1)} %update1.1.refs_2_.refs_0_), channel_id=1, source_target_pairs={{0,8},{4,12},{8,0},{12,4},{1,9},{5,13},{9,1},{13,5},{2,10},{6,14},... | collective-permute-start | bytes 196616 | tf_op jit(solution)/shard_map/ppermute | solution.py:223
  84.7 7.8 %collective-permute-start.18 = (f32[128,128]{1,0:T(8,128)S(1)}, f32[128,128]{1,0:T(8,128)S(1)}, u32[]{:S(2)}, u32[]{:S(2)}) collective-permute-start(f32[128,128]{1,0:T(8,128)S(1)} %update1.1.refs_2_.refs_0_), channel_id=1, source_target_pairs={{0,4},{4,0},{8,12},{12,8},{1,5},{5,1},{9,13},{13,9},{2,6},{6,2},{1... | collective-permute-start | bytes 196616 | tf_op jit(solution)/shard_map/ppermute | solution.py:223
  94.4 20.5 %collective-permute-start.29 = (f32[8,128,128]{2,1,0:T(8,128)S(1)}, f32[8,128,128]{2,1,0:T(8,128)S(1)}, u32[]{:S(2)}, u32[]{:S(2)}) collective-permute-start(f32[8,128,128]{2,1,0:T(8,128)S(1)} %merge3.1.refs_0_), channel_id=1, source_target_pairs={{0,2},{1,3},{2,0},{3,1},{4,6},{5,7},{6,4},{7,5},{8,10},{9,11},{10,... | collective-permute-start | bytes 1572872 | tf_op jit(solution)/shard_map/ppermute | solution.py:223
  97.7 6.7 %collective-permute-start.25 = (f32[128,128]{1,0:T(8,128)S(1)}, f32[128,128]{1,0:T(8,128)S(1)}, u32[]{:S(2)}, u32[]{:S(2)}) collective-permute-start(f32[128,128]{1,0:T(8,128)S(1)} %solve1.1.refs_0_.refs_6_.refs_10_), channel_id=1, source_target_pairs={{0,12},{4,8},{8,4},{12,0},{1,13},{5,9},{9,5},{13,1},{2,14},{6,10},... | collective-permute-start | bytes 196616 | tf_op jit(solution)/shard_map/ppermute | solution.py:223
  99.1 6.9 %collective-permute-start.24 = (f32[128,128]{1,0:T(8,128)S(1)}, f32[128,128]{1,0:T(8,128)S(1)}, u32[]{:S(2)}, u32[]{:S(2)}) collective-permute-start(f32[128,128]{1,0:T(8,128)S(1)} %solve1.1.refs_0_.refs_6_.refs_10_), channel_id=1, source_target_pairs={{0,8},{4,12},{8,0},{12,4},{1,9},{5,13},{9,1},{13,5},{2,10},{6,14},... | collective-permute-start | bytes 196616 | tf_op jit(solution)/shard_map/ppermute | solution.py:223
  99.1 6.9 %collective-permute-start.23 = (f32[128,128]{1,0:T(8,128)S(1)}, f32[128,128]{1,0:T(8,128)S(1)}, u32[]{:S(2)}, u32[]{:S(2)}) collective-permute-start(f32[128,128]{1,0:T(8,128)S(1)} %solve1.1.refs_0_.refs_6_.refs_10_), channel_id=1, source_target_pairs={{0,4},{4,0},{8,12},{12,8},{1,5},{5,1},{9,13},{13,9},{2,6},{6,2},{1... | collective-permute-start | bytes 196616 | tf_op jit(solution)/shard_map/ppermute | solution.py:223
  106.3 6.9 %collective-permute-start.28 = (f32[128,128]{1,0:T(8,128)S(1)}, f32[128,128]{1,0:T(8,128)S(1)}, u32[]{:S(2)}, u32[]{:S(2)}) collective-permute-start(f32[128,128]{1,0:T(8,128)S(1)} %update2.1.refs_0_), channel_id=1, source_target_pairs={{0,12},{4,8},{8,4},{12,0},{1,13},{5,9},{9,5},{13,1},{2,14},{6,10},... | collective-permute-start | bytes 196616 | tf_op jit(solution)/shard_map/ppermute | solution.py:223
  108.0 7.0 %collective-permute-start.27 = (f32[128,128]{1,0:T(8,128)S(1)}, f32[128,128]{1,0:T(8,128)S(1)}, u32[]{:S(2)}, u32[]{:S(2)}) collective-permute-start(f32[128,128]{1,0:T(8,128)S(1)} %update2.1.refs_0_), channel_id=1, source_target_pairs={{0,8},{4,12},{8,0},{12,4},{1,9},{5,13},{9,1},{13,5},{2,10},{6,14},... | collective-permute-start | bytes 196616 | tf_op jit(solution)/shard_map/ppermute | solution.py:223
  108.1 6.8 %collective-permute-start.26 = (f32[128,128]{1,0:T(8,128)S(1)}, f32[128,128]{1,0:T(8,128)S(1)}, u32[]{:S(2)}, u32[]{:S(2)}) collective-permute-start(f32[128,128]{1,0:T(8,128)S(1)} %update2.1.refs_0_), channel_id=1, source_target_pairs={{0,4},{4,0},{8,12},{12,8},{1,5},{5,1},{9,13},{13,9},{2,6},{6,2},{1... | collective-permute-start | bytes 196616 | tf_op jit(solution)/shard_map/ppermute | solution.py:223
  115.4 6.9 %collective-permute-start.32 = (f32[128,128]{1,0:T(8,128)S(1)}, f32[128,128]{1,0:T(8,128)S(1)}, u32[]{:S(2)}, u32[]{:S(2)}) collective-permute-start(f32[128,128]{1,0:T(8,128)S(1)} %solve2.1.refs_2_.refs_0_.refs_7_), channel_id=1, source_target_pairs={{0,12},{4,8},{8,4},{12,0},{1,13},{5,9},{9,5},{13,1},{2,14},{6,10},... | collective-permute-start | bytes 196616 | tf_op jit(solution)/shard_map/ppermute | solution.py:223
  117.0 7.5 %collective-permute-start.31 = (f32[128,128]{1,0:T(8,128)S(1)}, f32[128,128]{1,0:T(8,128)S(1)}, u32[]{:S(2)}, u32[]{:S(2)}) collective-permute-start(f32[128,128]{1,0:T(8,128)S(1)} %solve2.1.refs_2_.refs_0_.refs_7_), channel_id=1, source_target_pairs={{0,8},{4,12},{8,0},{12,4},{1,9},{5,13},{9,1},{13,5},{2,10},{6,14},... | collective-permute-start | bytes 196616 | tf_op jit(solution)/shard_map/ppermute | solution.py:223
  117.0 7.5 %collective-permute-start.30 = (f32[128,128]{1,0:T(8,128)S(1)}, f32[128,128]{1,0:T(8,128)S(1)}, u32[]{:S(2)}, u32[]{:S(2)}) collective-permute-start(f32[128,128]{1,0:T(8,128)S(1)} %solve2.1.refs_2_.refs_0_.refs_7_), channel_id=1, source_target_pairs={{0,4},{4,0},{8,12},{12,8},{1,5},{5,1},{9,13},{13,9},{2,6},{6,2},{1... | collective-permute-start | bytes 196616 | tf_op jit(solution)/shard_map/ppermute | solution.py:223
  124.8 6.8 %collective-permute-start.36 = (f32[128,128]{1,0:T(8,128)S(1)}, f32[128,128]{1,0:T(8,128)S(1)}, u32[]{:S(2)}, u32[]{:S(2)}) collective-permute-start(f32[128,128]{1,0:T(8,128)S(1)} %update3.1.refs_0_), channel_id=1, source_target_pairs={{0,12},{4,8},{8,4},{12,0},{1,13},{5,9},{9,5},{13,1},{2,14},{6,10},... | collective-permute-start | bytes 196616 | tf_op jit(solution)/shard_map/ppermute | solution.py:223
  126.4 7.1 %collective-permute-start.35 = (f32[128,128]{1,0:T(8,128)S(1)}, f32[128,128]{1,0:T(8,128)S(1)}, u32[]{:S(2)}, u32[]{:S(2)}) collective-permute-start(f32[128,128]{1,0:T(8,128)S(1)} %update3.1.refs_0_), channel_id=1, source_target_pairs={{0,8},{4,12},{8,0},{12,4},{1,9},{5,13},{9,1},{13,5},{2,10},{6,14},... | collective-permute-start | bytes 196616 | tf_op jit(solution)/shard_map/ppermute | solution.py:223
  126.4 7.1 %collective-permute-start.34 = (f32[128,128]{1,0:T(8,128)S(1)}, f32[128,128]{1,0:T(8,128)S(1)}, u32[]{:S(2)}, u32[]{:S(2)}) collective-permute-start(f32[128,128]{1,0:T(8,128)S(1)} %update3.1.refs_0_), channel_id=1, source_target_pairs={{0,4},{4,0},{8,12},{12,8},{1,5},{5,1},{9,13},{13,9},{2,6},{6,2},{1... | collective-permute-start | bytes 196616 | tf_op jit(solution)/shard_map/ppermute | solution.py:223
  (8 other events, 92.3 us)

commit v7 on v0

v7 whole, which is shorter than its diff:
```python
import functools

import jax
import jax.numpy as jnp
from jax import lax
from jax.experimental import pallas as pl
from jax.experimental.pallas import tpu as pltpu
from jax.sharding import PartitionSpec as P

HIGHEST = lax.Precision.HIGHEST
VMEM_LIMIT = 24 * 1024 * 1024


def any_mesh(
    right_side,
    earlier,
    inverse_diag,
    dense_tiles,
    left_factor,
    right_factor,
    tile_ranks,
    dense_flags,
):
    count_steps = right_side.shape[0]
    prev_cols = earlier.shape[0]
    rank_pad = left_factor.shape[3]
    tile_flags = dense_flags.astype(jnp.float32)
    columns = lax.broadcasted_iota(jnp.int32, tile_ranks.shape + (rank_pad,), 2)
    low_mask = (columns < tile_ranks[:, :, None]).astype(jnp.float32) * (1.0 - tile_flags)[
        :, :, None
    ]
    left_eff = left_factor * low_mask[:, :, None, :]
    tile_rows = (
        lax.all_gather(dense_tiles, "pcol", axis=3, tiled=True) * tile_flags[:, :, None, None]
    )
    inverse_rows = lax.all_gather(inverse_diag, "pcol", axis=2, tiled=True)
    early_sum = jnp.einsum(
        "kjrc,jcs->krs",
        tile_rows[:, :prev_cols],
        lax.all_gather(earlier, "prow", axis=1, tiled=True),
        precision=HIGHEST,
    )
    partial_value = jnp.einsum(
        "kjcq,jcs->kjqs", right_factor[:, :prev_cols], earlier, precision=HIGHEST
    )
    early_coeffs = lax.psum(partial_value, "prow")
    early_sum = early_sum + jnp.einsum(
        "kjrq,kjqs->krs", left_eff[:, :prev_cols], early_coeffs, precision=HIGHEST
    )
    pending = right_side - early_sum
    outputs = []
    for block_index in range(count_steps):
        residual_whole = lax.all_gather(pending[block_index], "prow", axis=0, tiled=True)
        solved_own = jnp.dot(inverse_rows[block_index], residual_whole, precision=HIGHEST)
        outputs.append(solved_own)
        if block_index + 1 < count_steps:
            solved_whole = lax.all_gather(solved_own, "prow", axis=0, tiled=True)
            column = prev_cols + block_index
            later = slice(block_index + 1, None)
            dense_part = jnp.einsum(
                "krc,cs->krs", tile_rows[later, column], solved_whole, precision=HIGHEST
            )
            projected = lax.psum(
                jnp.einsum(
                    "kcq,cs->kqs", right_factor[later, column], solved_own, precision=HIGHEST
                ),
                "prow",
            )
            low_part = jnp.einsum(
                "krq,kqs->krs", left_eff[later, column], projected, precision=HIGHEST
            )
            pending = pending.at[later].add(-(dense_part + low_part))
    return jnp.stack(outputs)


def halves(value, axis):
    high = value.astype(jnp.bfloat16)
    low = (value - high.astype(jnp.float32)).astype(jnp.bfloat16)
    return jnp.concatenate([high, low], axis=axis)


def dot_halves(left2, right2, dims=(((1,), (0,)), ((), ()))):
    rows = left2.shape[1 - dims[0][0][0]] // 2
    cols = right2.shape[1 - dims[0][1][0]] // 2
    out = lax.dot_general(left2, right2, dims, preferred_element_type=jnp.float32)
    return (out[:rows, :cols] + (out[:rows, cols:] + out[rows:, :cols])) + out[rows:, cols:]


def fill_ahead(out_ref, count, inv_ref, right_ref):
    nb = inv_ref.shape[1]
    share = right_ref.shape[2] // lax.axis_size("pcol")
    at = pl.multiple_of(lax.axis_index("pcol") * share, share)
    out_ref[:nb] = inv_ref[0]
    for col in range(count):
        place = nb + col * share
        out_ref[place : place + share] = right_ref[0, col, pl.ds(at, share), :]


def first_kernel(prev, ahead, known_ref, right_ref, right1_ref, inv_ref, sent_ref):
    nb, rank_pad = known_ref.shape[1], right_ref.shape[2]
    fill_ahead(sent_ref, prev + 1, inv_ref, right1_ref)
    for col in range(prev):
        known = known_ref[col]
        at = ahead + col * nb
        sent_ref[at : at + nb] = known
        at = ahead + prev * nb + col * rank_pad
        sent_ref[at : at + rank_pad] = dot_halves(halves(right_ref[0, col], 0), halves(known, 1))


def dense_kernel(rows, flags_ref, *refs):
    *dense_refs, out_ref = refs
    place = 0
    for (step, count), ref in zip(rows, dense_refs):
        for col in range(count):
            block = ref[0] if len(ref.shape) == 3 else ref[0, col] * flags_ref[step, col].astype(jnp.float32)
            out_ref[place] = block
            place += 1


def stack_kernel(*refs):
    *parts, out_ref = refs
    place = 0
    for ref in parts:
        out_ref[place : place + ref.shape[0]] = ref[...]
        place += ref.shape[0]


def masked_left(step, col, ranks_ref, flags_ref, left_ref):
    row_at = lax.broadcasted_iota(jnp.int32, left_ref.shape[2:], 0)
    flag = flags_ref[step, col].astype(jnp.float32)
    return left_ref[0, col] * jnp.where(row_at < ranks_ref[step, col], 1.0 - flag, 0.0)


OVER_ROWS = (((0,), (0,)), ((), ()))


def early_kernel(n, prev, begin, ahead, counts, *refs):
    strips, sources = refs[:n], refs[n : 2 * n]
    ranks_ref, flags_ref, left_ref, base_ref, inv_ref, right_ref, out_ref, scratch = refs[2 * n :]
    nb, rank_pad = inv_ref.shape[1], left_ref.shape[2]
    turn = lax.axis_index("pcol") ^ lax.axis_index("prow")
    total = base_ref[0]
    for col in range(prev):
        at = begin + col * nb
        for slot, ref in enumerate(sources):
            scratch[pl.ds(pl.multiple_of((turn ^ slot) * nb, nb), nb), :] = ref[at : at + nb]
        strip = jnp.concatenate([ref[col] for ref in strips], axis=1)
        total = total - dot_halves(halves(strip, 0), halves(scratch[...], 1))
    lefts, coeffs = [], []
    for col in range(prev):
        at = begin + prev * nb + col * rank_pad
        lefts.append(masked_left(0, col, ranks_ref, flags_ref, left_ref))
        coeffs.append(sum(ref[at : at + rank_pad] for ref in sources))
    left2 = halves(jnp.concatenate(lefts, axis=0), 1)
    coeff2 = halves(jnp.concatenate(coeffs, axis=0), 1)
    out_ref[ahead:] = total - dot_halves(left2, coeff2, OVER_ROWS)
    fill_ahead(out_ref, counts, inv_ref, right_ref)


def prepare_kernel(n, prev, step, first, size, known_at, last, *refs):
    dense, ahead = refs[:n], refs[n : n + 2]
    sources = refs[n + 2 : 2 * n + 2]
    solved = refs[2 * n + 2 : 2 * n + 1 + step]
    rest = refs[2 * n + 1 + step :]
    ranks_ref, flags_ref, left_ref, base_ref, out_ref, strip_ref, inv_ref, scratch, right_scr = rest
    nb = base_ref.shape[1]
    tiles, rank_pad = right_scr.shape[:2]
    share = rank_pad // n
    own_col, own_row = lax.axis_index("pcol"), lax.axis_index("prow")
    turn = own_col ^ own_row
    rows = ahead[0].shape[0] // (2 * n)

    for near in range(n):
        col_at = own_col ^ near
        for slot in range(n):
            at = ((near >> 1) * n + slot) * rows
            both = halves(ahead[near & 1][at : at + nb], 0)
            row_at = (own_row ^ slot) * nb
            lanes = pl.ds(pl.multiple_of(col_at * nb, nb), nb)
            inv_ref[pl.ds(pl.multiple_of(row_at, nb), nb), lanes] = both[:nb]
            inv_ref[pl.ds(pl.multiple_of(n * nb + row_at, nb), nb), lanes] = both[nb:]
            lanes = pl.ds(pl.multiple_of((turn ^ slot) * nb, nb), nb)
            ranks = pl.ds(pl.multiple_of(col_at * share, share), share)
            for tile in range(tiles):
                place = at + nb + tile * share
                right_scr[tile, ranks, lanes] = ahead[near & 1][place : place + share]

    def strip_of(tile):
        blocks = [ref[first + tile] for ref in dense]
        left = masked_left(step, tile, ranks_ref, flags_ref, left_ref)
        low = dot_halves(halves(left, 1), halves(right_scr[tile], 1), OVER_ROWS)
        return jnp.concatenate(blocks, axis=1) + low

    total = base_ref[0]
    for tile in range(prev):
        at = known_at + tile * nb
        for slot, ref in enumerate(sources):
            scratch[pl.ds(pl.multiple_of((turn ^ slot) * nb, nb), nb), :] = ref[at : at + nb]
        total = total - dot_halves(halves(strip_of(tile), 0), halves(scratch[...], 1))
    for index, ref in enumerate(solved):
        for d in range(n):
            rows_at = pl.ds(pl.multiple_of((own_col ^ d) * nb, nb), nb)
            scratch[d * nb : (d + 1) * nb] = ref[rows_at, :]
        total = total - dot_halves(halves(strip_of(prev + index), 0), halves(scratch[...], 1))
    out_ref[...] = total
    pair = halves(strip_of(tiles - 1), 0)
    for d in range(n):
        lanes = pl.ds(pl.multiple_of((own_col ^ d) * nb, nb), nb)
        strip_ref[0, :, lanes] = pair[:, d * nb : (d + 1) * nb]
        if last:
            strip_ref[1, :, lanes] = halves(dense[d][size - 1], 0)


def place_slots(n, at, nb, slots, scratch):
    own = lax.axis_index("prow")
    for slot, ref in enumerate(slots):
        scratch[pl.ds(pl.multiple_of((own ^ slot) * nb, nb), nb), :] = ref[at : at + nb]


def step_kernel(n, at, ahead, counts, *refs):
    inverse_ref, strip_ref, base_ref, *more, out_ref, solved_ref, scratch = refs[n:]
    nb = base_ref.shape[0]
    place_slots(n, at, nb, refs[:n], scratch)
    solved = dot_halves(inverse_ref[...], halves(scratch[...], 1))
    solved_ref[...] = solved
    out_ref[ahead:] = base_ref[...] - dot_halves(strip_ref[0], halves(solved, 1))
    if ahead:
        fill_ahead(out_ref, counts, *more)


def last_kernel(n, *refs):
    strip_ref, *solved, out_ref, scratch = refs[n:]
    nb = out_ref.shape[1]
    place_slots(n, 0, nb, refs[:n], scratch)
    own = pl.ds(pl.multiple_of(lax.axis_index("prow") * nb, nb), nb)
    for step, ref in enumerate(solved):
        out_ref[step] = ref[own, :]
    out_ref[len(solved)] = dot_halves(strip_ref[0], halves(scratch[...], 1))


def spec_of(shape, index=None):
    if index is None:
        return pl.BlockSpec(shape, lambda i: (0,) * len(shape))
    return pl.BlockSpec(shape, lambda i: index)


def square_mesh(
    n,
    right_side,
    earlier,
    inverse_diag,
    dense_tiles,
    left_factor,
    right_factor,
    tile_ranks,
    dense_flags,
):
    steps, nb, rhs = right_side.shape
    prev = earlier.shape[0]
    cols = dense_tiles.shape[1]
    rank_pad = left_factor.shape[3]
    left_t = jnp.swapaxes(left_factor, 2, 3)
    right_t = jnp.swapaxes(right_factor, 2, 3)
    params = pltpu.CompilerParams(vmem_limit_bytes=VMEM_LIMIT)
    f32 = jnp.float32

    def shift(value, axis, step):
        return lax.ppermute(value, axis, [(i, i ^ step) for i in range(n)])

    def over_rows(value):
        return [value] + [shift(value, "prow", d) for d in range(1, n)]

    def over_rows_forwarded(value):
        beside, across = shift(value, "prow", 1), shift(value, "prow", 2)
        return [value, beside, across, shift(across, "prow", 1)]

    any_spec = pl.BlockSpec(memory_space=pl.ANY)
    smem = pl.BlockSpec(memory_space=pltpu.SMEM)
    bf16 = jnp.bfloat16

    def pinned(value):
        return pltpu.with_memory_space_constraint(value, pltpu.HBM)

    def shaped(*shape, dtype=f32):
        return jax.ShapeDtypeStruct(shape, dtype)

    def call(kernel, name, shapes, args, specs, scratch=(), after=()):
        many = isinstance(shapes, list)
        out_specs = [spec_of(x.shape) for x in shapes] if many else spec_of(shapes.shape)

        def body(*refs):
            kernel(*refs[: len(args)], *refs[len(args) + len(after) :])

        return pl.pallas_call(
            body,
            grid=(1,),
            out_shape=shapes,
            in_specs=specs + [any_spec] * len(after),
            out_specs=out_specs,
            scratch_shapes=list(scratch),
            compiler_params=params,
            name=name,
        )(*args, *after)

    def blocks_of(value, step):
        return pinned(value), spec_of((1,) + value.shape[1:], (step,) + (0,) * (value.ndim - 1))

    def whole_of(value):
        return value, spec_of(value.shape)

    def run(kernel, name, shapes, pairs, scratch=(), after=()):
        args, specs = zip(*pairs)
        return call(kernel, name, shapes, list(args), list(specs), scratch, after)

    share = rank_pad // n
    ranks_flags = [(tile_ranks, smem), (dense_flags, smem)]
    source_room = pltpu.VMEM((n * nb, rhs), f32)
    aheads = [nb + (prev + step) * share for step in range(1, steps)] + [0]

    def over_cols(own):
        far = shift(own, "pcol", 2)
        return [own, shift(own, "pcol", 1), far, shift(far, "pcol", 1)]

    def shared_ahead(slots, ahead, step, after, after_far):
        head = spec_of((ahead, nb))
        shape = shaped(n * ahead, nb)
        own = run(stack_kernel, f"ahead{step}", shape, [(ref, head) for ref in slots], after=after)
        far = shift(own, "pcol", 2)
        shape = shaped(2 * n * ahead, nb)
        pairs = [whole_of(own), whole_of(far)]
        both = run(stack_kernel, f"aheads{step}", shape, pairs, after=after_far)
        return [both, shift(both, "pcol", 1)]

    sent = run(
        functools.partial(first_kernel, prev, aheads[0]),
        "first",
        shaped(aheads[0] + prev * (nb + rank_pad), rhs),
        [whole_of(pinned(earlier))]
        + [blocks_of(right_t, 0), blocks_of(right_t, 1), blocks_of(inverse_diag, 0)],
    )
    known = over_rows_forwarded(sent)
    own = run(
        functools.partial(dense_kernel, [(0, prev)]),
        "dense0",
        shaped(prev, nb, nb),
        [(dense_flags, smem), blocks_of(dense_tiles, 0)],
        after=[sent],
    )
    strips0 = over_cols(own)
    rows = [(step, prev + step) for step in range(1, steps)] + [(steps - 1, 1)]
    size = sum(count for _, count in rows)
    own = run(
        functools.partial(dense_kernel, rows),
        "dense",
        shaped(size, nb, nb),
        [(dense_flags, smem)]
        + [blocks_of(dense_tiles, step) for step in range(1, steps)]
        + [blocks_of(inverse_diag, steps - 1)],
        after=known[1:3] + strips0[1:],
    )
    dense = over_cols(own)

    pending = run(
        functools.partial(early_kernel, n, prev, aheads[0], aheads[1], prev + 2),
        "early",
        shaped(aheads[1] + nb, rhs),
        [whole_of(value) for value in strips0 + known]
        + ranks_flags
        + [blocks_of(left_t, 0), blocks_of(right_side, 0)]
        + [blocks_of(inverse_diag, 1), blocks_of(right_t, 2)],
        [source_room],
    )
    slots, solved = known, []
    for step in range(steps - 1):
        last = step + 2 == steps
        came = slots
        slots = over_rows_forwarded(pending) if aheads[step + 1] else over_rows(pending)
        later = shared_ahead(came, aheads[step], step, [pending], slots[1:3])
        tiles = prev + step + 1
        first = sum(count for row, count in rows[:-1] if row <= step)
        base, strip, inverse = run(
            functools.partial(
                prepare_kernel, n, prev, step + 1, first, size, aheads[0], last
            ),
            f"prepare{step}",
            [
                shaped(nb, rhs),
                shaped(1 + last, 2 * nb, n * nb, dtype=bf16),
                shaped(2 * n * nb, n * nb, dtype=bf16),
            ],
            [whole_of(value) for value in dense + later + known + solved]
            + ranks_flags
            + [blocks_of(left_t, step + 1), blocks_of(right_side, step + 1)],
            [source_room, pltpu.VMEM((tiles, rank_pad, n * nb), f32)],
        )
        ahead = aheads[step + 2] if step + 2 < len(aheads) else 0
        more = [blocks_of(inverse_diag, step + 2), blocks_of(right_t, step + 3)] if ahead else []
        pending, block = run(
            functools.partial(step_kernel, n, aheads[step + 1], ahead, tiles + 2),
            f"step{step}",
            [shaped(ahead + nb, rhs), shaped(n * nb, rhs)],
            [whole_of(value) for value in slots + [inverse]]
            + [(strip, spec_of((1, 2 * nb, n * nb), (0, 0, 0))), whole_of(base)]
            + more,
            [source_room],
        )
        solved.append(block)
    return run(
        functools.partial(last_kernel, n),
        "last",
        shaped(steps, nb, rhs),
        [whole_of(value) for value in over_rows(pending)]
        + [(strip, spec_of((1, 2 * nb, n * nb), (1, 0, 0)))]
        + [whole_of(value) for value in solved],
        [source_room],
    )


def solution(mesh):
    placed = (
        P("groups", "prow", "pcol"),
        P("groups", "prow", "pcol"),
        P("groups", "prow", "pcol"),
        P("groups", None, "prow", "pcol"),
        P("groups", None, "prow", None),
        P("groups", None, "prow", None),
        P("groups", None),
        P("groups", None),
    )
    n = mesh.shape["prow"]
    square = n == 4 and n == mesh.shape["pcol"]

    def local(*args):
        nb, cols = args[3].shape[2:]
        steps = args[0].shape[0]
        if square and steps == 4 and nb % 128 == 0 and cols % 128 == 0 and args[0].shape[2] % 128 == 0:
            return square_mesh(n, *args)
        return any_mesh(*args)

    return jax.shard_map(
        local, mesh=mesh, in_specs=placed, out_specs=P("groups", "prow", "pcol"), check_vma=False
    )
```

time: 333 us -> 134 us (0.40)
  blocking collectives: 117 us -> 0 us
  waiting for transfers between devices: 161 us -> 86.3 us
  starting transfers between devices: 0.2 us -> 28.6 us
  matrix products: 27.2 us -> 0 us
  Pallas kernels: 0 us -> 18.6 us
  between operations: 13.6 us -> 0.2 us
  other arithmetic: 11 us -> 0 us
    all_gather x7 -> x0, blocking collectives: 98.9 us -> none  [the longest x4 57.1 us: local(): lax.all_gather(pending[block_index], 'prow', axis=0, tiled=True)]
    psum x3 -> x0, waiting for transfers between devices: 86.6 us -> none  [the longest x2 52.3 us: local(): projected = lax.psum(projected, 'prow')]
    ppermute x0 -> x27, waiting for transfers between devices: none -> 86.3 us  [shift(): return lax.ppermute(value, axis, [(i, i ^ step) for i in range(n)])]
    all_gather x3 -> x0, waiting for transfers between devices: 72.2 us -> none  [the longest x1 48.4 us: local(): lax.all_gather(dense_tiles, 'pcol', axis=3, tiled=True)]
    ppermute x0 -> x27, starting transfers between devices: none -> 28.6 us  [shift(): return lax.ppermute(value, axis, [(i, i ^ step) for i in range(n)])]
    dot_general x14 -> x0, matrix products: 25.4 us -> none  [the longest x4 6.17 us: local(): jnp.dot(inverse_rows[block_index], residual_whole, precision=HIGHEST)]
    pallas_call x0 -> x17, Pallas kernels: none -> 18.6 us  [call(): pl.pallas_call(body, grid=(1,), out_shape=shapes, in_specs=specs + [any_s...]
    psum x1 -> x0, blocking collectives: 17.9 us -> none  [local(): projected = lax.psum(projected, 'prow')]
  transfers between devices with their start and end apart: 6 -> 27, of which waited for: 6 -> 22; matrix products, arithmetic and copies ran while one was open for 8% -> 0% of each run, Pallas kernels for 0% -> 8%
where the time goes in v7:
time: 134 us
  waiting for transfers between devices  86.3 us (64%)
  starting transfers between devices  28.6 us (21%)
  Pallas kernels  18.6 us (14%)
    ppermute x27, waiting for transfers between devices, shift(): return lax.ppermute(value, axis, [(i, i ^ step) for i in range(n)])  86.3 us
    ppermute x27, starting transfers between devices, shift(): return lax.ppermute(value, axis, [(i, i ^ step) for i in range(n)])  28.6 us
    pallas_call x17, Pallas kernels, call(): pl.pallas_call(body, grid=(1,), out_shape=shapes, in_specs=specs + [any_s...  18.6 us
  transfers between devices with their start and end apart: 27, of which 22 were waited for; matrix products, arithmetic and copies ran while one was open for 0% of the time, Pallas kernels for 8%

profile of v7, /device:TPU:0, one launch (start us, length us, event | category | flops | bytes accessed | tf_op | source)
XLA Modules:
  0.0 133.8 jit_solution(9902989960151558384)
XLA Ops:
  2.5 3.0 %collective-permute-start.1 = (f32[4,128,128]{2,1,0:T(8,128)S(1)}, f32[4,128,128]{2,1,0:T(8,128)S(1)}, u32[]{:S(2)}, u32[]{:S(2)}) collective-permute-start(f32[4,128,128]{2,1,0:T(8,128)S(1)} %dense0.1.refs_0_), channel_id=1, source_target_pairs={{0,2},{1,3},{2,0},{3,1},{4,6},{5,7},{6,4},{7,5},{8,10},{9,11},{10,... | collective-permute-start | bytes 786440 | tf_op jit(solution)/shard_map/ppermute | solution.py:268
  5.5 2.6 %collective-permute-start.4 = (f32[976,128]{1,0:T(8,128)S(1)}, f32[976,128]{1,0:T(8,128)S(1)}, u32[]{:S(2)}, u32[]{:S(2)}) collective-permute-start(f32[976,128]{1,0:T(8,128)S(1)} %first.1.refs_2_.refs_4_.refs_0_.refs_6_), channel_id=1, source_target_pairs={{0,8},{4,12},{8,0},{12,4},{1,9},{5,13},{9,1},{13,5},{2,10},{6,14},... | collective-permute-start | bytes 1499144 | tf_op jit(solution)/shard_map/ppermute | solution.py:268
  8.1 1.6 %collective-permute-start.3 = (f32[976,128]{1,0:T(8,128)S(1)}, f32[976,128]{1,0:T(8,128)S(1)}, u32[]{:S(2)}, u32[]{:S(2)}) collective-permute-start(f32[976,128]{1,0:T(8,128)S(1)} %first.1.refs_2_.refs_4_.refs_0_.refs_6_), channel_id=1, source_target_pairs={{0,4},{4,0},{8,12},{12,8},{1,5},{5,1},{9,13},{13,9},{2,6},{6,2},{1... | collective-permute-start | bytes 1499144 | tf_op jit(solution)/shard_map/ppermute | solution.py:268
  9.6 2.1 %collective-permute-done.1.refs_2_.refs_8_ = f32[4,128,128]{2,1,0:T(8,128)S(1)} collective-permute-done((f32[4,128,128]{2,1,0:T(8,128)S(1)}, f32[4,128,128]{2,1,0:T(8,128)S(1)}, u32[]{:S(2)}, u32[]{:S(2)}) %collective-permute-start.1) | collective-permute-done | bytes 262176 | tf_op jit(solution)/shard_map/ppermute | solution.py:268
  11.8 18.3 %collective-permute-done.4.refs_6_.refs_2_.refs_8_ = f32[976,128]{1,0:T(8,128)S(1)} collective-permute-done((f32[976,128]{1,0:T(8,128)S(1)}, f32[976,128]{1,0:T(8,128)S(1)}, u32[]{:S(2)}, u32[]{:S(2)}) %collective-permute-start.4) | collective-permute-done | bytes 499744 | tf_op jit(solution)/shard_map/ppermute | solution.py:268
  32.2 1.5 %collective-permute-start.5 = (f32[976,128]{1,0:T(8,128)S(1)}, f32[976,128]{1,0:T(8,128)S(1)}, u32[]{:S(2)}, u32[]{:S(2)}) collective-permute-start(f32[976,128]{1,0:T(8,128)S(1)} %collective-permute-done.4.refs_6_.refs_2_.refs_8_), channel_id=1, source_target_pairs={{0,4},{4,0},{8,12},{12,8},{1,5},{5,1},{9,13},{13,9},{2,6},{6,2},{1... | collective-permute-start | bytes 1499144 | tf_op jit(solution)/shard_map/ppermute | solution.py:268
  33.7 10.3 %collective-permute-done.5.refs_7_.refs_3_.refs_9_ = f32[976,128]{1,0:T(8,128)S(1)} collective-permute-done((f32[976,128]{1,0:T(8,128)S(1)}, f32[976,128]{1,0:T(8,128)S(1)}, u32[]{:S(2)}, u32[]{:S(2)}) %collective-permute-start.5) | collective-permute-done | bytes 499744 | tf_op jit(solution)/shard_map/ppermute | solution.py:268
  43.9 1.8 %early.1.refs_4_.refs_0_ = f32[352,128]{1,0:T(8,128)S(1)} custom-call(f32[4,128,128]{2,1,0:T(8,128)S(1)} %dense0.1.refs_0_, f32[4,128,128]{2,1,0:T(8,128)S(1)} %collective-permute-done.refs_1_.refs_7_, f32[4,128,128]{2,1,0:T(8,128)S(1)} %collective-permute-done.1.refs_2_.refs_8_, f32[4,128,128]{2,1,0:T(8,128)S(1)} %collective-permute-done.2.refs_3_.refs_9_, ...), custom_call_target="tpu_custom_call" | custom-call | tf_op jit(solution)/shard_map/early/pallas_call | solution.py:294
  45.8 1.6 %collective-permute-start.12 = (f32[832,128]{1,0:T(8,128)S(1)}, f32[832,128]{1,0:T(8,128)S(1)}, u32[]{:S(2)}, u32[]{:S(2)}) collective-permute-start(f32[832,128]{1,0:T(8,128)S(1)} %ahead0.1.refs_0_), channel_id=1, source_target_pairs={{0,2},{1,3},{2,0},{3,1},{4,6},{5,7},{6,4},{7,5},{8,10},{9,11},{10,... | collective-permute-start | bytes 1277960 | tf_op jit(solution)/shard_map/ppermute | solution.py:268
  47.4 14.6 %collective-permute-done.10.refs_2_ = f32[19,128,128]{2,1,0:T(8,128)S(1)} collective-permute-done((f32[19,128,128]{2,1,0:T(8,128)S(1)}, f32[19,128,128]{2,1,0:T(8,128)S(1)}, u32[]{:S(2)}, u32[]{:S(2)}) %collective-permute-start.10) | collective-permute-done | bytes 1245216 | tf_op jit(solution)/shard_map/ppermute | solution.py:268
  62.0 1.4 %collective-permute-start.6 = (f32[352,128]{1,0:T(8,128)S(1)}, f32[352,128]{1,0:T(8,128)S(1)}, u32[]{:S(2)}, u32[]{:S(2)}) collective-permute-start(f32[352,128]{1,0:T(8,128)S(1)} %early.1.refs_4_.refs_0_), channel_id=1, source_target_pairs={{0,4},{4,0},{8,12},{12,8},{1,5},{5,1},{9,13},{13,9},{2,6},{6,2},{1... | collective-permute-start | bytes 540680 | tf_op jit(solution)/shard_map/ppermute | solution.py:268
  63.5 2.2 %collective-permute-start.7 = (f32[352,128]{1,0:T(8,128)S(1)}, f32[352,128]{1,0:T(8,128)S(1)}, u32[]{:S(2)}, u32[]{:S(2)}) collective-permute-start(f32[352,128]{1,0:T(8,128)S(1)} %early.1.refs_4_.refs_0_), channel_id=1, source_target_pairs={{0,8},{4,12},{8,0},{12,4},{1,9},{5,13},{9,1},{13,5},{2,10},{6,14},... | collective-permute-start | bytes 540680 | tf_op jit(solution)/shard_map/ppermute | solution.py:268
  65.7 6.5 %collective-permute-done.6.refs_2_.refs_1_ = f32[352,128]{1,0:T(8,128)S(1)} collective-permute-done((f32[352,128]{1,0:T(8,128)S(1)}, f32[352,128]{1,0:T(8,128)S(1)}, u32[]{:S(2)}, u32[]{:S(2)}) %collective-permute-start.6) | collective-permute-done | bytes 180256 | tf_op jit(solution)/shard_map/ppermute | solution.py:268
  72.2 2.7 %collective-permute-done.7.refs_3_.refs_2_ = f32[352,128]{1,0:T(8,128)S(1)} collective-permute-done((f32[352,128]{1,0:T(8,128)S(1)}, f32[352,128]{1,0:T(8,128)S(1)}, u32[]{:S(2)}, u32[]{:S(2)}) %collective-permute-start.7) | collective-permute-done | bytes 180256 | tf_op jit(solution)/shard_map/ppermute | solution.py:268
  75.2 2.3 %collective-permute-done.13.refs_5_ = f32[1664,128]{1,0:T(8,128)S(1)} collective-permute-done((f32[1664,128]{1,0:T(8,128)S(1)}, f32[1664,128]{1,0:T(8,128)S(1)}, u32[]{:S(2)}, u32[]{:S(2)}) %collective-permute-start.13) | collective-permute-done | bytes 852000 | tf_op jit(solution)/shard_map/ppermute | solution.py:268
  77.5 2.6 %prepare0.1 = (f32[128,128]{1,0:T(8,128)S(1)}, bf16[1,256,512]{2,1,0:T(8,128)(2,1)S(1)}, bf16[1024,512]{1,0:T(8,128)(2,1)S(1)}) custom-call(f32[19,128,128]{2,1,0:T(8,128)S(1)} %dense.1.refs_0_, f32[19,128,128]{2,1,0:T(8,128)S(1)} %collective-permute-done.9.refs_1_, f32[19,128,128]{2,1,0:T(8,128)S(1)} %collective-permute-done.10.refs_2_, ...), custom_call_target="tpu_custom_call" | custom-call | tf_op jit(solution)/shard_map/prepare0/pallas_call | solution.py:294
  80.1 2.0 %collective-permute-done.8.refs_3_ = f32[352,128]{1,0:T(8,128)S(1)} collective-permute-done((f32[352,128]{1,0:T(8,128)S(1)}, f32[352,128]{1,0:T(8,128)S(1)}, u32[]{:S(2)}, u32[]{:S(2)}) %collective-permute-start.8) | collective-permute-done | bytes 180256 | tf_op jit(solution)/shard_map/ppermute | solution.py:268
  82.1 1.7 %step0.1 = (f32[368,128]{1,0:T(8,128)S(1)}, f32[512,128]{1,0:T(8,128)S(1)}) custom-call(f32[352,128]{1,0:T(8,128)S(1)} %early.1.refs_4_.refs_0_, f32[352,128]{1,0:T(8,128)S(1)} %collective-permute-done.6.refs_2_.refs_1_, f32[352,128]{1,0:T(8,128)S(1)} %collective-permute-done.7.refs_3_.refs_2_, f32[352,128]{1,0:T(8,128)S(1)} %collective-permute-done.8.refs_3_, ...), custom_call_target="tpu_custom_call" | custom-call | tf_op jit(solution)/shard_map/step0/pallas_call | solution.py:294
  84.7 2.3 %collective-permute-start.15 = (f32[368,128]{1,0:T(8,128)S(1)}, f32[368,128]{1,0:T(8,128)S(1)}, u32[]{:S(2)}, u32[]{:S(2)}) collective-permute-start(f32[368,128]{1,0:T(8,128)S(1)} %get-tuple-element.23.refs_4_.refs_0_), channel_id=1, source_target_pairs={{0,8},{4,12},{8,0},{12,4},{1,9},{5,13},{9,1},{13,5},{2,10},{6,14},... | collective-permute-start | bytes 565256 | tf_op jit(solution)/shard_map/ppermute | solution.py:268
  86.9 6.9 %collective-permute-done.14.refs_2_.refs_1_ = f32[368,128]{1,0:T(8,128)S(1)} collective-permute-done((f32[368,128]{1,0:T(8,128)S(1)}, f32[368,128]{1,0:T(8,128)S(1)}, u32[]{:S(2)}, u32[]{:S(2)}) %collective-permute-start.14) | collective-permute-done | bytes 188448 | tf_op jit(solution)/shard_map/ppermute | solution.py:268
  93.8 1.7 %collective-permute-done.15.refs_3_.refs_2_ = f32[368,128]{1,0:T(8,128)S(1)} collective-permute-done((f32[368,128]{1,0:T(8,128)S(1)}, f32[368,128]{1,0:T(8,128)S(1)}, u32[]{:S(2)}, u32[]{:S(2)}) %collective-permute-start.15) | collective-permute-done | bytes 188448 | tf_op jit(solution)/shard_map/ppermute | solution.py:268
  96.6 1.9 %collective-permute-done.18.refs_5_ = f32[1792,128]{1,0:T(8,128)S(1)} collective-permute-done((f32[1792,128]{1,0:T(8,128)S(1)}, f32[1792,128]{1,0:T(8,128)S(1)}, u32[]{:S(2)}, u32[]{:S(2)}) %collective-permute-start.18) | collective-permute-done | bytes 917536 | tf_op jit(solution)/shard_map/ppermute | solution.py:268
  98.5 2.8 %prepare1.1 = (f32[128,128]{1,0:T(8,128)S(1)}, bf16[1,256,512]{2,1,0:T(8,128)(2,1)S(1)}, bf16[1024,512]{1,0:T(8,128)(2,1)S(1)}) custom-call(f32[19,128,128]{2,1,0:T(8,128)S(1)} %dense.1.refs_0_, f32[19,128,128]{2,1,0:T(8,128)S(1)} %collective-permute-done.9.refs_1_, f32[19,128,128]{2,1,0:T(8,128)S(1)} %collective-permute-done.10.refs_2_, ...), custom_call_target="tpu_custom_call" | custom-call | tf_op jit(solution)/shard_map/prepare1/pallas_call | solution.py:294
  101.4 1.9 %collective-permute-done.16.refs_3_ = f32[368,128]{1,0:T(8,128)S(1)} collective-permute-done((f32[368,128]{1,0:T(8,128)S(1)}, f32[368,128]{1,0:T(8,128)S(1)}, u32[]{:S(2)}, u32[]{:S(2)}) %collective-permute-start.16) | collective-permute-done | bytes 188448 | tf_op jit(solution)/shard_map/ppermute | solution.py:268
  105.4 2.3 %collective-permute-start.20 = (f32[128,128]{1,0:T(8,128)S(1)}, f32[128,128]{1,0:T(8,128)S(1)}, u32[]{:S(2)}, u32[]{:S(2)}) collective-permute-start(f32[128,128]{1,0:T(8,128)S(1)} %get-tuple-element.28.refs_4_.refs_0_), channel_id=1, source_target_pairs={{0,8},{4,12},{8,0},{12,4},{1,9},{5,13},{9,1},{13,5},{2,10},{6,14},... | collective-permute-start | bytes 196616 | tf_op jit(solution)/shard_map/ppermute | solution.py:268
  107.7 1.9 %collective-permute-done.19.refs_2_.refs_1_ = f32[128,128]{1,0:T(8,128)S(1)} collective-permute-done((f32[128,128]{1,0:T(8,128)S(1)}, f32[128,128]{1,0:T(8,128)S(1)}, u32[]{:S(2)}, u32[]{:S(2)}) %collective-permute-start.19) | collective-permute-done | bytes 65568 | tf_op jit(solution)/shard_map/ppermute | solution.py:268
  111.0 5.9 %collective-permute-done.22.refs_1_ = f32[960,128]{1,0:T(8,128)S(1)} collective-permute-done((f32[960,128]{1,0:T(8,128)S(1)}, f32[960,128]{1,0:T(8,128)S(1)}, u32[]{:S(2)}, u32[]{:S(2)}) %collective-permute-start.22) | collective-permute-done | bytes 491552 | tf_op jit(solution)/shard_map/ppermute | solution.py:268
  117.0 2.0 %collective-permute-start.21 = (f32[128,128]{1,0:T(8,128)S(1)}, f32[128,128]{1,0:T(8,128)S(1)}, u32[]{:S(2)}, u32[]{:S(2)}) collective-permute-start(f32[128,128]{1,0:T(8,128)S(1)} %get-tuple-element.28.refs_4_.refs_0_), channel_id=1, source_target_pairs={{0,12},{4,8},{8,4},{12,0},{1,13},{5,9},{9,5},{13,1},{2,14},{6,10},... | collective-permute-start | bytes 196616 | tf_op jit(solution)/shard_map/ppermute | solution.py:268
  119.5 3.2 %prepare2.1 = (f32[128,128]{1,0:T(8,128)S(1)}, bf16[2,256,512]{2,1,0:T(8,128)(2,1)S(1)}, bf16[1024,512]{1,0:T(8,128)(2,1)S(1)}) custom-call(f32[19,128,128]{2,1,0:T(8,128)S(1)} %dense.1.refs_0_, f32[19,128,128]{2,1,0:T(8,128)S(1)} %collective-permute-done.9.refs_1_, f32[19,128,128]{2,1,0:T(8,128)S(1)} %collective-permute-done.10.refs_2_, ...), custom_call_target="tpu_custom_call" | custom-call | tf_op jit(solution)/shard_map/prepare2/pallas_call | solution.py:294
  124.1 2.5 %collective-permute-start.25 = (f32[128,128]{1,0:T(8,128)S(1)}, f32[128,128]{1,0:T(8,128)S(1)}, u32[]{:S(2)}, u32[]{:S(2)}) collective-permute-start(f32[128,128]{1,0:T(8,128)S(1)} %get-tuple-element.33.refs_0_), channel_id=1, source_target_pairs={{0,8},{4,12},{8,0},{12,4},{1,9},{5,13},{9,1},{13,5},{2,10},{6,14},... | collective-permute-start | bytes 196616 | tf_op jit(solution)/shard_map/ppermute | solution.py:268
  126.6 1.9 %collective-permute-start.26 = (f32[128,128]{1,0:T(8,128)S(1)}, f32[128,128]{1,0:T(8,128)S(1)}, u32[]{:S(2)}, u32[]{:S(2)}) collective-permute-start(f32[128,128]{1,0:T(8,128)S(1)} %get-tuple-element.33.refs_0_), channel_id=1, source_target_pairs={{0,12},{4,8},{8,4},{12,0},{1,13},{5,9},{9,5},{13,1},{2,14},{6,10},... | collective-permute-start | bytes 196616 | tf_op jit(solution)/shard_map/ppermute | solution.py:268
  128.8 2.9 %collective-permute-done.25.refs_2_ = f32[128,128]{1,0:T(8,128)S(1)} collective-permute-done((f32[128,128]{1,0:T(8,128)S(1)}, f32[128,128]{1,0:T(8,128)S(1)}, u32[]{:S(2)}, u32[]{:S(2)}) %collective-permute-start.25) | collective-permute-done | bytes 65568 | tf_op jit(solution)/shard_map/ppermute | solution.py:268
  (43 shorter events, 14.7 us)
Async XLA Ops:
  0.0 1.4 %copy-start = (s32[4,7]{1,0:T(4,128)S(1)}, s32[4,7]{1,0:T(4,128)}, u32[]{:S(2)}) copy-start(s32[4,7]{1,0:T(4,128)} %refs_13_.3) | copy-start | bytes 340
  2.5 41.5 %copy-start.1 = (s32[4,7]{1,0:T(4,128)S(1)}, s32[4,7]{1,0:T(4,128)}, u32[]{:S(2)}) copy-start(s32[4,7]{1,0:T(4,128)} %refs_12_.5) | copy-start | bytes 340
  2.5 9.3 %collective-permute-start.1 = (f32[4,128,128]{2,1,0:T(8,128)S(1)}, f32[4,128,128]{2,1,0:T(8,128)S(1)}, u32[]{:S(2)}, u32[]{:S(2)}) collective-permute-start(f32[4,128,128]{2,1,0:T(8,128)S(1)} %dense0.1.refs_0_), channel_id=1, source_target_pairs={{0,2},{1,3},{2,0},{3,1},{4,6},{5,7},{6,4},{7,5},{8,10},{9,11},{10,... | collective-permute-start | bytes 786440 | tf_op jit(solution)/shard_map/ppermute | solution.py:268
  5.5 24.6 %collective-permute-start.4 = (f32[976,128]{1,0:T(8,128)S(1)}, f32[976,128]{1,0:T(8,128)S(1)}, u32[]{:S(2)}, u32[]{:S(2)}) collective-permute-start(f32[976,128]{1,0:T(8,128)S(1)} %first.1.refs_2_.refs_4_.refs_0_.refs_6_), channel_id=1, source_target_pairs={{0,8},{4,12},{8,0},{12,4},{1,9},{5,13},{9,1},{13,5},{2,10},{6,14},... | collective-permute-start | bytes 1499144 | tf_op jit(solution)/shard_map/ppermute | solution.py:268
  8.1 22.2 %collective-permute-start.3 = (f32[976,128]{1,0:T(8,128)S(1)}, f32[976,128]{1,0:T(8,128)S(1)}, u32[]{:S(2)}, u32[]{:S(2)}) collective-permute-start(f32[976,128]{1,0:T(8,128)S(1)} %first.1.refs_2_.refs_4_.refs_0_.refs_6_), channel_id=1, source_target_pairs={{0,4},{4,0},{8,12},{12,8},{1,5},{5,1},{9,13},{13,9},{2,6},{6,2},{1... | collective-permute-start | bytes 1499144 | tf_op jit(solution)/shard_map/ppermute | solution.py:268
  9.6 2.1 %collective-permute-start = (f32[4,128,128]{2,1,0:T(8,128)S(1)}, f32[4,128,128]{2,1,0:T(8,128)S(1)}, u32[]{:S(2)}, u32[]{:S(2)}) collective-permute-start(f32[4,128,128]{2,1,0:T(8,128)S(1)} %dense0.1.refs_0_), channel_id=1, source_target_pairs={{0,1},{1,0},{2,3},{3,2},{4,5},{5,4},{6,7},{7,6},{8,9},{9,8},{10,11... | collective-permute-start | bytes 786440 | tf_op jit(solution)/shard_map/ppermute | solution.py:268
  11.8 18.5 %collective-permute-start.2 = (f32[4,128,128]{2,1,0:T(8,128)S(1)}, f32[4,128,128]{2,1,0:T(8,128)S(1)}, u32[]{:S(2)}, u32[]{:S(2)}) collective-permute-start(f32[4,128,128]{2,1,0:T(8,128)S(1)} %collective-permute-done.1.refs_2_.refs_8_), channel_id=1, source_target_pairs={{0,1},{1,0},{2,3},{3,2},{4,5},{5,4},{6,7},{7,6},{8,9},{9,8},{10,11... | collective-permute-start | bytes 786440 | tf_op jit(solution)/shard_map/ppermute | solution.py:268
  31.6 30.4 %collective-permute-start.10 = (f32[19,128,128]{2,1,0:T(8,128)S(1)}, f32[19,128,128]{2,1,0:T(8,128)S(1)}, u32[]{:S(2)}, u32[]{:S(2)}) collective-permute-start(f32[19,128,128]{2,1,0:T(8,128)S(1)} %dense.1.refs_0_), channel_id=1, source_target_pairs={{0,2},{1,3},{2,0},{3,1},{4,6},{5,7},{6,4},{7,5},{8,10},{9,11},{10,... | collective-permute-start | bytes 3735560 | tf_op jit(solution)/shard_map/ppermute | solution.py:268
  32.2 11.8 %collective-permute-start.5 = (f32[976,128]{1,0:T(8,128)S(1)}, f32[976,128]{1,0:T(8,128)S(1)}, u32[]{:S(2)}, u32[]{:S(2)}) collective-permute-start(f32[976,128]{1,0:T(8,128)S(1)} %collective-permute-done.4.refs_6_.refs_2_.refs_8_), channel_id=1, source_target_pairs={{0,4},{4,0},{8,12},{12,8},{1,5},{5,1},{9,13},{13,9},{2,6},{6,2},{1... | collective-permute-start | bytes 1499144 | tf_op jit(solution)/shard_map/ppermute | solution.py:268
  45.8 29.1 %collective-permute-start.12 = (f32[832,128]{1,0:T(8,128)S(1)}, f32[832,128]{1,0:T(8,128)S(1)}, u32[]{:S(2)}, u32[]{:S(2)}) collective-permute-start(f32[832,128]{1,0:T(8,128)S(1)} %ahead0.1.refs_0_), channel_id=1, source_target_pairs={{0,2},{1,3},{2,0},{3,1},{4,6},{5,7},{6,4},{7,5},{8,10},{9,11},{10,... | collective-permute-start | bytes 1277960 | tf_op jit(solution)/shard_map/ppermute | solution.py:268
  47.4 27.8 %collective-permute-start.9 = (f32[19,128,128]{2,1,0:T(8,128)S(1)}, f32[19,128,128]{2,1,0:T(8,128)S(1)}, u32[]{:S(2)}, u32[]{:S(2)}) collective-permute-start(f32[19,128,128]{2,1,0:T(8,128)S(1)} %dense.1.refs_0_), channel_id=1, source_target_pairs={{0,1},{1,0},{2,3},{3,2},{4,5},{5,4},{6,7},{7,6},{8,9},{9,8},{10,11... | collective-permute-start | bytes 3735560 | tf_op jit(solution)/shard_map/ppermute | solution.py:268
  62.0 15.4 %collective-permute-start.11 = (f32[19,128,128]{2,1,0:T(8,128)S(1)}, f32[19,128,128]{2,1,0:T(8,128)S(1)}, u32[]{:S(2)}, u32[]{:S(2)}) collective-permute-start(f32[19,128,128]{2,1,0:T(8,128)S(1)} %collective-permute-done.10.refs_2_), channel_id=1, source_target_pairs={{0,1},{1,0},{2,3},{3,2},{4,5},{5,4},{6,7},{7,6},{8,9},{9,8},{10,11... | collective-permute-start | bytes 3735560 | tf_op jit(solution)/shard_map/ppermute | solution.py:268
  62.0 10.2 %collective-permute-start.6 = (f32[352,128]{1,0:T(8,128)S(1)}, f32[352,128]{1,0:T(8,128)S(1)}, u32[]{:S(2)}, u32[]{:S(2)}) collective-permute-start(f32[352,128]{1,0:T(8,128)S(1)} %early.1.refs_4_.refs_0_), channel_id=1, source_target_pairs={{0,4},{4,0},{8,12},{12,8},{1,5},{5,1},{9,13},{13,9},{2,6},{6,2},{1... | collective-permute-start | bytes 540680 | tf_op jit(solution)/shard_map/ppermute | solution.py:268
  63.5 11.5 %collective-permute-start.7 = (f32[352,128]{1,0:T(8,128)S(1)}, f32[352,128]{1,0:T(8,128)S(1)}, u32[]{:S(2)}, u32[]{:S(2)}) collective-permute-start(f32[352,128]{1,0:T(8,128)S(1)} %early.1.refs_4_.refs_0_), channel_id=1, source_target_pairs={{0,8},{4,12},{8,0},{12,4},{1,9},{5,13},{9,1},{13,5},{2,10},{6,14},... | collective-permute-start | bytes 540680 | tf_op jit(solution)/shard_map/ppermute | solution.py:268
  75.0 2.4 %collective-permute-start.13 = (f32[1664,128]{1,0:T(8,128)S(1)}, f32[1664,128]{1,0:T(8,128)S(1)}, u32[]{:S(2)}, u32[]{:S(2)}) collective-permute-start(f32[1664,128]{1,0:T(8,128)S(1)} %aheads0.1.refs_4_), channel_id=1, source_target_pairs={{0,1},{1,0},{2,3},{3,2},{4,5},{5,4},{6,7},{7,6},{8,9},{9,8},{10,11... | collective-permute-start | bytes 2555912 | tf_op jit(solution)/shard_map/ppermute | solution.py:268
  75.1 7.0 %collective-permute-start.8 = (f32[352,128]{1,0:T(8,128)S(1)}, f32[352,128]{1,0:T(8,128)S(1)}, u32[]{:S(2)}, u32[]{:S(2)}) collective-permute-start(f32[352,128]{1,0:T(8,128)S(1)} %collective-permute-done.7.refs_3_.refs_2_), channel_id=1, source_target_pairs={{0,4},{4,0},{8,12},{12,8},{1,5},{5,1},{9,13},{13,9},{2,6},{6,2},{1... | collective-permute-start | bytes 540680 | tf_op jit(solution)/shard_map/ppermute | solution.py:268
  83.8 12.1 %collective-permute-start.17 = (f32[896,128]{1,0:T(8,128)S(1)}, f32[896,128]{1,0:T(8,128)S(1)}, u32[]{:S(2)}, u32[]{:S(2)}) collective-permute-start(f32[896,128]{1,0:T(8,128)S(1)} %ahead1.1.refs_0_), channel_id=1, source_target_pairs={{0,2},{1,3},{2,0},{3,1},{4,6},{5,7},{6,4},{7,5},{8,10},{9,11},{10,... | collective-permute-start | bytes 1376264 | tf_op jit(solution)/shard_map/ppermute | solution.py:268
  84.4 9.4 %collective-permute-start.14 = (f32[368,128]{1,0:T(8,128)S(1)}, f32[368,128]{1,0:T(8,128)S(1)}, u32[]{:S(2)}, u32[]{:S(2)}) collective-permute-start(f32[368,128]{1,0:T(8,128)S(1)} %get-tuple-element.23.refs_4_.refs_0_), channel_id=1, source_target_pairs={{0,4},{4,0},{8,12},{12,8},{1,5},{5,1},{9,13},{13,9},{2,6},{6,2},{1... | collective-permute-start | bytes 565256 | tf_op jit(solution)/shard_map/ppermute | solution.py:268
  84.7 10.9 %collective-permute-start.15 = (f32[368,128]{1,0:T(8,128)S(1)}, f32[368,128]{1,0:T(8,128)S(1)}, u32[]{:S(2)}, u32[]{:S(2)}) collective-permute-start(f32[368,128]{1,0:T(8,128)S(1)} %get-tuple-element.23.refs_4_.refs_0_), channel_id=1, source_target_pairs={{0,8},{4,12},{8,0},{12,4},{1,9},{5,13},{9,1},{13,5},{2,10},{6,14},... | collective-permute-start | bytes 565256 | tf_op jit(solution)/shard_map/ppermute | solution.py:268
  96.0 2.5 %collective-permute-start.18 = (f32[1792,128]{1,0:T(8,128)S(1)}, f32[1792,128]{1,0:T(8,128)S(1)}, u32[]{:S(2)}, u32[]{:S(2)}) collective-permute-start(f32[1792,128]{1,0:T(8,128)S(1)} %aheads1.1.refs_4_), channel_id=1, source_target_pairs={{0,1},{1,0},{2,3},{3,2},{4,5},{5,4},{6,7},{7,6},{8,9},{9,8},{10,11... | collective-permute-start | bytes 2752520 | tf_op jit(solution)/shard_map/ppermute | solution.py:268
  96.1 7.1 %collective-permute-start.16 = (f32[368,128]{1,0:T(8,128)S(1)}, f32[368,128]{1,0:T(8,128)S(1)}, u32[]{:S(2)}, u32[]{:S(2)}) collective-permute-start(f32[368,128]{1,0:T(8,128)S(1)} %collective-permute-done.15.refs_3_.refs_2_), channel_id=1, source_target_pairs={{0,4},{4,0},{8,12},{12,8},{1,5},{5,1},{9,13},{13,9},{2,6},{6,2},{1... | collective-permute-start | bytes 565256 | tf_op jit(solution)/shard_map/ppermute | solution.py:268
  104.0 12.9 %collective-permute-start.22 = (f32[960,128]{1,0:T(8,128)S(1)}, f32[960,128]{1,0:T(8,128)S(1)}, u32[]{:S(2)}, u32[]{:S(2)}) collective-permute-start(f32[960,128]{1,0:T(8,128)S(1)} %ahead2.1.refs_0_), channel_id=1, source_target_pairs={{0,2},{1,3},{2,0},{3,1},{4,6},{5,7},{6,4},{7,5},{8,10},{9,11},{10,... | collective-permute-start | bytes 1474568 | tf_op jit(solution)/shard_map/ppermute | solution.py:268
  105.2 4.5 %collective-permute-start.19 = (f32[128,128]{1,0:T(8,128)S(1)}, f32[128,128]{1,0:T(8,128)S(1)}, u32[]{:S(2)}, u32[]{:S(2)}) collective-permute-start(f32[128,128]{1,0:T(8,128)S(1)} %get-tuple-element.28.refs_4_.refs_0_), channel_id=1, source_target_pairs={{0,4},{4,0},{8,12},{12,8},{1,5},{5,1},{9,13},{13,9},{2,6},{6,2},{1... | collective-permute-start | bytes 196616 | tf_op jit(solution)/shard_map/ppermute | solution.py:268
  105.4 5.5 %collective-permute-start.20 = (f32[128,128]{1,0:T(8,128)S(1)}, f32[128,128]{1,0:T(8,128)S(1)}, u32[]{:S(2)}, u32[]{:S(2)}) collective-permute-start(f32[128,128]{1,0:T(8,128)S(1)} %get-tuple-element.28.refs_4_.refs_0_), channel_id=1, source_target_pairs={{0,8},{4,12},{8,0},{12,4},{1,9},{5,13},{9,1},{13,5},{2,10},{6,14},... | collective-permute-start | bytes 196616 | tf_op jit(solution)/shard_map/ppermute | solution.py:268
  116.9 2.6 %collective-permute-start.23 = (f32[1920,128]{1,0:T(8,128)S(1)}, f32[1920,128]{1,0:T(8,128)S(1)}, u32[]{:S(2)}, u32[]{:S(2)}) collective-permute-start(f32[1920,128]{1,0:T(8,128)S(1)} %aheads2.1.refs_4_), channel_id=1, source_target_pairs={{0,1},{1,0},{2,3},{3,2},{4,5},{5,4},{6,7},{7,6},{8,9},{9,8},{10,11... | collective-permute-start | bytes 2949128 | tf_op jit(solution)/shard_map/ppermute | solution.py:268
  117.0 6.3 %collective-permute-start.21 = (f32[128,128]{1,0:T(8,128)S(1)}, f32[128,128]{1,0:T(8,128)S(1)}, u32[]{:S(2)}, u32[]{:S(2)}) collective-permute-start(f32[128,128]{1,0:T(8,128)S(1)} %get-tuple-element.28.refs_4_.refs_0_), channel_id=1, source_target_pairs={{0,12},{4,8},{8,4},{12,0},{1,13},{5,9},{9,5},{13,1},{2,14},{6,10},... | collective-permute-start | bytes 196616 | tf_op jit(solution)/shard_map/ppermute | solution.py:268
  124.0 4.7 %collective-permute-start.24 = (f32[128,128]{1,0:T(8,128)S(1)}, f32[128,128]{1,0:T(8,128)S(1)}, u32[]{:S(2)}, u32[]{:S(2)}) collective-permute-start(f32[128,128]{1,0:T(8,128)S(1)} %get-tuple-element.33.refs_0_), channel_id=1, source_target_pairs={{0,4},{4,0},{8,12},{12,8},{1,5},{5,1},{9,13},{13,9},{2,6},{6,2},{1... | collective-permute-start | bytes 196616 | tf_op jit(solution)/shard_map/ppermute | solution.py:268
  124.1 7.5 %collective-permute-start.25 = (f32[128,128]{1,0:T(8,128)S(1)}, f32[128,128]{1,0:T(8,128)S(1)}, u32[]{:S(2)}, u32[]{:S(2)}) collective-permute-start(f32[128,128]{1,0:T(8,128)S(1)} %get-tuple-element.33.refs_0_), channel_id=1, source_target_pairs={{0,8},{4,12},{8,0},{12,4},{1,9},{5,13},{9,1},{13,5},{2,10},{6,14},... | collective-permute-start | bytes 196616 | tf_op jit(solution)/shard_map/ppermute | solution.py:268
  126.6 6.2 %collective-permute-start.26 = (f32[128,128]{1,0:T(8,128)S(1)}, f32[128,128]{1,0:T(8,128)S(1)}, u32[]{:S(2)}, u32[]{:S(2)}) collective-permute-start(f32[128,128]{1,0:T(8,128)S(1)} %get-tuple-element.33.refs_0_), channel_id=1, source_target_pairs={{0,12},{4,8},{8,4},{12,0},{1,13},{5,9},{9,5},{13,1},{2,14},{6,10},... | collective-permute-start | bytes 196616 | tf_op jit(solution)/shard_map/ppermute | solution.py:268

commit v8 on v7

--- a/solution.py
+++ b/solution.py
@@ -86,24 +86,27 @@
     return (out[:rows, :cols] + (out[:rows, cols:] + out[rows:, :cols])) + out[rows:, cols:]
 
 
-def fill_ahead(out_ref, count, inv_ref, right_ref):
+def fill_ahead(out_ref, begin, count, inv_ref, right_ref):
     nb = inv_ref.shape[1]
     share = right_ref.shape[2] // lax.axis_size("pcol")
     at = pl.multiple_of(lax.axis_index("pcol") * share, share)
-    out_ref[:nb] = inv_ref[0]
+    out_ref[begin : begin + nb] = inv_ref[0]
     for col in range(count):
-        place = nb + col * share
+        place = begin + nb + col * share
         out_ref[place : place + share] = right_ref[0, col, pl.ds(at, share), :]
 
 
-def first_kernel(prev, ahead, known_ref, right_ref, right1_ref, inv_ref, sent_ref):
+def first_kernel(prev, room, known_ref, *refs):
+    right_ref, right1_ref, right2_ref, inv_ref, inv1_ref, sent_ref = refs
     nb, rank_pad = known_ref.shape[1], right_ref.shape[2]
-    fill_ahead(sent_ref, prev + 1, inv_ref, right1_ref)
+    sent_ref[nb:room] = jnp.zeros((room - nb, sent_ref.shape[1]), jnp.float32)
+    fill_ahead(sent_ref, 0, prev + 1, inv_ref, right1_ref)
+    fill_ahead(sent_ref, room, prev + 2, inv1_ref, right2_ref)
     for col in range(prev):
         known = known_ref[col]
-        at = ahead + col * nb
+        at = 2 * room + col * nb
         sent_ref[at : at + nb] = known
-        at = ahead + prev * nb + col * rank_pad
+        at = 2 * room + prev * nb + col * rank_pad
         sent_ref[at : at + rank_pad] = dot_halves(halves(right_ref[0, col], 0), halves(known, 1))
 
 
@@ -154,7 +157,7 @@
     left2 = halves(jnp.concatenate(lefts, axis=0), 1)
     coeff2 = halves(jnp.concatenate(coeffs, axis=0), 1)
     out_ref[ahead:] = total - dot_halves(left2, coeff2, OVER_ROWS)
-    fill_ahead(out_ref, counts, inv_ref, right_ref)
+    fill_ahead(out_ref, 0, counts, inv_ref, right_ref)
 
 
 def prepare_kernel(n, prev, step, first, size, known_at, last, *refs):
@@ -217,15 +220,12 @@
         scratch[pl.ds(pl.multiple_of((own ^ slot) * nb, nb), nb), :] = ref[at : at + nb]
 
 
-def step_kernel(n, at, ahead, counts, *refs):
-    inverse_ref, strip_ref, base_ref, *more, out_ref, solved_ref, scratch = refs[n:]
-    nb = base_ref.shape[0]
-    place_slots(n, at, nb, refs[:n], scratch)
+def step_kernel(n, at, *refs):
+    inverse_ref, strip_ref, base_ref, out_ref, solved_ref, scratch = refs[n:]
+    place_slots(n, at, base_ref.shape[0], refs[:n], scratch)
     solved = dot_halves(inverse_ref[...], halves(scratch[...], 1))
     solved_ref[...] = solved
-    out_ref[ahead:] = base_ref[...] - dot_halves(strip_ref[0], halves(solved, 1))
-    if ahead:
-        fill_ahead(out_ref, counts, *more)
+    out_ref[...] = base_ref[...] - dot_halves(strip_ref[0], halves(solved, 1))
 
 
 def last_kernel(n, *refs):
@@ -315,28 +315,30 @@
     share = rank_pad // n
     ranks_flags = [(tile_ranks, smem), (dense_flags, smem)]
     source_room = pltpu.VMEM((n * nb, rhs), f32)
-    aheads = [nb + (prev + step) * share for step in range(1, steps)] + [0]
+    room1, room2 = nb + (prev + 2) * share, nb + (prev + 3) * share
 
     def over_cols(own):
         far = shift(own, "pcol", 2)
         return [own, shift(own, "pcol", 1), far, shift(far, "pcol", 1)]
 
-    def shared_ahead(slots, ahead, step, after, after_far):
-        head = spec_of((ahead, nb))
-        shape = shaped(n * ahead, nb)
-        own = run(stack_kernel, f"ahead{step}", shape, [(ref, head) for ref in slots], after=after)
-        far = shift(own, "pcol", 2)
-        shape = shaped(2 * n * ahead, nb)
-        pairs = [whole_of(own), whole_of(far)]
-        both = run(stack_kernel, f"aheads{step}", shape, pairs, after=after_far)
+    def ahead_far(slots, height, place, name, after):
+        head = pl.BlockSpec((height, nb), lambda i: (place, 0))
+        shape = shaped(n * height, nb)
+        own = run(stack_kernel, name, shape, [(ref, head) for ref in slots], after=after)
+        return [own, shift(own, "pcol", 2)]
+
+    def ahead_near(halfs, name, after):
+        shape = shaped(2 * halfs[0].shape[0], nb)
+        both = run(stack_kernel, name, shape, [whole_of(value) for value in halfs], after=after)
         return [both, shift(both, "pcol", 1)]
 
     sent = run(
-        functools.partial(first_kernel, prev, aheads[0]),
+        functools.partial(first_kernel, prev, room1),
         "first",
-        shaped(aheads[0] + prev * (nb + rank_pad), rhs),
+        shaped(2 * room1 + prev * (nb + rank_pad), rhs),
         [whole_of(pinned(earlier))]
-        + [blocks_of(right_t, 0), blocks_of(right_t, 1), blocks_of(inverse_diag, 0)],
+        + [blocks_of(right_t, step) for step in range(3)]
+        + [blocks_of(inverse_diag, step) for step in range(2)],
     )
     known = over_rows_forwarded(sent)
     own = run(
@@ -356,32 +358,27 @@
         [(dense_flags, smem)]
         + [blocks_of(dense_tiles, step) for step in range(1, steps)]
         + [blocks_of(inverse_diag, steps - 1)],
-        after=known[1:3] + strips0[1:],
+        after=[],
     )
     dense = over_cols(own)
 
     pending = run(
-        functools.partial(early_kernel, n, prev, aheads[0], aheads[1], prev + 2),
+        functools.partial(early_kernel, n, prev, 2 * room1, room2, prev + 3),
         "early",
-        shaped(aheads[1] + nb, rhs),
+        shaped(room2 + nb, rhs),
         [whole_of(value) for value in strips0 + known]
         + ranks_flags
         + [blocks_of(left_t, 0), blocks_of(right_side, 0)]
-        + [blocks_of(inverse_diag, 1), blocks_of(right_t, 2)],
+        + [blocks_of(inverse_diag, 2), blocks_of(right_t, 3)],
         [source_room],
     )
-    slots, solved = known, []
-    for step in range(steps - 1):
-        last = step + 2 == steps
-        came = slots
-        slots = over_rows_forwarded(pending) if aheads[step + 1] else over_rows(pending)
-        later = shared_ahead(came, aheads[step], step, [pending], slots[1:3])
-        tiles = prev + step + 1
-        first = sum(count for row, count in rows[:-1] if row <= step)
-        base, strip, inverse = run(
-            functools.partial(
-                prepare_kernel, n, prev, step + 1, first, size, aheads[0], last
-            ),
+
+    def prepare(step, later, solved):
+        last = step + 1 == steps
+        tiles = prev + step
+        first = sum(count for row, count in rows[:-1] if row < step)
+        return run(
+            functools.partial(prepare_kernel, n, prev, step, first, size, 2 * room1, last),
             f"prepare{step}",
             [
                 shaped(nb, rhs),
@@ -390,28 +387,43 @@
             ],
             [whole_of(value) for value in dense + later + known + solved]
             + ranks_flags
-            + [blocks_of(left_t, step + 1), blocks_of(right_side, step + 1)],
+            + [blocks_of(left_t, step), blocks_of(right_side, step)],
             [source_room, pltpu.VMEM((tiles, rank_pad, n * nb), f32)],
         )
-        ahead = aheads[step + 2] if step + 2 < len(aheads) else 0
-        more = [blocks_of(inverse_diag, step + 2), blocks_of(right_t, step + 3)] if ahead else []
-        pending, block = run(
-            functools.partial(step_kernel, n, aheads[step + 1], ahead, tiles + 2),
+
+    def solve(step, at, slots, prepared):
+        base, strip, inverse = prepared
+        return run(
+            functools.partial(step_kernel, n, at),
             f"step{step}",
-            [shaped(ahead + nb, rhs), shaped(n * nb, rhs)],
+            [shaped(nb, rhs), shaped(n * nb, rhs)],
             [whole_of(value) for value in slots + [inverse]]
-            + [(strip, spec_of((1, 2 * nb, n * nb), (0, 0, 0))), whole_of(base)]
-            + more,
+            + [(strip, spec_of((1, 2 * nb, n * nb), (0, 0, 0))), whole_of(base)],
             [source_room],
         )
-        solved.append(block)
+
+    slots = over_rows_forwarded(pending)
+    later1 = ahead_far(known, room1, 0, "ahead1", [pending])
+    later1 = ahead_near(later1, "aheads1", slots[1:3])
+    later2 = ahead_far(known, room1, 1, "ahead2", slots[1:3])
+    pending1, solved0 = solve(0, room2, slots, prepare(1, later1, []))
+
+    later3 = ahead_far(slots, room2, 0, "ahead3", [pending1])
+    later2 = ahead_near(later2, "aheads2", [pending1])
+    slots = over_rows(pending1)
+    pending2, solved1 = solve(1, 0, slots, prepare(2, later2, [solved0]))
+
+    slots = over_rows(pending2)
+    later3 = ahead_near(later3, "aheads3", [pending2])
+    prepared = prepare(3, later3, [solved0, solved1])
+    pending3, solved2 = solve(2, 0, slots, prepared)
     return run(
         functools.partial(last_kernel, n),
         "last",
         shaped(steps, nb, rhs),
-        [whole_of(value) for value in over_rows(pending)]
-        + [(strip, spec_of((1, 2 * nb, n * nb), (1, 0, 0)))]
-        + [whole_of(value) for value in solved],
+        [whole_of(value) for value in over_rows(pending3)]
+        + [(prepared[1], spec_of((1, 2 * nb, n * nb), (1, 0, 0)))]
+        + [whole_of(value) for value in (solved0, solved1, solved2)],
         [source_room],
     )
 

time: 134 us -> 113 us (0.84)
  waiting for transfers between devices: 86.3 us -> 64.5 us
  starting transfers between devices: 28.6 us -> 30.3 us
    ppermute x27, waiting for transfers between devices: 86.3 us -> 64.5 us  [shift(): return lax.ppermute(value, axis, [(i, i ^ step) for i in range(n)])]
    ppermute x27, starting transfers between devices: 28.6 us -> 30.3 us  [shift(): return lax.ppermute(value, axis, [(i, i ^ step) for i in range(n)])]
  transfers between devices with their start and end apart: 27 -> 27, of which waited for: 22 -> 15; matrix products, arithmetic and copies ran while one was open for 0% -> 0% of each run, Pallas kernels for 8% -> 13%
where the time goes in v8:
time: 113 us
  waiting for transfers between devices  64.5 us (57%)
  starting transfers between devices  30.3 us (27%)
  Pallas kernels  17.7 us (16%)
    ppermute x27, waiting for transfers between devices, shift(): return lax.ppermute(value, axis, [(i, i ^ step) for i in range(n)])  64.5 us
    ppermute x27, starting transfers between devices, shift(): return lax.ppermute(value, axis, [(i, i ^ step) for i in range(n)])  30.3 us
    pallas_call x17, Pallas kernels, call(): pl.pallas_call(body, grid=(1,), out_shape=shapes, in_specs=specs + [any_s...  17.7 us
  transfers between devices with their start and end apart: 27, of which 15 were waited for; matrix products, arithmetic and copies ran while one was open for 0% of the time, Pallas kernels for 13%

profile of v8, /device:TPU:0, one launch (start us, length us, event | category | flops | bytes accessed | tf_op | source)
XLA Modules:
  0.0 112.8 jit_solution(5257484378274361414)
XLA Ops:
  0.0 1.5 %first.1.refs_2_.refs_4_.refs_0_.refs_6_ = f32[1216,128]{1,0:T(8,128)S(1)} custom-call(f32[4,128,128]{2,1,0:T(8,128)} %refs_0_.3, f32[4,7,64,128]{3,2,1,0:T(8,128)} %bitcast.6, f32[4,7,64,128]{3,2,1,0:T(8,128)} %bitcast.7, f32[4,7,64,128]{3,2,1,0:T(8,128)} %bitcast.8, f32[4,128,128]{2,1,0:T(8,128)} %refs_4_.3, f32[4,128,128]{2,1,0:T(8,128)} %refs_4_.3), custom_call_target="tpu_custom_call" | custom-call | tf_op jit(solution)/shard_map/first/pallas_call | solution.py:294
  1.5 4.1 %collective-permute-start.4 = (f32[1216,128]{1,0:T(8,128)S(1)}, f32[1216,128]{1,0:T(8,128)S(1)}, u32[]{:S(2)}, u32[]{:S(2)}) collective-permute-start(f32[1216,128]{1,0:T(8,128)S(1)} %first.1.refs_2_.refs_4_.refs_0_.refs_6_), channel_id=1, source_target_pairs={{0,8},{4,12},{8,0},{12,4},{1,9},{5,13},{9,1},{13,5},{2,10},{6,14},... | collective-permute-start | bytes 1867784 | tf_op jit(solution)/shard_map/ppermute | solution.py:268
  5.6 1.4 %dense.1.refs_0_ = f32[19,128,128]{2,1,0:T(8,128)S(1)} custom-call(s32[4,7]{1,0:T(4,128)S(1)} %copy-done, f32[4,7,128,128]{3,2,1,0:T(8,128)} %refs_3_.1, f32[4,7,128,128]{3,2,1,0:T(8,128)} %refs_3_.1, f32[4,7,128,128]{3,2,1,0:T(8,128)} %refs_3_.1, f32[4,128,128]{2,1,0:T(8,128)} %refs_4_.3), custom_call_target="tpu_custom_call" | custom-call | tf_op jit(solution)/shard_map/dense/pallas_call | solution.py:294
  7.0 1.6 %collective-permute-start.10 = (f32[19,128,128]{2,1,0:T(8,128)S(1)}, f32[19,128,128]{2,1,0:T(8,128)S(1)}, u32[]{:S(2)}, u32[]{:S(2)}) collective-permute-start(f32[19,128,128]{2,1,0:T(8,128)S(1)} %dense.1.refs_0_), channel_id=1, source_target_pairs={{0,2},{1,3},{2,0},{3,1},{4,6},{5,7},{6,4},{7,5},{8,10},{9,11},{10,... | collective-permute-start | bytes 3735560 | tf_op jit(solution)/shard_map/ppermute | solution.py:268
  8.6 1.6 %collective-permute-start.3 = (f32[1216,128]{1,0:T(8,128)S(1)}, f32[1216,128]{1,0:T(8,128)S(1)}, u32[]{:S(2)}, u32[]{:S(2)}) collective-permute-start(f32[1216,128]{1,0:T(8,128)S(1)} %first.1.refs_2_.refs_4_.refs_0_.refs_6_), channel_id=1, source_target_pairs={{0,4},{4,0},{8,12},{12,8},{1,5},{5,1},{9,13},{13,9},{2,6},{6,2},{1... | collective-permute-start | bytes 1867784 | tf_op jit(solution)/shard_map/ppermute | solution.py:268
  10.2 22.9 %collective-permute-done.4.refs_6_.refs_2_.refs_8_ = f32[1216,128]{1,0:T(8,128)S(1)} collective-permute-done((f32[1216,128]{1,0:T(8,128)S(1)}, f32[1216,128]{1,0:T(8,128)S(1)}, u32[]{:S(2)}, u32[]{:S(2)}) %collective-permute-start.4) | collective-permute-done | bytes 622624 | tf_op jit(solution)/shard_map/ppermute | solution.py:268
  33.7 1.0 dense0.1.refs_0_
  34.8 1.6 %collective-permute-start.1 = (f32[4,128,128]{2,1,0:T(8,128)S(1)}, f32[4,128,128]{2,1,0:T(8,128)S(1)}, u32[]{:S(2)}, u32[]{:S(2)}) collective-permute-start(f32[4,128,128]{2,1,0:T(8,128)S(1)} %dense0.1.refs_0_), channel_id=1, source_target_pairs={{0,2},{1,3},{2,0},{3,1},{4,6},{5,7},{6,4},{7,5},{8,10},{9,11},{10,... | collective-permute-start | bytes 786440 | tf_op jit(solution)/shard_map/ppermute | solution.py:268
  36.4 6.5 %collective-permute-done.1.refs_2_ = f32[4,128,128]{2,1,0:T(8,128)S(1)} collective-permute-done((f32[4,128,128]{2,1,0:T(8,128)S(1)}, f32[4,128,128]{2,1,0:T(8,128)S(1)}, u32[]{:S(2)}, u32[]{:S(2)}) %collective-permute-start.1) | collective-permute-done | bytes 262176 | tf_op jit(solution)/shard_map/ppermute | solution.py:268
  42.8 1.5 %collective-permute-done.2.refs_3_ = f32[4,128,128]{2,1,0:T(8,128)S(1)} collective-permute-done((f32[4,128,128]{2,1,0:T(8,128)S(1)}, f32[4,128,128]{2,1,0:T(8,128)S(1)}, u32[]{:S(2)}, u32[]{:S(2)}) %collective-permute-start.2) | collective-permute-done | bytes 262176 | tf_op jit(solution)/shard_map/ppermute | solution.py:268
  44.4 5.0 %collective-permute-done.5.refs_7_.refs_3_.refs_9_ = f32[1216,128]{1,0:T(8,128)S(1)} collective-permute-done((f32[1216,128]{1,0:T(8,128)S(1)}, f32[1216,128]{1,0:T(8,128)S(1)}, u32[]{:S(2)}, u32[]{:S(2)}) %collective-permute-start.5) | collective-permute-done | bytes 622624 | tf_op jit(solution)/shard_map/ppermute | solution.py:268
  49.3 1.8 %early.1.refs_4_.refs_0_ = f32[368,128]{1,0:T(8,128)S(1)} custom-call(f32[4,128,128]{2,1,0:T(8,128)S(1)} %dense0.1.refs_0_, f32[4,128,128]{2,1,0:T(8,128)S(1)} %collective-permute-done.refs_1_, f32[4,128,128]{2,1,0:T(8,128)S(1)} %collective-permute-done.1.refs_2_, f32[4,128,128]{2,1,0:T(8,128)S(1)} %collective-permute-done.2.refs_3_, ...), custom_call_target="tpu_custom_call" | custom-call | tf_op jit(solution)/shard_map/early/pallas_call | solution.py:294
  52.4 1.3 %collective-permute-start.6 = (f32[368,128]{1,0:T(8,128)S(1)}, f32[368,128]{1,0:T(8,128)S(1)}, u32[]{:S(2)}, u32[]{:S(2)}) collective-permute-start(f32[368,128]{1,0:T(8,128)S(1)} %early.1.refs_4_.refs_0_), channel_id=1, source_target_pairs={{0,4},{4,0},{8,12},{12,8},{1,5},{5,1},{9,13},{13,9},{2,6},{6,2},{1... | collective-permute-start | bytes 565256 | tf_op jit(solution)/shard_map/ppermute | solution.py:268
  53.6 3.4 %collective-permute-start.7 = (f32[368,128]{1,0:T(8,128)S(1)}, f32[368,128]{1,0:T(8,128)S(1)}, u32[]{:S(2)}, u32[]{:S(2)}) collective-permute-start(f32[368,128]{1,0:T(8,128)S(1)} %early.1.refs_4_.refs_0_), channel_id=1, source_target_pairs={{0,8},{4,12},{8,0},{12,4},{1,9},{5,13},{9,1},{13,5},{2,10},{6,14},... | collective-permute-start | bytes 565256 | tf_op jit(solution)/shard_map/ppermute | solution.py:268
  57.0 5.8 %collective-permute-done.6.refs_2_.refs_1_.refs_4_ = f32[368,128]{1,0:T(8,128)S(1)} collective-permute-done((f32[368,128]{1,0:T(8,128)S(1)}, f32[368,128]{1,0:T(8,128)S(1)}, u32[]{:S(2)}, u32[]{:S(2)}) %collective-permute-start.6) | collective-permute-done | bytes 188448 | tf_op jit(solution)/shard_map/ppermute | solution.py:268
  62.8 2.9 %collective-permute-done.7.refs_3_.refs_2_.refs_5_ = f32[368,128]{1,0:T(8,128)S(1)} collective-permute-done((f32[368,128]{1,0:T(8,128)S(1)}, f32[368,128]{1,0:T(8,128)S(1)}, u32[]{:S(2)}, u32[]{:S(2)}) %collective-permute-start.7) | collective-permute-done | bytes 188448 | tf_op jit(solution)/shard_map/ppermute | solution.py:268
  66.9 1.5 %collective-permute-done.13.refs_5_ = f32[1792,128]{1,0:T(8,128)S(1)} collective-permute-done((f32[1792,128]{1,0:T(8,128)S(1)}, f32[1792,128]{1,0:T(8,128)S(1)}, u32[]{:S(2)}, u32[]{:S(2)}) %collective-permute-start.13) | collective-permute-done | bytes 917536 | tf_op jit(solution)/shard_map/ppermute | solution.py:268
  68.3 2.6 %prepare1.1 = (f32[128,128]{1,0:T(8,128)S(1)}, bf16[1,256,512]{2,1,0:T(8,128)(2,1)S(1)}, bf16[1024,512]{1,0:T(8,128)(2,1)S(1)}) custom-call(f32[19,128,128]{2,1,0:T(8,128)S(1)} %dense.1.refs_0_, f32[19,128,128]{2,1,0:T(8,128)S(1)} %collective-permute-done.9.refs_1_, f32[19,128,128]{2,1,0:T(8,128)S(1)} %collective-permute-done.10.refs_2_, ...), custom_call_target="tpu_custom_call" | custom-call | tf_op jit(solution)/shard_map/prepare1/pallas_call | solution.py:294
  70.9 2.4 %collective-permute-done.8.refs_3_ = f32[368,128]{1,0:T(8,128)S(1)} collective-permute-done((f32[368,128]{1,0:T(8,128)S(1)}, f32[368,128]{1,0:T(8,128)S(1)}, u32[]{:S(2)}, u32[]{:S(2)}) %collective-permute-start.8) | collective-permute-done | bytes 188448 | tf_op jit(solution)/shard_map/ppermute | solution.py:268
  74.1 4.8 %collective-permute-done.17.refs_1_ = f32[896,128]{1,0:T(8,128)S(1)} collective-permute-done((f32[896,128]{1,0:T(8,128)S(1)}, f32[896,128]{1,0:T(8,128)S(1)}, u32[]{:S(2)}, u32[]{:S(2)}) %collective-permute-start.17) | collective-permute-done | bytes 458784 | tf_op jit(solution)/shard_map/ppermute | solution.py:268
  80.0 2.7 %collective-permute-start.15 = (f32[128,128]{1,0:T(8,128)S(1)}, f32[128,128]{1,0:T(8,128)S(1)}, u32[]{:S(2)}, u32[]{:S(2)}) collective-permute-start(f32[128,128]{1,0:T(8,128)S(1)} %get-tuple-element.23.refs_2_.refs_0_.refs_4_), channel_id=1, source_target_pairs={{0,8},{4,12},{8,0},{12,4},{1,9},{5,13},{9,1},{13,5},{2,10},{6,14},... | collective-permute-start | bytes 196616 | tf_op jit(solution)/shard_map/ppermute | solution.py:268
  82.7 1.4 %collective-permute-start.16 = (f32[128,128]{1,0:T(8,128)S(1)}, f32[128,128]{1,0:T(8,128)S(1)}, u32[]{:S(2)}, u32[]{:S(2)}) collective-permute-start(f32[128,128]{1,0:T(8,128)S(1)} %get-tuple-element.23.refs_2_.refs_0_.refs_4_), channel_id=1, source_target_pairs={{0,12},{4,8},{8,4},{12,0},{1,13},{5,9},{9,5},{13,1},{2,14},{6,10},... | collective-permute-start | bytes 196616 | tf_op jit(solution)/shard_map/ppermute | solution.py:268
  84.1 2.8 %prepare2.1 = (f32[128,128]{1,0:T(8,128)S(1)}, bf16[1,256,512]{2,1,0:T(8,128)(2,1)S(1)}, bf16[1024,512]{1,0:T(8,128)(2,1)S(1)}) custom-call(f32[19,128,128]{2,1,0:T(8,128)S(1)} %dense.1.refs_0_, f32[19,128,128]{2,1,0:T(8,128)S(1)} %collective-permute-done.9.refs_1_, f32[19,128,128]{2,1,0:T(8,128)S(1)} %collective-permute-done.10.refs_2_, ...), custom_call_target="tpu_custom_call" | custom-call | tf_op jit(solution)/shard_map/prepare2/pallas_call | solution.py:294
  89.6 3.2 %collective-permute-done.22.refs_1_ = f32[960,128]{1,0:T(8,128)S(1)} collective-permute-done((f32[960,128]{1,0:T(8,128)S(1)}, f32[960,128]{1,0:T(8,128)S(1)}, u32[]{:S(2)}, u32[]{:S(2)}) %collective-permute-start.22) | collective-permute-done | bytes 491552 | tf_op jit(solution)/shard_map/ppermute | solution.py:268
  93.3 2.7 %collective-permute-start.20 = (f32[128,128]{1,0:T(8,128)S(1)}, f32[128,128]{1,0:T(8,128)S(1)}, u32[]{:S(2)}, u32[]{:S(2)}) collective-permute-start(f32[128,128]{1,0:T(8,128)S(1)} %get-tuple-element.28.refs_2_.refs_0_), channel_id=1, source_target_pairs={{0,8},{4,12},{8,0},{12,4},{1,9},{5,13},{9,1},{13,5},{2,10},{6,14},... | collective-permute-start | bytes 196616 | tf_op jit(solution)/shard_map/ppermute | solution.py:268
  96.0 1.4 %collective-permute-start.21 = (f32[128,128]{1,0:T(8,128)S(1)}, f32[128,128]{1,0:T(8,128)S(1)}, u32[]{:S(2)}, u32[]{:S(2)}) collective-permute-start(f32[128,128]{1,0:T(8,128)S(1)} %get-tuple-element.28.refs_2_.refs_0_), channel_id=1, source_target_pairs={{0,12},{4,8},{8,4},{12,0},{1,13},{5,9},{9,5},{13,1},{2,14},{6,10},... | collective-permute-start | bytes 196616 | tf_op jit(solution)/shard_map/ppermute | solution.py:268
  97.4 3.2 %prepare3.1 = (f32[128,128]{1,0:T(8,128)S(1)}, bf16[2,256,512]{2,1,0:T(8,128)(2,1)S(1)}, bf16[1024,512]{1,0:T(8,128)(2,1)S(1)}) custom-call(f32[19,128,128]{2,1,0:T(8,128)S(1)} %dense.1.refs_0_, f32[19,128,128]{2,1,0:T(8,128)S(1)} %collective-permute-done.9.refs_1_, f32[19,128,128]{2,1,0:T(8,128)S(1)} %collective-permute-done.10.refs_2_, ...), custom_call_target="tpu_custom_call" | custom-call | tf_op jit(solution)/shard_map/prepare3/pallas_call | solution.py:294
  100.6 1.5 %collective-permute-done.21.refs_3_ = f32[128,128]{1,0:T(8,128)S(1)} collective-permute-done((f32[128,128]{1,0:T(8,128)S(1)}, f32[128,128]{1,0:T(8,128)S(1)}, u32[]{:S(2)}, u32[]{:S(2)}) %collective-permute-start.21) | collective-permute-done | bytes 65568 | tf_op jit(solution)/shard_map/ppermute | solution.py:268
  102.8 1.2 %collective-permute-start.24 = (f32[128,128]{1,0:T(8,128)S(1)}, f32[128,128]{1,0:T(8,128)S(1)}, u32[]{:S(2)}, u32[]{:S(2)}) collective-permute-start(f32[128,128]{1,0:T(8,128)S(1)} %get-tuple-element.33.refs_0_), channel_id=1, source_target_pairs={{0,4},{4,0},{8,12},{12,8},{1,5},{5,1},{9,13},{13,9},{2,6},{6,2},{1... | collective-permute-start | bytes 196616 | tf_op jit(solution)/shard_map/ppermute | solution.py:268
  104.0 1.4 %collective-permute-start.25 = (f32[128,128]{1,0:T(8,128)S(1)}, f32[128,128]{1,0:T(8,128)S(1)}, u32[]{:S(2)}, u32[]{:S(2)}) collective-permute-start(f32[128,128]{1,0:T(8,128)S(1)} %get-tuple-element.33.refs_0_), channel_id=1, source_target_pairs={{0,8},{4,12},{8,0},{12,4},{1,9},{5,13},{9,1},{13,5},{2,10},{6,14},... | collective-permute-start | bytes 196616 | tf_op jit(solution)/shard_map/ppermute | solution.py:268
  105.5 1.8 %collective-permute-start.26 = (f32[128,128]{1,0:T(8,128)S(1)}, f32[128,128]{1,0:T(8,128)S(1)}, u32[]{:S(2)}, u32[]{:S(2)}) collective-permute-start(f32[128,128]{1,0:T(8,128)S(1)} %get-tuple-element.33.refs_0_), channel_id=1, source_target_pairs={{0,12},{4,8},{8,4},{12,0},{1,13},{5,9},{9,5},{13,1},{2,14},{6,10},... | collective-permute-start | bytes 196616 | tf_op jit(solution)/shard_map/ppermute | solution.py:268
  107.4 4.4 %collective-permute-done.25.refs_2_ = f32[128,128]{1,0:T(8,128)S(1)} collective-permute-done((f32[128,128]{1,0:T(8,128)S(1)}, f32[128,128]{1,0:T(8,128)S(1)}, u32[]{:S(2)}, u32[]{:S(2)}) %collective-permute-start.25) | collective-permute-done | bytes 65568 | tf_op jit(solution)/shard_map/ppermute | solution.py:268
  (43 shorter events, 9.9 us)
Async XLA Ops:
  0.0 5.6 %copy-start = (s32[4,7]{1,0:T(4,128)S(1)}, s32[4,7]{1,0:T(4,128)}, u32[]{:S(2)}) copy-start(s32[4,7]{1,0:T(4,128)} %refs_13_.3) | copy-start | bytes 340
  1.5 31.6 %collective-permute-start.4 = (f32[1216,128]{1,0:T(8,128)S(1)}, f32[1216,128]{1,0:T(8,128)S(1)}, u32[]{:S(2)}, u32[]{:S(2)}) collective-permute-start(f32[1216,128]{1,0:T(8,128)S(1)} %first.1.refs_2_.refs_4_.refs_0_.refs_6_), channel_id=1, source_target_pairs={{0,8},{4,12},{8,0},{12,4},{1,9},{5,13},{9,1},{13,5},{2,10},{6,14},... | collective-permute-start | bytes 1867784 | tf_op jit(solution)/shard_map/ppermute | solution.py:268
  7.0 42.3 %copy-start.1 = (s32[4,7]{1,0:T(4,128)S(1)}, s32[4,7]{1,0:T(4,128)}, u32[]{:S(2)}) copy-start(s32[4,7]{1,0:T(4,128)} %refs_12_.5) | copy-start | bytes 340
  7.0 44.8 %collective-permute-start.10 = (f32[19,128,128]{2,1,0:T(8,128)S(1)}, f32[19,128,128]{2,1,0:T(8,128)S(1)}, u32[]{:S(2)}, u32[]{:S(2)}) collective-permute-start(f32[19,128,128]{2,1,0:T(8,128)S(1)} %dense.1.refs_0_), channel_id=1, source_target_pairs={{0,2},{1,3},{2,0},{3,1},{4,6},{5,7},{6,4},{7,5},{8,10},{9,11},{10,... | collective-permute-start | bytes 3735560 | tf_op jit(solution)/shard_map/ppermute | solution.py:268
  8.6 35.8 %collective-permute-start.3 = (f32[1216,128]{1,0:T(8,128)S(1)}, f32[1216,128]{1,0:T(8,128)S(1)}, u32[]{:S(2)}, u32[]{:S(2)}) collective-permute-start(f32[1216,128]{1,0:T(8,128)S(1)} %first.1.refs_2_.refs_4_.refs_0_.refs_6_), channel_id=1, source_target_pairs={{0,4},{4,0},{8,12},{12,8},{1,5},{5,1},{9,13},{13,9},{2,6},{6,2},{1... | collective-permute-start | bytes 1867784 | tf_op jit(solution)/shard_map/ppermute | solution.py:268
  33.1 16.2 %collective-permute-start.5 = (f32[1216,128]{1,0:T(8,128)S(1)}, f32[1216,128]{1,0:T(8,128)S(1)}, u32[]{:S(2)}, u32[]{:S(2)}) collective-permute-start(f32[1216,128]{1,0:T(8,128)S(1)} %collective-permute-done.4.refs_6_.refs_2_.refs_8_), channel_id=1, source_target_pairs={{0,4},{4,0},{8,12},{12,8},{1,5},{5,1},{9,13},{13,9},{2,6},{6,2},{1... | collective-permute-start | bytes 1867784 | tf_op jit(solution)/shard_map/ppermute | solution.py:268
  34.8 8.0 %collective-permute-start.1 = (f32[4,128,128]{2,1,0:T(8,128)S(1)}, f32[4,128,128]{2,1,0:T(8,128)S(1)}, u32[]{:S(2)}, u32[]{:S(2)}) collective-permute-start(f32[4,128,128]{2,1,0:T(8,128)S(1)} %dense0.1.refs_0_), channel_id=1, source_target_pairs={{0,2},{1,3},{2,0},{3,1},{4,6},{5,7},{6,4},{7,5},{8,10},{9,11},{10,... | collective-permute-start | bytes 786440 | tf_op jit(solution)/shard_map/ppermute | solution.py:268
  36.4 6.5 %collective-permute-start = (f32[4,128,128]{2,1,0:T(8,128)S(1)}, f32[4,128,128]{2,1,0:T(8,128)S(1)}, u32[]{:S(2)}, u32[]{:S(2)}) collective-permute-start(f32[4,128,128]{2,1,0:T(8,128)S(1)} %dense0.1.refs_0_), channel_id=1, source_target_pairs={{0,1},{1,0},{2,3},{3,2},{4,5},{5,4},{6,7},{7,6},{8,9},{9,8},{10,11... | collective-permute-start | bytes 786440 | tf_op jit(solution)/shard_map/ppermute | solution.py:268
  42.8 1.5 %collective-permute-start.2 = (f32[4,128,128]{2,1,0:T(8,128)S(1)}, f32[4,128,128]{2,1,0:T(8,128)S(1)}, u32[]{:S(2)}, u32[]{:S(2)}) collective-permute-start(f32[4,128,128]{2,1,0:T(8,128)S(1)} %collective-permute-done.1.refs_2_), channel_id=1, source_target_pairs={{0,1},{1,0},{2,3},{3,2},{4,5},{5,4},{6,7},{7,6},{8,9},{9,8},{10,11... | collective-permute-start | bytes 786440 | tf_op jit(solution)/shard_map/ppermute | solution.py:268
  51.2 14.5 %collective-permute-start.12 = (f32[896,128]{1,0:T(8,128)S(1)}, f32[896,128]{1,0:T(8,128)S(1)}, u32[]{:S(2)}, u32[]{:S(2)}) collective-permute-start(f32[896,128]{1,0:T(8,128)S(1)} %ahead1.1.refs_0_), channel_id=1, source_target_pairs={{0,2},{1,3},{2,0},{3,1},{4,6},{5,7},{6,4},{7,5},{8,10},{9,11},{10,... | collective-permute-start | bytes 1376264 | tf_op jit(solution)/shard_map/ppermute | solution.py:268
  51.8 15.0 %collective-permute-start.9 = (f32[19,128,128]{2,1,0:T(8,128)S(1)}, f32[19,128,128]{2,1,0:T(8,128)S(1)}, u32[]{:S(2)}, u32[]{:S(2)}) collective-permute-start(f32[19,128,128]{2,1,0:T(8,128)S(1)} %dense.1.refs_0_), channel_id=1, source_target_pairs={{0,1},{1,0},{2,3},{3,2},{4,5},{5,4},{6,7},{7,6},{8,9},{9,8},{10,11... | collective-permute-start | bytes 3735560 | tf_op jit(solution)/shard_map/ppermute | solution.py:268
  51.8 15.0 %collective-permute-start.11 = (f32[19,128,128]{2,1,0:T(8,128)S(1)}, f32[19,128,128]{2,1,0:T(8,128)S(1)}, u32[]{:S(2)}, u32[]{:S(2)}) collective-permute-start(f32[19,128,128]{2,1,0:T(8,128)S(1)} %collective-permute-done.10.refs_2_), channel_id=1, source_target_pairs={{0,1},{1,0},{2,3},{3,2},{4,5},{5,4},{6,7},{7,6},{8,9},{9,8},{10,11... | collective-permute-start | bytes 3735560 | tf_op jit(solution)/shard_map/ppermute | solution.py:268
  52.4 10.4 %collective-permute-start.6 = (f32[368,128]{1,0:T(8,128)S(1)}, f32[368,128]{1,0:T(8,128)S(1)}, u32[]{:S(2)}, u32[]{:S(2)}) collective-permute-start(f32[368,128]{1,0:T(8,128)S(1)} %early.1.refs_4_.refs_0_), channel_id=1, source_target_pairs={{0,4},{4,0},{8,12},{12,8},{1,5},{5,1},{9,13},{13,9},{2,6},{6,2},{1... | collective-permute-start | bytes 565256 | tf_op jit(solution)/shard_map/ppermute | solution.py:268
  53.6 12.1 %collective-permute-start.7 = (f32[368,128]{1,0:T(8,128)S(1)}, f32[368,128]{1,0:T(8,128)S(1)}, u32[]{:S(2)}, u32[]{:S(2)}) collective-permute-start(f32[368,128]{1,0:T(8,128)S(1)} %early.1.refs_4_.refs_0_), channel_id=1, source_target_pairs={{0,8},{4,12},{8,0},{12,4},{1,9},{5,13},{9,1},{13,5},{2,10},{6,14},... | collective-permute-start | bytes 565256 | tf_op jit(solution)/shard_map/ppermute | solution.py:268
  65.8 2.5 %collective-permute-start.13 = (f32[1792,128]{1,0:T(8,128)S(1)}, f32[1792,128]{1,0:T(8,128)S(1)}, u32[]{:S(2)}, u32[]{:S(2)}) collective-permute-start(f32[1792,128]{1,0:T(8,128)S(1)} %aheads1.1.refs_4_), channel_id=1, source_target_pairs={{0,1},{1,0},{2,3},{3,2},{4,5},{5,4},{6,7},{7,6},{8,9},{9,8},{10,11... | collective-permute-start | bytes 2752520 | tf_op jit(solution)/shard_map/ppermute | solution.py:268
  65.9 13.0 %collective-permute-start.17 = (f32[896,128]{1,0:T(8,128)S(1)}, f32[896,128]{1,0:T(8,128)S(1)}, u32[]{:S(2)}, u32[]{:S(2)}) collective-permute-start(f32[896,128]{1,0:T(8,128)S(1)} %ahead2.1.refs_0_), channel_id=1, source_target_pairs={{0,2},{1,3},{2,0},{3,1},{4,6},{5,7},{6,4},{7,5},{8,10},{9,11},{10,... | collective-permute-start | bytes 1376264 | tf_op jit(solution)/shard_map/ppermute | solution.py:268
  66.5 6.8 %collective-permute-start.8 = (f32[368,128]{1,0:T(8,128)S(1)}, f32[368,128]{1,0:T(8,128)S(1)}, u32[]{:S(2)}, u32[]{:S(2)}) collective-permute-start(f32[368,128]{1,0:T(8,128)S(1)} %collective-permute-done.7.refs_3_.refs_2_.refs_5_), channel_id=1, source_target_pairs={{0,4},{4,0},{8,12},{12,8},{1,5},{5,1},{9,13},{13,9},{2,6},{6,2},{1... | collective-permute-start | bytes 565256 | tf_op jit(solution)/shard_map/ppermute | solution.py:268
  79.0 5.1 %collective-permute-start.18 = (f32[1792,128]{1,0:T(8,128)S(1)}, f32[1792,128]{1,0:T(8,128)S(1)}, u32[]{:S(2)}, u32[]{:S(2)}) collective-permute-start(f32[1792,128]{1,0:T(8,128)S(1)} %aheads2.1.refs_4_), channel_id=1, source_target_pairs={{0,1},{1,0},{2,3},{3,2},{4,5},{5,4},{6,7},{7,6},{8,9},{9,8},{10,11... | collective-permute-start | bytes 2752520 | tf_op jit(solution)/shard_map/ppermute | solution.py:268
  79.1 13.7 %collective-permute-start.22 = (f32[960,128]{1,0:T(8,128)S(1)}, f32[960,128]{1,0:T(8,128)S(1)}, u32[]{:S(2)}, u32[]{:S(2)}) collective-permute-start(f32[960,128]{1,0:T(8,128)S(1)} %ahead3.1.refs_0_), channel_id=1, source_target_pairs={{0,2},{1,3},{2,0},{3,1},{4,6},{5,7},{6,4},{7,5},{8,10},{9,11},{10,... | collective-permute-start | bytes 1474568 | tf_op jit(solution)/shard_map/ppermute | solution.py:268
  79.7 7.2 %collective-permute-start.14 = (f32[128,128]{1,0:T(8,128)S(1)}, f32[128,128]{1,0:T(8,128)S(1)}, u32[]{:S(2)}, u32[]{:S(2)}) collective-permute-start(f32[128,128]{1,0:T(8,128)S(1)} %get-tuple-element.23.refs_2_.refs_0_.refs_4_), channel_id=1, source_target_pairs={{0,4},{4,0},{8,12},{12,8},{1,5},{5,1},{9,13},{13,9},{2,6},{6,2},{1... | collective-permute-start | bytes 196616 | tf_op jit(solution)/shard_map/ppermute | solution.py:268
  80.0 7.8 %collective-permute-start.15 = (f32[128,128]{1,0:T(8,128)S(1)}, f32[128,128]{1,0:T(8,128)S(1)}, u32[]{:S(2)}, u32[]{:S(2)}) collective-permute-start(f32[128,128]{1,0:T(8,128)S(1)} %get-tuple-element.23.refs_2_.refs_0_.refs_4_), channel_id=1, source_target_pairs={{0,8},{4,12},{8,0},{12,4},{1,9},{5,13},{9,1},{13,5},{2,10},{6,14},... | collective-permute-start | bytes 196616 | tf_op jit(solution)/shard_map/ppermute | solution.py:268
  82.7 6.2 %collective-permute-start.16 = (f32[128,128]{1,0:T(8,128)S(1)}, f32[128,128]{1,0:T(8,128)S(1)}, u32[]{:S(2)}, u32[]{:S(2)}) collective-permute-start(f32[128,128]{1,0:T(8,128)S(1)} %get-tuple-element.23.refs_2_.refs_0_.refs_4_), channel_id=1, source_target_pairs={{0,12},{4,8},{8,4},{12,0},{1,13},{5,9},{9,5},{13,1},{2,14},{6,10},... | collective-permute-start | bytes 196616 | tf_op jit(solution)/shard_map/ppermute | solution.py:268
  92.8 4.5 %collective-permute-start.23 = (f32[1920,128]{1,0:T(8,128)S(1)}, f32[1920,128]{1,0:T(8,128)S(1)}, u32[]{:S(2)}, u32[]{:S(2)}) collective-permute-start(f32[1920,128]{1,0:T(8,128)S(1)} %aheads3.1.refs_4_), channel_id=1, source_target_pairs={{0,1},{1,0},{2,3},{3,2},{4,5},{5,4},{6,7},{7,6},{8,9},{9,8},{10,11... | collective-permute-start | bytes 2949128 | tf_op jit(solution)/shard_map/ppermute | solution.py:268
  92.9 7.6 %collective-permute-start.19 = (f32[128,128]{1,0:T(8,128)S(1)}, f32[128,128]{1,0:T(8,128)S(1)}, u32[]{:S(2)}, u32[]{:S(2)}) collective-permute-start(f32[128,128]{1,0:T(8,128)S(1)} %get-tuple-element.28.refs_2_.refs_0_), channel_id=1, source_target_pairs={{0,4},{4,0},{8,12},{12,8},{1,5},{5,1},{9,13},{13,9},{2,6},{6,2},{1... | collective-permute-start | bytes 196616 | tf_op jit(solution)/shard_map/ppermute | solution.py:268
  93.3 7.3 %collective-permute-start.20 = (f32[128,128]{1,0:T(8,128)S(1)}, f32[128,128]{1,0:T(8,128)S(1)}, u32[]{:S(2)}, u32[]{:S(2)}) collective-permute-start(f32[128,128]{1,0:T(8,128)S(1)} %get-tuple-element.28.refs_2_.refs_0_), channel_id=1, source_target_pairs={{0,8},{4,12},{8,0},{12,4},{1,9},{5,13},{9,1},{13,5},{2,10},{6,14},... | collective-permute-start | bytes 196616 | tf_op jit(solution)/shard_map/ppermute | solution.py:268
  96.0 6.1 %collective-permute-start.21 = (f32[128,128]{1,0:T(8,128)S(1)}, f32[128,128]{1,0:T(8,128)S(1)}, u32[]{:S(2)}, u32[]{:S(2)}) collective-permute-start(f32[128,128]{1,0:T(8,128)S(1)} %get-tuple-element.28.refs_2_.refs_0_), channel_id=1, source_target_pairs={{0,12},{4,8},{8,4},{12,0},{1,13},{5,9},{9,5},{13,1},{2,14},{6,10},... | collective-permute-start | bytes 196616 | tf_op jit(solution)/shard_map/ppermute | solution.py:268
  102.8 4.6 %collective-permute-start.24 = (f32[128,128]{1,0:T(8,128)S(1)}, f32[128,128]{1,0:T(8,128)S(1)}, u32[]{:S(2)}, u32[]{:S(2)}) collective-permute-start(f32[128,128]{1,0:T(8,128)S(1)} %get-tuple-element.33.refs_0_), channel_id=1, source_target_pairs={{0,4},{4,0},{8,12},{12,8},{1,5},{5,1},{9,13},{13,9},{2,6},{6,2},{1... | collective-permute-start | bytes 196616 | tf_op jit(solution)/shard_map/ppermute | solution.py:268
  104.0 7.8 %collective-permute-start.25 = (f32[128,128]{1,0:T(8,128)S(1)}, f32[128,128]{1,0:T(8,128)S(1)}, u32[]{:S(2)}, u32[]{:S(2)}) collective-permute-start(f32[128,128]{1,0:T(8,128)S(1)} %get-tuple-element.33.refs_0_), channel_id=1, source_target_pairs={{0,8},{4,12},{8,0},{12,4},{1,9},{5,13},{9,1},{13,5},{2,10},{6,14},... | collective-permute-start | bytes 196616 | tf_op jit(solution)/shard_map/ppermute | solution.py:268
  105.5 6.4 %collective-permute-start.26 = (f32[128,128]{1,0:T(8,128)S(1)}, f32[128,128]{1,0:T(8,128)S(1)}, u32[]{:S(2)}, u32[]{:S(2)}) collective-permute-start(f32[128,128]{1,0:T(8,128)S(1)} %get-tuple-element.33.refs_0_), channel_id=1, source_target_pairs={{0,12},{4,8},{8,4},{12,0},{1,13},{5,9},{9,5},{13,1},{2,14},{6,10},... | collective-permute-start | bytes 196616 | tf_op jit(solution)/shard_map/ppermute | solution.py:268

commit v9 on v8

--- a/solution.py
+++ b/solution.py
@@ -86,28 +86,20 @@
     return (out[:rows, :cols] + (out[:rows, cols:] + out[rows:, :cols])) + out[rows:, cols:]
 
 
-def fill_ahead(out_ref, begin, count, inv_ref, right_ref):
-    nb = inv_ref.shape[1]
+def first_kernel(prev, *refs):
+    known_ref, right_ref, inv_ref, ahead_ref, known_out = refs
+    steps, nb = right_ref.shape[0], inv_ref.shape[1]
     share = right_ref.shape[2] // lax.axis_size("pcol")
     at = pl.multiple_of(lax.axis_index("pcol") * share, share)
-    out_ref[begin : begin + nb] = inv_ref[0]
-    for col in range(count):
-        place = begin + nb + col * share
-        out_ref[place : place + share] = right_ref[0, col, pl.ds(at, share), :]
-
-
-def first_kernel(prev, room, known_ref, *refs):
-    right_ref, right1_ref, right2_ref, inv_ref, inv1_ref, sent_ref = refs
-    nb, rank_pad = known_ref.shape[1], right_ref.shape[2]
-    sent_ref[nb:room] = jnp.zeros((room - nb, sent_ref.shape[1]), jnp.float32)
-    fill_ahead(sent_ref, 0, prev + 1, inv_ref, right1_ref)
-    fill_ahead(sent_ref, room, prev + 2, inv1_ref, right2_ref)
-    for col in range(prev):
-        known = known_ref[col]
-        at = 2 * room + col * nb
-        sent_ref[at : at + nb] = known
-        at = 2 * room + prev * nb + col * rank_pad
-        sent_ref[at : at + rank_pad] = dot_halves(halves(right_ref[0, col], 0), halves(known, 1))
+    place = 0
+    for step in range(steps):
+        if step:
+            ahead_ref[place : place + nb] = inv_ref[step - 1]
+            place += nb
+        for col in range(prev + step):
+            ahead_ref[place : place + share] = right_ref[step, col, pl.ds(at, share), :]
+            place += share
+    known_out[...] = known_ref[...]
 
 
 def dense_kernel(rows, flags_ref, *refs):
@@ -120,12 +112,11 @@
             place += 1
 
 
-def stack_kernel(*refs):
+def stack_kernel(begin, *refs):
     *parts, out_ref = refs
-    place = 0
-    for ref in parts:
-        out_ref[place : place + ref.shape[0]] = ref[...]
-        place += ref.shape[0]
+    count = out_ref.shape[0] // len(parts)
+    for index, ref in enumerate(parts):
+        out_ref[index * count : (index + 1) * count] = ref[begin : begin + count]
 
 
 def masked_left(step, col, ranks_ref, flags_ref, left_ref):
@@ -137,55 +128,36 @@
 OVER_ROWS = (((0,), (0,)), ((), ()))
 
 
-def early_kernel(n, prev, begin, ahead, counts, *refs):
-    strips, sources = refs[:n], refs[n : 2 * n]
-    ranks_ref, flags_ref, left_ref, base_ref, inv_ref, right_ref, out_ref, scratch = refs[2 * n :]
-    nb, rank_pad = inv_ref.shape[1], left_ref.shape[2]
-    turn = lax.axis_index("pcol") ^ lax.axis_index("prow")
-    total = base_ref[0]
-    for col in range(prev):
-        at = begin + col * nb
-        for slot, ref in enumerate(sources):
-            scratch[pl.ds(pl.multiple_of((turn ^ slot) * nb, nb), nb), :] = ref[at : at + nb]
-        strip = jnp.concatenate([ref[col] for ref in strips], axis=1)
-        total = total - dot_halves(halves(strip, 0), halves(scratch[...], 1))
-    lefts, coeffs = [], []
-    for col in range(prev):
-        at = begin + prev * nb + col * rank_pad
-        lefts.append(masked_left(0, col, ranks_ref, flags_ref, left_ref))
-        coeffs.append(sum(ref[at : at + rank_pad] for ref in sources))
-    left2 = halves(jnp.concatenate(lefts, axis=0), 1)
-    coeff2 = halves(jnp.concatenate(coeffs, axis=0), 1)
-    out_ref[ahead:] = total - dot_halves(left2, coeff2, OVER_ROWS)
-    fill_ahead(out_ref, 0, counts, inv_ref, right_ref)
-
-
-def prepare_kernel(n, prev, step, first, size, known_at, last, *refs):
-    dense, ahead = refs[:n], refs[n : n + 2]
-    sources = refs[n + 2 : 2 * n + 2]
-    solved = refs[2 * n + 2 : 2 * n + 1 + step]
-    rest = refs[2 * n + 1 + step :]
-    ranks_ref, flags_ref, left_ref, base_ref, out_ref, strip_ref, inv_ref, scratch, right_scr = rest
+def prepare_kernel(n, prev, step, first, last, *refs):
+    refs = list(refs)
+    dense = [refs.pop(0) for _ in range(n)]
+    ahead = [refs.pop(0) for _ in range(2)]
+    sources = [refs.pop(0) for _ in range(n)]
+    solved = [refs.pop(0) for _ in range(step - 1)]
+    ranks_ref, flags_ref, left_ref, base_ref, out_ref, *outs, scratch, right_scr = refs
+    strip_ref, inv_ref = outs or (None, None)
     nb = base_ref.shape[1]
     tiles, rank_pad = right_scr.shape[:2]
     share = rank_pad // n
     own_col, own_row = lax.axis_index("pcol"), lax.axis_index("prow")
     turn = own_col ^ own_row
     rows = ahead[0].shape[0] // (2 * n)
+    head = nb if step else 0
 
     for near in range(n):
         col_at = own_col ^ near
         for slot in range(n):
             at = ((near >> 1) * n + slot) * rows
-            both = halves(ahead[near & 1][at : at + nb], 0)
-            row_at = (own_row ^ slot) * nb
-            lanes = pl.ds(pl.multiple_of(col_at * nb, nb), nb)
-            inv_ref[pl.ds(pl.multiple_of(row_at, nb), nb), lanes] = both[:nb]
-            inv_ref[pl.ds(pl.multiple_of(n * nb + row_at, nb), nb), lanes] = both[nb:]
+            if step:
+                both = halves(ahead[near & 1][at : at + nb], 0)
+                row_at = (own_row ^ slot) * nb
+                lanes = pl.ds(pl.multiple_of(col_at * nb, nb), nb)
+                inv_ref[pl.ds(pl.multiple_of(row_at, nb), nb), lanes] = both[:nb]
+                inv_ref[pl.ds(pl.multiple_of(n * nb + row_at, nb), nb), lanes] = both[nb:]
             lanes = pl.ds(pl.multiple_of((turn ^ slot) * nb, nb), nb)
             ranks = pl.ds(pl.multiple_of(col_at * share, share), share)
             for tile in range(tiles):
-                place = at + nb + tile * share
+                place = at + head + tile * share
                 right_scr[tile, ranks, lanes] = ahead[near & 1][place : place + share]
 
     def strip_of(tile):
@@ -196,9 +168,8 @@
 
     total = base_ref[0]
     for tile in range(prev):
-        at = known_at + tile * nb
         for slot, ref in enumerate(sources):
-            scratch[pl.ds(pl.multiple_of((turn ^ slot) * nb, nb), nb), :] = ref[at : at + nb]
+            scratch[pl.ds(pl.multiple_of((turn ^ slot) * nb, nb), nb), :] = ref[tile]
         total = total - dot_halves(halves(strip_of(tile), 0), halves(scratch[...], 1))
     for index, ref in enumerate(solved):
         for d in range(n):
@@ -206,23 +177,25 @@
             scratch[d * nb : (d + 1) * nb] = ref[rows_at, :]
         total = total - dot_halves(halves(strip_of(prev + index), 0), halves(scratch[...], 1))
     out_ref[...] = total
+    if not step:
+        return
     pair = halves(strip_of(tiles - 1), 0)
     for d in range(n):
         lanes = pl.ds(pl.multiple_of((own_col ^ d) * nb, nb), nb)
         strip_ref[0, :, lanes] = pair[:, d * nb : (d + 1) * nb]
         if last:
-            strip_ref[1, :, lanes] = halves(dense[d][size - 1], 0)
-
-
-def place_slots(n, at, nb, slots, scratch):
+            strip_ref[1, :, lanes] = halves(dense[d][first + tiles], 0)
+
+
+def place_slots(n, nb, slots, scratch):
     own = lax.axis_index("prow")
     for slot, ref in enumerate(slots):
-        scratch[pl.ds(pl.multiple_of((own ^ slot) * nb, nb), nb), :] = ref[at : at + nb]
-
-
-def step_kernel(n, at, *refs):
+        scratch[pl.ds(pl.multiple_of((own ^ slot) * nb, nb), nb), :] = ref[...]
+
+
+def step_kernel(n, *refs):
     inverse_ref, strip_ref, base_ref, out_ref, solved_ref, scratch = refs[n:]
-    place_slots(n, at, base_ref.shape[0], refs[:n], scratch)
+    place_slots(n, base_ref.shape[0], refs[:n], scratch)
     solved = dot_halves(inverse_ref[...], halves(scratch[...], 1))
     solved_ref[...] = solved
     out_ref[...] = base_ref[...] - dot_halves(strip_ref[0], halves(solved, 1))
@@ -231,7 +204,7 @@
 def last_kernel(n, *refs):
     strip_ref, *solved, out_ref, scratch = refs[n:]
     nb = out_ref.shape[1]
-    place_slots(n, 0, nb, refs[:n], scratch)
+    place_slots(n, nb, refs[:n], scratch)
     own = pl.ds(pl.multiple_of(lax.axis_index("prow") * nb, nb), nb)
     for step, ref in enumerate(solved):
         out_ref[step] = ref[own, :]
@@ -315,32 +288,40 @@
     share = rank_pad // n
     ranks_flags = [(tile_ranks, smem), (dense_flags, smem)]
     source_room = pltpu.VMEM((n * nb, rhs), f32)
-    room1, room2 = nb + (prev + 2) * share, nb + (prev + 3) * share
-
     def over_cols(own):
         far = shift(own, "pcol", 2)
         return [own, shift(own, "pcol", 1), far, shift(far, "pcol", 1)]
 
-    def ahead_far(slots, height, place, name, after):
-        head = pl.BlockSpec((height, nb), lambda i: (place, 0))
-        shape = shaped(n * height, nb)
-        own = run(stack_kernel, name, shape, [(ref, head) for ref in slots], after=after)
+    heights = [(nb if step else 0) + (prev + step) * share for step in range(steps)]
+
+    def ahead_far(step, after=()):
+        own = run(
+            functools.partial(stack_kernel, sum(heights[:step])),
+            f"ahead{step}",
+            shaped(n * heights[step], nb),
+            [whole_of(value) for value in ahead],
+            after=after,
+        )
         return [own, shift(own, "pcol", 2)]
 
-    def ahead_near(halfs, name, after):
-        shape = shaped(2 * halfs[0].shape[0], nb)
-        both = run(stack_kernel, name, shape, [whole_of(value) for value in halfs], after=after)
+    def ahead_near(step, halfs, after=()):
+        both = run(
+            functools.partial(stack_kernel, 0),
+            f"aheads{step}",
+            shaped(2 * n * heights[step], nb),
+            [whole_of(value) for value in halfs],
+            after=after,
+        )
         return [both, shift(both, "pcol", 1)]
 
-    sent = run(
-        functools.partial(first_kernel, prev, room1),
+    sent, known = run(
+        functools.partial(first_kernel, prev),
         "first",
-        shaped(2 * room1 + prev * (nb + rank_pad), rhs),
-        [whole_of(pinned(earlier))]
-        + [blocks_of(right_t, step) for step in range(3)]
-        + [blocks_of(inverse_diag, step) for step in range(2)],
-    )
-    known = over_rows_forwarded(sent)
+        [shaped(sum(heights), nb), shaped(*earlier.shape)],
+        [whole_of(pinned(value)) for value in (earlier, right_t, inverse_diag)],
+    )
+    ahead = over_rows_forwarded(sent)
+    known = over_rows_forwarded(known)
     own = run(
         functools.partial(dense_kernel, [(0, prev)]),
         "dense0",
@@ -358,43 +339,33 @@
         [(dense_flags, smem)]
         + [blocks_of(dense_tiles, step) for step in range(1, steps)]
         + [blocks_of(inverse_diag, steps - 1)],
-        after=[],
+        after=[sent],
     )
     dense = over_cols(own)
 
-    pending = run(
-        functools.partial(early_kernel, n, prev, 2 * room1, room2, prev + 3),
-        "early",
-        shaped(room2 + nb, rhs),
-        [whole_of(value) for value in strips0 + known]
-        + ranks_flags
-        + [blocks_of(left_t, 0), blocks_of(right_side, 0)]
-        + [blocks_of(inverse_diag, 2), blocks_of(right_t, 3)],
-        [source_room],
-    )
-
-    def prepare(step, later, solved):
+    def prepare(step, strips, later, solved=()):
         last = step + 1 == steps
         tiles = prev + step
+        outs = [
+            shaped(nb, rhs),
+            shaped(1 + last, 2 * nb, n * nb, dtype=bf16),
+            shaped(2 * n * nb, n * nb, dtype=bf16),
+        ]
         first = sum(count for row, count in rows[:-1] if row < step)
         return run(
-            functools.partial(prepare_kernel, n, prev, step, first, size, 2 * room1, last),
+            functools.partial(prepare_kernel, n, prev, step, first, last),
             f"prepare{step}",
-            [
-                shaped(nb, rhs),
-                shaped(1 + last, 2 * nb, n * nb, dtype=bf16),
-                shaped(2 * n * nb, n * nb, dtype=bf16),
-            ],
-            [whole_of(value) for value in dense + later + known + solved]
+            outs if step else outs[0],
+            [whole_of(value) for value in [*strips, *later, *known, *solved]]
             + ranks_flags
             + [blocks_of(left_t, step), blocks_of(right_side, step)],
             [source_room, pltpu.VMEM((tiles, rank_pad, n * nb), f32)],
         )
 
-    def solve(step, at, slots, prepared):
+    def solve(step, slots, prepared):
         base, strip, inverse = prepared
         return run(
-            functools.partial(step_kernel, n, at),
+            functools.partial(step_kernel, n),
             f"step{step}",
             [shaped(nb, rhs), shaped(n * nb, rhs)],
             [whole_of(value) for value in slots + [inverse]]
@@ -402,21 +373,16 @@
             [source_room],
         )
 
-    slots = over_rows_forwarded(pending)
-    later1 = ahead_far(known, room1, 0, "ahead1", [pending])
-    later1 = ahead_near(later1, "aheads1", slots[1:3])
-    later2 = ahead_far(known, room1, 1, "ahead2", slots[1:3])
-    pending1, solved0 = solve(0, room2, slots, prepare(1, later1, []))
-
-    later3 = ahead_far(slots, room2, 0, "ahead3", [pending1])
-    later2 = ahead_near(later2, "aheads2", [pending1])
-    slots = over_rows(pending1)
-    pending2, solved1 = solve(1, 0, slots, prepare(2, later2, [solved0]))
-
-    slots = over_rows(pending2)
-    later3 = ahead_near(later3, "aheads3", [pending2])
-    prepared = prepare(3, later3, [solved0, solved1])
-    pending3, solved2 = solve(2, 0, slots, prepared)
+    pending0 = prepare(0, strips0, ahead_near(0, ahead_far(0)))
+    later1 = ahead_near(1, ahead_far(1, []), [pending0])
+    later2 = ahead_far(2, [pending0])
+    pending1, solved0 = solve(0, over_rows(pending0), prepare(1, dense, later1))
+    later2 = ahead_near(2, later2, [pending1])
+    later3 = ahead_far(3, [pending1])
+    pending2, solved1 = solve(1, over_rows(pending1), prepare(2, dense, later2, [solved0]))
+    later3 = ahead_near(3, later3, [pending2])
+    prepared = prepare(3, dense, later3, [solved0, solved1])
+    pending3, solved2 = solve(2, over_rows(pending2), prepared)
     return run(
         functools.partial(last_kernel, n),
         "last",

time: 113 us -> 109 us (0.965)
  waiting for transfers between devices: 64.5 us -> 57.6 us
  starting transfers between devices: 30.3 us -> 32.4 us
    ppermute x27 -> x32, waiting for transfers between devices: 64.5 us -> 57.6 us  [shift(): return lax.ppermute(value, axis, [(i, i ^ step) for i in range(n)])]
    ppermute x27 -> x32, starting transfers between devices: 30.3 us -> 32.4 us  [shift(): return lax.ppermute(value, axis, [(i, i ^ step) for i in range(n)])]
    pallas_call x17 -> x19, Pallas kernels: 17.7 us -> 18.1 us  [call(): pl.pallas_call(body, grid=(1,), out_shape=shapes, in_specs=specs + [any_s...]
  transfers between devices with their start and end apart: 27 -> 32, of which waited for: 15 -> 13; matrix products, arithmetic and copies ran while one was open for 0% -> 0% of each run, Pallas kernels for 13% -> 12%
where the time goes in v9:
time: 109 us; the launch traced here: 108 us
  waiting for transfers between devices  57.6 us (53%)
  starting transfers between devices  32.4 us (30%)
  Pallas kernels  18.1 us (17%)
    ppermute x32, waiting for transfers between devices, shift(): return lax.ppermute(value, axis, [(i, i ^ step) for i in range(n)])  57.6 us
    ppermute x32, starting transfers between devices, shift(): return lax.ppermute(value, axis, [(i, i ^ step) for i in range(n)])  32.4 us
    pallas_call x19, Pallas kernels, call(): pl.pallas_call(body, grid=(1,), out_shape=shapes, in_specs=specs + [any_s...  18.1 us
  transfers between devices with their start and end apart: 32, of which 13 were waited for; matrix products, arithmetic and copies ran while one was open for 0% of the time, Pallas kernels for 12%

profile of v9, /device:TPU:0, one launch (start us, length us, event | category | flops | bytes accessed | tf_op | source)
XLA Modules:
  0.0 108.3 jit_solution(16259757666547035690)
XLA Ops:
  0.0 1.4 %first.1 = (f32[736,128]{1,0:T(8,128)S(1)}, f32[4,128,128]{2,1,0:T(8,128)S(1)}) custom-call(f32[4,128,128]{2,1,0:T(8,128)} %refs_0_.3, f32[4,7,64,128]{3,2,1,0:T(8,128)} %bitcast.6, f32[4,128,128]{2,1,0:T(8,128)} %refs_4_.1), custom_call_target="tpu_custom_call" | custom-call | tf_op jit(solution)/shard_map/first/pallas_call | solution.py:267
  1.4 1.4 %dense.1.refs_0_ = f32[19,128,128]{2,1,0:T(8,128)S(1)} custom-call(s32[4,7]{1,0:T(4,128)S(1)} %copy-done, f32[4,7,128,128]{3,2,1,0:T(8,128)} %refs_3_.1, f32[4,7,128,128]{3,2,1,0:T(8,128)} %refs_3_.1, f32[4,7,128,128]{3,2,1,0:T(8,128)} %refs_3_.1, f32[4,128,128]{2,1,0:T(8,128)} %refs_4_.1, f32[736,128]{1,0:T(8,128)S(1)} %get-tuple-element.22.refs_2_.refs_0_.refs_5_), custom_call_target="tpu_custom_call" | custom-call | tf_op jit(solution)/shard_map/dense/pallas_call | solution.py:267
  2.8 3.0 %collective-permute-start.15 = (f32[19,128,128]{2,1,0:T(8,128)S(1)}, f32[19,128,128]{2,1,0:T(8,128)S(1)}, u32[]{:S(2)}, u32[]{:S(2)}) collective-permute-start(f32[19,128,128]{2,1,0:T(8,128)S(1)} %dense.1.refs_0_), channel_id=1, source_target_pairs={{0,2},{1,3},{2,0},{3,1},{4,6},{5,7},{6,4},{7,5},{8,10},{9,11},{10,... | collective-permute-start | bytes 3735560 | tf_op jit(solution)/shard_map/ppermute | solution.py:241
  5.8 2.6 %collective-permute-start.4 = (f32[736,128]{1,0:T(8,128)S(1)}, f32[736,128]{1,0:T(8,128)S(1)}, u32[]{:S(2)}, u32[]{:S(2)}) collective-permute-start(f32[736,128]{1,0:T(8,128)S(1)} %get-tuple-element.22.refs_2_.refs_0_.refs_5_), channel_id=1, source_target_pairs={{0,8},{4,12},{8,0},{12,4},{1,9},{5,13},{9,1},{13,5},{2,10},{6,14},... | collective-permute-start | bytes 1130504 | tf_op jit(solution)/shard_map/ppermute | solution.py:241
  8.7 1.6 %collective-permute-start.3 = (f32[736,128]{1,0:T(8,128)S(1)}, f32[736,128]{1,0:T(8,128)S(1)}, u32[]{:S(2)}, u32[]{:S(2)}) collective-permute-start(f32[736,128]{1,0:T(8,128)S(1)} %get-tuple-element.22.refs_2_.refs_0_.refs_5_), channel_id=1, source_target_pairs={{0,4},{4,0},{8,12},{12,8},{1,5},{5,1},{9,13},{13,9},{2,6},{6,2},{1... | collective-permute-start | bytes 1130504 | tf_op jit(solution)/shard_map/ppermute | solution.py:241
  10.3 21.5 %collective-permute-done.4.refs_2_ = f32[736,128]{1,0:T(8,128)S(1)} collective-permute-done((f32[736,128]{1,0:T(8,128)S(1)}, f32[736,128]{1,0:T(8,128)S(1)}, u32[]{:S(2)}, u32[]{:S(2)}) %collective-permute-start.4) | collective-permute-done | bytes 376864 | tf_op jit(solution)/shard_map/ppermute | solution.py:241
  31.8 1.1 dense0.1.refs_0_
  33.4 3.0 %collective-permute-done.9.refs_8_ = f32[4,128,128]{2,1,0:T(8,128)S(1)} collective-permute-done((f32[4,128,128]{2,1,0:T(8,128)S(1)}, f32[4,128,128]{2,1,0:T(8,128)S(1)}, u32[]{:S(2)}, u32[]{:S(2)}) %collective-permute-start.9) | collective-permute-done | bytes 262176 | tf_op jit(solution)/shard_map/ppermute | solution.py:241
  37.0 7.4 %collective-permute-done.5.refs_3_ = f32[736,128]{1,0:T(8,128)S(1)} collective-permute-done((f32[736,128]{1,0:T(8,128)S(1)}, f32[736,128]{1,0:T(8,128)S(1)}, u32[]{:S(2)}, u32[]{:S(2)}) %collective-permute-start.5) | collective-permute-done | bytes 376864 | tf_op jit(solution)/shard_map/ppermute | solution.py:241
  45.0 1.6 %collective-permute-start.17 = (f32[832,128]{1,0:T(8,128)S(1)}, f32[832,128]{1,0:T(8,128)S(1)}, u32[]{:S(2)}, u32[]{:S(2)}) collective-permute-start(f32[832,128]{1,0:T(8,128)S(1)} %ahead1.1.refs_0_), channel_id=1, source_target_pairs={{0,2},{1,3},{2,0},{3,1},{4,6},{5,7},{6,4},{7,5},{8,10},{9,11},{10,... | collective-permute-start | bytes 1277960 | tf_op jit(solution)/shard_map/ppermute | solution.py:241
  46.6 4.2 %collective-permute-done.6.refs_1_ = f32[256,128]{1,0:T(8,128)S(1)} collective-permute-done((f32[256,128]{1,0:T(8,128)S(1)}, f32[256,128]{1,0:T(8,128)S(1)}, u32[]{:S(2)}, u32[]{:S(2)}) %collective-permute-start.6) | collective-permute-done | bytes 131104 | tf_op jit(solution)/shard_map/ppermute | solution.py:241
  51.5 4.0 %collective-permute-done.10.refs_9_ = f32[4,128,128]{2,1,0:T(8,128)S(1)} collective-permute-done((f32[4,128,128]{2,1,0:T(8,128)S(1)}, f32[4,128,128]{2,1,0:T(8,128)S(1)}, u32[]{:S(2)}, u32[]{:S(2)}) %collective-permute-start.10) | collective-permute-done | bytes 262176 | tf_op jit(solution)/shard_map/ppermute | solution.py:241
  56.0 1.1 %collective-permute-done.7.refs_5_ = f32[512,128]{1,0:T(8,128)S(1)} collective-permute-done((f32[512,128]{1,0:T(8,128)S(1)}, f32[512,128]{1,0:T(8,128)S(1)}, u32[]{:S(2)}, u32[]{:S(2)}) %collective-permute-start.7) | collective-permute-done | bytes 262176 | tf_op jit(solution)/shard_map/ppermute | solution.py:241
  57.1 2.2 %prepare0.1.refs_2_.refs_0_.refs_4_ = f32[128,128]{1,0:T(8,128)S(1)} custom-call(f32[4,128,128]{2,1,0:T(8,128)S(1)} %dense0.1.refs_0_, f32[4,128,128]{2,1,0:T(8,128)S(1)} %collective-permute-done.refs_1_, f32[4,128,128]{2,1,0:T(8,128)S(1)} %collective-permute-done.1.refs_2_, f32[4,128,128]{2,1,0:T(8,128)S(1)} %collective-permute-done.2.refs_3_, ...), custom_call_target="tpu_custom_call" | custom-call | tf_op jit(solution)/shard_map/prepare0/pallas_call | solution.py:267
  60.2 1.3 %collective-permute-start.11 = (f32[128,128]{1,0:T(8,128)S(1)}, f32[128,128]{1,0:T(8,128)S(1)}, u32[]{:S(2)}, u32[]{:S(2)}) collective-permute-start(f32[128,128]{1,0:T(8,128)S(1)} %prepare0.1.refs_2_.refs_0_.refs_4_), channel_id=1, source_target_pairs={{0,4},{4,0},{8,12},{12,8},{1,5},{5,1},{9,13},{13,9},{2,6},{6,2},{1... | collective-permute-start | bytes 196616 | tf_op jit(solution)/shard_map/ppermute | solution.py:241
  61.5 2.8 %collective-permute-start.12 = (f32[128,128]{1,0:T(8,128)S(1)}, f32[128,128]{1,0:T(8,128)S(1)}, u32[]{:S(2)}, u32[]{:S(2)}) collective-permute-start(f32[128,128]{1,0:T(8,128)S(1)} %prepare0.1.refs_2_.refs_0_.refs_4_), channel_id=1, source_target_pairs={{0,8},{4,12},{8,0},{12,4},{1,9},{5,13},{9,1},{13,5},{2,10},{6,14},... | collective-permute-start | bytes 196616 | tf_op jit(solution)/shard_map/ppermute | solution.py:241
  65.3 2.6 %prepare1.1 = (f32[128,128]{1,0:T(8,128)S(1)}, bf16[1,256,512]{2,1,0:T(8,128)(2,1)S(1)}, bf16[1024,512]{1,0:T(8,128)(2,1)S(1)}) custom-call(f32[19,128,128]{2,1,0:T(8,128)S(1)} %dense.1.refs_0_, f32[19,128,128]{2,1,0:T(8,128)S(1)} %collective-permute-done.14.refs_1_, f32[19,128,128]{2,1,0:T(8,128)S(1)} %collective-permute-done.15.refs_2_, ...), custom_call_target="tpu_custom_call" | custom-call | tf_op jit(solution)/shard_map/prepare1/pallas_call | solution.py:267
  68.0 2.5 %collective-permute-done.13.refs_3_ = f32[128,128]{1,0:T(8,128)S(1)} collective-permute-done((f32[128,128]{1,0:T(8,128)S(1)}, f32[128,128]{1,0:T(8,128)S(1)}, u32[]{:S(2)}, u32[]{:S(2)}) %collective-permute-start.13) | collective-permute-done | bytes 65568 | tf_op jit(solution)/shard_map/ppermute | solution.py:241
  71.2 1.3 %collective-permute-done.22.refs_1_ = f32[896,128]{1,0:T(8,128)S(1)} collective-permute-done((f32[896,128]{1,0:T(8,128)S(1)}, f32[896,128]{1,0:T(8,128)S(1)}, u32[]{:S(2)}, u32[]{:S(2)}) %collective-permute-start.22) | collective-permute-done | bytes 458784 | tf_op jit(solution)/shard_map/ppermute | solution.py:241
  73.2 1.3 %collective-permute-start.19 = (f32[128,128]{1,0:T(8,128)S(1)}, f32[128,128]{1,0:T(8,128)S(1)}, u32[]{:S(2)}, u32[]{:S(2)}) collective-permute-start(f32[128,128]{1,0:T(8,128)S(1)} %get-tuple-element.27.refs_2_.refs_0_.refs_4_), channel_id=1, source_target_pairs={{0,4},{4,0},{8,12},{12,8},{1,5},{5,1},{9,13},{13,9},{2,6},{6,2},{1... | collective-permute-start | bytes 196616 | tf_op jit(solution)/shard_map/ppermute | solution.py:241
  74.6 2.8 %collective-permute-start.20 = (f32[128,128]{1,0:T(8,128)S(1)}, f32[128,128]{1,0:T(8,128)S(1)}, u32[]{:S(2)}, u32[]{:S(2)}) collective-permute-start(f32[128,128]{1,0:T(8,128)S(1)} %get-tuple-element.27.refs_2_.refs_0_.refs_4_), channel_id=1, source_target_pairs={{0,8},{4,12},{8,0},{12,4},{1,9},{5,13},{9,1},{13,5},{2,10},{6,14},... | collective-permute-start | bytes 196616 | tf_op jit(solution)/shard_map/ppermute | solution.py:241
  78.1 2.8 %prepare2.1 = (f32[128,128]{1,0:T(8,128)S(1)}, bf16[1,256,512]{2,1,0:T(8,128)(2,1)S(1)}, bf16[1024,512]{1,0:T(8,128)(2,1)S(1)}) custom-call(f32[19,128,128]{2,1,0:T(8,128)S(1)} %dense.1.refs_0_, f32[19,128,128]{2,1,0:T(8,128)S(1)} %collective-permute-done.14.refs_1_, f32[19,128,128]{2,1,0:T(8,128)S(1)} %collective-permute-done.15.refs_2_, ...), custom_call_target="tpu_custom_call" | custom-call | tf_op jit(solution)/shard_map/prepare2/pallas_call | solution.py:267
  81.0 2.5 %collective-permute-done.21.refs_3_ = f32[128,128]{1,0:T(8,128)S(1)} collective-permute-done((f32[128,128]{1,0:T(8,128)S(1)}, f32[128,128]{1,0:T(8,128)S(1)}, u32[]{:S(2)}, u32[]{:S(2)}) %collective-permute-start.21) | collective-permute-done | bytes 65568 | tf_op jit(solution)/shard_map/ppermute | solution.py:241
  84.2 2.2 %collective-permute-done.27.refs_1_ = f32[960,128]{1,0:T(8,128)S(1)} collective-permute-done((f32[960,128]{1,0:T(8,128)S(1)}, f32[960,128]{1,0:T(8,128)S(1)}, u32[]{:S(2)}, u32[]{:S(2)}) %collective-permute-start.27) | collective-permute-done | bytes 491552 | tf_op jit(solution)/shard_map/ppermute | solution.py:241
  86.5 1.4 %collective-permute-start.24 = (f32[128,128]{1,0:T(8,128)S(1)}, f32[128,128]{1,0:T(8,128)S(1)}, u32[]{:S(2)}, u32[]{:S(2)}) collective-permute-start(f32[128,128]{1,0:T(8,128)S(1)} %get-tuple-element.32.refs_2_.refs_0_), channel_id=1, source_target_pairs={{0,4},{4,0},{8,12},{12,8},{1,5},{5,1},{9,13},{13,9},{2,6},{6,2},{1... | collective-permute-start | bytes 196616 | tf_op jit(solution)/shard_map/ppermute | solution.py:241
  87.9 2.7 %collective-permute-start.25 = (f32[128,128]{1,0:T(8,128)S(1)}, f32[128,128]{1,0:T(8,128)S(1)}, u32[]{:S(2)}, u32[]{:S(2)}) collective-permute-start(f32[128,128]{1,0:T(8,128)S(1)} %get-tuple-element.32.refs_2_.refs_0_), channel_id=1, source_target_pairs={{0,8},{4,12},{8,0},{12,4},{1,9},{5,13},{9,1},{13,5},{2,10},{6,14},... | collective-permute-start | bytes 196616 | tf_op jit(solution)/shard_map/ppermute | solution.py:241
  91.4 3.2 %prepare3.1 = (f32[128,128]{1,0:T(8,128)S(1)}, bf16[2,256,512]{2,1,0:T(8,128)(2,1)S(1)}, bf16[1024,512]{1,0:T(8,128)(2,1)S(1)}) custom-call(f32[19,128,128]{2,1,0:T(8,128)S(1)} %dense.1.refs_0_, f32[19,128,128]{2,1,0:T(8,128)S(1)} %collective-permute-done.14.refs_1_, f32[19,128,128]{2,1,0:T(8,128)S(1)} %collective-permute-done.15.refs_2_, ...), custom_call_target="tpu_custom_call" | custom-call | tf_op jit(solution)/shard_map/prepare3/pallas_call | solution.py:267
  94.6 2.1 %collective-permute-done.26.refs_3_ = f32[128,128]{1,0:T(8,128)S(1)} collective-permute-done((f32[128,128]{1,0:T(8,128)S(1)}, f32[128,128]{1,0:T(8,128)S(1)}, u32[]{:S(2)}, u32[]{:S(2)}) %collective-permute-start.26) | collective-permute-done | bytes 65568 | tf_op jit(solution)/shard_map/ppermute | solution.py:241
  97.5 1.7 %collective-permute-start.29 = (f32[128,128]{1,0:T(8,128)S(1)}, f32[128,128]{1,0:T(8,128)S(1)}, u32[]{:S(2)}, u32[]{:S(2)}) collective-permute-start(f32[128,128]{1,0:T(8,128)S(1)} %get-tuple-element.37.refs_0_), channel_id=1, source_target_pairs={{0,4},{4,0},{8,12},{12,8},{1,5},{5,1},{9,13},{13,9},{2,6},{6,2},{1... | collective-permute-start | bytes 196616 | tf_op jit(solution)/shard_map/ppermute | solution.py:241
  99.2 1.7 %collective-permute-start.30 = (f32[128,128]{1,0:T(8,128)S(1)}, f32[128,128]{1,0:T(8,128)S(1)}, u32[]{:S(2)}, u32[]{:S(2)}) collective-permute-start(f32[128,128]{1,0:T(8,128)S(1)} %get-tuple-element.37.refs_0_), channel_id=1, source_target_pairs={{0,8},{4,12},{8,0},{12,4},{1,9},{5,13},{9,1},{13,5},{2,10},{6,14},... | collective-permute-start | bytes 196616 | tf_op jit(solution)/shard_map/ppermute | solution.py:241
  100.9 1.2 %collective-permute-start.31 = (f32[128,128]{1,0:T(8,128)S(1)}, f32[128,128]{1,0:T(8,128)S(1)}, u32[]{:S(2)}, u32[]{:S(2)}) collective-permute-start(f32[128,128]{1,0:T(8,128)S(1)} %get-tuple-element.37.refs_0_), channel_id=1, source_target_pairs={{0,12},{4,8},{8,4},{12,0},{1,13},{5,9},{9,5},{13,1},{2,14},{6,10},... | collective-permute-start | bytes 196616 | tf_op jit(solution)/shard_map/ppermute | solution.py:241
  102.1 5.3 %collective-permute-done.30.refs_2_ = f32[128,128]{1,0:T(8,128)S(1)} collective-permute-done((f32[128,128]{1,0:T(8,128)S(1)}, f32[128,128]{1,0:T(8,128)S(1)}, u32[]{:S(2)}, u32[]{:S(2)}) %collective-permute-start.30) | collective-permute-done | bytes 65568 | tf_op jit(solution)/shard_map/ppermute | solution.py:241
  (55 shorter events, 10.6 us)
Async XLA Ops:
  2.8 48.1 %collective-permute-start.15 = (f32[19,128,128]{2,1,0:T(8,128)S(1)}, f32[19,128,128]{2,1,0:T(8,128)S(1)}, u32[]{:S(2)}, u32[]{:S(2)}) collective-permute-start(f32[19,128,128]{2,1,0:T(8,128)S(1)} %dense.1.refs_0_), channel_id=1, source_target_pairs={{0,2},{1,3},{2,0},{3,1},{4,6},{5,7},{6,4},{7,5},{8,10},{9,11},{10,... | collective-permute-start | bytes 3735560 | tf_op jit(solution)/shard_map/ppermute | solution.py:241
  5.8 26.0 %collective-permute-start.4 = (f32[736,128]{1,0:T(8,128)S(1)}, f32[736,128]{1,0:T(8,128)S(1)}, u32[]{:S(2)}, u32[]{:S(2)}) collective-permute-start(f32[736,128]{1,0:T(8,128)S(1)} %get-tuple-element.22.refs_2_.refs_0_.refs_5_), channel_id=1, source_target_pairs={{0,8},{4,12},{8,0},{12,4},{1,9},{5,13},{9,1},{13,5},{2,10},{6,14},... | collective-permute-start | bytes 1130504 | tf_op jit(solution)/shard_map/ppermute | solution.py:241
  8.4 27.9 %collective-permute-start.9 = (f32[4,128,128]{2,1,0:T(8,128)S(1)}, f32[4,128,128]{2,1,0:T(8,128)S(1)}, u32[]{:S(2)}, u32[]{:S(2)}) collective-permute-start(f32[4,128,128]{2,1,0:T(8,128)S(1)} %get-tuple-element.23.refs_6_), channel_id=1, source_target_pairs={{0,8},{4,12},{8,0},{12,4},{1,9},{5,13},{9,1},{13,5},{2,10},{6,14},... | collective-permute-start | bytes 786440 | tf_op jit(solution)/shard_map/ppermute | solution.py:241
  8.7 27.6 %collective-permute-start.3 = (f32[736,128]{1,0:T(8,128)S(1)}, f32[736,128]{1,0:T(8,128)S(1)}, u32[]{:S(2)}, u32[]{:S(2)}) collective-permute-start(f32[736,128]{1,0:T(8,128)S(1)} %get-tuple-element.22.refs_2_.refs_0_.refs_5_), channel_id=1, source_target_pairs={{0,4},{4,0},{8,12},{12,8},{1,5},{5,1},{9,13},{13,9},{2,6},{6,2},{1... | collective-permute-start | bytes 1130504 | tf_op jit(solution)/shard_map/ppermute | solution.py:241
  31.8 12.6 %collective-permute-start.5 = (f32[736,128]{1,0:T(8,128)S(1)}, f32[736,128]{1,0:T(8,128)S(1)}, u32[]{:S(2)}, u32[]{:S(2)}) collective-permute-start(f32[736,128]{1,0:T(8,128)S(1)} %collective-permute-done.4.refs_2_), channel_id=1, source_target_pairs={{0,4},{4,0},{8,12},{12,8},{1,5},{5,1},{9,13},{13,9},{2,6},{6,2},{1... | collective-permute-start | bytes 1130504 | tf_op jit(solution)/shard_map/ppermute | solution.py:241
  32.8 11.6 %collective-permute-start.1 = (f32[4,128,128]{2,1,0:T(8,128)S(1)}, f32[4,128,128]{2,1,0:T(8,128)S(1)}, u32[]{:S(2)}, u32[]{:S(2)}) collective-permute-start(f32[4,128,128]{2,1,0:T(8,128)S(1)} %dense0.1.refs_0_), channel_id=1, source_target_pairs={{0,2},{1,3},{2,0},{3,1},{4,6},{5,7},{6,4},{7,5},{8,10},{9,11},{10,... | collective-permute-start | bytes 786440 | tf_op jit(solution)/shard_map/ppermute | solution.py:241
  36.3 8.7 %collective-permute-start = (f32[4,128,128]{2,1,0:T(8,128)S(1)}, f32[4,128,128]{2,1,0:T(8,128)S(1)}, u32[]{:S(2)}, u32[]{:S(2)}) collective-permute-start(f32[4,128,128]{2,1,0:T(8,128)S(1)} %dense0.1.refs_0_), channel_id=1, source_target_pairs={{0,1},{1,0},{2,3},{3,2},{4,5},{5,4},{6,7},{7,6},{8,9},{9,8},{10,11... | collective-permute-start | bytes 786440 | tf_op jit(solution)/shard_map/ppermute | solution.py:241
  36.3 15.1 %collective-permute-start.8 = (f32[4,128,128]{2,1,0:T(8,128)S(1)}, f32[4,128,128]{2,1,0:T(8,128)S(1)}, u32[]{:S(2)}, u32[]{:S(2)}) collective-permute-start(f32[4,128,128]{2,1,0:T(8,128)S(1)} %get-tuple-element.23.refs_6_), channel_id=1, source_target_pairs={{0,4},{4,0},{8,12},{12,8},{1,5},{5,1},{9,13},{13,9},{2,6},{6,2},{1... | collective-permute-start | bytes 786440 | tf_op jit(solution)/shard_map/ppermute | solution.py:241
  44.4 11.1 %collective-permute-start.10 = (f32[4,128,128]{2,1,0:T(8,128)S(1)}, f32[4,128,128]{2,1,0:T(8,128)S(1)}, u32[]{:S(2)}, u32[]{:S(2)}) collective-permute-start(f32[4,128,128]{2,1,0:T(8,128)S(1)} %collective-permute-done.9.refs_8_), channel_id=1, source_target_pairs={{0,4},{4,0},{8,12},{12,8},{1,5},{5,1},{9,13},{13,9},{2,6},{6,2},{1... | collective-permute-start | bytes 786440 | tf_op jit(solution)/shard_map/ppermute | solution.py:241
  44.4 6.4 %collective-permute-start.6 = (f32[256,128]{1,0:T(8,128)S(1)}, f32[256,128]{1,0:T(8,128)S(1)}, u32[]{:S(2)}, u32[]{:S(2)}) collective-permute-start(f32[256,128]{1,0:T(8,128)S(1)} %ahead0.1.refs_0_), channel_id=1, source_target_pairs={{0,2},{1,3},{2,0},{3,1},{4,6},{5,7},{6,4},{7,5},{8,10},{9,11},{10,... | collective-permute-start | bytes 393224 | tf_op jit(solution)/shard_map/ppermute | solution.py:241
  45.0 14.3 %collective-permute-start.17 = (f32[832,128]{1,0:T(8,128)S(1)}, f32[832,128]{1,0:T(8,128)S(1)}, u32[]{:S(2)}, u32[]{:S(2)}) collective-permute-start(f32[832,128]{1,0:T(8,128)S(1)} %ahead1.1.refs_0_), channel_id=1, source_target_pairs={{0,2},{1,3},{2,0},{3,1},{4,6},{5,7},{6,4},{7,5},{8,10},{9,11},{10,... | collective-permute-start | bytes 1277960 | tf_op jit(solution)/shard_map/ppermute | solution.py:241
  50.9 10.7 %collective-permute-start.14 = (f32[19,128,128]{2,1,0:T(8,128)S(1)}, f32[19,128,128]{2,1,0:T(8,128)S(1)}, u32[]{:S(2)}, u32[]{:S(2)}) collective-permute-start(f32[19,128,128]{2,1,0:T(8,128)S(1)} %dense.1.refs_0_), channel_id=1, source_target_pairs={{0,1},{1,0},{2,3},{3,2},{4,5},{5,4},{6,7},{7,6},{8,9},{9,8},{10,11... | collective-permute-start | bytes 3735560 | tf_op jit(solution)/shard_map/ppermute | solution.py:241
  50.9 14.5 %collective-permute-start.16 = (f32[19,128,128]{2,1,0:T(8,128)S(1)}, f32[19,128,128]{2,1,0:T(8,128)S(1)}, u32[]{:S(2)}, u32[]{:S(2)}) collective-permute-start(f32[19,128,128]{2,1,0:T(8,128)S(1)} %collective-permute-done.15.refs_2_), channel_id=1, source_target_pairs={{0,1},{1,0},{2,3},{3,2},{4,5},{5,4},{6,7},{7,6},{8,9},{9,8},{10,11... | collective-permute-start | bytes 3735560 | tf_op jit(solution)/shard_map/ppermute | solution.py:241
  51.4 4.6 %collective-permute-start.2 = (f32[4,128,128]{2,1,0:T(8,128)S(1)}, f32[4,128,128]{2,1,0:T(8,128)S(1)}, u32[]{:S(2)}, u32[]{:S(2)}) collective-permute-start(f32[4,128,128]{2,1,0:T(8,128)S(1)} %collective-permute-done.1.refs_2_), channel_id=1, source_target_pairs={{0,1},{1,0},{2,3},{3,2},{4,5},{5,4},{6,7},{7,6},{8,9},{9,8},{10,11... | collective-permute-start | bytes 786440 | tf_op jit(solution)/shard_map/ppermute | solution.py:241
  55.5 1.5 %collective-permute-start.7 = (f32[512,128]{1,0:T(8,128)S(1)}, f32[512,128]{1,0:T(8,128)S(1)}, u32[]{:S(2)}, u32[]{:S(2)}) collective-permute-start(f32[512,128]{1,0:T(8,128)S(1)} %aheads0.1.refs_4_), channel_id=1, source_target_pairs={{0,1},{1,0},{2,3},{3,2},{4,5},{5,4},{6,7},{7,6},{8,9},{9,8},{10,11... | collective-permute-start | bytes 786440 | tf_op jit(solution)/shard_map/ppermute | solution.py:241
  59.4 4.9 %collective-permute-start.18 = (f32[1664,128]{1,0:T(8,128)S(1)}, f32[1664,128]{1,0:T(8,128)S(1)}, u32[]{:S(2)}, u32[]{:S(2)}) collective-permute-start(f32[1664,128]{1,0:T(8,128)S(1)} %aheads1.1.refs_4_), channel_id=1, source_target_pairs={{0,1},{1,0},{2,3},{3,2},{4,5},{5,4},{6,7},{7,6},{8,9},{9,8},{10,11... | collective-permute-start | bytes 2555912 | tf_op jit(solution)/shard_map/ppermute | solution.py:241
  59.6 12.9 %collective-permute-start.22 = (f32[896,128]{1,0:T(8,128)S(1)}, f32[896,128]{1,0:T(8,128)S(1)}, u32[]{:S(2)}, u32[]{:S(2)}) collective-permute-start(f32[896,128]{1,0:T(8,128)S(1)} %ahead2.1.refs_0_), channel_id=1, source_target_pairs={{0,2},{1,3},{2,0},{3,1},{4,6},{5,7},{6,4},{7,5},{8,10},{9,11},{10,... | collective-permute-start | bytes 1376264 | tf_op jit(solution)/shard_map/ppermute | solution.py:241
  60.2 7.7 %collective-permute-start.11 = (f32[128,128]{1,0:T(8,128)S(1)}, f32[128,128]{1,0:T(8,128)S(1)}, u32[]{:S(2)}, u32[]{:S(2)}) collective-permute-start(f32[128,128]{1,0:T(8,128)S(1)} %prepare0.1.refs_2_.refs_0_.refs_4_), channel_id=1, source_target_pairs={{0,4},{4,0},{8,12},{12,8},{1,5},{5,1},{9,13},{13,9},{2,6},{6,2},{1... | collective-permute-start | bytes 196616 | tf_op jit(solution)/shard_map/ppermute | solution.py:241
  61.5 6.4 %collective-permute-start.12 = (f32[128,128]{1,0:T(8,128)S(1)}, f32[128,128]{1,0:T(8,128)S(1)}, u32[]{:S(2)}, u32[]{:S(2)}) collective-permute-start(f32[128,128]{1,0:T(8,128)S(1)} %prepare0.1.refs_2_.refs_0_.refs_4_), channel_id=1, source_target_pairs={{0,8},{4,12},{8,0},{12,4},{1,9},{5,13},{9,1},{13,5},{2,10},{6,14},... | collective-permute-start | bytes 196616 | tf_op jit(solution)/shard_map/ppermute | solution.py:241
  64.3 6.1 %collective-permute-start.13 = (f32[128,128]{1,0:T(8,128)S(1)}, f32[128,128]{1,0:T(8,128)S(1)}, u32[]{:S(2)}, u32[]{:S(2)}) collective-permute-start(f32[128,128]{1,0:T(8,128)S(1)} %prepare0.1.refs_2_.refs_0_.refs_4_), channel_id=1, source_target_pairs={{0,12},{4,8},{8,4},{12,0},{1,13},{5,9},{9,5},{13,1},{2,14},{6,10},... | collective-permute-start | bytes 196616 | tf_op jit(solution)/shard_map/ppermute | solution.py:241
  72.6 5.6 %collective-permute-start.23 = (f32[1792,128]{1,0:T(8,128)S(1)}, f32[1792,128]{1,0:T(8,128)S(1)}, u32[]{:S(2)}, u32[]{:S(2)}) collective-permute-start(f32[1792,128]{1,0:T(8,128)S(1)} %aheads2.1.refs_4_), channel_id=1, source_target_pairs={{0,1},{1,0},{2,3},{3,2},{4,5},{5,4},{6,7},{7,6},{8,9},{9,8},{10,11... | collective-permute-start | bytes 2752520 | tf_op jit(solution)/shard_map/ppermute | solution.py:241
  72.7 13.7 %collective-permute-start.27 = (f32[960,128]{1,0:T(8,128)S(1)}, f32[960,128]{1,0:T(8,128)S(1)}, u32[]{:S(2)}, u32[]{:S(2)}) collective-permute-start(f32[960,128]{1,0:T(8,128)S(1)} %ahead3.1.refs_0_), channel_id=1, source_target_pairs={{0,2},{1,3},{2,0},{3,1},{4,6},{5,7},{6,4},{7,5},{8,10},{9,11},{10,... | collective-permute-start | bytes 1474568 | tf_op jit(solution)/shard_map/ppermute | solution.py:241
  73.2 7.7 %collective-permute-start.19 = (f32[128,128]{1,0:T(8,128)S(1)}, f32[128,128]{1,0:T(8,128)S(1)}, u32[]{:S(2)}, u32[]{:S(2)}) collective-permute-start(f32[128,128]{1,0:T(8,128)S(1)} %get-tuple-element.27.refs_2_.refs_0_.refs_4_), channel_id=1, source_target_pairs={{0,4},{4,0},{8,12},{12,8},{1,5},{5,1},{9,13},{13,9},{2,6},{6,2},{1... | collective-permute-start | bytes 196616 | tf_op jit(solution)/shard_map/ppermute | solution.py:241
  74.6 6.4 %collective-permute-start.20 = (f32[128,128]{1,0:T(8,128)S(1)}, f32[128,128]{1,0:T(8,128)S(1)}, u32[]{:S(2)}, u32[]{:S(2)}) collective-permute-start(f32[128,128]{1,0:T(8,128)S(1)} %get-tuple-element.27.refs_2_.refs_0_.refs_4_), channel_id=1, source_target_pairs={{0,8},{4,12},{8,0},{12,4},{1,9},{5,13},{9,1},{13,5},{2,10},{6,14},... | collective-permute-start | bytes 196616 | tf_op jit(solution)/shard_map/ppermute | solution.py:241
  77.3 6.1 %collective-permute-start.21 = (f32[128,128]{1,0:T(8,128)S(1)}, f32[128,128]{1,0:T(8,128)S(1)}, u32[]{:S(2)}, u32[]{:S(2)}) collective-permute-start(f32[128,128]{1,0:T(8,128)S(1)} %get-tuple-element.27.refs_2_.refs_0_.refs_4_), channel_id=1, source_target_pairs={{0,12},{4,8},{8,4},{12,0},{1,13},{5,9},{9,5},{13,1},{2,14},{6,10},... | collective-permute-start | bytes 196616 | tf_op jit(solution)/shard_map/ppermute | solution.py:241
  86.4 5.0 %collective-permute-start.28 = (f32[1920,128]{1,0:T(8,128)S(1)}, f32[1920,128]{1,0:T(8,128)S(1)}, u32[]{:S(2)}, u32[]{:S(2)}) collective-permute-start(f32[1920,128]{1,0:T(8,128)S(1)} %aheads3.1.refs_4_), channel_id=1, source_target_pairs={{0,1},{1,0},{2,3},{3,2},{4,5},{5,4},{6,7},{7,6},{8,9},{9,8},{10,11... | collective-permute-start | bytes 2949128 | tf_op jit(solution)/shard_map/ppermute | solution.py:241
  86.5 8.1 %collective-permute-start.24 = (f32[128,128]{1,0:T(8,128)S(1)}, f32[128,128]{1,0:T(8,128)S(1)}, u32[]{:S(2)}, u32[]{:S(2)}) collective-permute-start(f32[128,128]{1,0:T(8,128)S(1)} %get-tuple-element.32.refs_2_.refs_0_), channel_id=1, source_target_pairs={{0,4},{4,0},{8,12},{12,8},{1,5},{5,1},{9,13},{13,9},{2,6},{6,2},{1... | collective-permute-start | bytes 196616 | tf_op jit(solution)/shard_map/ppermute | solution.py:241
  87.9 6.7 %collective-permute-start.25 = (f32[128,128]{1,0:T(8,128)S(1)}, f32[128,128]{1,0:T(8,128)S(1)}, u32[]{:S(2)}, u32[]{:S(2)}) collective-permute-start(f32[128,128]{1,0:T(8,128)S(1)} %get-tuple-element.32.refs_2_.refs_0_), channel_id=1, source_target_pairs={{0,8},{4,12},{8,0},{12,4},{1,9},{5,13},{9,1},{13,5},{2,10},{6,14},... | collective-permute-start | bytes 196616 | tf_op jit(solution)/shard_map/ppermute | solution.py:241
  90.6 6.1 %collective-permute-start.26 = (f32[128,128]{1,0:T(8,128)S(1)}, f32[128,128]{1,0:T(8,128)S(1)}, u32[]{:S(2)}, u32[]{:S(2)}) collective-permute-start(f32[128,128]{1,0:T(8,128)S(1)} %get-tuple-element.32.refs_2_.refs_0_), channel_id=1, source_target_pairs={{0,12},{4,8},{8,4},{12,0},{1,13},{5,9},{9,5},{13,1},{2,14},{6,10},... | collective-permute-start | bytes 196616 | tf_op jit(solution)/shard_map/ppermute | solution.py:241
  97.5 4.6 %collective-permute-start.29 = (f32[128,128]{1,0:T(8,128)S(1)}, f32[128,128]{1,0:T(8,128)S(1)}, u32[]{:S(2)}, u32[]{:S(2)}) collective-permute-start(f32[128,128]{1,0:T(8,128)S(1)} %get-tuple-element.37.refs_0_), channel_id=1, source_target_pairs={{0,4},{4,0},{8,12},{12,8},{1,5},{5,1},{9,13},{13,9},{2,6},{6,2},{1... | collective-permute-start | bytes 196616 | tf_op jit(solution)/shard_map/ppermute | solution.py:241
  99.2 8.1 %collective-permute-start.30 = (f32[128,128]{1,0:T(8,128)S(1)}, f32[128,128]{1,0:T(8,128)S(1)}, u32[]{:S(2)}, u32[]{:S(2)}) collective-permute-start(f32[128,128]{1,0:T(8,128)S(1)} %get-tuple-element.37.refs_0_), channel_id=1, source_target_pairs={{0,8},{4,12},{8,0},{12,4},{1,9},{5,13},{9,1},{13,5},{2,10},{6,14},... | collective-permute-start | bytes 196616 | tf_op jit(solution)/shard_map/ppermute | solution.py:241
  100.9 6.4 %collective-permute-start.31 = (f32[128,128]{1,0:T(8,128)S(1)}, f32[128,128]{1,0:T(8,128)S(1)}, u32[]{:S(2)}, u32[]{:S(2)}) collective-permute-start(f32[128,128]{1,0:T(8,128)S(1)} %get-tuple-element.37.refs_0_), channel_id=1, source_target_pairs={{0,12},{4,8},{8,4},{12,0},{1,13},{5,9},{9,5},{13,1},{2,14},{6,10},... | collective-permute-start | bytes 196616 | tf_op jit(solution)/shard_map/ppermute | solution.py:241
  (2 other events, 14.0 us)

commit v10 on v9

--- a/solution.py
+++ b/solution.py
@@ -86,20 +86,19 @@
     return (out[:rows, :cols] + (out[:rows, cols:] + out[rows:, :cols])) + out[rows:, cols:]
 
 
-def first_kernel(prev, *refs):
-    known_ref, right_ref, inv_ref, ahead_ref, known_out = refs
-    steps, nb = right_ref.shape[0], inv_ref.shape[1]
+def send_kernel(prev, rows, *refs):
+    right_ref, inv_ref, out_ref = refs
+    nb = inv_ref.shape[1]
     share = right_ref.shape[2] // lax.axis_size("pcol")
     at = pl.multiple_of(lax.axis_index("pcol") * share, share)
     place = 0
-    for step in range(steps):
+    for step in rows:
         if step:
-            ahead_ref[place : place + nb] = inv_ref[step - 1]
+            out_ref[place : place + nb] = inv_ref[step - 1]
             place += nb
         for col in range(prev + step):
-            ahead_ref[place : place + share] = right_ref[step, col, pl.ds(at, share), :]
+            out_ref[place : place + share] = right_ref[step, col, pl.ds(at, share), :]
             place += share
-    known_out[...] = known_ref[...]
 
 
 def dense_kernel(rows, flags_ref, *refs):
@@ -294,12 +293,21 @@
 
     heights = [(nb if step else 0) + (prev + step) * share for step in range(steps)]
 
-    def ahead_far(step, after=()):
+    def sent(rows, after=()):
+        return run(
+            functools.partial(send_kernel, prev, rows),
+            f"send{rows[0]}",
+            shaped(sum(heights[step] for step in rows), nb),
+            [whole_of(pinned(value)) for value in (right_t, inverse_diag)],
+            after=after,
+        )
+
+    def ahead_far(step, slots, begin, after=()):
         own = run(
-            functools.partial(stack_kernel, sum(heights[:step])),
+            functools.partial(stack_kernel, begin),
             f"ahead{step}",
             shaped(n * heights[step], nb),
-            [whole_of(value) for value in ahead],
+            [whole_of(value) for value in slots],
             after=after,
         )
         return [own, shift(own, "pcol", 2)]
@@ -314,20 +322,17 @@
         )
         return [both, shift(both, "pcol", 1)]
 
-    sent, known = run(
-        functools.partial(first_kernel, prev),
-        "first",
-        [shaped(sum(heights), nb), shaped(*earlier.shape)],
-        [whole_of(pinned(value)) for value in (earlier, right_t, inverse_diag)],
-    )
-    ahead = over_rows_forwarded(sent)
-    known = over_rows_forwarded(known)
+    first = sent((0,))
+    ahead0 = over_rows(first)
+    far0 = ahead_far(0, ahead0, 0)
+    ahead = over_rows_forwarded(sent(tuple(range(1, steps)), ahead0[1:]))
+    known = over_rows_forwarded(earlier)
     own = run(
         functools.partial(dense_kernel, [(0, prev)]),
         "dense0",
         shaped(prev, nb, nb),
         [(dense_flags, smem), blocks_of(dense_tiles, 0)],
-        after=[sent],
+        after=far0[1:],
     )
     strips0 = over_cols(own)
     rows = [(step, prev + step) for step in range(1, steps)] + [(steps - 1, 1)]
@@ -339,7 +344,7 @@
         [(dense_flags, smem)]
         + [blocks_of(dense_tiles, step) for step in range(1, steps)]
         + [blocks_of(inverse_diag, steps - 1)],
-        after=[sent],
+        after=[first],
     )
     dense = over_cols(own)
 
@@ -351,9 +356,9 @@
             shaped(1 + last, 2 * nb, n * nb, dtype=bf16),
             shaped(2 * n * nb, n * nb, dtype=bf16),
         ]
-        first = sum(count for row, count in rows[:-1] if row < step)
+        begin = sum(count for row, count in rows[:-1] if row < step)
         return run(
-            functools.partial(prepare_kernel, n, prev, step, first, last),
+            functools.partial(prepare_kernel, n, prev, step, begin, last),
             f"prepare{step}",
             outs if step else outs[0],
             [whole_of(value) for value in [*strips, *later, *known, *solved]]
@@ -373,12 +378,12 @@
             [source_room],
         )
 
-    pending0 = prepare(0, strips0, ahead_near(0, ahead_far(0)))
-    later1 = ahead_near(1, ahead_far(1, []), [pending0])
-    later2 = ahead_far(2, [pending0])
+    pending0 = prepare(0, strips0, ahead_near(0, far0))
+    later1 = ahead_near(1, ahead_far(1, ahead, 0, known[1:]), [pending0])
+    later2 = ahead_far(2, ahead, heights[1], [pending0])
     pending1, solved0 = solve(0, over_rows(pending0), prepare(1, dense, later1))
     later2 = ahead_near(2, later2, [pending1])
-    later3 = ahead_far(3, [pending1])
+    later3 = ahead_far(3, ahead, heights[1] + heights[2], [pending1])
     pending2, solved1 = solve(1, over_rows(pending1), prepare(2, dense, later2, [solved0]))
     later3 = ahead_near(3, later3, [pending2])
     prepared = prepare(3, dense, later3, [solved0, solved1])

time: 109 us -> 121 us (1.11)
  waiting for transfers between devices: 57.6 us -> 66.3 us
  starting transfers between devices: 32.4 us -> 34.2 us
    ppermute x32 -> x35, waiting for transfers between devices: 57.6 us -> 66.3 us  [shift(): return lax.ppermute(value, axis, [(i, i ^ step) for i in range(n)])]
    ppermute x32 -> x35, starting transfers between devices: 32.4 us -> 34.2 us  [shift(): return lax.ppermute(value, axis, [(i, i ^ step) for i in range(n)])]
    pallas_call x19 -> x20, Pallas kernels: 18.1 us -> 19.2 us  [call(): pl.pallas_call(body, grid=(1,), out_shape=shapes, in_specs=specs + [any_s...]
  transfers between devices with their start and end apart: 32 -> 35, of which waited for: 13 -> 17; matrix products, arithmetic and copies ran while one was open for 0% -> 0% of each run, Pallas kernels for 12% -> 12%
where the time goes in v10:
time: 121 us
  waiting for transfers between devices  66.3 us (55%)
  starting transfers between devices  34.2 us (28%)
  Pallas kernels  19.2 us (16%)
    ppermute x35, waiting for transfers between devices, shift(): return lax.ppermute(value, axis, [(i, i ^ step) for i in range(n)])  66.3 us
    ppermute x35, starting transfers between devices, shift(): return lax.ppermute(value, axis, [(i, i ^ step) for i in range(n)])  34.2 us
    pallas_call x20, Pallas kernels, call(): pl.pallas_call(body, grid=(1,), out_shape=shapes, in_specs=specs + [any_s...  19.2 us
  transfers between devices with their start and end apart: 35, of which 17 were waited for; matrix products, arithmetic and copies ran while one was open for 0% of the time, Pallas kernels for 12%

profile of v10, /device:TPU:0, one launch (start us, length us, event | category | flops | bytes accessed | tf_op | source)
XLA Modules:
  0.0 120.7 jit_solution(2348346821131926567)
XLA Ops:
  1.9 1.4 %dense.1.refs_0_ = f32[19,128,128]{2,1,0:T(8,128)S(1)} custom-call(s32[4,7]{1,0:T(4,128)S(1)} %copy-done.1, f32[4,7,128,128]{3,2,1,0:T(8,128)} %refs_3_.1, f32[4,7,128,128]{3,2,1,0:T(8,128)} %refs_3_.1, f32[4,7,128,128]{3,2,1,0:T(8,128)} %refs_3_.1, f32[4,128,128]{2,1,0:T(8,128)} %refs_1_.7, f32[64,128]{1,0:T(8,128)S(1)} %send0.1.refs_0_.refs_5_), custom_call_target="tpu_custom_call" | custom-call | tf_op jit(solution)/shard_map/dense/pallas_call | solution.py:266
  3.3 3.0 %collective-permute-start.15 = (f32[19,128,128]{2,1,0:T(8,128)S(1)}, f32[19,128,128]{2,1,0:T(8,128)S(1)}, u32[]{:S(2)}, u32[]{:S(2)}) collective-permute-start(f32[19,128,128]{2,1,0:T(8,128)S(1)} %dense.1.refs_0_), channel_id=1, source_target_pairs={{0,2},{1,3},{2,0},{3,1},{4,6},{5,7},{6,4},{7,5},{8,10},{9,11},{10,... | collective-permute-start | bytes 3735560 | tf_op jit(solution)/shard_map/ppermute | solution.py:240
  6.3 1.6 %collective-permute-start = (f32[64,128]{1,0:T(8,128)S(1)}, f32[64,128]{1,0:T(8,128)S(1)}, u32[]{:S(2)}, u32[]{:S(2)}) collective-permute-start(f32[64,128]{1,0:T(8,128)S(1)} %send0.1.refs_0_.refs_5_), channel_id=1, source_target_pairs={{0,4},{4,0},{8,12},{12,8},{1,5},{5,1},{9,13},{13,9},{2,6},{6,2},{1... | collective-permute-start | bytes 98312 | tf_op jit(solution)/shard_map/ppermute | solution.py:240
  7.9 2.6 %collective-permute-start.1 = (f32[64,128]{1,0:T(8,128)S(1)}, f32[64,128]{1,0:T(8,128)S(1)}, u32[]{:S(2)}, u32[]{:S(2)}) collective-permute-start(f32[64,128]{1,0:T(8,128)S(1)} %send0.1.refs_0_.refs_5_), channel_id=1, source_target_pairs={{0,8},{4,12},{8,0},{12,4},{1,9},{5,13},{9,1},{13,5},{2,10},{6,14},... | collective-permute-start | bytes 98312 | tf_op jit(solution)/shard_map/ppermute | solution.py:240
  10.7 2.3 %collective-permute-done.1.refs_2_.refs_3_ = f32[64,128]{1,0:T(8,128)S(1)} collective-permute-done((f32[64,128]{1,0:T(8,128)S(1)}, f32[64,128]{1,0:T(8,128)S(1)}, u32[]{:S(2)}, u32[]{:S(2)}) %collective-permute-start.1) | collective-permute-done | bytes 32800 | tf_op jit(solution)/shard_map/ppermute | solution.py:240
  13.0 3.2 %collective-permute-done.2.refs_3_.refs_4_ = f32[64,128]{1,0:T(8,128)S(1)} collective-permute-done((f32[64,128]{1,0:T(8,128)S(1)}, f32[64,128]{1,0:T(8,128)S(1)}, u32[]{:S(2)}, u32[]{:S(2)}) %collective-permute-start.2) | collective-permute-done | bytes 32800 | tf_op jit(solution)/shard_map/ppermute | solution.py:240
  17.6 2.9 %collective-permute-start.9 = (f32[4,128,128]{2,1,0:T(8,128)S(1)}, f32[4,128,128]{2,1,0:T(8,128)S(1)}, u32[]{:S(2)}, u32[]{:S(2)}) collective-permute-start(f32[4,128,128]{2,1,0:T(8,128)S(1)} %copy-done), channel_id=1, source_target_pairs={{0,8},{4,12},{8,0},{12,4},{1,9},{5,13},{9,1},{13,5},{2,10},{6,14},... | collective-permute-start | bytes 786440 | tf_op jit(solution)/shard_map/ppermute | solution.py:240
  21.1 15.4 %collective-permute-done.3.refs_2_.refs_1_ = f32[256,128]{1,0:T(8,128)S(1)} collective-permute-done((f32[256,128]{1,0:T(8,128)S(1)}, f32[256,128]{1,0:T(8,128)S(1)}, u32[]{:S(2)}, u32[]{:S(2)}) %collective-permute-start.3) | collective-permute-done | bytes 131104 | tf_op jit(solution)/shard_map/ppermute | solution.py:240
  36.5 1.8 %collective-permute-start.8 = (f32[4,128,128]{2,1,0:T(8,128)S(1)}, f32[4,128,128]{2,1,0:T(8,128)S(1)}, u32[]{:S(2)}, u32[]{:S(2)}) collective-permute-start(f32[4,128,128]{2,1,0:T(8,128)S(1)} %copy-done), channel_id=1, source_target_pairs={{0,4},{4,0},{8,12},{12,8},{1,5},{5,1},{9,13},{13,9},{2,6},{6,2},{1... | collective-permute-start | bytes 786440 | tf_op jit(solution)/shard_map/ppermute | solution.py:240
  38.6 4.8 %collective-permute-done.9.refs_8_.refs_5_ = f32[4,128,128]{2,1,0:T(8,128)S(1)} collective-permute-done((f32[4,128,128]{2,1,0:T(8,128)S(1)}, f32[4,128,128]{2,1,0:T(8,128)S(1)}, u32[]{:S(2)}, u32[]{:S(2)}) %collective-permute-start.9) | collective-permute-done | bytes 262176 | tf_op jit(solution)/shard_map/ppermute | solution.py:240
  44.5 4.5 %collective-permute-done.8.refs_7_.refs_4_ = f32[4,128,128]{2,1,0:T(8,128)S(1)} collective-permute-done((f32[4,128,128]{2,1,0:T(8,128)S(1)}, f32[4,128,128]{2,1,0:T(8,128)S(1)}, u32[]{:S(2)}, u32[]{:S(2)}) %collective-permute-start.8) | collective-permute-done | bytes 262176 | tf_op jit(solution)/shard_map/ppermute | solution.py:240
  49.5 12.4 %collective-permute-done.10.refs_9_.refs_6_ = f32[4,128,128]{2,1,0:T(8,128)S(1)} collective-permute-done((f32[4,128,128]{2,1,0:T(8,128)S(1)}, f32[4,128,128]{2,1,0:T(8,128)S(1)}, u32[]{:S(2)}, u32[]{:S(2)}) %collective-permute-start.10) | collective-permute-done | bytes 262176 | tf_op jit(solution)/shard_map/ppermute | solution.py:240
  63.5 4.1 %collective-permute-done.4.refs_1_ = f32[4,128,128]{2,1,0:T(8,128)S(1)} collective-permute-done((f32[4,128,128]{2,1,0:T(8,128)S(1)}, f32[4,128,128]{2,1,0:T(8,128)S(1)}, u32[]{:S(2)}, u32[]{:S(2)}) %collective-permute-start.4) | collective-permute-done | bytes 262176 | tf_op jit(solution)/shard_map/ppermute | solution.py:240
  68.0 2.3 %prepare0.1.refs_2_.refs_0_.refs_4_ = f32[128,128]{1,0:T(8,128)S(1)} custom-call(f32[4,128,128]{2,1,0:T(8,128)S(1)} %dense0.1.refs_0_, f32[4,128,128]{2,1,0:T(8,128)S(1)} %collective-permute-done.4.refs_1_, f32[4,128,128]{2,1,0:T(8,128)S(1)} %collective-permute-done.5.refs_2_, f32[4,128,128]{2,1,0:T(8,128)S(1)} %collective-permute-done.6.refs_3_, ...), custom_call_target="tpu_custom_call" | custom-call | tf_op jit(solution)/shard_map/prepare0/pallas_call | solution.py:266
  70.2 3.5 %collective-permute-done.20.refs_1_ = f32[832,128]{1,0:T(8,128)S(1)} collective-permute-done((f32[832,128]{1,0:T(8,128)S(1)}, f32[832,128]{1,0:T(8,128)S(1)}, u32[]{:S(2)}, u32[]{:S(2)}) %collective-permute-start.20) | collective-permute-done | bytes 426016 | tf_op jit(solution)/shard_map/ppermute | solution.py:240
  74.5 2.8 %collective-permute-start.12 = (f32[128,128]{1,0:T(8,128)S(1)}, f32[128,128]{1,0:T(8,128)S(1)}, u32[]{:S(2)}, u32[]{:S(2)}) collective-permute-start(f32[128,128]{1,0:T(8,128)S(1)} %prepare0.1.refs_2_.refs_0_.refs_4_), channel_id=1, source_target_pairs={{0,8},{4,12},{8,0},{12,4},{1,9},{5,13},{9,1},{13,5},{2,10},{6,14},... | collective-permute-start | bytes 196616 | tf_op jit(solution)/shard_map/ppermute | solution.py:240
  77.3 1.6 %collective-permute-start.13 = (f32[128,128]{1,0:T(8,128)S(1)}, f32[128,128]{1,0:T(8,128)S(1)}, u32[]{:S(2)}, u32[]{:S(2)}) collective-permute-start(f32[128,128]{1,0:T(8,128)S(1)} %prepare0.1.refs_2_.refs_0_.refs_4_), channel_id=1, source_target_pairs={{0,12},{4,8},{8,4},{12,0},{1,13},{5,9},{9,5},{13,1},{2,14},{6,10},... | collective-permute-start | bytes 196616 | tf_op jit(solution)/shard_map/ppermute | solution.py:240
  78.9 2.6 %prepare1.1 = (f32[128,128]{1,0:T(8,128)S(1)}, bf16[1,256,512]{2,1,0:T(8,128)(2,1)S(1)}, bf16[1024,512]{1,0:T(8,128)(2,1)S(1)}) custom-call(f32[19,128,128]{2,1,0:T(8,128)S(1)} %dense.1.refs_0_, f32[19,128,128]{2,1,0:T(8,128)S(1)} %collective-permute-done.14.refs_1_, f32[19,128,128]{2,1,0:T(8,128)S(1)} %collective-permute-done.15.refs_2_, ...), custom_call_target="tpu_custom_call" | custom-call | tf_op jit(solution)/shard_map/prepare1/pallas_call | solution.py:266
  82.2 1.3 %collective-permute-done.13.refs_3_ = f32[128,128]{1,0:T(8,128)S(1)} collective-permute-done((f32[128,128]{1,0:T(8,128)S(1)}, f32[128,128]{1,0:T(8,128)S(1)}, u32[]{:S(2)}, u32[]{:S(2)}) %collective-permute-start.13) | collective-permute-done | bytes 65568 | tf_op jit(solution)/shard_map/ppermute | solution.py:240
  84.2 2.7 %collective-permute-done.25.refs_1_ = f32[896,128]{1,0:T(8,128)S(1)} collective-permute-done((f32[896,128]{1,0:T(8,128)S(1)}, f32[896,128]{1,0:T(8,128)S(1)}, u32[]{:S(2)}, u32[]{:S(2)}) %collective-permute-start.25) | collective-permute-done | bytes 458784 | tf_op jit(solution)/shard_map/ppermute | solution.py:240
  87.6 2.8 %collective-permute-start.23 = (f32[128,128]{1,0:T(8,128)S(1)}, f32[128,128]{1,0:T(8,128)S(1)}, u32[]{:S(2)}, u32[]{:S(2)}) collective-permute-start(f32[128,128]{1,0:T(8,128)S(1)} %get-tuple-element.23.refs_2_.refs_0_.refs_4_), channel_id=1, source_target_pairs={{0,8},{4,12},{8,0},{12,4},{1,9},{5,13},{9,1},{13,5},{2,10},{6,14},... | collective-permute-start | bytes 196616 | tf_op jit(solution)/shard_map/ppermute | solution.py:240
  90.4 1.6 %collective-permute-start.24 = (f32[128,128]{1,0:T(8,128)S(1)}, f32[128,128]{1,0:T(8,128)S(1)}, u32[]{:S(2)}, u32[]{:S(2)}) collective-permute-start(f32[128,128]{1,0:T(8,128)S(1)} %get-tuple-element.23.refs_2_.refs_0_.refs_4_), channel_id=1, source_target_pairs={{0,12},{4,8},{8,4},{12,0},{1,13},{5,9},{9,5},{13,1},{2,14},{6,10},... | collective-permute-start | bytes 196616 | tf_op jit(solution)/shard_map/ppermute | solution.py:240
  92.0 2.8 %prepare2.1 = (f32[128,128]{1,0:T(8,128)S(1)}, bf16[1,256,512]{2,1,0:T(8,128)(2,1)S(1)}, bf16[1024,512]{1,0:T(8,128)(2,1)S(1)}) custom-call(f32[19,128,128]{2,1,0:T(8,128)S(1)} %dense.1.refs_0_, f32[19,128,128]{2,1,0:T(8,128)S(1)} %collective-permute-done.14.refs_1_, f32[19,128,128]{2,1,0:T(8,128)S(1)} %collective-permute-done.15.refs_2_, ...), custom_call_target="tpu_custom_call" | custom-call | tf_op jit(solution)/shard_map/prepare2/pallas_call | solution.py:266
  95.3 1.3 %collective-permute-done.24.refs_3_ = f32[128,128]{1,0:T(8,128)S(1)} collective-permute-done((f32[128,128]{1,0:T(8,128)S(1)}, f32[128,128]{1,0:T(8,128)S(1)}, u32[]{:S(2)}, u32[]{:S(2)}) %collective-permute-start.24) | collective-permute-done | bytes 65568 | tf_op jit(solution)/shard_map/ppermute | solution.py:240
  97.3 3.4 %collective-permute-done.30.refs_1_ = f32[960,128]{1,0:T(8,128)S(1)} collective-permute-done((f32[960,128]{1,0:T(8,128)S(1)}, f32[960,128]{1,0:T(8,128)S(1)}, u32[]{:S(2)}, u32[]{:S(2)}) %collective-permute-start.30) | collective-permute-done | bytes 491552 | tf_op jit(solution)/shard_map/ppermute | solution.py:240
  101.0 2.8 %collective-permute-start.28 = (f32[128,128]{1,0:T(8,128)S(1)}, f32[128,128]{1,0:T(8,128)S(1)}, u32[]{:S(2)}, u32[]{:S(2)}) collective-permute-start(f32[128,128]{1,0:T(8,128)S(1)} %get-tuple-element.28.refs_2_.refs_0_), channel_id=1, source_target_pairs={{0,8},{4,12},{8,0},{12,4},{1,9},{5,13},{9,1},{13,5},{2,10},{6,14},... | collective-permute-start | bytes 196616 | tf_op jit(solution)/shard_map/ppermute | solution.py:240
  103.7 1.6 %collective-permute-start.29 = (f32[128,128]{1,0:T(8,128)S(1)}, f32[128,128]{1,0:T(8,128)S(1)}, u32[]{:S(2)}, u32[]{:S(2)}) collective-permute-start(f32[128,128]{1,0:T(8,128)S(1)} %get-tuple-element.28.refs_2_.refs_0_), channel_id=1, source_target_pairs={{0,12},{4,8},{8,4},{12,0},{1,13},{5,9},{9,5},{13,1},{2,14},{6,10},... | collective-permute-start | bytes 196616 | tf_op jit(solution)/shard_map/ppermute | solution.py:240
  105.3 3.2 %prepare3.1 = (f32[128,128]{1,0:T(8,128)S(1)}, bf16[2,256,512]{2,1,0:T(8,128)(2,1)S(1)}, bf16[1024,512]{1,0:T(8,128)(2,1)S(1)}) custom-call(f32[19,128,128]{2,1,0:T(8,128)S(1)} %dense.1.refs_0_, f32[19,128,128]{2,1,0:T(8,128)S(1)} %collective-permute-done.14.refs_1_, f32[19,128,128]{2,1,0:T(8,128)S(1)} %collective-permute-done.15.refs_2_, ...), custom_call_target="tpu_custom_call" | custom-call | tf_op jit(solution)/shard_map/prepare3/pallas_call | solution.py:266
  108.5 1.3 %collective-permute-done.29.refs_3_ = f32[128,128]{1,0:T(8,128)S(1)} collective-permute-done((f32[128,128]{1,0:T(8,128)S(1)}, f32[128,128]{1,0:T(8,128)S(1)}, u32[]{:S(2)}, u32[]{:S(2)}) %collective-permute-start.29) | collective-permute-done | bytes 65568 | tf_op jit(solution)/shard_map/ppermute | solution.py:240
  111.9 1.4 %collective-permute-start.33 = (f32[128,128]{1,0:T(8,128)S(1)}, f32[128,128]{1,0:T(8,128)S(1)}, u32[]{:S(2)}, u32[]{:S(2)}) collective-permute-start(f32[128,128]{1,0:T(8,128)S(1)} %get-tuple-element.33.refs_0_), channel_id=1, source_target_pairs={{0,8},{4,12},{8,0},{12,4},{1,9},{5,13},{9,1},{13,5},{2,10},{6,14},... | collective-permute-start | bytes 196616 | tf_op jit(solution)/shard_map/ppermute | solution.py:240
  113.2 1.8 %collective-permute-start.34 = (f32[128,128]{1,0:T(8,128)S(1)}, f32[128,128]{1,0:T(8,128)S(1)}, u32[]{:S(2)}, u32[]{:S(2)}) collective-permute-start(f32[128,128]{1,0:T(8,128)S(1)} %get-tuple-element.33.refs_0_), channel_id=1, source_target_pairs={{0,12},{4,8},{8,4},{12,0},{1,13},{5,9},{9,5},{13,1},{2,14},{6,10},... | collective-permute-start | bytes 196616 | tf_op jit(solution)/shard_map/ppermute | solution.py:240
  115.0 4.7 %collective-permute-done.33.refs_2_ = f32[128,128]{1,0:T(8,128)S(1)} collective-permute-done((f32[128,128]{1,0:T(8,128)S(1)}, f32[128,128]{1,0:T(8,128)S(1)}, u32[]{:S(2)}, u32[]{:S(2)}) %collective-permute-start.33) | collective-permute-done | bytes 65568 | tf_op jit(solution)/shard_map/ppermute | solution.py:240
  (66 shorter events, 15.2 us)
Async XLA Ops:
  3.3 59.2 %collective-permute-start.15 = (f32[19,128,128]{2,1,0:T(8,128)S(1)}, f32[19,128,128]{2,1,0:T(8,128)S(1)}, u32[]{:S(2)}, u32[]{:S(2)}) collective-permute-start(f32[19,128,128]{2,1,0:T(8,128)S(1)} %dense.1.refs_0_), channel_id=1, source_target_pairs={{0,2},{1,3},{2,0},{3,1},{4,6},{5,7},{6,4},{7,5},{8,10},{9,11},{10,... | collective-permute-start | bytes 3735560 | tf_op jit(solution)/shard_map/ppermute | solution.py:240
  7.9 5.1 %collective-permute-start.1 = (f32[64,128]{1,0:T(8,128)S(1)}, f32[64,128]{1,0:T(8,128)S(1)}, u32[]{:S(2)}, u32[]{:S(2)}) collective-permute-start(f32[64,128]{1,0:T(8,128)S(1)} %send0.1.refs_0_.refs_5_), channel_id=1, source_target_pairs={{0,8},{4,12},{8,0},{12,4},{1,9},{5,13},{9,1},{13,5},{2,10},{6,14},... | collective-permute-start | bytes 98312 | tf_op jit(solution)/shard_map/ppermute | solution.py:240
  10.5 5.7 %collective-permute-start.2 = (f32[64,128]{1,0:T(8,128)S(1)}, f32[64,128]{1,0:T(8,128)S(1)}, u32[]{:S(2)}, u32[]{:S(2)}) collective-permute-start(f32[64,128]{1,0:T(8,128)S(1)} %send0.1.refs_0_.refs_5_), channel_id=1, source_target_pairs={{0,12},{4,8},{8,4},{12,0},{1,13},{5,9},{9,5},{13,1},{2,14},{6,10},... | collective-permute-start | bytes 98312 | tf_op jit(solution)/shard_map/ppermute | solution.py:240
  17.5 20.9 %collective-permute-start.18 = (f32[672,128]{1,0:T(8,128)S(1)}, f32[672,128]{1,0:T(8,128)S(1)}, u32[]{:S(2)}, u32[]{:S(2)}) collective-permute-start(f32[672,128]{1,0:T(8,128)S(1)} %send1.1.refs_0_), channel_id=1, source_target_pairs={{0,8},{4,12},{8,0},{12,4},{1,9},{5,13},{9,1},{13,5},{2,10},{6,14},... | collective-permute-start | bytes 1032200 | tf_op jit(solution)/shard_map/ppermute | solution.py:240
  17.6 25.8 %collective-permute-start.9 = (f32[4,128,128]{2,1,0:T(8,128)S(1)}, f32[4,128,128]{2,1,0:T(8,128)S(1)}, u32[]{:S(2)}, u32[]{:S(2)}) collective-permute-start(f32[4,128,128]{2,1,0:T(8,128)S(1)} %copy-done), channel_id=1, source_target_pairs={{0,8},{4,12},{8,0},{12,4},{1,9},{5,13},{9,1},{13,5},{2,10},{6,14},... | collective-permute-start | bytes 786440 | tf_op jit(solution)/shard_map/ppermute | solution.py:240
  20.5 16.0 %collective-permute-start.3 = (f32[256,128]{1,0:T(8,128)S(1)}, f32[256,128]{1,0:T(8,128)S(1)}, u32[]{:S(2)}, u32[]{:S(2)}) collective-permute-start(f32[256,128]{1,0:T(8,128)S(1)} %ahead0.1.refs_0_), channel_id=1, source_target_pairs={{0,2},{1,3},{2,0},{3,1},{4,6},{5,7},{6,4},{7,5},{8,10},{9,11},{10,... | collective-permute-start | bytes 393224 | tf_op jit(solution)/shard_map/ppermute | solution.py:240
  21.1 27.9 %collective-permute-start.17 = (f32[672,128]{1,0:T(8,128)S(1)}, f32[672,128]{1,0:T(8,128)S(1)}, u32[]{:S(2)}, u32[]{:S(2)}) collective-permute-start(f32[672,128]{1,0:T(8,128)S(1)} %send1.1.refs_0_), channel_id=1, source_target_pairs={{0,4},{4,0},{8,12},{12,8},{1,5},{5,1},{9,13},{13,9},{2,6},{6,2},{1... | collective-permute-start | bytes 1032200 | tf_op jit(solution)/shard_map/ppermute | solution.py:240
  36.5 12.4 %collective-permute-start.8 = (f32[4,128,128]{2,1,0:T(8,128)S(1)}, f32[4,128,128]{2,1,0:T(8,128)S(1)}, u32[]{:S(2)}, u32[]{:S(2)}) collective-permute-start(f32[4,128,128]{2,1,0:T(8,128)S(1)} %copy-done), channel_id=1, source_target_pairs={{0,4},{4,0},{8,12},{12,8},{1,5},{5,1},{9,13},{13,9},{2,6},{6,2},{1... | collective-permute-start | bytes 786440 | tf_op jit(solution)/shard_map/ppermute | solution.py:240
  38.4 23.5 %collective-permute-start.19 = (f32[672,128]{1,0:T(8,128)S(1)}, f32[672,128]{1,0:T(8,128)S(1)}, u32[]{:S(2)}, u32[]{:S(2)}) collective-permute-start(f32[672,128]{1,0:T(8,128)S(1)} %collective-permute-done.18.refs_2_), channel_id=1, source_target_pairs={{0,4},{4,0},{8,12},{12,8},{1,5},{5,1},{9,13},{13,9},{2,6},{6,2},{1... | collective-permute-start | bytes 1032200 | tf_op jit(solution)/shard_map/ppermute | solution.py:240
  43.4 18.5 %collective-permute-start.10 = (f32[4,128,128]{2,1,0:T(8,128)S(1)}, f32[4,128,128]{2,1,0:T(8,128)S(1)}, u32[]{:S(2)}, u32[]{:S(2)}) collective-permute-start(f32[4,128,128]{2,1,0:T(8,128)S(1)} %collective-permute-done.9.refs_8_.refs_5_), channel_id=1, source_target_pairs={{0,4},{4,0},{8,12},{12,8},{1,5},{5,1},{9,13},{13,9},{2,6},{6,2},{1... | collective-permute-start | bytes 786440 | tf_op jit(solution)/shard_map/ppermute | solution.py:240
  49.0 14.1 %collective-permute-start.7 = (f32[512,128]{1,0:T(8,128)S(1)}, f32[512,128]{1,0:T(8,128)S(1)}, u32[]{:S(2)}, u32[]{:S(2)}) collective-permute-start(f32[512,128]{1,0:T(8,128)S(1)} %aheads0.1.refs_4_), channel_id=1, source_target_pairs={{0,1},{1,0},{2,3},{3,2},{4,5},{5,4},{6,7},{7,6},{8,9},{9,8},{10,11... | collective-permute-start | bytes 786440 | tf_op jit(solution)/shard_map/ppermute | solution.py:240
  49.0 14.1 %collective-permute-start.5 = (f32[4,128,128]{2,1,0:T(8,128)S(1)}, f32[4,128,128]{2,1,0:T(8,128)S(1)}, u32[]{:S(2)}, u32[]{:S(2)}) collective-permute-start(f32[4,128,128]{2,1,0:T(8,128)S(1)} %dense0.1.refs_0_), channel_id=1, source_target_pairs={{0,2},{1,3},{2,0},{3,1},{4,6},{5,7},{6,4},{7,5},{8,10},{9,11},{10,... | collective-permute-start | bytes 786440 | tf_op jit(solution)/shard_map/ppermute | solution.py:240
  61.9 11.8 %collective-permute-start.20 = (f32[832,128]{1,0:T(8,128)S(1)}, f32[832,128]{1,0:T(8,128)S(1)}, u32[]{:S(2)}, u32[]{:S(2)}) collective-permute-start(f32[832,128]{1,0:T(8,128)S(1)} %ahead1.1.refs_0_), channel_id=1, source_target_pairs={{0,2},{1,3},{2,0},{3,1},{4,6},{5,7},{6,4},{7,5},{8,10},{9,11},{10,... | collective-permute-start | bytes 1277960 | tf_op jit(solution)/shard_map/ppermute | solution.py:240
  62.5 12.0 %collective-permute-start.14 = (f32[19,128,128]{2,1,0:T(8,128)S(1)}, f32[19,128,128]{2,1,0:T(8,128)S(1)}, u32[]{:S(2)}, u32[]{:S(2)}) collective-permute-start(f32[19,128,128]{2,1,0:T(8,128)S(1)} %dense.1.refs_0_), channel_id=1, source_target_pairs={{0,1},{1,0},{2,3},{3,2},{4,5},{5,4},{6,7},{7,6},{8,9},{9,8},{10,11... | collective-permute-start | bytes 3735560 | tf_op jit(solution)/shard_map/ppermute | solution.py:240
  62.5 16.4 %collective-permute-start.16 = (f32[19,128,128]{2,1,0:T(8,128)S(1)}, f32[19,128,128]{2,1,0:T(8,128)S(1)}, u32[]{:S(2)}, u32[]{:S(2)}) collective-permute-start(f32[19,128,128]{2,1,0:T(8,128)S(1)} %collective-permute-done.15.refs_2_), channel_id=1, source_target_pairs={{0,1},{1,0},{2,3},{3,2},{4,5},{5,4},{6,7},{7,6},{8,9},{9,8},{10,11... | collective-permute-start | bytes 3735560 | tf_op jit(solution)/shard_map/ppermute | solution.py:240
  63.0 4.6 %collective-permute-start.4 = (f32[4,128,128]{2,1,0:T(8,128)S(1)}, f32[4,128,128]{2,1,0:T(8,128)S(1)}, u32[]{:S(2)}, u32[]{:S(2)}) collective-permute-start(f32[4,128,128]{2,1,0:T(8,128)S(1)} %dense0.1.refs_0_), channel_id=1, source_target_pairs={{0,1},{1,0},{2,3},{3,2},{4,5},{5,4},{6,7},{7,6},{8,9},{9,8},{10,11... | collective-permute-start | bytes 786440 | tf_op jit(solution)/shard_map/ppermute | solution.py:240
  63.1 4.9 %collective-permute-start.6 = (f32[4,128,128]{2,1,0:T(8,128)S(1)}, f32[4,128,128]{2,1,0:T(8,128)S(1)}, u32[]{:S(2)}, u32[]{:S(2)}) collective-permute-start(f32[4,128,128]{2,1,0:T(8,128)S(1)} %collective-permute-done.5.refs_2_), channel_id=1, source_target_pairs={{0,1},{1,0},{2,3},{3,2},{4,5},{5,4},{6,7},{7,6},{8,9},{9,8},{10,11... | collective-permute-start | bytes 786440 | tf_op jit(solution)/shard_map/ppermute | solution.py:240
  73.9 13.0 %collective-permute-start.25 = (f32[896,128]{1,0:T(8,128)S(1)}, f32[896,128]{1,0:T(8,128)S(1)}, u32[]{:S(2)}, u32[]{:S(2)}) collective-permute-start(f32[896,128]{1,0:T(8,128)S(1)} %ahead2.1.refs_0_), channel_id=1, source_target_pairs={{0,2},{1,3},{2,0},{3,1},{4,6},{5,7},{6,4},{7,5},{8,10},{9,11},{10,... | collective-permute-start | bytes 1376264 | tf_op jit(solution)/shard_map/ppermute | solution.py:240
  74.5 7.0 %collective-permute-start.11 = (f32[128,128]{1,0:T(8,128)S(1)}, f32[128,128]{1,0:T(8,128)S(1)}, u32[]{:S(2)}, u32[]{:S(2)}) collective-permute-start(f32[128,128]{1,0:T(8,128)S(1)} %prepare0.1.refs_2_.refs_0_.refs_4_), channel_id=1, source_target_pairs={{0,4},{4,0},{8,12},{12,8},{1,5},{5,1},{9,13},{13,9},{2,6},{6,2},{1... | collective-permute-start | bytes 196616 | tf_op jit(solution)/shard_map/ppermute | solution.py:240
  74.5 7.7 %collective-permute-start.12 = (f32[128,128]{1,0:T(8,128)S(1)}, f32[128,128]{1,0:T(8,128)S(1)}, u32[]{:S(2)}, u32[]{:S(2)}) collective-permute-start(f32[128,128]{1,0:T(8,128)S(1)} %prepare0.1.refs_2_.refs_0_.refs_4_), channel_id=1, source_target_pairs={{0,8},{4,12},{8,0},{12,4},{1,9},{5,13},{9,1},{13,5},{2,10},{6,14},... | collective-permute-start | bytes 196616 | tf_op jit(solution)/shard_map/ppermute | solution.py:240
  77.3 6.2 %collective-permute-start.13 = (f32[128,128]{1,0:T(8,128)S(1)}, f32[128,128]{1,0:T(8,128)S(1)}, u32[]{:S(2)}, u32[]{:S(2)}) collective-permute-start(f32[128,128]{1,0:T(8,128)S(1)} %prepare0.1.refs_2_.refs_0_.refs_4_), channel_id=1, source_target_pairs={{0,12},{4,8},{8,4},{12,0},{1,13},{5,9},{9,5},{13,1},{2,14},{6,10},... | collective-permute-start | bytes 196616 | tf_op jit(solution)/shard_map/ppermute | solution.py:240
  86.9 5.1 %collective-permute-start.26 = (f32[1792,128]{1,0:T(8,128)S(1)}, f32[1792,128]{1,0:T(8,128)S(1)}, u32[]{:S(2)}, u32[]{:S(2)}) collective-permute-start(f32[1792,128]{1,0:T(8,128)S(1)} %aheads2.1.refs_4_), channel_id=1, source_target_pairs={{0,1},{1,0},{2,3},{3,2},{4,5},{5,4},{6,7},{7,6},{8,9},{9,8},{10,11... | collective-permute-start | bytes 2752520 | tf_op jit(solution)/shard_map/ppermute | solution.py:240
  87.0 13.7 %collective-permute-start.30 = (f32[960,128]{1,0:T(8,128)S(1)}, f32[960,128]{1,0:T(8,128)S(1)}, u32[]{:S(2)}, u32[]{:S(2)}) collective-permute-start(f32[960,128]{1,0:T(8,128)S(1)} %ahead3.1.refs_0_), channel_id=1, source_target_pairs={{0,2},{1,3},{2,0},{3,1},{4,6},{5,7},{6,4},{7,5},{8,10},{9,11},{10,... | collective-permute-start | bytes 1474568 | tf_op jit(solution)/shard_map/ppermute | solution.py:240
  87.6 7.2 %collective-permute-start.22 = (f32[128,128]{1,0:T(8,128)S(1)}, f32[128,128]{1,0:T(8,128)S(1)}, u32[]{:S(2)}, u32[]{:S(2)}) collective-permute-start(f32[128,128]{1,0:T(8,128)S(1)} %get-tuple-element.23.refs_2_.refs_0_.refs_4_), channel_id=1, source_target_pairs={{0,4},{4,0},{8,12},{12,8},{1,5},{5,1},{9,13},{13,9},{2,6},{6,2},{1... | collective-permute-start | bytes 196616 | tf_op jit(solution)/shard_map/ppermute | solution.py:240
  87.6 7.7 %collective-permute-start.23 = (f32[128,128]{1,0:T(8,128)S(1)}, f32[128,128]{1,0:T(8,128)S(1)}, u32[]{:S(2)}, u32[]{:S(2)}) collective-permute-start(f32[128,128]{1,0:T(8,128)S(1)} %get-tuple-element.23.refs_2_.refs_0_.refs_4_), channel_id=1, source_target_pairs={{0,8},{4,12},{8,0},{12,4},{1,9},{5,13},{9,1},{13,5},{2,10},{6,14},... | collective-permute-start | bytes 196616 | tf_op jit(solution)/shard_map/ppermute | solution.py:240
  90.4 6.2 %collective-permute-start.24 = (f32[128,128]{1,0:T(8,128)S(1)}, f32[128,128]{1,0:T(8,128)S(1)}, u32[]{:S(2)}, u32[]{:S(2)}) collective-permute-start(f32[128,128]{1,0:T(8,128)S(1)} %get-tuple-element.23.refs_2_.refs_0_.refs_4_), channel_id=1, source_target_pairs={{0,12},{4,8},{8,4},{12,0},{1,13},{5,9},{9,5},{13,1},{2,14},{6,10},... | collective-permute-start | bytes 196616 | tf_op jit(solution)/shard_map/ppermute | solution.py:240
  100.8 4.5 %collective-permute-start.31 = (f32[1920,128]{1,0:T(8,128)S(1)}, f32[1920,128]{1,0:T(8,128)S(1)}, u32[]{:S(2)}, u32[]{:S(2)}) collective-permute-start(f32[1920,128]{1,0:T(8,128)S(1)} %aheads3.1.refs_4_), channel_id=1, source_target_pairs={{0,1},{1,0},{2,3},{3,2},{4,5},{5,4},{6,7},{7,6},{8,9},{9,8},{10,11... | collective-permute-start | bytes 2949128 | tf_op jit(solution)/shard_map/ppermute | solution.py:240
  100.9 7.6 %collective-permute-start.27 = (f32[128,128]{1,0:T(8,128)S(1)}, f32[128,128]{1,0:T(8,128)S(1)}, u32[]{:S(2)}, u32[]{:S(2)}) collective-permute-start(f32[128,128]{1,0:T(8,128)S(1)} %get-tuple-element.28.refs_2_.refs_0_), channel_id=1, source_target_pairs={{0,4},{4,0},{8,12},{12,8},{1,5},{5,1},{9,13},{13,9},{2,6},{6,2},{1... | collective-permute-start | bytes 196616 | tf_op jit(solution)/shard_map/ppermute | solution.py:240
  101.0 7.6 %collective-permute-start.28 = (f32[128,128]{1,0:T(8,128)S(1)}, f32[128,128]{1,0:T(8,128)S(1)}, u32[]{:S(2)}, u32[]{:S(2)}) collective-permute-start(f32[128,128]{1,0:T(8,128)S(1)} %get-tuple-element.28.refs_2_.refs_0_), channel_id=1, source_target_pairs={{0,8},{4,12},{8,0},{12,4},{1,9},{5,13},{9,1},{13,5},{2,10},{6,14},... | collective-permute-start | bytes 196616 | tf_op jit(solution)/shard_map/ppermute | solution.py:240
  103.7 6.1 %collective-permute-start.29 = (f32[128,128]{1,0:T(8,128)S(1)}, f32[128,128]{1,0:T(8,128)S(1)}, u32[]{:S(2)}, u32[]{:S(2)}) collective-permute-start(f32[128,128]{1,0:T(8,128)S(1)} %get-tuple-element.28.refs_2_.refs_0_), channel_id=1, source_target_pairs={{0,12},{4,8},{8,4},{12,0},{1,13},{5,9},{9,5},{13,1},{2,14},{6,10},... | collective-permute-start | bytes 196616 | tf_op jit(solution)/shard_map/ppermute | solution.py:240
  111.9 7.9 %collective-permute-start.33 = (f32[128,128]{1,0:T(8,128)S(1)}, f32[128,128]{1,0:T(8,128)S(1)}, u32[]{:S(2)}, u32[]{:S(2)}) collective-permute-start(f32[128,128]{1,0:T(8,128)S(1)} %get-tuple-element.33.refs_0_), channel_id=1, source_target_pairs={{0,8},{4,12},{8,0},{12,4},{1,9},{5,13},{9,1},{13,5},{2,10},{6,14},... | collective-permute-start | bytes 196616 | tf_op jit(solution)/shard_map/ppermute | solution.py:240
  113.2 6.5 %collective-permute-start.34 = (f32[128,128]{1,0:T(8,128)S(1)}, f32[128,128]{1,0:T(8,128)S(1)}, u32[]{:S(2)}, u32[]{:S(2)}) collective-permute-start(f32[128,128]{1,0:T(8,128)S(1)} %get-tuple-element.33.refs_0_), channel_id=1, source_target_pairs={{0,12},{4,8},{8,4},{12,0},{1,13},{5,9},{9,5},{13,1},{2,14},{6,10},... | collective-permute-start | bytes 196616 | tf_op jit(solution)/shard_map/ppermute | solution.py:240
  (7 other events, 90.9 us)

commit v11 on v9

--- a/solution.py
+++ b/solution.py
@@ -87,7 +87,7 @@
 
 
 def first_kernel(prev, *refs):
-    known_ref, right_ref, inv_ref, ahead_ref, known_out = refs
+    right_ref, inv_ref, ahead_ref = refs
     steps, nb = right_ref.shape[0], inv_ref.shape[1]
     share = right_ref.shape[2] // lax.axis_size("pcol")
     at = pl.multiple_of(lax.axis_index("pcol") * share, share)
@@ -99,7 +99,6 @@
         for col in range(prev + step):
             ahead_ref[place : place + share] = right_ref[step, col, pl.ds(at, share), :]
             place += share
-    known_out[...] = known_ref[...]
 
 
 def dense_kernel(rows, flags_ref, *refs):
@@ -314,14 +313,14 @@
         )
         return [both, shift(both, "pcol", 1)]
 
-    sent, known = run(
+    (sent,) = run(
         functools.partial(first_kernel, prev),
         "first",
-        [shaped(sum(heights), nb), shaped(*earlier.shape)],
-        [whole_of(pinned(value)) for value in (earlier, right_t, inverse_diag)],
+        [shaped(sum(heights), nb)],
+        [whole_of(pinned(value)) for value in (right_t, inverse_diag)],
     )
     ahead = over_rows_forwarded(sent)
-    known = over_rows_forwarded(known)
+    known = over_rows_forwarded(earlier)
     own = run(
         functools.partial(dense_kernel, [(0, prev)]),
         "dense0",
@@ -373,8 +372,8 @@
             [source_room],
         )
 
-    pending0 = prepare(0, strips0, ahead_near(0, ahead_far(0)))
-    later1 = ahead_near(1, ahead_far(1, []), [pending0])
+    pending0 = prepare(0, strips0, ahead_near(0, ahead_far(0, [])))
+    later1 = ahead_near(1, ahead_far(1, known[1:]), [pending0])
     later2 = ahead_far(2, [pending0])
     pending1, solved0 = solve(0, over_rows(pending0), prepare(1, dense, later1))
     later2 = ahead_near(2, later2, [pending1])

time: 109 us -> 117 us (1.073)
  waiting for transfers between devices: 57.6 us -> 66.5 us
    ppermute x32, waiting for transfers between devices: 57.6 us -> 66.5 us  [shift(): return lax.ppermute(value, axis, [(i, i ^ step) for i in range(n)])]
  transfers between devices with their start and end apart: 32 -> 32, of which waited for: 13 -> 16; matrix products, arithmetic and copies ran while one was open for 0% -> 0% of each run, Pallas kernels for 12% -> 12%
where the time goes in v11:
time: 117 us
  waiting for transfers between devices  66.5 us (57%)
  starting transfers between devices  32.3 us (28%)
  Pallas kernels  18 us (15%)
    ppermute x32, waiting for transfers between devices, shift(): return lax.ppermute(value, axis, [(i, i ^ step) for i in range(n)])  66.5 us
    ppermute x32, starting transfers between devices, shift(): return lax.ppermute(value, axis, [(i, i ^ step) for i in range(n)])  32.3 us
    pallas_call x19, Pallas kernels, call(): pl.pallas_call(body, grid=(1,), out_shape=shapes, in_specs=specs + [any_s...  18 us
  transfers between devices with their start and end apart: 32, of which 16 were waited for; matrix products, arithmetic and copies ran while one was open for 0% of the time, Pallas kernels for 12%

profile of v11, /device:TPU:0, one launch (start us, length us, event | category | flops | bytes accessed | tf_op | source)
XLA Modules:
  0.0 117.1 jit_solution(6842162080554944011)
XLA Ops:
  0.0 1.3 %first.1.refs_2_.refs_0_.refs_5_ = f32[736,128]{1,0:T(8,128)S(1)} custom-call(f32[4,7,64,128]{3,2,1,0:T(8,128)} %bitcast.6, f32[4,128,128]{2,1,0:T(8,128)} %refs_4_.1), custom_call_target="tpu_custom_call" | custom-call | tf_op jit(solution)/shard_map/first/pallas_call | solution.py:266
  1.3 1.4 %dense.1.refs_0_ = f32[19,128,128]{2,1,0:T(8,128)S(1)} custom-call(s32[4,7]{1,0:T(4,128)S(1)} %copy-done.1, f32[4,7,128,128]{3,2,1,0:T(8,128)} %refs_3_.1, f32[4,7,128,128]{3,2,1,0:T(8,128)} %refs_3_.1, f32[4,7,128,128]{3,2,1,0:T(8,128)} %refs_3_.1, f32[4,128,128]{2,1,0:T(8,128)} %refs_4_.1, f32[736,128]{1,0:T(8,128)S(1)} %first.1.refs_2_.refs_0_.refs_5_), custom_call_target="tpu_custom_call" | custom-call | tf_op jit(solution)/shard_map/dense/pallas_call | solution.py:266
  2.7 3.0 %collective-permute-start.15 = (f32[19,128,128]{2,1,0:T(8,128)S(1)}, f32[19,128,128]{2,1,0:T(8,128)S(1)}, u32[]{:S(2)}, u32[]{:S(2)}) collective-permute-start(f32[19,128,128]{2,1,0:T(8,128)S(1)} %dense.1.refs_0_), channel_id=1, source_target_pairs={{0,2},{1,3},{2,0},{3,1},{4,6},{5,7},{6,4},{7,5},{8,10},{9,11},{10,... | collective-permute-start | bytes 3735560 | tf_op jit(solution)/shard_map/ppermute | solution.py:240
  5.7 2.6 %collective-permute-start.4 = (f32[736,128]{1,0:T(8,128)S(1)}, f32[736,128]{1,0:T(8,128)S(1)}, u32[]{:S(2)}, u32[]{:S(2)}) collective-permute-start(f32[736,128]{1,0:T(8,128)S(1)} %first.1.refs_2_.refs_0_.refs_5_), channel_id=1, source_target_pairs={{0,8},{4,12},{8,0},{12,4},{1,9},{5,13},{9,1},{13,5},{2,10},{6,14},... | collective-permute-start | bytes 1130504 | tf_op jit(solution)/shard_map/ppermute | solution.py:240
  8.7 1.6 %collective-permute-start.8 = (f32[4,128,128]{2,1,0:T(8,128)S(1)}, f32[4,128,128]{2,1,0:T(8,128)S(1)}, u32[]{:S(2)}, u32[]{:S(2)}) collective-permute-start(f32[4,128,128]{2,1,0:T(8,128)S(1)} %copy-done), channel_id=1, source_target_pairs={{0,4},{4,0},{8,12},{12,8},{1,5},{5,1},{9,13},{13,9},{2,6},{6,2},{1... | collective-permute-start | bytes 786440 | tf_op jit(solution)/shard_map/ppermute | solution.py:240
  10.7 21.1 %collective-permute-done.4.refs_2_ = f32[736,128]{1,0:T(8,128)S(1)} collective-permute-done((f32[736,128]{1,0:T(8,128)S(1)}, f32[736,128]{1,0:T(8,128)S(1)}, u32[]{:S(2)}, u32[]{:S(2)}) %collective-permute-start.4) | collective-permute-done | bytes 376864 | tf_op jit(solution)/shard_map/ppermute | solution.py:240
  31.8 4.5 %collective-permute-done.9.refs_8_.refs_5_ = f32[4,128,128]{2,1,0:T(8,128)S(1)} collective-permute-done((f32[4,128,128]{2,1,0:T(8,128)S(1)}, f32[4,128,128]{2,1,0:T(8,128)S(1)}, u32[]{:S(2)}, u32[]{:S(2)}) %collective-permute-start.9) | collective-permute-done | bytes 262176 | tf_op jit(solution)/shard_map/ppermute | solution.py:240
  36.9 1.0 dense0.1.refs_0_
  38.6 11.7 %collective-permute-done.10.refs_9_.refs_6_ = f32[4,128,128]{2,1,0:T(8,128)S(1)} collective-permute-done((f32[4,128,128]{2,1,0:T(8,128)S(1)}, f32[4,128,128]{2,1,0:T(8,128)S(1)}, u32[]{:S(2)}, u32[]{:S(2)}) %collective-permute-start.10) | collective-permute-done | bytes 262176 | tf_op jit(solution)/shard_map/ppermute | solution.py:240
  50.8 1.6 %collective-permute-start.6 = (f32[256,128]{1,0:T(8,128)S(1)}, f32[256,128]{1,0:T(8,128)S(1)}, u32[]{:S(2)}, u32[]{:S(2)}) collective-permute-start(f32[256,128]{1,0:T(8,128)S(1)} %ahead0.1.refs_0_), channel_id=1, source_target_pairs={{0,2},{1,3},{2,0},{3,1},{4,6},{5,7},{6,4},{7,5},{8,10},{9,11},{10,... | collective-permute-start | bytes 393224 | tf_op jit(solution)/shard_map/ppermute | solution.py:240
  53.0 11.8 %collective-permute-done.6.refs_1_ = f32[256,128]{1,0:T(8,128)S(1)} collective-permute-done((f32[256,128]{1,0:T(8,128)S(1)}, f32[256,128]{1,0:T(8,128)S(1)}, u32[]{:S(2)}, u32[]{:S(2)}) %collective-permute-start.6) | collective-permute-done | bytes 131104 | tf_op jit(solution)/shard_map/ppermute | solution.py:240
  65.4 0.9 collective-permute-done.2.refs_3_
  66.7 2.2 %prepare0.1.refs_2_.refs_0_.refs_4_ = f32[128,128]{1,0:T(8,128)S(1)} custom-call(f32[4,128,128]{2,1,0:T(8,128)S(1)} %dense0.1.refs_0_, f32[4,128,128]{2,1,0:T(8,128)S(1)} %collective-permute-done.refs_1_, f32[4,128,128]{2,1,0:T(8,128)S(1)} %collective-permute-done.1.refs_2_, f32[4,128,128]{2,1,0:T(8,128)S(1)} %collective-permute-done.2.refs_3_, ...), custom_call_target="tpu_custom_call" | custom-call | tf_op jit(solution)/shard_map/prepare0/pallas_call | solution.py:266
  70.1 4.0 %collective-permute-start.12 = (f32[128,128]{1,0:T(8,128)S(1)}, f32[128,128]{1,0:T(8,128)S(1)}, u32[]{:S(2)}, u32[]{:S(2)}) collective-permute-start(f32[128,128]{1,0:T(8,128)S(1)} %prepare0.1.refs_2_.refs_0_.refs_4_), channel_id=1, source_target_pairs={{0,8},{4,12},{8,0},{12,4},{1,9},{5,13},{9,1},{13,5},{2,10},{6,14},... | collective-permute-start | bytes 196616 | tf_op jit(solution)/shard_map/ppermute | solution.py:240
  74.0 0.9 collective-permute-start.13
  75.0 2.6 %prepare1.1 = (f32[128,128]{1,0:T(8,128)S(1)}, bf16[1,256,512]{2,1,0:T(8,128)(2,1)S(1)}, bf16[1024,512]{1,0:T(8,128)(2,1)S(1)}) custom-call(f32[19,128,128]{2,1,0:T(8,128)S(1)} %dense.1.refs_0_, f32[19,128,128]{2,1,0:T(8,128)S(1)} %collective-permute-done.14.refs_1_, f32[19,128,128]{2,1,0:T(8,128)S(1)} %collective-permute-done.15.refs_2_, ...), custom_call_target="tpu_custom_call" | custom-call | tf_op jit(solution)/shard_map/prepare1/pallas_call | solution.py:266
  77.6 1.1 collective-permute-done.12.refs_2_
  78.7 1.5 %collective-permute-done.13.refs_3_ = f32[128,128]{1,0:T(8,128)S(1)} collective-permute-done((f32[128,128]{1,0:T(8,128)S(1)}, f32[128,128]{1,0:T(8,128)S(1)}, u32[]{:S(2)}, u32[]{:S(2)}) %collective-permute-start.13) | collective-permute-done | bytes 65568 | tf_op jit(solution)/shard_map/ppermute | solution.py:240
  80.9 1.2 %collective-permute-done.22.refs_1_ = f32[896,128]{1,0:T(8,128)S(1)} collective-permute-done((f32[896,128]{1,0:T(8,128)S(1)}, f32[896,128]{1,0:T(8,128)S(1)}, u32[]{:S(2)}, u32[]{:S(2)}) %collective-permute-start.22) | collective-permute-done | bytes 458784 | tf_op jit(solution)/shard_map/ppermute | solution.py:240
  83.3 3.7 %collective-permute-start.20 = (f32[128,128]{1,0:T(8,128)S(1)}, f32[128,128]{1,0:T(8,128)S(1)}, u32[]{:S(2)}, u32[]{:S(2)}) collective-permute-start(f32[128,128]{1,0:T(8,128)S(1)} %get-tuple-element.23.refs_2_.refs_0_.refs_4_), channel_id=1, source_target_pairs={{0,8},{4,12},{8,0},{12,4},{1,9},{5,13},{9,1},{13,5},{2,10},{6,14},... | collective-permute-start | bytes 196616 | tf_op jit(solution)/shard_map/ppermute | solution.py:240
  87.3 2.8 %prepare2.1 = (f32[128,128]{1,0:T(8,128)S(1)}, bf16[1,256,512]{2,1,0:T(8,128)(2,1)S(1)}, bf16[1024,512]{1,0:T(8,128)(2,1)S(1)}) custom-call(f32[19,128,128]{2,1,0:T(8,128)S(1)} %dense.1.refs_0_, f32[19,128,128]{2,1,0:T(8,128)S(1)} %collective-permute-done.14.refs_1_, f32[19,128,128]{2,1,0:T(8,128)S(1)} %collective-permute-done.15.refs_2_, ...), custom_call_target="tpu_custom_call" | custom-call | tf_op jit(solution)/shard_map/prepare2/pallas_call | solution.py:266
  90.1 1.0 collective-permute-done.20.refs_2_
  91.1 2.0 %collective-permute-done.21.refs_3_ = f32[128,128]{1,0:T(8,128)S(1)} collective-permute-done((f32[128,128]{1,0:T(8,128)S(1)}, f32[128,128]{1,0:T(8,128)S(1)}, u32[]{:S(2)}, u32[]{:S(2)}) %collective-permute-start.21) | collective-permute-done | bytes 65568 | tf_op jit(solution)/shard_map/ppermute | solution.py:240
  93.9 2.1 %collective-permute-done.27.refs_1_ = f32[960,128]{1,0:T(8,128)S(1)} collective-permute-done((f32[960,128]{1,0:T(8,128)S(1)}, f32[960,128]{1,0:T(8,128)S(1)}, u32[]{:S(2)}, u32[]{:S(2)}) %collective-permute-start.27) | collective-permute-done | bytes 491552 | tf_op jit(solution)/shard_map/ppermute | solution.py:240
  96.3 4.0 %collective-permute-start.25 = (f32[128,128]{1,0:T(8,128)S(1)}, f32[128,128]{1,0:T(8,128)S(1)}, u32[]{:S(2)}, u32[]{:S(2)}) collective-permute-start(f32[128,128]{1,0:T(8,128)S(1)} %get-tuple-element.28.refs_2_.refs_0_), channel_id=1, source_target_pairs={{0,8},{4,12},{8,0},{12,4},{1,9},{5,13},{9,1},{13,5},{2,10},{6,14},... | collective-permute-start | bytes 196616 | tf_op jit(solution)/shard_map/ppermute | solution.py:240
  100.6 3.2 %prepare3.1 = (f32[128,128]{1,0:T(8,128)S(1)}, bf16[2,256,512]{2,1,0:T(8,128)(2,1)S(1)}, bf16[1024,512]{1,0:T(8,128)(2,1)S(1)}) custom-call(f32[19,128,128]{2,1,0:T(8,128)S(1)} %dense.1.refs_0_, f32[19,128,128]{2,1,0:T(8,128)S(1)} %collective-permute-done.14.refs_1_, f32[19,128,128]{2,1,0:T(8,128)S(1)} %collective-permute-done.15.refs_2_, ...), custom_call_target="tpu_custom_call" | custom-call | tf_op jit(solution)/shard_map/prepare3/pallas_call | solution.py:266
  104.5 1.9 %collective-permute-done.26.refs_3_ = f32[128,128]{1,0:T(8,128)S(1)} collective-permute-done((f32[128,128]{1,0:T(8,128)S(1)}, f32[128,128]{1,0:T(8,128)S(1)}, u32[]{:S(2)}, u32[]{:S(2)}) %collective-permute-start.26) | collective-permute-done | bytes 65568 | tf_op jit(solution)/shard_map/ppermute | solution.py:240
  107.1 1.1 collective-permute-start.29
  108.2 1.5 %collective-permute-start.30 = (f32[128,128]{1,0:T(8,128)S(1)}, f32[128,128]{1,0:T(8,128)S(1)}, u32[]{:S(2)}, u32[]{:S(2)}) collective-permute-start(f32[128,128]{1,0:T(8,128)S(1)} %get-tuple-element.33.refs_0_), channel_id=1, source_target_pairs={{0,8},{4,12},{8,0},{12,4},{1,9},{5,13},{9,1},{13,5},{2,10},{6,14},... | collective-permute-start | bytes 196616 | tf_op jit(solution)/shard_map/ppermute | solution.py:240
  109.8 1.8 %collective-permute-start.31 = (f32[128,128]{1,0:T(8,128)S(1)}, f32[128,128]{1,0:T(8,128)S(1)}, u32[]{:S(2)}, u32[]{:S(2)}) collective-permute-start(f32[128,128]{1,0:T(8,128)S(1)} %get-tuple-element.33.refs_0_), channel_id=1, source_target_pairs={{0,12},{4,8},{8,4},{12,0},{1,13},{5,9},{9,5},{13,1},{2,14},{6,10},... | collective-permute-start | bytes 196616 | tf_op jit(solution)/shard_map/ppermute | solution.py:240
  111.8 4.3 %collective-permute-done.30.refs_2_ = f32[128,128]{1,0:T(8,128)S(1)} collective-permute-done((f32[128,128]{1,0:T(8,128)S(1)}, f32[128,128]{1,0:T(8,128)S(1)}, u32[]{:S(2)}, u32[]{:S(2)}) %collective-permute-start.30) | collective-permute-done | bytes 65568 | tf_op jit(solution)/shard_map/ppermute | solution.py:240
  116.1 1.0 last.1
  (57 shorter events, 10.3 us)
Async XLA Ops:
  2.7 49.7 %collective-permute-start.15 = (f32[19,128,128]{2,1,0:T(8,128)S(1)}, f32[19,128,128]{2,1,0:T(8,128)S(1)}, u32[]{:S(2)}, u32[]{:S(2)}) collective-permute-start(f32[19,128,128]{2,1,0:T(8,128)S(1)} %dense.1.refs_0_), channel_id=1, source_target_pairs={{0,2},{1,3},{2,0},{3,1},{4,6},{5,7},{6,4},{7,5},{8,10},{9,11},{10,... | collective-permute-start | bytes 3735560 | tf_op jit(solution)/shard_map/ppermute | solution.py:240
  5.7 26.1 %collective-permute-start.4 = (f32[736,128]{1,0:T(8,128)S(1)}, f32[736,128]{1,0:T(8,128)S(1)}, u32[]{:S(2)}, u32[]{:S(2)}) collective-permute-start(f32[736,128]{1,0:T(8,128)S(1)} %first.1.refs_2_.refs_0_.refs_5_), channel_id=1, source_target_pairs={{0,8},{4,12},{8,0},{12,4},{1,9},{5,13},{9,1},{13,5},{2,10},{6,14},... | collective-permute-start | bytes 1130504 | tf_op jit(solution)/shard_map/ppermute | solution.py:240
  8.3 28.0 %collective-permute-start.9 = (f32[4,128,128]{2,1,0:T(8,128)S(1)}, f32[4,128,128]{2,1,0:T(8,128)S(1)}, u32[]{:S(2)}, u32[]{:S(2)}) collective-permute-start(f32[4,128,128]{2,1,0:T(8,128)S(1)} %copy-done), channel_id=1, source_target_pairs={{0,8},{4,12},{8,0},{12,4},{1,9},{5,13},{9,1},{13,5},{2,10},{6,14},... | collective-permute-start | bytes 786440 | tf_op jit(solution)/shard_map/ppermute | solution.py:240
  8.7 29.3 %collective-permute-start.8 = (f32[4,128,128]{2,1,0:T(8,128)S(1)}, f32[4,128,128]{2,1,0:T(8,128)S(1)}, u32[]{:S(2)}, u32[]{:S(2)}) collective-permute-start(f32[4,128,128]{2,1,0:T(8,128)S(1)} %copy-done), channel_id=1, source_target_pairs={{0,4},{4,0},{8,12},{12,8},{1,5},{5,1},{9,13},{13,9},{2,6},{6,2},{1... | collective-permute-start | bytes 786440 | tf_op jit(solution)/shard_map/ppermute | solution.py:240
  10.2 28.3 %collective-permute-start.3 = (f32[736,128]{1,0:T(8,128)S(1)}, f32[736,128]{1,0:T(8,128)S(1)}, u32[]{:S(2)}, u32[]{:S(2)}) collective-permute-start(f32[736,128]{1,0:T(8,128)S(1)} %first.1.refs_2_.refs_0_.refs_5_), channel_id=1, source_target_pairs={{0,4},{4,0},{8,12},{12,8},{1,5},{5,1},{9,13},{13,9},{2,6},{6,2},{1... | collective-permute-start | bytes 1130504 | tf_op jit(solution)/shard_map/ppermute | solution.py:240
  31.8 18.4 %collective-permute-start.5 = (f32[736,128]{1,0:T(8,128)S(1)}, f32[736,128]{1,0:T(8,128)S(1)}, u32[]{:S(2)}, u32[]{:S(2)}) collective-permute-start(f32[736,128]{1,0:T(8,128)S(1)} %collective-permute-done.4.refs_2_), channel_id=1, source_target_pairs={{0,4},{4,0},{8,12},{12,8},{1,5},{5,1},{9,13},{13,9},{2,6},{6,2},{1... | collective-permute-start | bytes 1130504 | tf_op jit(solution)/shard_map/ppermute | solution.py:240
  36.3 13.9 %collective-permute-start.10 = (f32[4,128,128]{2,1,0:T(8,128)S(1)}, f32[4,128,128]{2,1,0:T(8,128)S(1)}, u32[]{:S(2)}, u32[]{:S(2)}) collective-permute-start(f32[4,128,128]{2,1,0:T(8,128)S(1)} %collective-permute-done.9.refs_8_.refs_5_), channel_id=1, source_target_pairs={{0,4},{4,0},{8,12},{12,8},{1,5},{5,1},{9,13},{13,9},{2,6},{6,2},{1... | collective-permute-start | bytes 786440 | tf_op jit(solution)/shard_map/ppermute | solution.py:240
  38.0 14.5 %collective-permute-start.1 = (f32[4,128,128]{2,1,0:T(8,128)S(1)}, f32[4,128,128]{2,1,0:T(8,128)S(1)}, u32[]{:S(2)}, u32[]{:S(2)}) collective-permute-start(f32[4,128,128]{2,1,0:T(8,128)S(1)} %dense0.1.refs_0_), channel_id=1, source_target_pairs={{0,2},{1,3},{2,0},{3,1},{4,6},{5,7},{6,4},{7,5},{8,10},{9,11},{10,... | collective-permute-start | bytes 786440 | tf_op jit(solution)/shard_map/ppermute | solution.py:240
  38.6 26.3 %collective-permute-start = (f32[4,128,128]{2,1,0:T(8,128)S(1)}, f32[4,128,128]{2,1,0:T(8,128)S(1)}, u32[]{:S(2)}, u32[]{:S(2)}) collective-permute-start(f32[4,128,128]{2,1,0:T(8,128)S(1)} %dense0.1.refs_0_), channel_id=1, source_target_pairs={{0,1},{1,0},{2,3},{3,2},{4,5},{5,4},{6,7},{7,6},{8,9},{9,8},{10,11... | collective-permute-start | bytes 786440 | tf_op jit(solution)/shard_map/ppermute | solution.py:240
  50.3 18.7 %collective-permute-start.17 = (f32[832,128]{1,0:T(8,128)S(1)}, f32[832,128]{1,0:T(8,128)S(1)}, u32[]{:S(2)}, u32[]{:S(2)}) collective-permute-start(f32[832,128]{1,0:T(8,128)S(1)} %ahead1.1.refs_0_), channel_id=1, source_target_pairs={{0,2},{1,3},{2,0},{3,1},{4,6},{5,7},{6,4},{7,5},{8,10},{9,11},{10,... | collective-permute-start | bytes 1277960 | tf_op jit(solution)/shard_map/ppermute | solution.py:240
  50.8 14.0 %collective-permute-start.6 = (f32[256,128]{1,0:T(8,128)S(1)}, f32[256,128]{1,0:T(8,128)S(1)}, u32[]{:S(2)}, u32[]{:S(2)}) collective-permute-start(f32[256,128]{1,0:T(8,128)S(1)} %ahead0.1.refs_0_), channel_id=1, source_target_pairs={{0,2},{1,3},{2,0},{3,1},{4,6},{5,7},{6,4},{7,5},{8,10},{9,11},{10,... | collective-permute-start | bytes 393224 | tf_op jit(solution)/shard_map/ppermute | solution.py:240
  52.4 17.6 %collective-permute-start.14 = (f32[19,128,128]{2,1,0:T(8,128)S(1)}, f32[19,128,128]{2,1,0:T(8,128)S(1)}, u32[]{:S(2)}, u32[]{:S(2)}) collective-permute-start(f32[19,128,128]{2,1,0:T(8,128)S(1)} %dense.1.refs_0_), channel_id=1, source_target_pairs={{0,1},{1,0},{2,3},{3,2},{4,5},{5,4},{6,7},{7,6},{8,9},{9,8},{10,11... | collective-permute-start | bytes 3735560 | tf_op jit(solution)/shard_map/ppermute | solution.py:240
  52.5 22.5 %collective-permute-start.16 = (f32[19,128,128]{2,1,0:T(8,128)S(1)}, f32[19,128,128]{2,1,0:T(8,128)S(1)}, u32[]{:S(2)}, u32[]{:S(2)}) collective-permute-start(f32[19,128,128]{2,1,0:T(8,128)S(1)} %collective-permute-done.15.refs_2_), channel_id=1, source_target_pairs={{0,1},{1,0},{2,3},{3,2},{4,5},{5,4},{6,7},{7,6},{8,9},{9,8},{10,11... | collective-permute-start | bytes 3735560 | tf_op jit(solution)/shard_map/ppermute | solution.py:240
  64.8 1.5 %collective-permute-start.2 = (f32[4,128,128]{2,1,0:T(8,128)S(1)}, f32[4,128,128]{2,1,0:T(8,128)S(1)}, u32[]{:S(2)}, u32[]{:S(2)}) collective-permute-start(f32[4,128,128]{2,1,0:T(8,128)S(1)} %collective-permute-done.1.refs_2_), channel_id=1, source_target_pairs={{0,1},{1,0},{2,3},{3,2},{4,5},{5,4},{6,7},{7,6},{8,9},{9,8},{10,11... | collective-permute-start | bytes 786440 | tf_op jit(solution)/shard_map/ppermute | solution.py:240
  64.8 1.9 %collective-permute-start.7 = (f32[512,128]{1,0:T(8,128)S(1)}, f32[512,128]{1,0:T(8,128)S(1)}, u32[]{:S(2)}, u32[]{:S(2)}) collective-permute-start(f32[512,128]{1,0:T(8,128)S(1)} %aheads0.1.refs_4_), channel_id=1, source_target_pairs={{0,1},{1,0},{2,3},{3,2},{4,5},{5,4},{6,7},{7,6},{8,9},{9,8},{10,11... | collective-permute-start | bytes 786440 | tf_op jit(solution)/shard_map/ppermute | solution.py:240
  69.0 5.0 %collective-permute-start.18 = (f32[1664,128]{1,0:T(8,128)S(1)}, f32[1664,128]{1,0:T(8,128)S(1)}, u32[]{:S(2)}, u32[]{:S(2)}) collective-permute-start(f32[1664,128]{1,0:T(8,128)S(1)} %aheads1.1.refs_4_), channel_id=1, source_target_pairs={{0,1},{1,0},{2,3},{3,2},{4,5},{5,4},{6,7},{7,6},{8,9},{9,8},{10,11... | collective-permute-start | bytes 2555912 | tf_op jit(solution)/shard_map/ppermute | solution.py:240
  69.4 12.8 %collective-permute-start.22 = (f32[896,128]{1,0:T(8,128)S(1)}, f32[896,128]{1,0:T(8,128)S(1)}, u32[]{:S(2)}, u32[]{:S(2)}) collective-permute-start(f32[896,128]{1,0:T(8,128)S(1)} %ahead2.1.refs_0_), channel_id=1, source_target_pairs={{0,2},{1,3},{2,0},{3,1},{4,6},{5,7},{6,4},{7,5},{8,10},{9,11},{10,... | collective-permute-start | bytes 1376264 | tf_op jit(solution)/shard_map/ppermute | solution.py:240
  69.9 7.7 %collective-permute-start.11 = (f32[128,128]{1,0:T(8,128)S(1)}, f32[128,128]{1,0:T(8,128)S(1)}, u32[]{:S(2)}, u32[]{:S(2)}) collective-permute-start(f32[128,128]{1,0:T(8,128)S(1)} %prepare0.1.refs_2_.refs_0_.refs_4_), channel_id=1, source_target_pairs={{0,4},{4,0},{8,12},{12,8},{1,5},{5,1},{9,13},{13,9},{2,6},{6,2},{1... | collective-permute-start | bytes 196616 | tf_op jit(solution)/shard_map/ppermute | solution.py:240
  70.1 8.6 %collective-permute-start.12 = (f32[128,128]{1,0:T(8,128)S(1)}, f32[128,128]{1,0:T(8,128)S(1)}, u32[]{:S(2)}, u32[]{:S(2)}) collective-permute-start(f32[128,128]{1,0:T(8,128)S(1)} %prepare0.1.refs_2_.refs_0_.refs_4_), channel_id=1, source_target_pairs={{0,8},{4,12},{8,0},{12,4},{1,9},{5,13},{9,1},{13,5},{2,10},{6,14},... | collective-permute-start | bytes 196616 | tf_op jit(solution)/shard_map/ppermute | solution.py:240
  74.0 6.2 %collective-permute-start.13 = (f32[128,128]{1,0:T(8,128)S(1)}, f32[128,128]{1,0:T(8,128)S(1)}, u32[]{:S(2)}, u32[]{:S(2)}) collective-permute-start(f32[128,128]{1,0:T(8,128)S(1)} %prepare0.1.refs_2_.refs_0_.refs_4_), channel_id=1, source_target_pairs={{0,12},{4,8},{8,4},{12,0},{1,13},{5,9},{9,5},{13,1},{2,14},{6,10},... | collective-permute-start | bytes 196616 | tf_op jit(solution)/shard_map/ppermute | solution.py:240
  82.2 5.1 %collective-permute-start.23 = (f32[1792,128]{1,0:T(8,128)S(1)}, f32[1792,128]{1,0:T(8,128)S(1)}, u32[]{:S(2)}, u32[]{:S(2)}) collective-permute-start(f32[1792,128]{1,0:T(8,128)S(1)} %aheads2.1.refs_4_), channel_id=1, source_target_pairs={{0,1},{1,0},{2,3},{3,2},{4,5},{5,4},{6,7},{7,6},{8,9},{9,8},{10,11... | collective-permute-start | bytes 2752520 | tf_op jit(solution)/shard_map/ppermute | solution.py:240
  82.3 13.7 %collective-permute-start.27 = (f32[960,128]{1,0:T(8,128)S(1)}, f32[960,128]{1,0:T(8,128)S(1)}, u32[]{:S(2)}, u32[]{:S(2)}) collective-permute-start(f32[960,128]{1,0:T(8,128)S(1)} %ahead3.1.refs_0_), channel_id=1, source_target_pairs={{0,2},{1,3},{2,0},{3,1},{4,6},{5,7},{6,4},{7,5},{8,10},{9,11},{10,... | collective-permute-start | bytes 1474568 | tf_op jit(solution)/shard_map/ppermute | solution.py:240
  82.9 7.2 %collective-permute-start.19 = (f32[128,128]{1,0:T(8,128)S(1)}, f32[128,128]{1,0:T(8,128)S(1)}, u32[]{:S(2)}, u32[]{:S(2)}) collective-permute-start(f32[128,128]{1,0:T(8,128)S(1)} %get-tuple-element.23.refs_2_.refs_0_.refs_4_), channel_id=1, source_target_pairs={{0,4},{4,0},{8,12},{12,8},{1,5},{5,1},{9,13},{13,9},{2,6},{6,2},{1... | collective-permute-start | bytes 196616 | tf_op jit(solution)/shard_map/ppermute | solution.py:240
  83.3 7.8 %collective-permute-start.20 = (f32[128,128]{1,0:T(8,128)S(1)}, f32[128,128]{1,0:T(8,128)S(1)}, u32[]{:S(2)}, u32[]{:S(2)}) collective-permute-start(f32[128,128]{1,0:T(8,128)S(1)} %get-tuple-element.23.refs_2_.refs_0_.refs_4_), channel_id=1, source_target_pairs={{0,8},{4,12},{8,0},{12,4},{1,9},{5,13},{9,1},{13,5},{2,10},{6,14},... | collective-permute-start | bytes 196616 | tf_op jit(solution)/shard_map/ppermute | solution.py:240
  87.0 6.2 %collective-permute-start.21 = (f32[128,128]{1,0:T(8,128)S(1)}, f32[128,128]{1,0:T(8,128)S(1)}, u32[]{:S(2)}, u32[]{:S(2)}) collective-permute-start(f32[128,128]{1,0:T(8,128)S(1)} %get-tuple-element.23.refs_2_.refs_0_.refs_4_), channel_id=1, source_target_pairs={{0,12},{4,8},{8,4},{12,0},{1,13},{5,9},{9,5},{13,1},{2,14},{6,10},... | collective-permute-start | bytes 196616 | tf_op jit(solution)/shard_map/ppermute | solution.py:240
  96.1 4.5 %collective-permute-start.28 = (f32[1920,128]{1,0:T(8,128)S(1)}, f32[1920,128]{1,0:T(8,128)S(1)}, u32[]{:S(2)}, u32[]{:S(2)}) collective-permute-start(f32[1920,128]{1,0:T(8,128)S(1)} %aheads3.1.refs_4_), channel_id=1, source_target_pairs={{0,1},{1,0},{2,3},{3,2},{4,5},{5,4},{6,7},{7,6},{8,9},{9,8},{10,11... | collective-permute-start | bytes 2949128 | tf_op jit(solution)/shard_map/ppermute | solution.py:240
  96.1 7.7 %collective-permute-start.24 = (f32[128,128]{1,0:T(8,128)S(1)}, f32[128,128]{1,0:T(8,128)S(1)}, u32[]{:S(2)}, u32[]{:S(2)}) collective-permute-start(f32[128,128]{1,0:T(8,128)S(1)} %get-tuple-element.28.refs_2_.refs_0_), channel_id=1, source_target_pairs={{0,4},{4,0},{8,12},{12,8},{1,5},{5,1},{9,13},{13,9},{2,6},{6,2},{1... | collective-permute-start | bytes 196616 | tf_op jit(solution)/shard_map/ppermute | solution.py:240
  96.3 8.2 %collective-permute-start.25 = (f32[128,128]{1,0:T(8,128)S(1)}, f32[128,128]{1,0:T(8,128)S(1)}, u32[]{:S(2)}, u32[]{:S(2)}) collective-permute-start(f32[128,128]{1,0:T(8,128)S(1)} %get-tuple-element.28.refs_2_.refs_0_), channel_id=1, source_target_pairs={{0,8},{4,12},{8,0},{12,4},{1,9},{5,13},{9,1},{13,5},{2,10},{6,14},... | collective-permute-start | bytes 196616 | tf_op jit(solution)/shard_map/ppermute | solution.py:240
  100.3 6.1 %collective-permute-start.26 = (f32[128,128]{1,0:T(8,128)S(1)}, f32[128,128]{1,0:T(8,128)S(1)}, u32[]{:S(2)}, u32[]{:S(2)}) collective-permute-start(f32[128,128]{1,0:T(8,128)S(1)} %get-tuple-element.28.refs_2_.refs_0_), channel_id=1, source_target_pairs={{0,12},{4,8},{8,4},{12,0},{1,13},{5,9},{9,5},{13,1},{2,14},{6,10},... | collective-permute-start | bytes 196616 | tf_op jit(solution)/shard_map/ppermute | solution.py:240
  107.1 4.7 %collective-permute-start.29 = (f32[128,128]{1,0:T(8,128)S(1)}, f32[128,128]{1,0:T(8,128)S(1)}, u32[]{:S(2)}, u32[]{:S(2)}) collective-permute-start(f32[128,128]{1,0:T(8,128)S(1)} %get-tuple-element.33.refs_0_), channel_id=1, source_target_pairs={{0,4},{4,0},{8,12},{12,8},{1,5},{5,1},{9,13},{13,9},{2,6},{6,2},{1... | collective-permute-start | bytes 196616 | tf_op jit(solution)/shard_map/ppermute | solution.py:240
  108.2 7.8 %collective-permute-start.30 = (f32[128,128]{1,0:T(8,128)S(1)}, f32[128,128]{1,0:T(8,128)S(1)}, u32[]{:S(2)}, u32[]{:S(2)}) collective-permute-start(f32[128,128]{1,0:T(8,128)S(1)} %get-tuple-element.33.refs_0_), channel_id=1, source_target_pairs={{0,8},{4,12},{8,0},{12,4},{1,9},{5,13},{9,1},{13,5},{2,10},{6,14},... | collective-permute-start | bytes 196616 | tf_op jit(solution)/shard_map/ppermute | solution.py:240
  109.8 6.3 %collective-permute-start.31 = (f32[128,128]{1,0:T(8,128)S(1)}, f32[128,128]{1,0:T(8,128)S(1)}, u32[]{:S(2)}, u32[]{:S(2)}) collective-permute-start(f32[128,128]{1,0:T(8,128)S(1)} %get-tuple-element.33.refs_0_), channel_id=1, source_target_pairs={{0,12},{4,8},{8,4},{12,0},{1,13},{5,9},{9,5},{13,1},{2,14},{6,10},... | collective-permute-start | bytes 196616 | tf_op jit(solution)/shard_map/ppermute | solution.py:240
  (3 other events, 24.8 us)

commit v12 on v9

--- a/solution.py
+++ b/solution.py
@@ -373,8 +373,8 @@
             [source_room],
         )
 
-    pending0 = prepare(0, strips0, ahead_near(0, ahead_far(0)))
-    later1 = ahead_near(1, ahead_far(1, []), [pending0])
+    pending0 = prepare(0, strips0, ahead_near(0, ahead_far(0, [])))
+    later1 = ahead_near(1, ahead_far(1, known[1:2]), [pending0])
     later2 = ahead_far(2, [pending0])
     pending1, solved0 = solve(0, over_rows(pending0), prepare(1, dense, later1))
     later2 = ahead_near(2, later2, [pending1])

time: 109 us -> 113 us (1.037)
  waiting for transfers between devices: 57.6 us -> 61.2 us
    ppermute x32, waiting for transfers between devices: 57.6 us -> 61.2 us  [shift(): return lax.ppermute(value, axis, [(i, i ^ step) for i in range(n)])]
  transfers between devices with their start and end apart: 32 -> 32, of which waited for: 13 -> 18; matrix products, arithmetic and copies ran while one was open for 0% -> 0% of each run, Pallas kernels for 12% -> 12%
where the time goes in v12:
time: 113 us
  waiting for transfers between devices  61.2 us (54%)
  starting transfers between devices  33 us (29%)
  Pallas kernels  18.1 us (16%)
    ppermute x32, waiting for transfers between devices, shift(): return lax.ppermute(value, axis, [(i, i ^ step) for i in range(n)])  61.2 us
    ppermute x32, starting transfers between devices, shift(): return lax.ppermute(value, axis, [(i, i ^ step) for i in range(n)])  33 us
    pallas_call x19, Pallas kernels, call(): pl.pallas_call(body, grid=(1,), out_shape=shapes, in_specs=specs + [any_s...  18.1 us
  transfers between devices with their start and end apart: 32, of which 18 were waited for; matrix products, arithmetic and copies ran while one was open for 0% of the time, Pallas kernels for 12%

profile of v12, /device:TPU:0, one launch (start us, length us, event | category | flops | bytes accessed | tf_op | source)
XLA Modules:
  0.0 112.6 jit_solution(5475547166559590704)
XLA Ops:
  0.0 1.4 %first.1 = (f32[736,128]{1,0:T(8,128)S(1)}, f32[4,128,128]{2,1,0:T(8,128)S(1)}) custom-call(f32[4,128,128]{2,1,0:T(8,128)} %refs_0_.3, f32[4,7,64,128]{3,2,1,0:T(8,128)} %bitcast.6, f32[4,128,128]{2,1,0:T(8,128)} %refs_4_.1), custom_call_target="tpu_custom_call" | custom-call | tf_op jit(solution)/shard_map/first/pallas_call | solution.py:267
  1.4 1.4 %dense.1.refs_0_ = f32[19,128,128]{2,1,0:T(8,128)S(1)} custom-call(s32[4,7]{1,0:T(4,128)S(1)} %copy-done, f32[4,7,128,128]{3,2,1,0:T(8,128)} %refs_3_.1, f32[4,7,128,128]{3,2,1,0:T(8,128)} %refs_3_.1, f32[4,7,128,128]{3,2,1,0:T(8,128)} %refs_3_.1, f32[4,128,128]{2,1,0:T(8,128)} %refs_4_.1, f32[736,128]{1,0:T(8,128)S(1)} %get-tuple-element.22.refs_2_.refs_0_.refs_5_), custom_call_target="tpu_custom_call" | custom-call | tf_op jit(solution)/shard_map/dense/pallas_call | solution.py:267
  2.8 3.0 %collective-permute-start.15 = (f32[19,128,128]{2,1,0:T(8,128)S(1)}, f32[19,128,128]{2,1,0:T(8,128)S(1)}, u32[]{:S(2)}, u32[]{:S(2)}) collective-permute-start(f32[19,128,128]{2,1,0:T(8,128)S(1)} %dense.1.refs_0_), channel_id=1, source_target_pairs={{0,2},{1,3},{2,0},{3,1},{4,6},{5,7},{6,4},{7,5},{8,10},{9,11},{10,... | collective-permute-start | bytes 3735560 | tf_op jit(solution)/shard_map/ppermute | solution.py:241
  5.8 2.6 %collective-permute-start.4 = (f32[736,128]{1,0:T(8,128)S(1)}, f32[736,128]{1,0:T(8,128)S(1)}, u32[]{:S(2)}, u32[]{:S(2)}) collective-permute-start(f32[736,128]{1,0:T(8,128)S(1)} %get-tuple-element.22.refs_2_.refs_0_.refs_5_), channel_id=1, source_target_pairs={{0,8},{4,12},{8,0},{12,4},{1,9},{5,13},{9,1},{13,5},{2,10},{6,14},... | collective-permute-start | bytes 1130504 | tf_op jit(solution)/shard_map/ppermute | solution.py:241
  8.7 1.6 %collective-permute-start.3 = (f32[736,128]{1,0:T(8,128)S(1)}, f32[736,128]{1,0:T(8,128)S(1)}, u32[]{:S(2)}, u32[]{:S(2)}) collective-permute-start(f32[736,128]{1,0:T(8,128)S(1)} %get-tuple-element.22.refs_2_.refs_0_.refs_5_), channel_id=1, source_target_pairs={{0,4},{4,0},{8,12},{12,8},{1,5},{5,1},{9,13},{13,9},{2,6},{6,2},{1... | collective-permute-start | bytes 1130504 | tf_op jit(solution)/shard_map/ppermute | solution.py:241
  10.3 21.5 %collective-permute-done.4.refs_2_ = f32[736,128]{1,0:T(8,128)S(1)} collective-permute-done((f32[736,128]{1,0:T(8,128)S(1)}, f32[736,128]{1,0:T(8,128)S(1)}, u32[]{:S(2)}, u32[]{:S(2)}) %collective-permute-start.4) | collective-permute-done | bytes 376864 | tf_op jit(solution)/shard_map/ppermute | solution.py:241
  31.8 2.0 %collective-permute-start.8 = (f32[4,128,128]{2,1,0:T(8,128)S(1)}, f32[4,128,128]{2,1,0:T(8,128)S(1)}, u32[]{:S(2)}, u32[]{:S(2)}) collective-permute-start(f32[4,128,128]{2,1,0:T(8,128)S(1)} %get-tuple-element.23.refs_6_), channel_id=1, source_target_pairs={{0,4},{4,0},{8,12},{12,8},{1,5},{5,1},{9,13},{13,9},{2,6},{6,2},{1... | collective-permute-start | bytes 786440 | tf_op jit(solution)/shard_map/ppermute | solution.py:241
  33.8 1.0 dense0.1.refs_0_
  34.9 1.5 %collective-permute-done.9.refs_8_ = f32[4,128,128]{2,1,0:T(8,128)S(1)} collective-permute-done((f32[4,128,128]{2,1,0:T(8,128)S(1)}, f32[4,128,128]{2,1,0:T(8,128)S(1)}, u32[]{:S(2)}, u32[]{:S(2)}) %collective-permute-start.9) | collective-permute-done | bytes 262176 | tf_op jit(solution)/shard_map/ppermute | solution.py:241
  36.8 7.6 %collective-permute-done.5.refs_3_ = f32[736,128]{1,0:T(8,128)S(1)} collective-permute-done((f32[736,128]{1,0:T(8,128)S(1)}, f32[736,128]{1,0:T(8,128)S(1)}, u32[]{:S(2)}, u32[]{:S(2)}) %collective-permute-start.5) | collective-permute-done | bytes 376864 | tf_op jit(solution)/shard_map/ppermute | solution.py:241
  44.4 5.6 %collective-permute-done.8.refs_7_.refs_4_ = f32[4,128,128]{2,1,0:T(8,128)S(1)} collective-permute-done((f32[4,128,128]{2,1,0:T(8,128)S(1)}, f32[4,128,128]{2,1,0:T(8,128)S(1)}, u32[]{:S(2)}, u32[]{:S(2)}) %collective-permute-start.8) | collective-permute-done | bytes 262176 | tf_op jit(solution)/shard_map/ppermute | solution.py:241
  50.5 1.6 %collective-permute-start.17 = (f32[832,128]{1,0:T(8,128)S(1)}, f32[832,128]{1,0:T(8,128)S(1)}, u32[]{:S(2)}, u32[]{:S(2)}) collective-permute-start(f32[832,128]{1,0:T(8,128)S(1)} %ahead1.1.refs_0_), channel_id=1, source_target_pairs={{0,2},{1,3},{2,0},{3,1},{4,6},{5,7},{6,4},{7,5},{8,10},{9,11},{10,... | collective-permute-start | bytes 1277960 | tf_op jit(solution)/shard_map/ppermute | solution.py:241
  52.1 4.2 %collective-permute-done.6.refs_1_ = f32[256,128]{1,0:T(8,128)S(1)} collective-permute-done((f32[256,128]{1,0:T(8,128)S(1)}, f32[256,128]{1,0:T(8,128)S(1)}, u32[]{:S(2)}, u32[]{:S(2)}) %collective-permute-start.6) | collective-permute-done | bytes 131104 | tf_op jit(solution)/shard_map/ppermute | solution.py:241
  57.5 4.0 %collective-permute-done.2.refs_3_ = f32[4,128,128]{2,1,0:T(8,128)S(1)} collective-permute-done((f32[4,128,128]{2,1,0:T(8,128)S(1)}, f32[4,128,128]{2,1,0:T(8,128)S(1)}, u32[]{:S(2)}, u32[]{:S(2)}) %collective-permute-start.2) | collective-permute-done | bytes 262176 | tf_op jit(solution)/shard_map/ppermute | solution.py:241
  61.9 2.3 %prepare0.1.refs_2_.refs_0_.refs_4_ = f32[128,128]{1,0:T(8,128)S(1)} custom-call(f32[4,128,128]{2,1,0:T(8,128)S(1)} %dense0.1.refs_0_, f32[4,128,128]{2,1,0:T(8,128)S(1)} %collective-permute-done.refs_1_, f32[4,128,128]{2,1,0:T(8,128)S(1)} %collective-permute-done.1.refs_2_, f32[4,128,128]{2,1,0:T(8,128)S(1)} %collective-permute-done.2.refs_3_, ...), custom_call_target="tpu_custom_call" | custom-call | tf_op jit(solution)/shard_map/prepare0/pallas_call | solution.py:267
  65.2 4.1 %collective-permute-start.12 = (f32[128,128]{1,0:T(8,128)S(1)}, f32[128,128]{1,0:T(8,128)S(1)}, u32[]{:S(2)}, u32[]{:S(2)}) collective-permute-start(f32[128,128]{1,0:T(8,128)S(1)} %prepare0.1.refs_2_.refs_0_.refs_4_), channel_id=1, source_target_pairs={{0,8},{4,12},{8,0},{12,4},{1,9},{5,13},{9,1},{13,5},{2,10},{6,14},... | collective-permute-start | bytes 196616 | tf_op jit(solution)/shard_map/ppermute | solution.py:241
  69.3 1.2 %collective-permute-start.13 = (f32[128,128]{1,0:T(8,128)S(1)}, f32[128,128]{1,0:T(8,128)S(1)}, u32[]{:S(2)}, u32[]{:S(2)}) collective-permute-start(f32[128,128]{1,0:T(8,128)S(1)} %prepare0.1.refs_2_.refs_0_.refs_4_), channel_id=1, source_target_pairs={{0,12},{4,8},{8,4},{12,0},{1,13},{5,9},{9,5},{13,1},{2,14},{6,10},... | collective-permute-start | bytes 196616 | tf_op jit(solution)/shard_map/ppermute | solution.py:241
  70.5 2.6 %prepare1.1 = (f32[128,128]{1,0:T(8,128)S(1)}, bf16[1,256,512]{2,1,0:T(8,128)(2,1)S(1)}, bf16[1024,512]{1,0:T(8,128)(2,1)S(1)}) custom-call(f32[19,128,128]{2,1,0:T(8,128)S(1)} %dense.1.refs_0_, f32[19,128,128]{2,1,0:T(8,128)S(1)} %collective-permute-done.14.refs_1_, f32[19,128,128]{2,1,0:T(8,128)S(1)} %collective-permute-done.15.refs_2_, ...), custom_call_target="tpu_custom_call" | custom-call | tf_op jit(solution)/shard_map/prepare1/pallas_call | solution.py:267
  73.4 2.1 %collective-permute-done.13.refs_3_ = f32[128,128]{1,0:T(8,128)S(1)} collective-permute-done((f32[128,128]{1,0:T(8,128)S(1)}, f32[128,128]{1,0:T(8,128)S(1)}, u32[]{:S(2)}, u32[]{:S(2)}) %collective-permute-start.13) | collective-permute-done | bytes 65568 | tf_op jit(solution)/shard_map/ppermute | solution.py:241
  76.2 1.4 %collective-permute-done.22.refs_1_ = f32[896,128]{1,0:T(8,128)S(1)} collective-permute-done((f32[896,128]{1,0:T(8,128)S(1)}, f32[896,128]{1,0:T(8,128)S(1)}, u32[]{:S(2)}, u32[]{:S(2)}) %collective-permute-start.22) | collective-permute-done | bytes 458784 | tf_op jit(solution)/shard_map/ppermute | solution.py:241
  78.8 3.7 %collective-permute-start.20 = (f32[128,128]{1,0:T(8,128)S(1)}, f32[128,128]{1,0:T(8,128)S(1)}, u32[]{:S(2)}, u32[]{:S(2)}) collective-permute-start(f32[128,128]{1,0:T(8,128)S(1)} %get-tuple-element.27.refs_2_.refs_0_.refs_4_), channel_id=1, source_target_pairs={{0,8},{4,12},{8,0},{12,4},{1,9},{5,13},{9,1},{13,5},{2,10},{6,14},... | collective-permute-start | bytes 196616 | tf_op jit(solution)/shard_map/ppermute | solution.py:241
  82.7 2.8 %prepare2.1 = (f32[128,128]{1,0:T(8,128)S(1)}, bf16[1,256,512]{2,1,0:T(8,128)(2,1)S(1)}, bf16[1024,512]{1,0:T(8,128)(2,1)S(1)}) custom-call(f32[19,128,128]{2,1,0:T(8,128)S(1)} %dense.1.refs_0_, f32[19,128,128]{2,1,0:T(8,128)S(1)} %collective-permute-done.14.refs_1_, f32[19,128,128]{2,1,0:T(8,128)S(1)} %collective-permute-done.15.refs_2_, ...), custom_call_target="tpu_custom_call" | custom-call | tf_op jit(solution)/shard_map/prepare2/pallas_call | solution.py:267
  85.6 1.0 collective-permute-done.20.refs_2_
  86.6 2.0 %collective-permute-done.21.refs_3_ = f32[128,128]{1,0:T(8,128)S(1)} collective-permute-done((f32[128,128]{1,0:T(8,128)S(1)}, f32[128,128]{1,0:T(8,128)S(1)}, u32[]{:S(2)}, u32[]{:S(2)}) %collective-permute-start.21) | collective-permute-done | bytes 65568 | tf_op jit(solution)/shard_map/ppermute | solution.py:241
  89.4 2.1 %collective-permute-done.27.refs_1_ = f32[960,128]{1,0:T(8,128)S(1)} collective-permute-done((f32[960,128]{1,0:T(8,128)S(1)}, f32[960,128]{1,0:T(8,128)S(1)}, u32[]{:S(2)}, u32[]{:S(2)}) %collective-permute-start.27) | collective-permute-done | bytes 491552 | tf_op jit(solution)/shard_map/ppermute | solution.py:241
  91.7 4.0 %collective-permute-start.25 = (f32[128,128]{1,0:T(8,128)S(1)}, f32[128,128]{1,0:T(8,128)S(1)}, u32[]{:S(2)}, u32[]{:S(2)}) collective-permute-start(f32[128,128]{1,0:T(8,128)S(1)} %get-tuple-element.32.refs_2_.refs_0_), channel_id=1, source_target_pairs={{0,8},{4,12},{8,0},{12,4},{1,9},{5,13},{9,1},{13,5},{2,10},{6,14},... | collective-permute-start | bytes 196616 | tf_op jit(solution)/shard_map/ppermute | solution.py:241
  96.1 3.2 %prepare3.1 = (f32[128,128]{1,0:T(8,128)S(1)}, bf16[2,256,512]{2,1,0:T(8,128)(2,1)S(1)}, bf16[1024,512]{1,0:T(8,128)(2,1)S(1)}) custom-call(f32[19,128,128]{2,1,0:T(8,128)S(1)} %dense.1.refs_0_, f32[19,128,128]{2,1,0:T(8,128)S(1)} %collective-permute-done.14.refs_1_, f32[19,128,128]{2,1,0:T(8,128)S(1)} %collective-permute-done.15.refs_2_, ...), custom_call_target="tpu_custom_call" | custom-call | tf_op jit(solution)/shard_map/prepare3/pallas_call | solution.py:267
  100.0 1.9 %collective-permute-done.26.refs_3_ = f32[128,128]{1,0:T(8,128)S(1)} collective-permute-done((f32[128,128]{1,0:T(8,128)S(1)}, f32[128,128]{1,0:T(8,128)S(1)}, u32[]{:S(2)}, u32[]{:S(2)}) %collective-permute-start.26) | collective-permute-done | bytes 65568 | tf_op jit(solution)/shard_map/ppermute | solution.py:241
  102.6 1.1 %collective-permute-start.29 = (f32[128,128]{1,0:T(8,128)S(1)}, f32[128,128]{1,0:T(8,128)S(1)}, u32[]{:S(2)}, u32[]{:S(2)}) collective-permute-start(f32[128,128]{1,0:T(8,128)S(1)} %get-tuple-element.37.refs_0_), channel_id=1, source_target_pairs={{0,4},{4,0},{8,12},{12,8},{1,5},{5,1},{9,13},{13,9},{2,6},{6,2},{1... | collective-permute-start | bytes 196616 | tf_op jit(solution)/shard_map/ppermute | solution.py:241
  103.7 1.5 %collective-permute-start.30 = (f32[128,128]{1,0:T(8,128)S(1)}, f32[128,128]{1,0:T(8,128)S(1)}, u32[]{:S(2)}, u32[]{:S(2)}) collective-permute-start(f32[128,128]{1,0:T(8,128)S(1)} %get-tuple-element.37.refs_0_), channel_id=1, source_target_pairs={{0,8},{4,12},{8,0},{12,4},{1,9},{5,13},{9,1},{13,5},{2,10},{6,14},... | collective-permute-start | bytes 196616 | tf_op jit(solution)/shard_map/ppermute | solution.py:241
  105.2 1.8 %collective-permute-start.31 = (f32[128,128]{1,0:T(8,128)S(1)}, f32[128,128]{1,0:T(8,128)S(1)}, u32[]{:S(2)}, u32[]{:S(2)}) collective-permute-start(f32[128,128]{1,0:T(8,128)S(1)} %get-tuple-element.37.refs_0_), channel_id=1, source_target_pairs={{0,12},{4,8},{8,4},{12,0},{1,13},{5,9},{9,5},{13,1},{2,14},{6,10},... | collective-permute-start | bytes 196616 | tf_op jit(solution)/shard_map/ppermute | solution.py:241
  107.3 4.3 %collective-permute-done.30.refs_2_ = f32[128,128]{1,0:T(8,128)S(1)} collective-permute-done((f32[128,128]{1,0:T(8,128)S(1)}, f32[128,128]{1,0:T(8,128)S(1)}, u32[]{:S(2)}, u32[]{:S(2)}) %collective-permute-start.30) | collective-permute-done | bytes 65568 | tf_op jit(solution)/shard_map/ppermute | solution.py:241
  (55 shorter events, 10.2 us)
Async XLA Ops:
  2.8 53.6 %collective-permute-start.15 = (f32[19,128,128]{2,1,0:T(8,128)S(1)}, f32[19,128,128]{2,1,0:T(8,128)S(1)}, u32[]{:S(2)}, u32[]{:S(2)}) collective-permute-start(f32[19,128,128]{2,1,0:T(8,128)S(1)} %dense.1.refs_0_), channel_id=1, source_target_pairs={{0,2},{1,3},{2,0},{3,1},{4,6},{5,7},{6,4},{7,5},{8,10},{9,11},{10,... | collective-permute-start | bytes 3735560 | tf_op jit(solution)/shard_map/ppermute | solution.py:241
  5.8 26.0 %collective-permute-start.4 = (f32[736,128]{1,0:T(8,128)S(1)}, f32[736,128]{1,0:T(8,128)S(1)}, u32[]{:S(2)}, u32[]{:S(2)}) collective-permute-start(f32[736,128]{1,0:T(8,128)S(1)} %get-tuple-element.22.refs_2_.refs_0_.refs_5_), channel_id=1, source_target_pairs={{0,8},{4,12},{8,0},{12,4},{1,9},{5,13},{9,1},{13,5},{2,10},{6,14},... | collective-permute-start | bytes 1130504 | tf_op jit(solution)/shard_map/ppermute | solution.py:241
  8.4 27.9 %collective-permute-start.9 = (f32[4,128,128]{2,1,0:T(8,128)S(1)}, f32[4,128,128]{2,1,0:T(8,128)S(1)}, u32[]{:S(2)}, u32[]{:S(2)}) collective-permute-start(f32[4,128,128]{2,1,0:T(8,128)S(1)} %get-tuple-element.23.refs_6_), channel_id=1, source_target_pairs={{0,8},{4,12},{8,0},{12,4},{1,9},{5,13},{9,1},{13,5},{2,10},{6,14},... | collective-permute-start | bytes 786440 | tf_op jit(solution)/shard_map/ppermute | solution.py:241
  8.7 28.1 %collective-permute-start.3 = (f32[736,128]{1,0:T(8,128)S(1)}, f32[736,128]{1,0:T(8,128)S(1)}, u32[]{:S(2)}, u32[]{:S(2)}) collective-permute-start(f32[736,128]{1,0:T(8,128)S(1)} %get-tuple-element.22.refs_2_.refs_0_.refs_5_), channel_id=1, source_target_pairs={{0,4},{4,0},{8,12},{12,8},{1,5},{5,1},{9,13},{13,9},{2,6},{6,2},{1... | collective-permute-start | bytes 1130504 | tf_op jit(solution)/shard_map/ppermute | solution.py:241
  31.8 12.6 %collective-permute-start.5 = (f32[736,128]{1,0:T(8,128)S(1)}, f32[736,128]{1,0:T(8,128)S(1)}, u32[]{:S(2)}, u32[]{:S(2)}) collective-permute-start(f32[736,128]{1,0:T(8,128)S(1)} %collective-permute-done.4.refs_2_), channel_id=1, source_target_pairs={{0,4},{4,0},{8,12},{12,8},{1,5},{5,1},{9,13},{13,9},{2,6},{6,2},{1... | collective-permute-start | bytes 1130504 | tf_op jit(solution)/shard_map/ppermute | solution.py:241
  31.8 18.2 %collective-permute-start.8 = (f32[4,128,128]{2,1,0:T(8,128)S(1)}, f32[4,128,128]{2,1,0:T(8,128)S(1)}, u32[]{:S(2)}, u32[]{:S(2)}) collective-permute-start(f32[4,128,128]{2,1,0:T(8,128)S(1)} %get-tuple-element.23.refs_6_), channel_id=1, source_target_pairs={{0,4},{4,0},{8,12},{12,8},{1,5},{5,1},{9,13},{13,9},{2,6},{6,2},{1... | collective-permute-start | bytes 786440 | tf_op jit(solution)/shard_map/ppermute | solution.py:241
  36.3 14.2 %collective-permute-start.1 = (f32[4,128,128]{2,1,0:T(8,128)S(1)}, f32[4,128,128]{2,1,0:T(8,128)S(1)}, u32[]{:S(2)}, u32[]{:S(2)}) collective-permute-start(f32[4,128,128]{2,1,0:T(8,128)S(1)} %dense0.1.refs_0_), channel_id=1, source_target_pairs={{0,2},{1,3},{2,0},{3,1},{4,6},{5,7},{6,4},{7,5},{8,10},{9,11},{10,... | collective-permute-start | bytes 786440 | tf_op jit(solution)/shard_map/ppermute | solution.py:241
  36.8 20.1 %collective-permute-start = (f32[4,128,128]{2,1,0:T(8,128)S(1)}, f32[4,128,128]{2,1,0:T(8,128)S(1)}, u32[]{:S(2)}, u32[]{:S(2)}) collective-permute-start(f32[4,128,128]{2,1,0:T(8,128)S(1)} %dense0.1.refs_0_), channel_id=1, source_target_pairs={{0,1},{1,0},{2,3},{3,2},{4,5},{5,4},{6,7},{7,6},{8,9},{9,8},{10,11... | collective-permute-start | bytes 786440 | tf_op jit(solution)/shard_map/ppermute | solution.py:241
  44.4 12.6 %collective-permute-start.10 = (f32[4,128,128]{2,1,0:T(8,128)S(1)}, f32[4,128,128]{2,1,0:T(8,128)S(1)}, u32[]{:S(2)}, u32[]{:S(2)}) collective-permute-start(f32[4,128,128]{2,1,0:T(8,128)S(1)} %collective-permute-done.9.refs_8_), channel_id=1, source_target_pairs={{0,4},{4,0},{8,12},{12,8},{1,5},{5,1},{9,13},{13,9},{2,6},{6,2},{1... | collective-permute-start | bytes 786440 | tf_op jit(solution)/shard_map/ppermute | solution.py:241
  50.0 6.4 %collective-permute-start.6 = (f32[256,128]{1,0:T(8,128)S(1)}, f32[256,128]{1,0:T(8,128)S(1)}, u32[]{:S(2)}, u32[]{:S(2)}) collective-permute-start(f32[256,128]{1,0:T(8,128)S(1)} %ahead0.1.refs_0_), channel_id=1, source_target_pairs={{0,2},{1,3},{2,0},{3,1},{4,6},{5,7},{6,4},{7,5},{8,10},{9,11},{10,... | collective-permute-start | bytes 393224 | tf_op jit(solution)/shard_map/ppermute | solution.py:241
  50.5 13.9 %collective-permute-start.17 = (f32[832,128]{1,0:T(8,128)S(1)}, f32[832,128]{1,0:T(8,128)S(1)}, u32[]{:S(2)}, u32[]{:S(2)}) collective-permute-start(f32[832,128]{1,0:T(8,128)S(1)} %ahead1.1.refs_0_), channel_id=1, source_target_pairs={{0,2},{1,3},{2,0},{3,1},{4,6},{5,7},{6,4},{7,5},{8,10},{9,11},{10,... | collective-permute-start | bytes 1277960 | tf_op jit(solution)/shard_map/ppermute | solution.py:241
  56.4 8.8 %collective-permute-start.14 = (f32[19,128,128]{2,1,0:T(8,128)S(1)}, f32[19,128,128]{2,1,0:T(8,128)S(1)}, u32[]{:S(2)}, u32[]{:S(2)}) collective-permute-start(f32[19,128,128]{2,1,0:T(8,128)S(1)} %dense.1.refs_0_), channel_id=1, source_target_pairs={{0,1},{1,0},{2,3},{3,2},{4,5},{5,4},{6,7},{7,6},{8,9},{9,8},{10,11... | collective-permute-start | bytes 3735560 | tf_op jit(solution)/shard_map/ppermute | solution.py:241
  56.4 14.1 %collective-permute-start.16 = (f32[19,128,128]{2,1,0:T(8,128)S(1)}, f32[19,128,128]{2,1,0:T(8,128)S(1)}, u32[]{:S(2)}, u32[]{:S(2)}) collective-permute-start(f32[19,128,128]{2,1,0:T(8,128)S(1)} %collective-permute-done.15.refs_2_), channel_id=1, source_target_pairs={{0,1},{1,0},{2,3},{3,2},{4,5},{5,4},{6,7},{7,6},{8,9},{9,8},{10,11... | collective-permute-start | bytes 3735560 | tf_op jit(solution)/shard_map/ppermute | solution.py:241
  56.9 4.6 %collective-permute-start.2 = (f32[4,128,128]{2,1,0:T(8,128)S(1)}, f32[4,128,128]{2,1,0:T(8,128)S(1)}, u32[]{:S(2)}, u32[]{:S(2)}) collective-permute-start(f32[4,128,128]{2,1,0:T(8,128)S(1)} %collective-permute-done.1.refs_2_), channel_id=1, source_target_pairs={{0,1},{1,0},{2,3},{3,2},{4,5},{5,4},{6,7},{7,6},{8,9},{9,8},{10,11... | collective-permute-start | bytes 786440 | tf_op jit(solution)/shard_map/ppermute | solution.py:241
  57.0 4.8 %collective-permute-start.7 = (f32[512,128]{1,0:T(8,128)S(1)}, f32[512,128]{1,0:T(8,128)S(1)}, u32[]{:S(2)}, u32[]{:S(2)}) collective-permute-start(f32[512,128]{1,0:T(8,128)S(1)} %aheads0.1.refs_4_), channel_id=1, source_target_pairs={{0,1},{1,0},{2,3},{3,2},{4,5},{5,4},{6,7},{7,6},{8,9},{9,8},{10,11... | collective-permute-start | bytes 786440 | tf_op jit(solution)/shard_map/ppermute | solution.py:241
  64.5 4.8 %collective-permute-start.18 = (f32[1664,128]{1,0:T(8,128)S(1)}, f32[1664,128]{1,0:T(8,128)S(1)}, u32[]{:S(2)}, u32[]{:S(2)}) collective-permute-start(f32[1664,128]{1,0:T(8,128)S(1)} %aheads1.1.refs_4_), channel_id=1, source_target_pairs={{0,1},{1,0},{2,3},{3,2},{4,5},{5,4},{6,7},{7,6},{8,9},{9,8},{10,11... | collective-permute-start | bytes 2555912 | tf_op jit(solution)/shard_map/ppermute | solution.py:241
  64.6 13.0 %collective-permute-start.22 = (f32[896,128]{1,0:T(8,128)S(1)}, f32[896,128]{1,0:T(8,128)S(1)}, u32[]{:S(2)}, u32[]{:S(2)}) collective-permute-start(f32[896,128]{1,0:T(8,128)S(1)} %ahead2.1.refs_0_), channel_id=1, source_target_pairs={{0,2},{1,3},{2,0},{3,1},{4,6},{5,7},{6,4},{7,5},{8,10},{9,11},{10,... | collective-permute-start | bytes 1376264 | tf_op jit(solution)/shard_map/ppermute | solution.py:241
  65.2 7.9 %collective-permute-start.11 = (f32[128,128]{1,0:T(8,128)S(1)}, f32[128,128]{1,0:T(8,128)S(1)}, u32[]{:S(2)}, u32[]{:S(2)}) collective-permute-start(f32[128,128]{1,0:T(8,128)S(1)} %prepare0.1.refs_2_.refs_0_.refs_4_), channel_id=1, source_target_pairs={{0,4},{4,0},{8,12},{12,8},{1,5},{5,1},{9,13},{13,9},{2,6},{6,2},{1... | collective-permute-start | bytes 196616 | tf_op jit(solution)/shard_map/ppermute | solution.py:241
  65.2 8.2 %collective-permute-start.12 = (f32[128,128]{1,0:T(8,128)S(1)}, f32[128,128]{1,0:T(8,128)S(1)}, u32[]{:S(2)}, u32[]{:S(2)}) collective-permute-start(f32[128,128]{1,0:T(8,128)S(1)} %prepare0.1.refs_2_.refs_0_.refs_4_), channel_id=1, source_target_pairs={{0,8},{4,12},{8,0},{12,4},{1,9},{5,13},{9,1},{13,5},{2,10},{6,14},... | collective-permute-start | bytes 196616 | tf_op jit(solution)/shard_map/ppermute | solution.py:241
  69.3 6.2 %collective-permute-start.13 = (f32[128,128]{1,0:T(8,128)S(1)}, f32[128,128]{1,0:T(8,128)S(1)}, u32[]{:S(2)}, u32[]{:S(2)}) collective-permute-start(f32[128,128]{1,0:T(8,128)S(1)} %prepare0.1.refs_2_.refs_0_.refs_4_), channel_id=1, source_target_pairs={{0,12},{4,8},{8,4},{12,0},{1,13},{5,9},{9,5},{13,1},{2,14},{6,10},... | collective-permute-start | bytes 196616 | tf_op jit(solution)/shard_map/ppermute | solution.py:241
  77.7 5.1 %collective-permute-start.23 = (f32[1792,128]{1,0:T(8,128)S(1)}, f32[1792,128]{1,0:T(8,128)S(1)}, u32[]{:S(2)}, u32[]{:S(2)}) collective-permute-start(f32[1792,128]{1,0:T(8,128)S(1)} %aheads2.1.refs_4_), channel_id=1, source_target_pairs={{0,1},{1,0},{2,3},{3,2},{4,5},{5,4},{6,7},{7,6},{8,9},{9,8},{10,11... | collective-permute-start | bytes 2752520 | tf_op jit(solution)/shard_map/ppermute | solution.py:241
  77.8 13.7 %collective-permute-start.27 = (f32[960,128]{1,0:T(8,128)S(1)}, f32[960,128]{1,0:T(8,128)S(1)}, u32[]{:S(2)}, u32[]{:S(2)}) collective-permute-start(f32[960,128]{1,0:T(8,128)S(1)} %ahead3.1.refs_0_), channel_id=1, source_target_pairs={{0,2},{1,3},{2,0},{3,1},{4,6},{5,7},{6,4},{7,5},{8,10},{9,11},{10,... | collective-permute-start | bytes 1474568 | tf_op jit(solution)/shard_map/ppermute | solution.py:241
  78.4 7.2 %collective-permute-start.19 = (f32[128,128]{1,0:T(8,128)S(1)}, f32[128,128]{1,0:T(8,128)S(1)}, u32[]{:S(2)}, u32[]{:S(2)}) collective-permute-start(f32[128,128]{1,0:T(8,128)S(1)} %get-tuple-element.27.refs_2_.refs_0_.refs_4_), channel_id=1, source_target_pairs={{0,4},{4,0},{8,12},{12,8},{1,5},{5,1},{9,13},{13,9},{2,6},{6,2},{1... | collective-permute-start | bytes 196616 | tf_op jit(solution)/shard_map/ppermute | solution.py:241
  78.8 7.8 %collective-permute-start.20 = (f32[128,128]{1,0:T(8,128)S(1)}, f32[128,128]{1,0:T(8,128)S(1)}, u32[]{:S(2)}, u32[]{:S(2)}) collective-permute-start(f32[128,128]{1,0:T(8,128)S(1)} %get-tuple-element.27.refs_2_.refs_0_.refs_4_), channel_id=1, source_target_pairs={{0,8},{4,12},{8,0},{12,4},{1,9},{5,13},{9,1},{13,5},{2,10},{6,14},... | collective-permute-start | bytes 196616 | tf_op jit(solution)/shard_map/ppermute | solution.py:241
  82.5 6.2 %collective-permute-start.21 = (f32[128,128]{1,0:T(8,128)S(1)}, f32[128,128]{1,0:T(8,128)S(1)}, u32[]{:S(2)}, u32[]{:S(2)}) collective-permute-start(f32[128,128]{1,0:T(8,128)S(1)} %get-tuple-element.27.refs_2_.refs_0_.refs_4_), channel_id=1, source_target_pairs={{0,12},{4,8},{8,4},{12,0},{1,13},{5,9},{9,5},{13,1},{2,14},{6,10},... | collective-permute-start | bytes 196616 | tf_op jit(solution)/shard_map/ppermute | solution.py:241
  91.6 4.5 %collective-permute-start.28 = (f32[1920,128]{1,0:T(8,128)S(1)}, f32[1920,128]{1,0:T(8,128)S(1)}, u32[]{:S(2)}, u32[]{:S(2)}) collective-permute-start(f32[1920,128]{1,0:T(8,128)S(1)} %aheads3.1.refs_4_), channel_id=1, source_target_pairs={{0,1},{1,0},{2,3},{3,2},{4,5},{5,4},{6,7},{7,6},{8,9},{9,8},{10,11... | collective-permute-start | bytes 2949128 | tf_op jit(solution)/shard_map/ppermute | solution.py:241
  91.6 7.6 %collective-permute-start.24 = (f32[128,128]{1,0:T(8,128)S(1)}, f32[128,128]{1,0:T(8,128)S(1)}, u32[]{:S(2)}, u32[]{:S(2)}) collective-permute-start(f32[128,128]{1,0:T(8,128)S(1)} %get-tuple-element.32.refs_2_.refs_0_), channel_id=1, source_target_pairs={{0,4},{4,0},{8,12},{12,8},{1,5},{5,1},{9,13},{13,9},{2,6},{6,2},{1... | collective-permute-start | bytes 196616 | tf_op jit(solution)/shard_map/ppermute | solution.py:241
  91.7 8.3 %collective-permute-start.25 = (f32[128,128]{1,0:T(8,128)S(1)}, f32[128,128]{1,0:T(8,128)S(1)}, u32[]{:S(2)}, u32[]{:S(2)}) collective-permute-start(f32[128,128]{1,0:T(8,128)S(1)} %get-tuple-element.32.refs_2_.refs_0_), channel_id=1, source_target_pairs={{0,8},{4,12},{8,0},{12,4},{1,9},{5,13},{9,1},{13,5},{2,10},{6,14},... | collective-permute-start | bytes 196616 | tf_op jit(solution)/shard_map/ppermute | solution.py:241
  95.8 6.1 %collective-permute-start.26 = (f32[128,128]{1,0:T(8,128)S(1)}, f32[128,128]{1,0:T(8,128)S(1)}, u32[]{:S(2)}, u32[]{:S(2)}) collective-permute-start(f32[128,128]{1,0:T(8,128)S(1)} %get-tuple-element.32.refs_2_.refs_0_), channel_id=1, source_target_pairs={{0,12},{4,8},{8,4},{12,0},{1,13},{5,9},{9,5},{13,1},{2,14},{6,10},... | collective-permute-start | bytes 196616 | tf_op jit(solution)/shard_map/ppermute | solution.py:241
  102.6 4.7 %collective-permute-start.29 = (f32[128,128]{1,0:T(8,128)S(1)}, f32[128,128]{1,0:T(8,128)S(1)}, u32[]{:S(2)}, u32[]{:S(2)}) collective-permute-start(f32[128,128]{1,0:T(8,128)S(1)} %get-tuple-element.37.refs_0_), channel_id=1, source_target_pairs={{0,4},{4,0},{8,12},{12,8},{1,5},{5,1},{9,13},{13,9},{2,6},{6,2},{1... | collective-permute-start | bytes 196616 | tf_op jit(solution)/shard_map/ppermute | solution.py:241
  103.7 7.8 %collective-permute-start.30 = (f32[128,128]{1,0:T(8,128)S(1)}, f32[128,128]{1,0:T(8,128)S(1)}, u32[]{:S(2)}, u32[]{:S(2)}) collective-permute-start(f32[128,128]{1,0:T(8,128)S(1)} %get-tuple-element.37.refs_0_), channel_id=1, source_target_pairs={{0,8},{4,12},{8,0},{12,4},{1,9},{5,13},{9,1},{13,5},{2,10},{6,14},... | collective-permute-start | bytes 196616 | tf_op jit(solution)/shard_map/ppermute | solution.py:241
  105.2 6.3 %collective-permute-start.31 = (f32[128,128]{1,0:T(8,128)S(1)}, f32[128,128]{1,0:T(8,128)S(1)}, u32[]{:S(2)}, u32[]{:S(2)}) collective-permute-start(f32[128,128]{1,0:T(8,128)S(1)} %get-tuple-element.37.refs_0_), channel_id=1, source_target_pairs={{0,12},{4,8},{8,4},{12,0},{1,13},{5,9},{9,5},{13,1},{2,14},{6,10},... | collective-permute-start | bytes 196616 | tf_op jit(solution)/shard_map/ppermute | solution.py:241
  (2 other events, 18.8 us)

commit v13 on v12

--- a/solution.py
+++ b/solution.py
@@ -373,8 +373,8 @@
             [source_room],
         )
 
-    pending0 = prepare(0, strips0, ahead_near(0, ahead_far(0, [])))
-    later1 = ahead_near(1, ahead_far(1, known[1:2]), [pending0])
+    pending0 = prepare(0, strips0, ahead_near(0, ahead_far(0, known[1:3])))
+    later1 = ahead_near(1, ahead_far(1, known[1:3]), [pending0])
     later2 = ahead_far(2, [pending0])
     pending1, solved0 = solve(0, over_rows(pending0), prepare(1, dense, later1))
     later2 = ahead_near(2, later2, [pending1])

time: 113 us -> 115 us (1.018)
  starting transfers between devices: 33 us -> 34.4 us
    ppermute x32, starting transfers between devices: 33 us -> 34.4 us  [shift(): return lax.ppermute(value, axis, [(i, i ^ step) for i in range(n)])]
  transfers between devices with their start and end apart: 32 -> 32, of which waited for: 18 -> 14; matrix products, arithmetic and copies ran while one was open for 0% -> 0% of each run, Pallas kernels for 12% -> 12%
where the time goes in v13:
time: 115 us; the launch traced here: 114 us
  waiting for transfers between devices  61.7 us (54%)
  starting transfers between devices  34.4 us (30%)
  Pallas kernels  18.1 us (16%)
    ppermute x32, waiting for transfers between devices, shift(): return lax.ppermute(value, axis, [(i, i ^ step) for i in range(n)])  61.7 us
    ppermute x32, starting transfers between devices, shift(): return lax.ppermute(value, axis, [(i, i ^ step) for i in range(n)])  34.4 us
    pallas_call x19, Pallas kernels, call(): pl.pallas_call(body, grid=(1,), out_shape=shapes, in_specs=specs + [any_s...  18.1 us
  transfers between devices with their start and end apart: 32, of which 14 were waited for; matrix products, arithmetic and copies ran while one was open for 0% of the time, Pallas kernels for 12%

profile of v13, /device:TPU:0, one launch (start us, length us, event | category | flops | bytes accessed | tf_op | source)
XLA Modules:
  0.0 114.5 jit_solution(16791342734295737771)
XLA Ops:
  0.0 1.4 %first.1 = (f32[736,128]{1,0:T(8,128)S(1)}, f32[4,128,128]{2,1,0:T(8,128)S(1)}) custom-call(f32[4,128,128]{2,1,0:T(8,128)} %refs_0_.3, f32[4,7,64,128]{3,2,1,0:T(8,128)} %bitcast.6, f32[4,128,128]{2,1,0:T(8,128)} %refs_4_.1), custom_call_target="tpu_custom_call" | custom-call | tf_op jit(solution)/shard_map/first/pallas_call | solution.py:267
  1.4 1.4 %dense.1.refs_0_ = f32[19,128,128]{2,1,0:T(8,128)S(1)} custom-call(s32[4,7]{1,0:T(4,128)S(1)} %copy-done, f32[4,7,128,128]{3,2,1,0:T(8,128)} %refs_3_.1, f32[4,7,128,128]{3,2,1,0:T(8,128)} %refs_3_.1, f32[4,7,128,128]{3,2,1,0:T(8,128)} %refs_3_.1, f32[4,128,128]{2,1,0:T(8,128)} %refs_4_.1, f32[736,128]{1,0:T(8,128)S(1)} %get-tuple-element.22.refs_2_.refs_0_.refs_5_), custom_call_target="tpu_custom_call" | custom-call | tf_op jit(solution)/shard_map/dense/pallas_call | solution.py:267
  2.8 3.0 %collective-permute-start.15 = (f32[19,128,128]{2,1,0:T(8,128)S(1)}, f32[19,128,128]{2,1,0:T(8,128)S(1)}, u32[]{:S(2)}, u32[]{:S(2)}) collective-permute-start(f32[19,128,128]{2,1,0:T(8,128)S(1)} %dense.1.refs_0_), channel_id=1, source_target_pairs={{0,2},{1,3},{2,0},{3,1},{4,6},{5,7},{6,4},{7,5},{8,10},{9,11},{10,... | collective-permute-start | bytes 3735560 | tf_op jit(solution)/shard_map/ppermute | solution.py:241
  5.8 2.6 %collective-permute-start.4 = (f32[736,128]{1,0:T(8,128)S(1)}, f32[736,128]{1,0:T(8,128)S(1)}, u32[]{:S(2)}, u32[]{:S(2)}) collective-permute-start(f32[736,128]{1,0:T(8,128)S(1)} %get-tuple-element.22.refs_2_.refs_0_.refs_5_), channel_id=1, source_target_pairs={{0,8},{4,12},{8,0},{12,4},{1,9},{5,13},{9,1},{13,5},{2,10},{6,14},... | collective-permute-start | bytes 1130504 | tf_op jit(solution)/shard_map/ppermute | solution.py:241
  8.7 1.6 %collective-permute-start.3 = (f32[736,128]{1,0:T(8,128)S(1)}, f32[736,128]{1,0:T(8,128)S(1)}, u32[]{:S(2)}, u32[]{:S(2)}) collective-permute-start(f32[736,128]{1,0:T(8,128)S(1)} %get-tuple-element.22.refs_2_.refs_0_.refs_5_), channel_id=1, source_target_pairs={{0,4},{4,0},{8,12},{12,8},{1,5},{5,1},{9,13},{13,9},{2,6},{6,2},{1... | collective-permute-start | bytes 1130504 | tf_op jit(solution)/shard_map/ppermute | solution.py:241
  10.3 21.5 %collective-permute-done.4.refs_2_ = f32[736,128]{1,0:T(8,128)S(1)} collective-permute-done((f32[736,128]{1,0:T(8,128)S(1)}, f32[736,128]{1,0:T(8,128)S(1)}, u32[]{:S(2)}, u32[]{:S(2)}) %collective-permute-start.4) | collective-permute-done | bytes 376864 | tf_op jit(solution)/shard_map/ppermute | solution.py:241
  31.8 2.0 %collective-permute-start.6 = (f32[4,128,128]{2,1,0:T(8,128)S(1)}, f32[4,128,128]{2,1,0:T(8,128)S(1)}, u32[]{:S(2)}, u32[]{:S(2)}) collective-permute-start(f32[4,128,128]{2,1,0:T(8,128)S(1)} %get-tuple-element.23.refs_6_), channel_id=1, source_target_pairs={{0,4},{4,0},{8,12},{12,8},{1,5},{5,1},{9,13},{13,9},{2,6},{6,2},{1... | collective-permute-start | bytes 786440 | tf_op jit(solution)/shard_map/ppermute | solution.py:241
  34.9 1.5 %collective-permute-done.7.refs_5_.refs_8_ = f32[4,128,128]{2,1,0:T(8,128)S(1)} collective-permute-done((f32[4,128,128]{2,1,0:T(8,128)S(1)}, f32[4,128,128]{2,1,0:T(8,128)S(1)}, u32[]{:S(2)}, u32[]{:S(2)}) %collective-permute-start.7) | collective-permute-done | bytes 262176 | tf_op jit(solution)/shard_map/ppermute | solution.py:241
  36.8 13.1 %collective-permute-done.6.refs_4_.refs_7_ = f32[4,128,128]{2,1,0:T(8,128)S(1)} collective-permute-done((f32[4,128,128]{2,1,0:T(8,128)S(1)}, f32[4,128,128]{2,1,0:T(8,128)S(1)}, u32[]{:S(2)}, u32[]{:S(2)}) %collective-permute-start.6) | collective-permute-done | bytes 262176 | tf_op jit(solution)/shard_map/ppermute | solution.py:241
  50.6 1.6 %collective-permute-start.17 = (f32[832,128]{1,0:T(8,128)S(1)}, f32[832,128]{1,0:T(8,128)S(1)}, u32[]{:S(2)}, u32[]{:S(2)}) collective-permute-start(f32[832,128]{1,0:T(8,128)S(1)} %ahead1.1.refs_0_), channel_id=1, source_target_pairs={{0,2},{1,3},{2,0},{3,1},{4,6},{5,7},{6,4},{7,5},{8,10},{9,11},{10,... | collective-permute-start | bytes 1277960 | tf_op jit(solution)/shard_map/ppermute | solution.py:241
  52.2 4.2 %collective-permute-done.8.refs_1_ = f32[256,128]{1,0:T(8,128)S(1)} collective-permute-done((f32[256,128]{1,0:T(8,128)S(1)}, f32[256,128]{1,0:T(8,128)S(1)}, u32[]{:S(2)}, u32[]{:S(2)}) %collective-permute-start.8) | collective-permute-done | bytes 131104 | tf_op jit(solution)/shard_map/ppermute | solution.py:241
  57.0 1.7 %collective-permute-done.10.refs_9_ = f32[4,128,128]{2,1,0:T(8,128)S(1)} collective-permute-done((f32[4,128,128]{2,1,0:T(8,128)S(1)}, f32[4,128,128]{2,1,0:T(8,128)S(1)}, u32[]{:S(2)}, u32[]{:S(2)}) %collective-permute-start.10) | collective-permute-done | bytes 262176 | tf_op jit(solution)/shard_map/ppermute | solution.py:241
  58.6 2.8 %collective-permute-done.2.refs_3_ = f32[4,128,128]{2,1,0:T(8,128)S(1)} collective-permute-done((f32[4,128,128]{2,1,0:T(8,128)S(1)}, f32[4,128,128]{2,1,0:T(8,128)S(1)}, u32[]{:S(2)}, u32[]{:S(2)}) %collective-permute-start.2) | collective-permute-done | bytes 262176 | tf_op jit(solution)/shard_map/ppermute | solution.py:241
  61.8 2.3 %prepare0.1.refs_2_.refs_0_.refs_4_ = f32[128,128]{1,0:T(8,128)S(1)} custom-call(f32[4,128,128]{2,1,0:T(8,128)S(1)} %dense0.1.refs_0_, f32[4,128,128]{2,1,0:T(8,128)S(1)} %collective-permute-done.refs_1_, f32[4,128,128]{2,1,0:T(8,128)S(1)} %collective-permute-done.1.refs_2_, f32[4,128,128]{2,1,0:T(8,128)S(1)} %collective-permute-done.2.refs_3_, ...), custom_call_target="tpu_custom_call" | custom-call | tf_op jit(solution)/shard_map/prepare0/pallas_call | solution.py:267
  65.8 1.7 %collective-permute-start.11 = (f32[128,128]{1,0:T(8,128)S(1)}, f32[128,128]{1,0:T(8,128)S(1)}, u32[]{:S(2)}, u32[]{:S(2)}) collective-permute-start(f32[128,128]{1,0:T(8,128)S(1)} %prepare0.1.refs_2_.refs_0_.refs_4_), channel_id=1, source_target_pairs={{0,4},{4,0},{8,12},{12,8},{1,5},{5,1},{9,13},{13,9},{2,6},{6,2},{1... | collective-permute-start | bytes 196616 | tf_op jit(solution)/shard_map/ppermute | solution.py:241
  67.5 2.4 %collective-permute-start.12 = (f32[128,128]{1,0:T(8,128)S(1)}, f32[128,128]{1,0:T(8,128)S(1)}, u32[]{:S(2)}, u32[]{:S(2)}) collective-permute-start(f32[128,128]{1,0:T(8,128)S(1)} %prepare0.1.refs_2_.refs_0_.refs_4_), channel_id=1, source_target_pairs={{0,8},{4,12},{8,0},{12,4},{1,9},{5,13},{9,1},{13,5},{2,10},{6,14},... | collective-permute-start | bytes 196616 | tf_op jit(solution)/shard_map/ppermute | solution.py:241
  71.1 2.6 %prepare1.1 = (f32[128,128]{1,0:T(8,128)S(1)}, bf16[1,256,512]{2,1,0:T(8,128)(2,1)S(1)}, bf16[1024,512]{1,0:T(8,128)(2,1)S(1)}) custom-call(f32[19,128,128]{2,1,0:T(8,128)S(1)} %dense.1.refs_0_, f32[19,128,128]{2,1,0:T(8,128)S(1)} %collective-permute-done.14.refs_1_, f32[19,128,128]{2,1,0:T(8,128)S(1)} %collective-permute-done.15.refs_2_, ...), custom_call_target="tpu_custom_call" | custom-call | tf_op jit(solution)/shard_map/prepare1/pallas_call | solution.py:267
  73.8 2.3 %collective-permute-done.13.refs_3_ = f32[128,128]{1,0:T(8,128)S(1)} collective-permute-done((f32[128,128]{1,0:T(8,128)S(1)}, f32[128,128]{1,0:T(8,128)S(1)}, u32[]{:S(2)}, u32[]{:S(2)}) %collective-permute-start.13) | collective-permute-done | bytes 65568 | tf_op jit(solution)/shard_map/ppermute | solution.py:241
  76.8 1.4 %collective-permute-done.22.refs_1_ = f32[896,128]{1,0:T(8,128)S(1)} collective-permute-done((f32[896,128]{1,0:T(8,128)S(1)}, f32[896,128]{1,0:T(8,128)S(1)}, u32[]{:S(2)}, u32[]{:S(2)}) %collective-permute-start.22) | collective-permute-done | bytes 458784 | tf_op jit(solution)/shard_map/ppermute | solution.py:241
  79.0 1.7 %collective-permute-start.19 = (f32[128,128]{1,0:T(8,128)S(1)}, f32[128,128]{1,0:T(8,128)S(1)}, u32[]{:S(2)}, u32[]{:S(2)}) collective-permute-start(f32[128,128]{1,0:T(8,128)S(1)} %get-tuple-element.27.refs_2_.refs_0_.refs_4_), channel_id=1, source_target_pairs={{0,4},{4,0},{8,12},{12,8},{1,5},{5,1},{9,13},{13,9},{2,6},{6,2},{1... | collective-permute-start | bytes 196616 | tf_op jit(solution)/shard_map/ppermute | solution.py:241
  80.7 2.4 %collective-permute-start.20 = (f32[128,128]{1,0:T(8,128)S(1)}, f32[128,128]{1,0:T(8,128)S(1)}, u32[]{:S(2)}, u32[]{:S(2)}) collective-permute-start(f32[128,128]{1,0:T(8,128)S(1)} %get-tuple-element.27.refs_2_.refs_0_.refs_4_), channel_id=1, source_target_pairs={{0,8},{4,12},{8,0},{12,4},{1,9},{5,13},{9,1},{13,5},{2,10},{6,14},... | collective-permute-start | bytes 196616 | tf_op jit(solution)/shard_map/ppermute | solution.py:241
  84.2 2.8 %prepare2.1 = (f32[128,128]{1,0:T(8,128)S(1)}, bf16[1,256,512]{2,1,0:T(8,128)(2,1)S(1)}, bf16[1024,512]{1,0:T(8,128)(2,1)S(1)}) custom-call(f32[19,128,128]{2,1,0:T(8,128)S(1)} %dense.1.refs_0_, f32[19,128,128]{2,1,0:T(8,128)S(1)} %collective-permute-done.14.refs_1_, f32[19,128,128]{2,1,0:T(8,128)S(1)} %collective-permute-done.15.refs_2_, ...), custom_call_target="tpu_custom_call" | custom-call | tf_op jit(solution)/shard_map/prepare2/pallas_call | solution.py:267
  87.1 2.2 %collective-permute-done.21.refs_3_ = f32[128,128]{1,0:T(8,128)S(1)} collective-permute-done((f32[128,128]{1,0:T(8,128)S(1)}, f32[128,128]{1,0:T(8,128)S(1)}, u32[]{:S(2)}, u32[]{:S(2)}) %collective-permute-start.21) | collective-permute-done | bytes 65568 | tf_op jit(solution)/shard_map/ppermute | solution.py:241
  90.0 2.1 %collective-permute-done.27.refs_1_ = f32[960,128]{1,0:T(8,128)S(1)} collective-permute-done((f32[960,128]{1,0:T(8,128)S(1)}, f32[960,128]{1,0:T(8,128)S(1)}, u32[]{:S(2)}, u32[]{:S(2)}) %collective-permute-start.27) | collective-permute-done | bytes 491552 | tf_op jit(solution)/shard_map/ppermute | solution.py:241
  92.2 1.8 %collective-permute-start.24 = (f32[128,128]{1,0:T(8,128)S(1)}, f32[128,128]{1,0:T(8,128)S(1)}, u32[]{:S(2)}, u32[]{:S(2)}) collective-permute-start(f32[128,128]{1,0:T(8,128)S(1)} %get-tuple-element.32.refs_2_.refs_0_), channel_id=1, source_target_pairs={{0,4},{4,0},{8,12},{12,8},{1,5},{5,1},{9,13},{13,9},{2,6},{6,2},{1... | collective-permute-start | bytes 196616 | tf_op jit(solution)/shard_map/ppermute | solution.py:241
  94.0 2.3 %collective-permute-start.25 = (f32[128,128]{1,0:T(8,128)S(1)}, f32[128,128]{1,0:T(8,128)S(1)}, u32[]{:S(2)}, u32[]{:S(2)}) collective-permute-start(f32[128,128]{1,0:T(8,128)S(1)} %get-tuple-element.32.refs_2_.refs_0_), channel_id=1, source_target_pairs={{0,8},{4,12},{8,0},{12,4},{1,9},{5,13},{9,1},{13,5},{2,10},{6,14},... | collective-permute-start | bytes 196616 | tf_op jit(solution)/shard_map/ppermute | solution.py:241
  97.5 3.2 %prepare3.1 = (f32[128,128]{1,0:T(8,128)S(1)}, bf16[2,256,512]{2,1,0:T(8,128)(2,1)S(1)}, bf16[1024,512]{1,0:T(8,128)(2,1)S(1)}) custom-call(f32[19,128,128]{2,1,0:T(8,128)S(1)} %dense.1.refs_0_, f32[19,128,128]{2,1,0:T(8,128)S(1)} %collective-permute-done.14.refs_1_, f32[19,128,128]{2,1,0:T(8,128)S(1)} %collective-permute-done.15.refs_2_, ...), custom_call_target="tpu_custom_call" | custom-call | tf_op jit(solution)/shard_map/prepare3/pallas_call | solution.py:267
  100.7 2.1 %collective-permute-done.26.refs_3_ = f32[128,128]{1,0:T(8,128)S(1)} collective-permute-done((f32[128,128]{1,0:T(8,128)S(1)}, f32[128,128]{1,0:T(8,128)S(1)}, u32[]{:S(2)}, u32[]{:S(2)}) %collective-permute-start.26) | collective-permute-done | bytes 65568 | tf_op jit(solution)/shard_map/ppermute | solution.py:241
  103.6 1.7 %collective-permute-start.29 = (f32[128,128]{1,0:T(8,128)S(1)}, f32[128,128]{1,0:T(8,128)S(1)}, u32[]{:S(2)}, u32[]{:S(2)}) collective-permute-start(f32[128,128]{1,0:T(8,128)S(1)} %get-tuple-element.37.refs_0_), channel_id=1, source_target_pairs={{0,4},{4,0},{8,12},{12,8},{1,5},{5,1},{9,13},{13,9},{2,6},{6,2},{1... | collective-permute-start | bytes 196616 | tf_op jit(solution)/shard_map/ppermute | solution.py:241
  105.3 1.3 %collective-permute-start.30 = (f32[128,128]{1,0:T(8,128)S(1)}, f32[128,128]{1,0:T(8,128)S(1)}, u32[]{:S(2)}, u32[]{:S(2)}) collective-permute-start(f32[128,128]{1,0:T(8,128)S(1)} %get-tuple-element.37.refs_0_), channel_id=1, source_target_pairs={{0,8},{4,12},{8,0},{12,4},{1,9},{5,13},{9,1},{13,5},{2,10},{6,14},... | collective-permute-start | bytes 196616 | tf_op jit(solution)/shard_map/ppermute | solution.py:241
  106.6 1.5 %collective-permute-start.31 = (f32[128,128]{1,0:T(8,128)S(1)}, f32[128,128]{1,0:T(8,128)S(1)}, u32[]{:S(2)}, u32[]{:S(2)}) collective-permute-start(f32[128,128]{1,0:T(8,128)S(1)} %get-tuple-element.37.refs_0_), channel_id=1, source_target_pairs={{0,12},{4,8},{8,4},{12,0},{1,13},{5,9},{9,5},{13,1},{2,14},{6,10},... | collective-permute-start | bytes 196616 | tf_op jit(solution)/shard_map/ppermute | solution.py:241
  108.0 5.4 %collective-permute-done.30.refs_2_ = f32[128,128]{1,0:T(8,128)S(1)} collective-permute-done((f32[128,128]{1,0:T(8,128)S(1)}, f32[128,128]{1,0:T(8,128)S(1)}, u32[]{:S(2)}, u32[]{:S(2)}) %collective-permute-start.30) | collective-permute-done | bytes 65568 | tf_op jit(solution)/shard_map/ppermute | solution.py:241
  (55 shorter events, 12.8 us)
Async XLA Ops:
  2.8 53.6 %collective-permute-start.15 = (f32[19,128,128]{2,1,0:T(8,128)S(1)}, f32[19,128,128]{2,1,0:T(8,128)S(1)}, u32[]{:S(2)}, u32[]{:S(2)}) collective-permute-start(f32[19,128,128]{2,1,0:T(8,128)S(1)} %dense.1.refs_0_), channel_id=1, source_target_pairs={{0,2},{1,3},{2,0},{3,1},{4,6},{5,7},{6,4},{7,5},{8,10},{9,11},{10,... | collective-permute-start | bytes 3735560 | tf_op jit(solution)/shard_map/ppermute | solution.py:241
  5.8 26.0 %collective-permute-start.4 = (f32[736,128]{1,0:T(8,128)S(1)}, f32[736,128]{1,0:T(8,128)S(1)}, u32[]{:S(2)}, u32[]{:S(2)}) collective-permute-start(f32[736,128]{1,0:T(8,128)S(1)} %get-tuple-element.22.refs_2_.refs_0_.refs_5_), channel_id=1, source_target_pairs={{0,8},{4,12},{8,0},{12,4},{1,9},{5,13},{9,1},{13,5},{2,10},{6,14},... | collective-permute-start | bytes 1130504 | tf_op jit(solution)/shard_map/ppermute | solution.py:241
  8.4 27.9 %collective-permute-start.7 = (f32[4,128,128]{2,1,0:T(8,128)S(1)}, f32[4,128,128]{2,1,0:T(8,128)S(1)}, u32[]{:S(2)}, u32[]{:S(2)}) collective-permute-start(f32[4,128,128]{2,1,0:T(8,128)S(1)} %get-tuple-element.23.refs_6_), channel_id=1, source_target_pairs={{0,8},{4,12},{8,0},{12,4},{1,9},{5,13},{9,1},{13,5},{2,10},{6,14},... | collective-permute-start | bytes 786440 | tf_op jit(solution)/shard_map/ppermute | solution.py:241
  8.7 41.2 %collective-permute-start.3 = (f32[736,128]{1,0:T(8,128)S(1)}, f32[736,128]{1,0:T(8,128)S(1)}, u32[]{:S(2)}, u32[]{:S(2)}) collective-permute-start(f32[736,128]{1,0:T(8,128)S(1)} %get-tuple-element.22.refs_2_.refs_0_.refs_5_), channel_id=1, source_target_pairs={{0,4},{4,0},{8,12},{12,8},{1,5},{5,1},{9,13},{13,9},{2,6},{6,2},{1... | collective-permute-start | bytes 1130504 | tf_op jit(solution)/shard_map/ppermute | solution.py:241
  31.8 18.2 %collective-permute-start.5 = (f32[736,128]{1,0:T(8,128)S(1)}, f32[736,128]{1,0:T(8,128)S(1)}, u32[]{:S(2)}, u32[]{:S(2)}) collective-permute-start(f32[736,128]{1,0:T(8,128)S(1)} %collective-permute-done.4.refs_2_), channel_id=1, source_target_pairs={{0,4},{4,0},{8,12},{12,8},{1,5},{5,1},{9,13},{13,9},{2,6},{6,2},{1... | collective-permute-start | bytes 1130504 | tf_op jit(solution)/shard_map/ppermute | solution.py:241
  31.8 18.1 %collective-permute-start.6 = (f32[4,128,128]{2,1,0:T(8,128)S(1)}, f32[4,128,128]{2,1,0:T(8,128)S(1)}, u32[]{:S(2)}, u32[]{:S(2)}) collective-permute-start(f32[4,128,128]{2,1,0:T(8,128)S(1)} %get-tuple-element.23.refs_6_), channel_id=1, source_target_pairs={{0,4},{4,0},{8,12},{12,8},{1,5},{5,1},{9,13},{13,9},{2,6},{6,2},{1... | collective-permute-start | bytes 786440 | tf_op jit(solution)/shard_map/ppermute | solution.py:241
  36.3 14.2 %collective-permute-start.1 = (f32[4,128,128]{2,1,0:T(8,128)S(1)}, f32[4,128,128]{2,1,0:T(8,128)S(1)}, u32[]{:S(2)}, u32[]{:S(2)}) collective-permute-start(f32[4,128,128]{2,1,0:T(8,128)S(1)} %dense0.1.refs_0_), channel_id=1, source_target_pairs={{0,2},{1,3},{2,0},{3,1},{4,6},{5,7},{6,4},{7,5},{8,10},{9,11},{10,... | collective-permute-start | bytes 786440 | tf_op jit(solution)/shard_map/ppermute | solution.py:241
  49.9 7.0 %collective-permute-start = (f32[4,128,128]{2,1,0:T(8,128)S(1)}, f32[4,128,128]{2,1,0:T(8,128)S(1)}, u32[]{:S(2)}, u32[]{:S(2)}) collective-permute-start(f32[4,128,128]{2,1,0:T(8,128)S(1)} %dense0.1.refs_0_), channel_id=1, source_target_pairs={{0,1},{1,0},{2,3},{3,2},{4,5},{5,4},{6,7},{7,6},{8,9},{9,8},{10,11... | collective-permute-start | bytes 786440 | tf_op jit(solution)/shard_map/ppermute | solution.py:241
  49.9 8.7 %collective-permute-start.10 = (f32[4,128,128]{2,1,0:T(8,128)S(1)}, f32[4,128,128]{2,1,0:T(8,128)S(1)}, u32[]{:S(2)}, u32[]{:S(2)}) collective-permute-start(f32[4,128,128]{2,1,0:T(8,128)S(1)} %collective-permute-done.7.refs_5_.refs_8_), channel_id=1, source_target_pairs={{0,4},{4,0},{8,12},{12,8},{1,5},{5,1},{9,13},{13,9},{2,6},{6,2},{1... | collective-permute-start | bytes 786440 | tf_op jit(solution)/shard_map/ppermute | solution.py:241
  50.0 6.4 %collective-permute-start.8 = (f32[256,128]{1,0:T(8,128)S(1)}, f32[256,128]{1,0:T(8,128)S(1)}, u32[]{:S(2)}, u32[]{:S(2)}) collective-permute-start(f32[256,128]{1,0:T(8,128)S(1)} %ahead0.1.refs_0_), channel_id=1, source_target_pairs={{0,2},{1,3},{2,0},{3,1},{4,6},{5,7},{6,4},{7,5},{8,10},{9,11},{10,... | collective-permute-start | bytes 393224 | tf_op jit(solution)/shard_map/ppermute | solution.py:241
  50.6 14.5 %collective-permute-start.17 = (f32[832,128]{1,0:T(8,128)S(1)}, f32[832,128]{1,0:T(8,128)S(1)}, u32[]{:S(2)}, u32[]{:S(2)}) collective-permute-start(f32[832,128]{1,0:T(8,128)S(1)} %ahead1.1.refs_0_), channel_id=1, source_target_pairs={{0,2},{1,3},{2,0},{3,1},{4,6},{5,7},{6,4},{7,5},{8,10},{9,11},{10,... | collective-permute-start | bytes 1277960 | tf_op jit(solution)/shard_map/ppermute | solution.py:241
  56.3 11.2 %collective-permute-start.14 = (f32[19,128,128]{2,1,0:T(8,128)S(1)}, f32[19,128,128]{2,1,0:T(8,128)S(1)}, u32[]{:S(2)}, u32[]{:S(2)}) collective-permute-start(f32[19,128,128]{2,1,0:T(8,128)S(1)} %dense.1.refs_0_), channel_id=1, source_target_pairs={{0,1},{1,0},{2,3},{3,2},{4,5},{5,4},{6,7},{7,6},{8,9},{9,8},{10,11... | collective-permute-start | bytes 3735560 | tf_op jit(solution)/shard_map/ppermute | solution.py:241
  56.3 14.8 %collective-permute-start.16 = (f32[19,128,128]{2,1,0:T(8,128)S(1)}, f32[19,128,128]{2,1,0:T(8,128)S(1)}, u32[]{:S(2)}, u32[]{:S(2)}) collective-permute-start(f32[19,128,128]{2,1,0:T(8,128)S(1)} %collective-permute-done.15.refs_2_), channel_id=1, source_target_pairs={{0,1},{1,0},{2,3},{3,2},{4,5},{5,4},{6,7},{7,6},{8,9},{9,8},{10,11... | collective-permute-start | bytes 3735560 | tf_op jit(solution)/shard_map/ppermute | solution.py:241
  56.9 4.6 %collective-permute-start.2 = (f32[4,128,128]{2,1,0:T(8,128)S(1)}, f32[4,128,128]{2,1,0:T(8,128)S(1)}, u32[]{:S(2)}, u32[]{:S(2)}) collective-permute-start(f32[4,128,128]{2,1,0:T(8,128)S(1)} %collective-permute-done.1.refs_2_), channel_id=1, source_target_pairs={{0,1},{1,0},{2,3},{3,2},{4,5},{5,4},{6,7},{7,6},{8,9},{9,8},{10,11... | collective-permute-start | bytes 786440 | tf_op jit(solution)/shard_map/ppermute | solution.py:241
  58.6 3.2 %collective-permute-start.9 = (f32[512,128]{1,0:T(8,128)S(1)}, f32[512,128]{1,0:T(8,128)S(1)}, u32[]{:S(2)}, u32[]{:S(2)}) collective-permute-start(f32[512,128]{1,0:T(8,128)S(1)} %aheads0.1.refs_4_), channel_id=1, source_target_pairs={{0,1},{1,0},{2,3},{3,2},{4,5},{5,4},{6,7},{7,6},{8,9},{9,8},{10,11... | collective-permute-start | bytes 786440 | tf_op jit(solution)/shard_map/ppermute | solution.py:241
  65.1 4.8 %collective-permute-start.18 = (f32[1664,128]{1,0:T(8,128)S(1)}, f32[1664,128]{1,0:T(8,128)S(1)}, u32[]{:S(2)}, u32[]{:S(2)}) collective-permute-start(f32[1664,128]{1,0:T(8,128)S(1)} %aheads1.1.refs_4_), channel_id=1, source_target_pairs={{0,1},{1,0},{2,3},{3,2},{4,5},{5,4},{6,7},{7,6},{8,9},{9,8},{10,11... | collective-permute-start | bytes 2555912 | tf_op jit(solution)/shard_map/ppermute | solution.py:241
  65.2 13.0 %collective-permute-start.22 = (f32[896,128]{1,0:T(8,128)S(1)}, f32[896,128]{1,0:T(8,128)S(1)}, u32[]{:S(2)}, u32[]{:S(2)}) collective-permute-start(f32[896,128]{1,0:T(8,128)S(1)} %ahead2.1.refs_0_), channel_id=1, source_target_pairs={{0,2},{1,3},{2,0},{3,1},{4,6},{5,7},{6,4},{7,5},{8,10},{9,11},{10,... | collective-permute-start | bytes 1376264 | tf_op jit(solution)/shard_map/ppermute | solution.py:241
  65.8 8.0 %collective-permute-start.11 = (f32[128,128]{1,0:T(8,128)S(1)}, f32[128,128]{1,0:T(8,128)S(1)}, u32[]{:S(2)}, u32[]{:S(2)}) collective-permute-start(f32[128,128]{1,0:T(8,128)S(1)} %prepare0.1.refs_2_.refs_0_.refs_4_), channel_id=1, source_target_pairs={{0,4},{4,0},{8,12},{12,8},{1,5},{5,1},{9,13},{13,9},{2,6},{6,2},{1... | collective-permute-start | bytes 196616 | tf_op jit(solution)/shard_map/ppermute | solution.py:241
  67.5 6.2 %collective-permute-start.12 = (f32[128,128]{1,0:T(8,128)S(1)}, f32[128,128]{1,0:T(8,128)S(1)}, u32[]{:S(2)}, u32[]{:S(2)}) collective-permute-start(f32[128,128]{1,0:T(8,128)S(1)} %prepare0.1.refs_2_.refs_0_.refs_4_), channel_id=1, source_target_pairs={{0,8},{4,12},{8,0},{12,4},{1,9},{5,13},{9,1},{13,5},{2,10},{6,14},... | collective-permute-start | bytes 196616 | tf_op jit(solution)/shard_map/ppermute | solution.py:241
  69.9 6.2 %collective-permute-start.13 = (f32[128,128]{1,0:T(8,128)S(1)}, f32[128,128]{1,0:T(8,128)S(1)}, u32[]{:S(2)}, u32[]{:S(2)}) collective-permute-start(f32[128,128]{1,0:T(8,128)S(1)} %prepare0.1.refs_2_.refs_0_.refs_4_), channel_id=1, source_target_pairs={{0,12},{4,8},{8,4},{12,0},{1,13},{5,9},{9,5},{13,1},{2,14},{6,10},... | collective-permute-start | bytes 196616 | tf_op jit(solution)/shard_map/ppermute | solution.py:241
  78.3 6.0 %collective-permute-start.23 = (f32[1792,128]{1,0:T(8,128)S(1)}, f32[1792,128]{1,0:T(8,128)S(1)}, u32[]{:S(2)}, u32[]{:S(2)}) collective-permute-start(f32[1792,128]{1,0:T(8,128)S(1)} %aheads2.1.refs_4_), channel_id=1, source_target_pairs={{0,1},{1,0},{2,3},{3,2},{4,5},{5,4},{6,7},{7,6},{8,9},{9,8},{10,11... | collective-permute-start | bytes 2752520 | tf_op jit(solution)/shard_map/ppermute | solution.py:241
  78.4 13.7 %collective-permute-start.27 = (f32[960,128]{1,0:T(8,128)S(1)}, f32[960,128]{1,0:T(8,128)S(1)}, u32[]{:S(2)}, u32[]{:S(2)}) collective-permute-start(f32[960,128]{1,0:T(8,128)S(1)} %ahead3.1.refs_0_), channel_id=1, source_target_pairs={{0,2},{1,3},{2,0},{3,1},{4,6},{5,7},{6,4},{7,5},{8,10},{9,11},{10,... | collective-permute-start | bytes 1474568 | tf_op jit(solution)/shard_map/ppermute | solution.py:241
  79.0 8.1 %collective-permute-start.19 = (f32[128,128]{1,0:T(8,128)S(1)}, f32[128,128]{1,0:T(8,128)S(1)}, u32[]{:S(2)}, u32[]{:S(2)}) collective-permute-start(f32[128,128]{1,0:T(8,128)S(1)} %get-tuple-element.27.refs_2_.refs_0_.refs_4_), channel_id=1, source_target_pairs={{0,4},{4,0},{8,12},{12,8},{1,5},{5,1},{9,13},{13,9},{2,6},{6,2},{1... | collective-permute-start | bytes 196616 | tf_op jit(solution)/shard_map/ppermute | solution.py:241
  80.7 6.4 %collective-permute-start.20 = (f32[128,128]{1,0:T(8,128)S(1)}, f32[128,128]{1,0:T(8,128)S(1)}, u32[]{:S(2)}, u32[]{:S(2)}) collective-permute-start(f32[128,128]{1,0:T(8,128)S(1)} %get-tuple-element.27.refs_2_.refs_0_.refs_4_), channel_id=1, source_target_pairs={{0,8},{4,12},{8,0},{12,4},{1,9},{5,13},{9,1},{13,5},{2,10},{6,14},... | collective-permute-start | bytes 196616 | tf_op jit(solution)/shard_map/ppermute | solution.py:241
  83.1 6.2 %collective-permute-start.21 = (f32[128,128]{1,0:T(8,128)S(1)}, f32[128,128]{1,0:T(8,128)S(1)}, u32[]{:S(2)}, u32[]{:S(2)}) collective-permute-start(f32[128,128]{1,0:T(8,128)S(1)} %get-tuple-element.27.refs_2_.refs_0_.refs_4_), channel_id=1, source_target_pairs={{0,12},{4,8},{8,4},{12,0},{1,13},{5,9},{9,5},{13,1},{2,14},{6,10},... | collective-permute-start | bytes 196616 | tf_op jit(solution)/shard_map/ppermute | solution.py:241
  92.2 5.4 %collective-permute-start.28 = (f32[1920,128]{1,0:T(8,128)S(1)}, f32[1920,128]{1,0:T(8,128)S(1)}, u32[]{:S(2)}, u32[]{:S(2)}) collective-permute-start(f32[1920,128]{1,0:T(8,128)S(1)} %aheads3.1.refs_4_), channel_id=1, source_target_pairs={{0,1},{1,0},{2,3},{3,2},{4,5},{5,4},{6,7},{7,6},{8,9},{9,8},{10,11... | collective-permute-start | bytes 2949128 | tf_op jit(solution)/shard_map/ppermute | solution.py:241
  92.2 8.5 %collective-permute-start.24 = (f32[128,128]{1,0:T(8,128)S(1)}, f32[128,128]{1,0:T(8,128)S(1)}, u32[]{:S(2)}, u32[]{:S(2)}) collective-permute-start(f32[128,128]{1,0:T(8,128)S(1)} %get-tuple-element.32.refs_2_.refs_0_), channel_id=1, source_target_pairs={{0,4},{4,0},{8,12},{12,8},{1,5},{5,1},{9,13},{13,9},{2,6},{6,2},{1... | collective-permute-start | bytes 196616 | tf_op jit(solution)/shard_map/ppermute | solution.py:241
  94.0 6.7 %collective-permute-start.25 = (f32[128,128]{1,0:T(8,128)S(1)}, f32[128,128]{1,0:T(8,128)S(1)}, u32[]{:S(2)}, u32[]{:S(2)}) collective-permute-start(f32[128,128]{1,0:T(8,128)S(1)} %get-tuple-element.32.refs_2_.refs_0_), channel_id=1, source_target_pairs={{0,8},{4,12},{8,0},{12,4},{1,9},{5,13},{9,1},{13,5},{2,10},{6,14},... | collective-permute-start | bytes 196616 | tf_op jit(solution)/shard_map/ppermute | solution.py:241
  96.4 6.5 %collective-permute-start.26 = (f32[128,128]{1,0:T(8,128)S(1)}, f32[128,128]{1,0:T(8,128)S(1)}, u32[]{:S(2)}, u32[]{:S(2)}) collective-permute-start(f32[128,128]{1,0:T(8,128)S(1)} %get-tuple-element.32.refs_2_.refs_0_), channel_id=1, source_target_pairs={{0,12},{4,8},{8,4},{12,0},{1,13},{5,9},{9,5},{13,1},{2,14},{6,10},... | collective-permute-start | bytes 196616 | tf_op jit(solution)/shard_map/ppermute | solution.py:241
  103.6 4.5 %collective-permute-start.29 = (f32[128,128]{1,0:T(8,128)S(1)}, f32[128,128]{1,0:T(8,128)S(1)}, u32[]{:S(2)}, u32[]{:S(2)}) collective-permute-start(f32[128,128]{1,0:T(8,128)S(1)} %get-tuple-element.37.refs_0_), channel_id=1, source_target_pairs={{0,4},{4,0},{8,12},{12,8},{1,5},{5,1},{9,13},{13,9},{2,6},{6,2},{1... | collective-permute-start | bytes 196616 | tf_op jit(solution)/shard_map/ppermute | solution.py:241
  105.3 8.2 %collective-permute-start.30 = (f32[128,128]{1,0:T(8,128)S(1)}, f32[128,128]{1,0:T(8,128)S(1)}, u32[]{:S(2)}, u32[]{:S(2)}) collective-permute-start(f32[128,128]{1,0:T(8,128)S(1)} %get-tuple-element.37.refs_0_), channel_id=1, source_target_pairs={{0,8},{4,12},{8,0},{12,4},{1,9},{5,13},{9,1},{13,5},{2,10},{6,14},... | collective-permute-start | bytes 196616 | tf_op jit(solution)/shard_map/ppermute | solution.py:241
  106.6 6.9 %collective-permute-start.31 = (f32[128,128]{1,0:T(8,128)S(1)}, f32[128,128]{1,0:T(8,128)S(1)}, u32[]{:S(2)}, u32[]{:S(2)}) collective-permute-start(f32[128,128]{1,0:T(8,128)S(1)} %get-tuple-element.37.refs_0_), channel_id=1, source_target_pairs={{0,12},{4,8},{8,4},{12,0},{1,13},{5,9},{9,5},{13,1},{2,14},{6,10},... | collective-permute-start | bytes 196616 | tf_op jit(solution)/shard_map/ppermute | solution.py:241
  (2 other events, 13.2 us)

commit v14 on v9

--- a/solution.py
+++ b/solution.py
@@ -80,10 +80,13 @@
 
 
 def dot_halves(left2, right2, dims=(((1,), (0,)), ((), ()))):
-    rows = left2.shape[1 - dims[0][0][0]] // 2
-    cols = right2.shape[1 - dims[0][1][0]] // 2
-    out = lax.dot_general(left2, right2, dims, preferred_element_type=jnp.float32)
-    return (out[:rows, :cols] + (out[:rows, cols:] + out[rows:, :cols])) + out[rows:, cols:]
+    axis_left, axis_right = 1 - dims[0][0][0], 1 - dims[0][1][0]
+    rows, cols = left2.shape[axis_left] // 2, right2.shape[axis_right] // 2
+    high_left = left2[:rows] if axis_left == 0 else left2[:, :rows]
+    high_right, low_right = right2[:, :cols], right2[:, cols:]
+    out = lax.dot_general(left2, high_right, dims, preferred_element_type=jnp.float32)
+    rest = lax.dot_general(high_left, low_right, dims, preferred_element_type=jnp.float32)
+    return out[:rows] + (out[rows:] + rest)
 
 
 def first_kernel(prev, *refs):

time: 109 us -> 109 us (level)
  Pallas kernels: 18.1 us -> 19.7 us
  waiting for transfers between devices: 57.6 us -> 56.4 us
    pallas_call x19, Pallas kernels: 18.1 us -> 19.7 us  [call(): pl.pallas_call(body, grid=(1,), out_shape=shapes, in_specs=specs + [any_s...]
    ppermute x32, waiting for transfers between devices: 57.6 us -> 56.4 us  [shift(): return lax.ppermute(value, axis, [(i, i ^ step) for i in range(n)])]
  transfers between devices with their start and end apart: 32 -> 32, of which waited for: 13 -> 13; matrix products, arithmetic and copies ran while one was open for 0% -> 0% of each run, Pallas kernels for 12% -> 14%
where the time goes in v14:
time: 109 us
  waiting for transfers between devices  56.4 us (52%)
  starting transfers between devices  32.3 us (30%)
  Pallas kernels  19.7 us (18%)
    ppermute x32, waiting for transfers between devices, shift(): return lax.ppermute(value, axis, [(i, i ^ step) for i in range(n)])  56.4 us
    ppermute x32, starting transfers between devices, shift(): return lax.ppermute(value, axis, [(i, i ^ step) for i in range(n)])  32.3 us
    pallas_call x19, Pallas kernels, call(): pl.pallas_call(body, grid=(1,), out_shape=shapes, in_specs=specs + [any_s...  19.7 us
  transfers between devices with their start and end apart: 32, of which 13 were waited for; matrix products, arithmetic and copies ran while one was open for 0% of the time, Pallas kernels for 14%

profile of v14, /device:TPU:0, one launch (start us, length us, event | category | flops | bytes accessed | tf_op | source)
XLA Modules:
  0.0 108.7 jit_solution(3568591240699545741)
XLA Ops:
  0.0 1.4 %first.1 = (f32[736,128]{1,0:T(8,128)S(1)}, f32[4,128,128]{2,1,0:T(8,128)S(1)}) custom-call(f32[4,128,128]{2,1,0:T(8,128)} %refs_0_.3, f32[4,7,64,128]{3,2,1,0:T(8,128)} %bitcast.6, f32[4,128,128]{2,1,0:T(8,128)} %refs_4_.1), custom_call_target="tpu_custom_call" | custom-call | tf_op jit(solution)/shard_map/first/pallas_call | solution.py:270
  1.4 1.4 %dense.1.refs_0_ = f32[19,128,128]{2,1,0:T(8,128)S(1)} custom-call(s32[4,7]{1,0:T(4,128)S(1)} %copy-done, f32[4,7,128,128]{3,2,1,0:T(8,128)} %refs_3_.1, f32[4,7,128,128]{3,2,1,0:T(8,128)} %refs_3_.1, f32[4,7,128,128]{3,2,1,0:T(8,128)} %refs_3_.1, f32[4,128,128]{2,1,0:T(8,128)} %refs_4_.1, f32[736,128]{1,0:T(8,128)S(1)} %get-tuple-element.22.refs_2_.refs_0_.refs_5_), custom_call_target="tpu_custom_call" | custom-call | tf_op jit(solution)/shard_map/dense/pallas_call | solution.py:270
  2.8 3.0 %collective-permute-start.15 = (f32[19,128,128]{2,1,0:T(8,128)S(1)}, f32[19,128,128]{2,1,0:T(8,128)S(1)}, u32[]{:S(2)}, u32[]{:S(2)}) collective-permute-start(f32[19,128,128]{2,1,0:T(8,128)S(1)} %dense.1.refs_0_), channel_id=1, source_target_pairs={{0,2},{1,3},{2,0},{3,1},{4,6},{5,7},{6,4},{7,5},{8,10},{9,11},{10,... | collective-permute-start | bytes 3735560 | tf_op jit(solution)/shard_map/ppermute | solution.py:244
  5.8 2.6 %collective-permute-start.4 = (f32[736,128]{1,0:T(8,128)S(1)}, f32[736,128]{1,0:T(8,128)S(1)}, u32[]{:S(2)}, u32[]{:S(2)}) collective-permute-start(f32[736,128]{1,0:T(8,128)S(1)} %get-tuple-element.22.refs_2_.refs_0_.refs_5_), channel_id=1, source_target_pairs={{0,8},{4,12},{8,0},{12,4},{1,9},{5,13},{9,1},{13,5},{2,10},{6,14},... | collective-permute-start | bytes 1130504 | tf_op jit(solution)/shard_map/ppermute | solution.py:244
  8.7 1.6 %collective-permute-start.3 = (f32[736,128]{1,0:T(8,128)S(1)}, f32[736,128]{1,0:T(8,128)S(1)}, u32[]{:S(2)}, u32[]{:S(2)}) collective-permute-start(f32[736,128]{1,0:T(8,128)S(1)} %get-tuple-element.22.refs_2_.refs_0_.refs_5_), channel_id=1, source_target_pairs={{0,4},{4,0},{8,12},{12,8},{1,5},{5,1},{9,13},{13,9},{2,6},{6,2},{1... | collective-permute-start | bytes 1130504 | tf_op jit(solution)/shard_map/ppermute | solution.py:244
  10.3 21.5 %collective-permute-done.4.refs_2_ = f32[736,128]{1,0:T(8,128)S(1)} collective-permute-done((f32[736,128]{1,0:T(8,128)S(1)}, f32[736,128]{1,0:T(8,128)S(1)}, u32[]{:S(2)}, u32[]{:S(2)}) %collective-permute-start.4) | collective-permute-done | bytes 376864 | tf_op jit(solution)/shard_map/ppermute | solution.py:244
  31.8 1.1 dense0.1.refs_0_
  33.4 3.0 %collective-permute-done.9.refs_8_ = f32[4,128,128]{2,1,0:T(8,128)S(1)} collective-permute-done((f32[4,128,128]{2,1,0:T(8,128)S(1)}, f32[4,128,128]{2,1,0:T(8,128)S(1)}, u32[]{:S(2)}, u32[]{:S(2)}) %collective-permute-start.9) | collective-permute-done | bytes 262176 | tf_op jit(solution)/shard_map/ppermute | solution.py:244
  37.0 7.4 %collective-permute-done.5.refs_3_ = f32[736,128]{1,0:T(8,128)S(1)} collective-permute-done((f32[736,128]{1,0:T(8,128)S(1)}, f32[736,128]{1,0:T(8,128)S(1)}, u32[]{:S(2)}, u32[]{:S(2)}) %collective-permute-start.5) | collective-permute-done | bytes 376864 | tf_op jit(solution)/shard_map/ppermute | solution.py:244
  45.0 1.6 %collective-permute-start.17 = (f32[832,128]{1,0:T(8,128)S(1)}, f32[832,128]{1,0:T(8,128)S(1)}, u32[]{:S(2)}, u32[]{:S(2)}) collective-permute-start(f32[832,128]{1,0:T(8,128)S(1)} %ahead1.1.refs_0_), channel_id=1, source_target_pairs={{0,2},{1,3},{2,0},{3,1},{4,6},{5,7},{6,4},{7,5},{8,10},{9,11},{10,... | collective-permute-start | bytes 1277960 | tf_op jit(solution)/shard_map/ppermute | solution.py:244
  46.6 4.2 %collective-permute-done.6.refs_1_ = f32[256,128]{1,0:T(8,128)S(1)} collective-permute-done((f32[256,128]{1,0:T(8,128)S(1)}, f32[256,128]{1,0:T(8,128)S(1)}, u32[]{:S(2)}, u32[]{:S(2)}) %collective-permute-start.6) | collective-permute-done | bytes 131104 | tf_op jit(solution)/shard_map/ppermute | solution.py:244
  51.5 4.0 %collective-permute-done.10.refs_9_ = f32[4,128,128]{2,1,0:T(8,128)S(1)} collective-permute-done((f32[4,128,128]{2,1,0:T(8,128)S(1)}, f32[4,128,128]{2,1,0:T(8,128)S(1)}, u32[]{:S(2)}, u32[]{:S(2)}) %collective-permute-start.10) | collective-permute-done | bytes 262176 | tf_op jit(solution)/shard_map/ppermute | solution.py:244
  56.0 1.1 %collective-permute-done.7.refs_5_ = f32[512,128]{1,0:T(8,128)S(1)} collective-permute-done((f32[512,128]{1,0:T(8,128)S(1)}, f32[512,128]{1,0:T(8,128)S(1)}, u32[]{:S(2)}, u32[]{:S(2)}) %collective-permute-start.7) | collective-permute-done | bytes 262176 | tf_op jit(solution)/shard_map/ppermute | solution.py:244
  57.1 2.4 %prepare0.1.refs_2_.refs_0_.refs_4_ = f32[128,128]{1,0:T(8,128)S(1)} custom-call(f32[4,128,128]{2,1,0:T(8,128)S(1)} %dense0.1.refs_0_, f32[4,128,128]{2,1,0:T(8,128)S(1)} %collective-permute-done.refs_1_, f32[4,128,128]{2,1,0:T(8,128)S(1)} %collective-permute-done.1.refs_2_, f32[4,128,128]{2,1,0:T(8,128)S(1)} %collective-permute-done.2.refs_3_, ...), custom_call_target="tpu_custom_call" | custom-call | tf_op jit(solution)/shard_map/prepare0/pallas_call | solution.py:270
  60.4 1.3 %collective-permute-start.11 = (f32[128,128]{1,0:T(8,128)S(1)}, f32[128,128]{1,0:T(8,128)S(1)}, u32[]{:S(2)}, u32[]{:S(2)}) collective-permute-start(f32[128,128]{1,0:T(8,128)S(1)} %prepare0.1.refs_2_.refs_0_.refs_4_), channel_id=1, source_target_pairs={{0,4},{4,0},{8,12},{12,8},{1,5},{5,1},{9,13},{13,9},{2,6},{6,2},{1... | collective-permute-start | bytes 196616 | tf_op jit(solution)/shard_map/ppermute | solution.py:244
  61.7 2.8 %collective-permute-start.12 = (f32[128,128]{1,0:T(8,128)S(1)}, f32[128,128]{1,0:T(8,128)S(1)}, u32[]{:S(2)}, u32[]{:S(2)}) collective-permute-start(f32[128,128]{1,0:T(8,128)S(1)} %prepare0.1.refs_2_.refs_0_.refs_4_), channel_id=1, source_target_pairs={{0,8},{4,12},{8,0},{12,4},{1,9},{5,13},{9,1},{13,5},{2,10},{6,14},... | collective-permute-start | bytes 196616 | tf_op jit(solution)/shard_map/ppermute | solution.py:244
  65.5 2.7 %prepare1.1 = (f32[128,128]{1,0:T(8,128)S(1)}, bf16[1,256,512]{2,1,0:T(8,128)(2,1)S(1)}, bf16[1024,512]{1,0:T(8,128)(2,1)S(1)}) custom-call(f32[19,128,128]{2,1,0:T(8,128)S(1)} %dense.1.refs_0_, f32[19,128,128]{2,1,0:T(8,128)S(1)} %collective-permute-done.14.refs_1_, f32[19,128,128]{2,1,0:T(8,128)S(1)} %collective-permute-done.15.refs_2_, ...), custom_call_target="tpu_custom_call" | custom-call | tf_op jit(solution)/shard_map/prepare1/pallas_call | solution.py:270
  68.3 2.3 %collective-permute-done.13.refs_3_ = f32[128,128]{1,0:T(8,128)S(1)} collective-permute-done((f32[128,128]{1,0:T(8,128)S(1)}, f32[128,128]{1,0:T(8,128)S(1)}, u32[]{:S(2)}, u32[]{:S(2)}) %collective-permute-start.13) | collective-permute-done | bytes 65568 | tf_op jit(solution)/shard_map/ppermute | solution.py:244
  71.6 1.1 %collective-permute-done.22.refs_1_ = f32[896,128]{1,0:T(8,128)S(1)} collective-permute-done((f32[896,128]{1,0:T(8,128)S(1)}, f32[896,128]{1,0:T(8,128)S(1)}, u32[]{:S(2)}, u32[]{:S(2)}) %collective-permute-start.22) | collective-permute-done | bytes 458784 | tf_op jit(solution)/shard_map/ppermute | solution.py:244
  73.4 1.3 %collective-permute-start.19 = (f32[128,128]{1,0:T(8,128)S(1)}, f32[128,128]{1,0:T(8,128)S(1)}, u32[]{:S(2)}, u32[]{:S(2)}) collective-permute-start(f32[128,128]{1,0:T(8,128)S(1)} %get-tuple-element.27.refs_2_.refs_0_.refs_4_), channel_id=1, source_target_pairs={{0,4},{4,0},{8,12},{12,8},{1,5},{5,1},{9,13},{13,9},{2,6},{6,2},{1... | collective-permute-start | bytes 196616 | tf_op jit(solution)/shard_map/ppermute | solution.py:244
  74.7 2.8 %collective-permute-start.20 = (f32[128,128]{1,0:T(8,128)S(1)}, f32[128,128]{1,0:T(8,128)S(1)}, u32[]{:S(2)}, u32[]{:S(2)}) collective-permute-start(f32[128,128]{1,0:T(8,128)S(1)} %get-tuple-element.27.refs_2_.refs_0_.refs_4_), channel_id=1, source_target_pairs={{0,8},{4,12},{8,0},{12,4},{1,9},{5,13},{9,1},{13,5},{2,10},{6,14},... | collective-permute-start | bytes 196616 | tf_op jit(solution)/shard_map/ppermute | solution.py:244
  78.3 3.1 %prepare2.1 = (f32[128,128]{1,0:T(8,128)S(1)}, bf16[1,256,512]{2,1,0:T(8,128)(2,1)S(1)}, bf16[1024,512]{1,0:T(8,128)(2,1)S(1)}) custom-call(f32[19,128,128]{2,1,0:T(8,128)S(1)} %dense.1.refs_0_, f32[19,128,128]{2,1,0:T(8,128)S(1)} %collective-permute-done.14.refs_1_, f32[19,128,128]{2,1,0:T(8,128)S(1)} %collective-permute-done.15.refs_2_, ...), custom_call_target="tpu_custom_call" | custom-call | tf_op jit(solution)/shard_map/prepare2/pallas_call | solution.py:270
  81.4 2.2 %collective-permute-done.21.refs_3_ = f32[128,128]{1,0:T(8,128)S(1)} collective-permute-done((f32[128,128]{1,0:T(8,128)S(1)}, f32[128,128]{1,0:T(8,128)S(1)}, u32[]{:S(2)}, u32[]{:S(2)}) %collective-permute-start.21) | collective-permute-done | bytes 65568 | tf_op jit(solution)/shard_map/ppermute | solution.py:244
  84.6 1.9 %collective-permute-done.27.refs_1_ = f32[960,128]{1,0:T(8,128)S(1)} collective-permute-done((f32[960,128]{1,0:T(8,128)S(1)}, f32[960,128]{1,0:T(8,128)S(1)}, u32[]{:S(2)}, u32[]{:S(2)}) %collective-permute-start.27) | collective-permute-done | bytes 491552 | tf_op jit(solution)/shard_map/ppermute | solution.py:244
  86.7 1.4 %collective-permute-start.24 = (f32[128,128]{1,0:T(8,128)S(1)}, f32[128,128]{1,0:T(8,128)S(1)}, u32[]{:S(2)}, u32[]{:S(2)}) collective-permute-start(f32[128,128]{1,0:T(8,128)S(1)} %get-tuple-element.32.refs_2_.refs_0_), channel_id=1, source_target_pairs={{0,4},{4,0},{8,12},{12,8},{1,5},{5,1},{9,13},{13,9},{2,6},{6,2},{1... | collective-permute-start | bytes 196616 | tf_op jit(solution)/shard_map/ppermute | solution.py:244
  88.1 2.7 %collective-permute-start.25 = (f32[128,128]{1,0:T(8,128)S(1)}, f32[128,128]{1,0:T(8,128)S(1)}, u32[]{:S(2)}, u32[]{:S(2)}) collective-permute-start(f32[128,128]{1,0:T(8,128)S(1)} %get-tuple-element.32.refs_2_.refs_0_), channel_id=1, source_target_pairs={{0,8},{4,12},{8,0},{12,4},{1,9},{5,13},{9,1},{13,5},{2,10},{6,14},... | collective-permute-start | bytes 196616 | tf_op jit(solution)/shard_map/ppermute | solution.py:244
  91.6 3.5 %prepare3.1 = (f32[128,128]{1,0:T(8,128)S(1)}, bf16[2,256,512]{2,1,0:T(8,128)(2,1)S(1)}, bf16[1024,512]{1,0:T(8,128)(2,1)S(1)}) custom-call(f32[19,128,128]{2,1,0:T(8,128)S(1)} %dense.1.refs_0_, f32[19,128,128]{2,1,0:T(8,128)S(1)} %collective-permute-done.14.refs_1_, f32[19,128,128]{2,1,0:T(8,128)S(1)} %collective-permute-done.15.refs_2_, ...), custom_call_target="tpu_custom_call" | custom-call | tf_op jit(solution)/shard_map/prepare3/pallas_call | solution.py:270
  95.1 1.8 %collective-permute-done.26.refs_3_ = f32[128,128]{1,0:T(8,128)S(1)} collective-permute-done((f32[128,128]{1,0:T(8,128)S(1)}, f32[128,128]{1,0:T(8,128)S(1)}, u32[]{:S(2)}, u32[]{:S(2)}) %collective-permute-start.26) | collective-permute-done | bytes 65568 | tf_op jit(solution)/shard_map/ppermute | solution.py:244
  97.9 1.7 %collective-permute-start.29 = (f32[128,128]{1,0:T(8,128)S(1)}, f32[128,128]{1,0:T(8,128)S(1)}, u32[]{:S(2)}, u32[]{:S(2)}) collective-permute-start(f32[128,128]{1,0:T(8,128)S(1)} %get-tuple-element.37.refs_0_), channel_id=1, source_target_pairs={{0,4},{4,0},{8,12},{12,8},{1,5},{5,1},{9,13},{13,9},{2,6},{6,2},{1... | collective-permute-start | bytes 196616 | tf_op jit(solution)/shard_map/ppermute | solution.py:244
  99.6 1.7 %collective-permute-start.30 = (f32[128,128]{1,0:T(8,128)S(1)}, f32[128,128]{1,0:T(8,128)S(1)}, u32[]{:S(2)}, u32[]{:S(2)}) collective-permute-start(f32[128,128]{1,0:T(8,128)S(1)} %get-tuple-element.37.refs_0_), channel_id=1, source_target_pairs={{0,8},{4,12},{8,0},{12,4},{1,9},{5,13},{9,1},{13,5},{2,10},{6,14},... | collective-permute-start | bytes 196616 | tf_op jit(solution)/shard_map/ppermute | solution.py:244
  101.3 1.2 %collective-permute-start.31 = (f32[128,128]{1,0:T(8,128)S(1)}, f32[128,128]{1,0:T(8,128)S(1)}, u32[]{:S(2)}, u32[]{:S(2)}) collective-permute-start(f32[128,128]{1,0:T(8,128)S(1)} %get-tuple-element.37.refs_0_), channel_id=1, source_target_pairs={{0,12},{4,8},{8,4},{12,0},{1,13},{5,9},{9,5},{13,1},{2,14},{6,10},... | collective-permute-start | bytes 196616 | tf_op jit(solution)/shard_map/ppermute | solution.py:244
  102.4 5.3 %collective-permute-done.30.refs_2_ = f32[128,128]{1,0:T(8,128)S(1)} collective-permute-done((f32[128,128]{1,0:T(8,128)S(1)}, f32[128,128]{1,0:T(8,128)S(1)}, u32[]{:S(2)}, u32[]{:S(2)}) %collective-permute-start.30) | collective-permute-done | bytes 65568 | tf_op jit(solution)/shard_map/ppermute | solution.py:244
  (55 shorter events, 11.3 us)
Async XLA Ops:
  2.8 48.1 %collective-permute-start.15 = (f32[19,128,128]{2,1,0:T(8,128)S(1)}, f32[19,128,128]{2,1,0:T(8,128)S(1)}, u32[]{:S(2)}, u32[]{:S(2)}) collective-permute-start(f32[19,128,128]{2,1,0:T(8,128)S(1)} %dense.1.refs_0_), channel_id=1, source_target_pairs={{0,2},{1,3},{2,0},{3,1},{4,6},{5,7},{6,4},{7,5},{8,10},{9,11},{10,... | collective-permute-start | bytes 3735560 | tf_op jit(solution)/shard_map/ppermute | solution.py:244
  5.8 26.0 %collective-permute-start.4 = (f32[736,128]{1,0:T(8,128)S(1)}, f32[736,128]{1,0:T(8,128)S(1)}, u32[]{:S(2)}, u32[]{:S(2)}) collective-permute-start(f32[736,128]{1,0:T(8,128)S(1)} %get-tuple-element.22.refs_2_.refs_0_.refs_5_), channel_id=1, source_target_pairs={{0,8},{4,12},{8,0},{12,4},{1,9},{5,13},{9,1},{13,5},{2,10},{6,14},... | collective-permute-start | bytes 1130504 | tf_op jit(solution)/shard_map/ppermute | solution.py:244
  8.4 27.9 %collective-permute-start.9 = (f32[4,128,128]{2,1,0:T(8,128)S(1)}, f32[4,128,128]{2,1,0:T(8,128)S(1)}, u32[]{:S(2)}, u32[]{:S(2)}) collective-permute-start(f32[4,128,128]{2,1,0:T(8,128)S(1)} %get-tuple-element.23.refs_6_), channel_id=1, source_target_pairs={{0,8},{4,12},{8,0},{12,4},{1,9},{5,13},{9,1},{13,5},{2,10},{6,14},... | collective-permute-start | bytes 786440 | tf_op jit(solution)/shard_map/ppermute | solution.py:244
  8.7 27.6 %collective-permute-start.3 = (f32[736,128]{1,0:T(8,128)S(1)}, f32[736,128]{1,0:T(8,128)S(1)}, u32[]{:S(2)}, u32[]{:S(2)}) collective-permute-start(f32[736,128]{1,0:T(8,128)S(1)} %get-tuple-element.22.refs_2_.refs_0_.refs_5_), channel_id=1, source_target_pairs={{0,4},{4,0},{8,12},{12,8},{1,5},{5,1},{9,13},{13,9},{2,6},{6,2},{1... | collective-permute-start | bytes 1130504 | tf_op jit(solution)/shard_map/ppermute | solution.py:244
  31.8 12.6 %collective-permute-start.5 = (f32[736,128]{1,0:T(8,128)S(1)}, f32[736,128]{1,0:T(8,128)S(1)}, u32[]{:S(2)}, u32[]{:S(2)}) collective-permute-start(f32[736,128]{1,0:T(8,128)S(1)} %collective-permute-done.4.refs_2_), channel_id=1, source_target_pairs={{0,4},{4,0},{8,12},{12,8},{1,5},{5,1},{9,13},{13,9},{2,6},{6,2},{1... | collective-permute-start | bytes 1130504 | tf_op jit(solution)/shard_map/ppermute | solution.py:244
  32.8 11.6 %collective-permute-start.1 = (f32[4,128,128]{2,1,0:T(8,128)S(1)}, f32[4,128,128]{2,1,0:T(8,128)S(1)}, u32[]{:S(2)}, u32[]{:S(2)}) collective-permute-start(f32[4,128,128]{2,1,0:T(8,128)S(1)} %dense0.1.refs_0_), channel_id=1, source_target_pairs={{0,2},{1,3},{2,0},{3,1},{4,6},{5,7},{6,4},{7,5},{8,10},{9,11},{10,... | collective-permute-start | bytes 786440 | tf_op jit(solution)/shard_map/ppermute | solution.py:244
  36.3 8.7 %collective-permute-start = (f32[4,128,128]{2,1,0:T(8,128)S(1)}, f32[4,128,128]{2,1,0:T(8,128)S(1)}, u32[]{:S(2)}, u32[]{:S(2)}) collective-permute-start(f32[4,128,128]{2,1,0:T(8,128)S(1)} %dense0.1.refs_0_), channel_id=1, source_target_pairs={{0,1},{1,0},{2,3},{3,2},{4,5},{5,4},{6,7},{7,6},{8,9},{9,8},{10,11... | collective-permute-start | bytes 786440 | tf_op jit(solution)/shard_map/ppermute | solution.py:244
  36.3 15.1 %collective-permute-start.8 = (f32[4,128,128]{2,1,0:T(8,128)S(1)}, f32[4,128,128]{2,1,0:T(8,128)S(1)}, u32[]{:S(2)}, u32[]{:S(2)}) collective-permute-start(f32[4,128,128]{2,1,0:T(8,128)S(1)} %get-tuple-element.23.refs_6_), channel_id=1, source_target_pairs={{0,4},{4,0},{8,12},{12,8},{1,5},{5,1},{9,13},{13,9},{2,6},{6,2},{1... | collective-permute-start | bytes 786440 | tf_op jit(solution)/shard_map/ppermute | solution.py:244
  44.4 11.1 %collective-permute-start.10 = (f32[4,128,128]{2,1,0:T(8,128)S(1)}, f32[4,128,128]{2,1,0:T(8,128)S(1)}, u32[]{:S(2)}, u32[]{:S(2)}) collective-permute-start(f32[4,128,128]{2,1,0:T(8,128)S(1)} %collective-permute-done.9.refs_8_), channel_id=1, source_target_pairs={{0,4},{4,0},{8,12},{12,8},{1,5},{5,1},{9,13},{13,9},{2,6},{6,2},{1... | collective-permute-start | bytes 786440 | tf_op jit(solution)/shard_map/ppermute | solution.py:244
  44.4 6.4 %collective-permute-start.6 = (f32[256,128]{1,0:T(8,128)S(1)}, f32[256,128]{1,0:T(8,128)S(1)}, u32[]{:S(2)}, u32[]{:S(2)}) collective-permute-start(f32[256,128]{1,0:T(8,128)S(1)} %ahead0.1.refs_0_), channel_id=1, source_target_pairs={{0,2},{1,3},{2,0},{3,1},{4,6},{5,7},{6,4},{7,5},{8,10},{9,11},{10,... | collective-permute-start | bytes 393224 | tf_op jit(solution)/shard_map/ppermute | solution.py:244
  45.0 14.5 %collective-permute-start.17 = (f32[832,128]{1,0:T(8,128)S(1)}, f32[832,128]{1,0:T(8,128)S(1)}, u32[]{:S(2)}, u32[]{:S(2)}) collective-permute-start(f32[832,128]{1,0:T(8,128)S(1)} %ahead1.1.refs_0_), channel_id=1, source_target_pairs={{0,2},{1,3},{2,0},{3,1},{4,6},{5,7},{6,4},{7,5},{8,10},{9,11},{10,... | collective-permute-start | bytes 1277960 | tf_op jit(solution)/shard_map/ppermute | solution.py:244
  50.9 10.8 %collective-permute-start.14 = (f32[19,128,128]{2,1,0:T(8,128)S(1)}, f32[19,128,128]{2,1,0:T(8,128)S(1)}, u32[]{:S(2)}, u32[]{:S(2)}) collective-permute-start(f32[19,128,128]{2,1,0:T(8,128)S(1)} %dense.1.refs_0_), channel_id=1, source_target_pairs={{0,1},{1,0},{2,3},{3,2},{4,5},{5,4},{6,7},{7,6},{8,9},{9,8},{10,11... | collective-permute-start | bytes 3735560 | tf_op jit(solution)/shard_map/ppermute | solution.py:244
  50.9 14.6 %collective-permute-start.16 = (f32[19,128,128]{2,1,0:T(8,128)S(1)}, f32[19,128,128]{2,1,0:T(8,128)S(1)}, u32[]{:S(2)}, u32[]{:S(2)}) collective-permute-start(f32[19,128,128]{2,1,0:T(8,128)S(1)} %collective-permute-done.15.refs_2_), channel_id=1, source_target_pairs={{0,1},{1,0},{2,3},{3,2},{4,5},{5,4},{6,7},{7,6},{8,9},{9,8},{10,11... | collective-permute-start | bytes 3735560 | tf_op jit(solution)/shard_map/ppermute | solution.py:244
  51.4 4.6 %collective-permute-start.2 = (f32[4,128,128]{2,1,0:T(8,128)S(1)}, f32[4,128,128]{2,1,0:T(8,128)S(1)}, u32[]{:S(2)}, u32[]{:S(2)}) collective-permute-start(f32[4,128,128]{2,1,0:T(8,128)S(1)} %collective-permute-done.1.refs_2_), channel_id=1, source_target_pairs={{0,1},{1,0},{2,3},{3,2},{4,5},{5,4},{6,7},{7,6},{8,9},{9,8},{10,11... | collective-permute-start | bytes 786440 | tf_op jit(solution)/shard_map/ppermute | solution.py:244
  55.5 1.5 %collective-permute-start.7 = (f32[512,128]{1,0:T(8,128)S(1)}, f32[512,128]{1,0:T(8,128)S(1)}, u32[]{:S(2)}, u32[]{:S(2)}) collective-permute-start(f32[512,128]{1,0:T(8,128)S(1)} %aheads0.1.refs_4_), channel_id=1, source_target_pairs={{0,1},{1,0},{2,3},{3,2},{4,5},{5,4},{6,7},{7,6},{8,9},{9,8},{10,11... | collective-permute-start | bytes 786440 | tf_op jit(solution)/shard_map/ppermute | solution.py:244
  59.6 4.9 %collective-permute-start.18 = (f32[1664,128]{1,0:T(8,128)S(1)}, f32[1664,128]{1,0:T(8,128)S(1)}, u32[]{:S(2)}, u32[]{:S(2)}) collective-permute-start(f32[1664,128]{1,0:T(8,128)S(1)} %aheads1.1.refs_4_), channel_id=1, source_target_pairs={{0,1},{1,0},{2,3},{3,2},{4,5},{5,4},{6,7},{7,6},{8,9},{9,8},{10,11... | collective-permute-start | bytes 2555912 | tf_op jit(solution)/shard_map/ppermute | solution.py:244
  59.8 12.9 %collective-permute-start.22 = (f32[896,128]{1,0:T(8,128)S(1)}, f32[896,128]{1,0:T(8,128)S(1)}, u32[]{:S(2)}, u32[]{:S(2)}) collective-permute-start(f32[896,128]{1,0:T(8,128)S(1)} %ahead2.1.refs_0_), channel_id=1, source_target_pairs={{0,2},{1,3},{2,0},{3,1},{4,6},{5,7},{6,4},{7,5},{8,10},{9,11},{10,... | collective-permute-start | bytes 1376264 | tf_op jit(solution)/shard_map/ppermute | solution.py:244
  60.4 7.9 %collective-permute-start.11 = (f32[128,128]{1,0:T(8,128)S(1)}, f32[128,128]{1,0:T(8,128)S(1)}, u32[]{:S(2)}, u32[]{:S(2)}) collective-permute-start(f32[128,128]{1,0:T(8,128)S(1)} %prepare0.1.refs_2_.refs_0_.refs_4_), channel_id=1, source_target_pairs={{0,4},{4,0},{8,12},{12,8},{1,5},{5,1},{9,13},{13,9},{2,6},{6,2},{1... | collective-permute-start | bytes 196616 | tf_op jit(solution)/shard_map/ppermute | solution.py:244
  61.7 6.6 %collective-permute-start.12 = (f32[128,128]{1,0:T(8,128)S(1)}, f32[128,128]{1,0:T(8,128)S(1)}, u32[]{:S(2)}, u32[]{:S(2)}) collective-permute-start(f32[128,128]{1,0:T(8,128)S(1)} %prepare0.1.refs_2_.refs_0_.refs_4_), channel_id=1, source_target_pairs={{0,8},{4,12},{8,0},{12,4},{1,9},{5,13},{9,1},{13,5},{2,10},{6,14},... | collective-permute-start | bytes 196616 | tf_op jit(solution)/shard_map/ppermute | solution.py:244
  64.5 6.1 %collective-permute-start.13 = (f32[128,128]{1,0:T(8,128)S(1)}, f32[128,128]{1,0:T(8,128)S(1)}, u32[]{:S(2)}, u32[]{:S(2)}) collective-permute-start(f32[128,128]{1,0:T(8,128)S(1)} %prepare0.1.refs_2_.refs_0_.refs_4_), channel_id=1, source_target_pairs={{0,12},{4,8},{8,4},{12,0},{1,13},{5,9},{9,5},{13,1},{2,14},{6,10},... | collective-permute-start | bytes 196616 | tf_op jit(solution)/shard_map/ppermute | solution.py:244
  72.7 5.6 %collective-permute-start.23 = (f32[1792,128]{1,0:T(8,128)S(1)}, f32[1792,128]{1,0:T(8,128)S(1)}, u32[]{:S(2)}, u32[]{:S(2)}) collective-permute-start(f32[1792,128]{1,0:T(8,128)S(1)} %aheads2.1.refs_4_), channel_id=1, source_target_pairs={{0,1},{1,0},{2,3},{3,2},{4,5},{5,4},{6,7},{7,6},{8,9},{9,8},{10,11... | collective-permute-start | bytes 2752520 | tf_op jit(solution)/shard_map/ppermute | solution.py:244
  72.8 13.7 %collective-permute-start.27 = (f32[960,128]{1,0:T(8,128)S(1)}, f32[960,128]{1,0:T(8,128)S(1)}, u32[]{:S(2)}, u32[]{:S(2)}) collective-permute-start(f32[960,128]{1,0:T(8,128)S(1)} %ahead3.1.refs_0_), channel_id=1, source_target_pairs={{0,2},{1,3},{2,0},{3,1},{4,6},{5,7},{6,4},{7,5},{8,10},{9,11},{10,... | collective-permute-start | bytes 1474568 | tf_op jit(solution)/shard_map/ppermute | solution.py:244
  73.4 8.0 %collective-permute-start.19 = (f32[128,128]{1,0:T(8,128)S(1)}, f32[128,128]{1,0:T(8,128)S(1)}, u32[]{:S(2)}, u32[]{:S(2)}) collective-permute-start(f32[128,128]{1,0:T(8,128)S(1)} %get-tuple-element.27.refs_2_.refs_0_.refs_4_), channel_id=1, source_target_pairs={{0,4},{4,0},{8,12},{12,8},{1,5},{5,1},{9,13},{13,9},{2,6},{6,2},{1... | collective-permute-start | bytes 196616 | tf_op jit(solution)/shard_map/ppermute | solution.py:244
  74.7 6.7 %collective-permute-start.20 = (f32[128,128]{1,0:T(8,128)S(1)}, f32[128,128]{1,0:T(8,128)S(1)}, u32[]{:S(2)}, u32[]{:S(2)}) collective-permute-start(f32[128,128]{1,0:T(8,128)S(1)} %get-tuple-element.27.refs_2_.refs_0_.refs_4_), channel_id=1, source_target_pairs={{0,8},{4,12},{8,0},{12,4},{1,9},{5,13},{9,1},{13,5},{2,10},{6,14},... | collective-permute-start | bytes 196616 | tf_op jit(solution)/shard_map/ppermute | solution.py:244
  77.5 6.1 %collective-permute-start.21 = (f32[128,128]{1,0:T(8,128)S(1)}, f32[128,128]{1,0:T(8,128)S(1)}, u32[]{:S(2)}, u32[]{:S(2)}) collective-permute-start(f32[128,128]{1,0:T(8,128)S(1)} %get-tuple-element.27.refs_2_.refs_0_.refs_4_), channel_id=1, source_target_pairs={{0,12},{4,8},{8,4},{12,0},{1,13},{5,9},{9,5},{13,1},{2,14},{6,10},... | collective-permute-start | bytes 196616 | tf_op jit(solution)/shard_map/ppermute | solution.py:244
  86.6 5.0 %collective-permute-start.28 = (f32[1920,128]{1,0:T(8,128)S(1)}, f32[1920,128]{1,0:T(8,128)S(1)}, u32[]{:S(2)}, u32[]{:S(2)}) collective-permute-start(f32[1920,128]{1,0:T(8,128)S(1)} %aheads3.1.refs_4_), channel_id=1, source_target_pairs={{0,1},{1,0},{2,3},{3,2},{4,5},{5,4},{6,7},{7,6},{8,9},{9,8},{10,11... | collective-permute-start | bytes 2949128 | tf_op jit(solution)/shard_map/ppermute | solution.py:244
  86.7 8.4 %collective-permute-start.24 = (f32[128,128]{1,0:T(8,128)S(1)}, f32[128,128]{1,0:T(8,128)S(1)}, u32[]{:S(2)}, u32[]{:S(2)}) collective-permute-start(f32[128,128]{1,0:T(8,128)S(1)} %get-tuple-element.32.refs_2_.refs_0_), channel_id=1, source_target_pairs={{0,4},{4,0},{8,12},{12,8},{1,5},{5,1},{9,13},{13,9},{2,6},{6,2},{1... | collective-permute-start | bytes 196616 | tf_op jit(solution)/shard_map/ppermute | solution.py:244
  88.1 7.0 %collective-permute-start.25 = (f32[128,128]{1,0:T(8,128)S(1)}, f32[128,128]{1,0:T(8,128)S(1)}, u32[]{:S(2)}, u32[]{:S(2)}) collective-permute-start(f32[128,128]{1,0:T(8,128)S(1)} %get-tuple-element.32.refs_2_.refs_0_), channel_id=1, source_target_pairs={{0,8},{4,12},{8,0},{12,4},{1,9},{5,13},{9,1},{13,5},{2,10},{6,14},... | collective-permute-start | bytes 196616 | tf_op jit(solution)/shard_map/ppermute | solution.py:244
  90.8 6.1 %collective-permute-start.26 = (f32[128,128]{1,0:T(8,128)S(1)}, f32[128,128]{1,0:T(8,128)S(1)}, u32[]{:S(2)}, u32[]{:S(2)}) collective-permute-start(f32[128,128]{1,0:T(8,128)S(1)} %get-tuple-element.32.refs_2_.refs_0_), channel_id=1, source_target_pairs={{0,12},{4,8},{8,4},{12,0},{1,13},{5,9},{9,5},{13,1},{2,14},{6,10},... | collective-permute-start | bytes 196616 | tf_op jit(solution)/shard_map/ppermute | solution.py:244
  97.9 4.6 %collective-permute-start.29 = (f32[128,128]{1,0:T(8,128)S(1)}, f32[128,128]{1,0:T(8,128)S(1)}, u32[]{:S(2)}, u32[]{:S(2)}) collective-permute-start(f32[128,128]{1,0:T(8,128)S(1)} %get-tuple-element.37.refs_0_), channel_id=1, source_target_pairs={{0,4},{4,0},{8,12},{12,8},{1,5},{5,1},{9,13},{13,9},{2,6},{6,2},{1... | collective-permute-start | bytes 196616 | tf_op jit(solution)/shard_map/ppermute | solution.py:244
  99.6 8.1 %collective-permute-start.30 = (f32[128,128]{1,0:T(8,128)S(1)}, f32[128,128]{1,0:T(8,128)S(1)}, u32[]{:S(2)}, u32[]{:S(2)}) collective-permute-start(f32[128,128]{1,0:T(8,128)S(1)} %get-tuple-element.37.refs_0_), channel_id=1, source_target_pairs={{0,8},{4,12},{8,0},{12,4},{1,9},{5,13},{9,1},{13,5},{2,10},{6,14},... | collective-permute-start | bytes 196616 | tf_op jit(solution)/shard_map/ppermute | solution.py:244
  101.3 6.4 %collective-permute-start.31 = (f32[128,128]{1,0:T(8,128)S(1)}, f32[128,128]{1,0:T(8,128)S(1)}, u32[]{:S(2)}, u32[]{:S(2)}) collective-permute-start(f32[128,128]{1,0:T(8,128)S(1)} %get-tuple-element.37.refs_0_), channel_id=1, source_target_pairs={{0,12},{4,8},{8,4},{12,0},{1,13},{5,9},{9,5},{13,1},{2,14},{6,10},... | collective-permute-start | bytes 196616 | tf_op jit(solution)/shard_map/ppermute | solution.py:244
  (2 other events, 14.0 us)
